TPU v7x, 32 devices: a whole 2x2x4 slice. The times are simulated.
32 devices in a mesh: row: 4 (over y, core), col: 8 (over z, x).
Axes of the slice: x: 2, y: 2, z: 4, core: 2. Of those that a mesh axis runs over, the one named last changes fastest.
Arguments:
- hidden: bfloat16 [512, 24576], P(None, 'row'), may hold values from -6 to 6
- down_weight: bfloat16 [24576, 6144], P('row', 'col'), may hold values from -0.0390625 to 0.0390625
- residual: bfloat16 [512, 6144], P('row', 'col'), may hold values from -260 to 260
- gain: bfloat16 [6144], P('col'), may hold values from 0.099609375 to 1.8984375
- qk_weight: bfloat16 [6144, 12288], P(None, 'col'), may hold values from -0.078125 to 0.078125
Outputs:
- stream: bfloat16 [512, 6144], P('row', 'col')
- queries_keys: bfloat16 [512, 12288], P('row', 'col')
All inputs are finite; a program needn't handle non-finite values.
Results may differ from a plain program's by a relative error of at most 0.015.
Values may be sent and summed in bfloat16 or wider, within the bound.
No kernel may reach another device: no remote copies, remote signals or barrier semaphores. Data moves between devices by JAX's collectives and lax.ppermute only.
A program may use at most 64 MiB of HBM per device.

v0:
```python
import jax
import jax.numpy as jnp
from jax import lax
from jax.sharding import PartitionSpec as P


def joined(value, axis, join):
    pieces = jax.tree.map(lambda part: lax.all_gather(part, axis), value)
    head = jax.tree.map(lambda part: part[0], pieces)
    tail = jax.tree.map(lambda part: part[1:], pieces)
    total, _ = lax.scan(lambda total, section: (join(total, section), None), head, tail)
    return total


def combine_moments(first, second):
    count_a, mean_a, spread_a = first
    count_b, mean_b, spread_b = second
    count = count_a + count_b
    delta = mean_b - mean_a
    mean = mean_a + delta * count_b / count
    spread = spread_a + spread_b + delta * delta * count_a * count_b / count
    return (count, mean, spread)


def per_device(hidden, down_weight, residual, gain, qk_weight):
    tok_rows = residual.shape[0]
    mlp = lax.psum_scatter(
        jnp.dot(hidden, down_weight, preferred_element_type=jnp.float32).astype(jnp.bfloat16),
        "row",
        scatter_dimension=0,
        tiled=True,
    ).astype(jnp.float32)
    stream = (residual.astype(jnp.float32) + mlp).astype(jnp.bfloat16)
    values = stream.astype(jnp.float32)
    local_width = values.shape[1]
    local_mean = jnp.mean(values, axis=1)
    local_dev = values - local_mean[:, None]
    local_spread = jnp.sum(local_dev * local_dev, axis=1)
    counts = jnp.full((tok_rows,), float(local_width), jnp.float32)
    total_count, mean_flat, spread_flat = joined(
        (counts, local_mean, local_spread), "col", combine_moments
    )
    mean = mean_flat[:, None]
    var = (spread_flat / total_count)[:, None]
    normed = ((values - mean) / jnp.sqrt(var + 1e-06) * gain.astype(jnp.float32)[None, :]).astype(
        jnp.bfloat16
    )
    product = jnp.dot(
        lax.all_gather(normed, "col", axis=1, tiled=True),
        qk_weight,
        preferred_element_type=jnp.float32,
    )
    return (stream, product.astype(jnp.bfloat16))


def solution(mesh):
    placed = (P(None, "row"), P("row", "col"), P("row", "col"), P("col"), P(None, "col"))
    return jax.shard_map(
        per_device,
        mesh=mesh,
        in_specs=placed,
        out_specs=(P("row", "col"), P("row", "col")),
        check_vma=False,
    )
```

profile of v0, /device:TPU:0, one launch (start us, length us, event | category | flops | bytes accessed | tf_op | source)
XLA Modules:
  0.0 142.6 jit_solution(18174983322066662123)
XLA Ops:
  7.2 0.0 copy-start.2
  7.2 0.0 copy-start.1
  7.2 0.0 reduce-scatter.2.cloned.1.call-start
  7.2 10.7 %convolution_convert_fusion.1 = bf16[512,768]{1,0:T(8,128)(2,1)} fusion(bf16[512,6144]{1,0:T(8,128)(2,1)} %param.7, bf16[6144,768]{1,0:T(8,128)(2,1)} %param.8), kind=kOutput, calls=%fused_computation.7 | convolution fusion | flops 4832231424 | bytes 16515072 | tf_op jit(solution)/shard_map/dot_general | solution.py:28
  17.9 0.0 reduce-scatter.2.cloned.1.call-update
  17.9 0.0 all-gather.6.cloned.1.call-start
  18.0 0.0 copy-done.2
  18.0 26.0 %reduce-scatter.2.cloned.1.call-done = bf16[128,768]{1,0:T(8,128)(2,1)} async-done(((bf16[512,768]{1,0:T(8,128)(2,1)}), bf16[128,768]{1,0:T(8,128)(2,1)}) %reduce-scatter.2.cloned.1.call-update) | async-done | bytes 196624 | tf_op jit(solution)/shard_map/reduce_scatter | solution.py:27
  44.1 0.0 copy-done.1
  44.1 1.1 convert_reduce_fusion
  45.1 0.0 copy-start
  45.1 0.2 fusion.2
  45.3 20.4 %all-gather.3 = f32[8,1,128]{2,1,0:T(1,128)S(1)} all-gather(f32[1,1,128]{2,1,0:T(1,128)S(1)} %bitcast.35), channel_id=3, replica_groups=mesh['row'=4,'col'=8] {'col'}, dimensions={0}, use_global_device_ids=true | all-gather | bytes 4608 | tf_op jit(solution)/shard_map/all_gather | solution.py:8
  65.7 16.1 %all-gather.2 = f32[8,1,128]{2,1,0:T(1,128)S(1)} all-gather(f32[1,1,128]{2,1,0:T(1,128)S(1)} %get-tuple-element.100), channel_id=2, replica_groups=mesh['row'=4,'col'=8] {'col'}, dimensions={0}, use_global_device_ids=true | all-gather | bytes 4608 | tf_op jit(solution)/shard_map/all_gather | solution.py:8
  81.9 0.4 while.16
  82.3 0.8 fusion.5
  83.2 0.0 all-gather.6.cloned.1.call-update
  83.2 42.4 %all-gather.6.cloned.1.call-done = bf16[128,6144]{1,0:T(8,128)(2,1)} async-done(((bf16[128,768]{1,0:T(8,128)(2,1)}), bf16[128,6144]{1,0:T(8,128)(2,1)}) %all-gather.6.cloned.1.call-update) | async-done | bytes 1572880 | tf_op jit(solution)/shard_map/all_gather | solution.py:49
  125.6 10.2 %convolution_convert_fusion = bf16[128,1536]{1,0:T(8,128)(2,1)} fusion(bf16[128,6144]{1,0:T(8,128)(2,1)} %all-gather.6.cloned.1.call-done, bf16[6144,1536]{1,0:T(8,128)(2,1)} %param.11), kind=kOutput, calls=%fused_computation.6 | convolution fusion | flops 2416115712 | bytes 20840448 | tf_op jit(solution)/shard_map/dot_general | solution.py:48
  135.8 0.0 copy-done
  (24 shorter events, 0.3 us)
Async XLA Ops:
  7.2 10.8 %copy-start.2 = (bf16[768]{0:T(1024)(128)(2,1)S(1)}, bf16[768]{0:T(1024)(128)(2,1)}, u32[]{:S(2)}) copy-start(bf16[768]{0:T(1024)(128)(2,1)} %param.10) | copy-start | bytes 4612
  7.2 36.9 %copy-start.1 = (bf16[128,768]{1,0:T(8,128)(2,1)S(1)}, bf16[128,768]{1,0:T(8,128)(2,1)}, u32[]{:S(2)}) copy-start(bf16[128,768]{1,0:T(8,128)(2,1)} %param.9) | copy-start | bytes 589828
  7.2 36.9 %reduce-scatter.2.cloned.1.call-start = ((), (), s32[]{:S(2)}) async-start(), calls=%async_computation.1 | async-start | bytes 983040 | tf_op jit(solution)/shard_map/reduce_scatter | solution.py:27
  17.9 107.7 %all-gather.6.cloned.1.call-start = ((), (), s32[]{:S(2)}) async-start(), calls=%async_computation.2 | async-start | bytes 1769472 | tf_op jit(solution)/shard_map/all_gather | solution.py:49
  45.1 90.7 %copy-start = (bf16[128,768]{1,0:T(8,128)(2,1)}, bf16[128,768]{1,0:T(8,128)(2,1)S(1)}, u32[]{:S(2)}) copy-start(bf16[128,768]{1,0:T(8,128)(2,1)S(1)} %get-tuple-element.98) | copy-start | bytes 589828
Sparse Core Ops, SparseCore 0:
  18.1 25.9 reduce-scatter.1
  83.3 42.2 all-gather.5
where the time goes:
time: 143 us
  waiting for transfers between devices  68.5 us (48%)
  blocking collectives  36.5 us (26%)
  matrix products  20.9 us (15%)
  between operations  14.1 us (10%)
  other arithmetic  2.42 us (2%)
    all_gather x1, waiting for transfers between devices, per_device(): lax.all_gather(normed, 'col', axis=1, tiled=True)  42.4 us
    all_gather x2, blocking collectives, joined(): pieces = jax.tree.map(lambda part: lax.all_gather(part, axis), value)  36.5 us
    reduce_scatter x1, waiting for transfers between devices, per_device(): lax.psum_scatter(jnp.dot(hidden, down_weight, preferred_element_type=jnp....  26 us
    dot_general x1, matrix products, per_device(): jnp.dot(hidden, down_weight, preferred_element_type=jnp.float32)  10.7 us
    dot_general x1, matrix products, per_device(): jnp.dot(lax.all_gather(normed, 'col', axis=1, tiled=True), qk_weight, pre...  10.2 us
  transfers between devices with their start and end apart: 2, of which 2 were waited for; matrix products, arithmetic and copies ran while one was open for 0% of the time, Pallas kernels for 0%

commit v1 on v0

v1 whole, which is shorter than its diff:
```python
import jax
import jax.numpy as jnp
from jax import lax
from jax.sharding import PartitionSpec as P

CORES = 2


def folded(count):
    return list(range(0, 1)) + list(range(1, count, 2)) + list(range(2, count, 2))[::-1]


def split_of(count):
    x = 1
    while (2 * x) * (2 * x) <= count:
        x *= 2
    return count // x, x


def solution(mesh):
    rows, cols = mesh.shape["row"], mesh.shape["col"]
    chips_y = rows // CORES
    chips_z, chips_x = split_of(cols)
    ring_z, ring_x = folded(chips_z), folded(chips_x)

    doublings = [1 << i for i in range(cols.bit_length() - 1)]
    sibling = [(r, r ^ 1) for r in range(rows)]

    def along_y(step):
        return [(r, (r + CORES * step) % rows) for r in range(rows)]

    def after(ring, place):
        return ring[(ring.index(place) + 1) % len(ring)]

    next_z = [(c, after(ring_z, c // chips_x) * chips_x + c % chips_x) for c in range(cols)]
    next_x = [(c, c // chips_x * chips_x + after(ring_x, c % chips_x)) for c in range(cols)]

    def per_device(hidden, down_weight, residual, gain, qk_weight):
        tok = residual.shape[0]
        width = residual.shape[1]
        me_row = lax.axis_index("row")
        me_col = lax.axis_index("col")
        gains = gain
        for bit in doublings:
            other = lax.ppermute(gains, "col", [(c, c ^ bit) for c in range(cols)])
            low, high = jnp.concatenate([gains, other]), jnp.concatenate([other, gains])
            gains = jnp.where(me_col & bit == 0, low, high)
        partial = jnp.dot(hidden, down_weight, preferred_element_type=jnp.float32).astype(jnp.bfloat16)
        blocks = partial.reshape(chips_y, CORES, tok, width)
        core = me_row % CORES
        give = lax.dynamic_index_in_dim(blocks, 1 - core, 1, keepdims=False)
        keep = lax.dynamic_index_in_dim(blocks, core, 1, keepdims=False)
        got = lax.ppermute(give, "row", sibling)
        both = keep.astype(jnp.float32) + got.astype(jnp.float32)
        chip = me_row // CORES
        total = lax.dynamic_index_in_dim(both, chip, 0, keepdims=False)
        both = both.astype(jnp.bfloat16)
        for step in range(1, chips_y):
            block = lax.dynamic_index_in_dim(both, (chip + step) % chips_y, 0, keepdims=False)
            total = total + lax.ppermute(block, "row", along_y(step)).astype(jnp.float32)
        stream = (residual.astype(jnp.float32) + total).astype(jnp.bfloat16)

        place_z = jnp.array([ring_z.index(z) for z in range(chips_z)])[me_col // chips_x]
        place_x = jnp.array([ring_x.index(x) for x in range(chips_x)])[me_col % chips_x]
        order_z, order_x = jnp.array(ring_z), jnp.array(ring_x)
        full = jnp.zeros((tok, width * cols), jnp.bfloat16)
        block = stream
        for hop_z in range(chips_z):
            z = order_z[(place_z - hop_z) % chips_z]
            sent = block
            if hop_z + 1 < chips_z:
                block = lax.ppermute(sent, "col", next_z)
            for hop_x in range(chips_x):
                x = order_x[(place_x - hop_x) % chips_x]
                full = lax.dynamic_update_slice(full, sent, (0, (z * chips_x + x) * width))
                if hop_x + 1 < chips_x:
                    sent = lax.ppermute(sent, "col", next_x)

        values = full.astype(jnp.float32)
        mean = jnp.mean(values, axis=1, keepdims=True)
        dev = values - mean
        var = jnp.mean(dev * dev, axis=1, keepdims=True)
        normed = (dev / jnp.sqrt(var + 1e-06) * gains.astype(jnp.float32)[None, :]).astype(jnp.bfloat16)
        product = jnp.dot(normed, qk_weight, preferred_element_type=jnp.float32)
        return stream, product.astype(jnp.bfloat16)

    placed = (P(None, "row"), P("row", "col"), P("row", "col"), P("col"), P(None, "col"))
    return jax.shard_map(
        per_device,
        mesh=mesh,
        in_specs=placed,
        out_specs=(P("row", "col"), P("row", "col")),
        check_vma=False,
    )
```

time: 143 us -> 64.3 us (0.45)
  waiting for transfers between devices: 68.5 us -> 18 us
  blocking collectives: 36.5 us -> 0 us
  starting transfers between devices: 0.08 us -> 16.4 us
  between operations: 14.1 us -> 7.36 us
  local copies, waits for them, and re-layouts: 0.02 us -> 1.6 us
    all_gather x1 -> x0, waiting for transfers between devices: 42.4 us -> none  [per_device(): lax.all_gather(normed, 'col', axis=1, tiled=True)]
    all_gather x2 -> x0, blocking collectives: 36.5 us -> none  [joined(): pieces = jax.tree.map(lambda part: lax.all_gather(part, axis), value)]
    reduce_scatter x1 -> x0, waiting for transfers between devices: 26 us -> none  [per_device(): lax.psum_scatter(jnp.dot(hidden, down_weight, preferred_element_type=jnp....]
    ppermute x0 -> x12, waiting for transfers between devices: none -> 18 us  [the longest x3 10.5 us: per_device(): block = lax.ppermute(sent, 'col', next_z)]
    ppermute x0 -> x12, starting transfers between devices: none -> 16.4 us  [the longest x3 5.78 us: per_device(): other = lax.ppermute(gains, 'col', [(c, c ^ bit) for c in range(cols)])]
  transfers between devices with their start and end apart: 2 -> 12, of which waited for: 2 -> 6; matrix products, arithmetic and copies ran while one was open for 0% -> 2% of each run, Pallas kernels for 0% -> 0%
where the time goes in v1:
time: 64.3 us; the launch traced here: 64 us
  matrix products  19.7 us (31%)
  waiting for transfers between devices  18 us (28%)
  starting transfers between devices  16.4 us (26%)
  between operations  7.36 us (11%)
  local copies, waits for them, and re-layouts  1.6 us (2%)
  other arithmetic  1.04 us (2%)
    ppermute x3, waiting for transfers between devices, per_device(): block = lax.ppermute(sent, 'col', next_z)  10.5 us
    dot_general x1, matrix products, per_device(): jnp.dot(hidden, down_weight, preferred_element_type=jnp.float32)  9.93 us
    dot_general x1, matrix products, per_device(): product = jnp.dot(normed, qk_weight, preferred_element_type=jnp.float32)  9.78 us
    ppermute x3, starting transfers between devices, per_device(): other = lax.ppermute(gains, 'col', [(c, c ^ bit) for c in range(cols)])  5.78 us
    ppermute x4, starting transfers between devices, per_device(): sent = lax.ppermute(sent, 'col', next_x)  4.18 us
    ppermute x4, waiting for transfers between devices, per_device(): sent = lax.ppermute(sent, 'col', next_x)  4.12 us
    ppermute x3, starting transfers between devices, per_device(): block = lax.ppermute(sent, 'col', next_z)  2.94 us
    ppermute x1, starting transfers between devices, per_device(): lax.ppermute(block, 'row', along_y(step)).astype(jnp.float32)  2.94 us
  transfers between devices with their start and end apart: 12, of which 6 were waited for; matrix products, arithmetic and copies ran while one was open for 2% of the time, Pallas kernels for 0%

profile of v1, /device:TPU:0, one launch (start us, length us, event | category | flops | bytes accessed | tf_op | source)
XLA Modules:
  0.0 64.0 jit_solution(13944790829266409603)
XLA Ops:
  0.6 9.9 %convolution_convert_fusion.1 = bf16[512,768]{1,0:T(8,128)(2,1)S(1)} fusion(bf16[512,6144]{1,0:T(8,128)(2,1)} %param.9, bf16[6144,768]{1,0:T(8,128)(2,1)} %param.10), kind=kOutput, calls=%fused_computation.11 | convolution fusion | flops 4832231424 | bytes 16515072 | tf_op jit(solution)/shard_map/dot_general | solution.py:48
  10.7 0.5 collective-permute-start
  11.2 1.3 %collective-permute-done = bf16[2,128,768]{2,1,0:T(8,128)(2,1)S(1)} collective-permute-done((bf16[2,128,768]{2,1,0:T(8,128)(2,1)S(1)}, bf16[2,128,768]{2,1,0:T(8,128)(2,1)S(1)}, u32[]{:S(2)}, u32[]{:S(2)}) %collective-permute-start) | collective-permute-done | bytes 393248 | tf_op jit(solution)/shard_map/ppermute | solution.py:53
  12.7 2.9 %collective-permute-start.1 = (bf16[128,768]{1,0:T(8,128)(2,1)S(1)}, bf16[128,768]{1,0:T(8,128)(2,1)S(1)}, u32[]{:S(2)}, u32[]{:S(2)}) collective-permute-start(bf16[128,768]{1,0:T(8,128)(2,1)S(1)} %fusion.11), channel_id=1, source_target_pairs={{0,16},{8,24},{16,0},{24,8},{1,17},{9,25},{17,1},{25,9},{2,18},{10... | collective-permute-start | bytes 589832 | tf_op jit(solution)/shard_map/ppermute | solution.py:60
  15.6 1.5 %collective-permute-start.9 = (bf16[768]{0:T(1024)(128)(2,1)S(1)}, bf16[768]{0:T(1024)(128)(2,1)S(1)}, u32[]{:S(2)}, u32[]{:S(2)}) collective-permute-start(bf16[768]{0:T(1024)(128)(2,1)S(1)} %copy-done.3), channel_id=1, source_target_pairs={{0,1},{1,0},{2,3},{3,2},{4,5},{5,4},{6,7},{7,6},{8,9},{9,8},{10,11... | collective-permute-start | bytes 4616 | tf_op jit(solution)/shard_map/ppermute | solution.py:45
  17.1 0.6 dynamic_slice.49
  21.7 0.7 %fusion.14 = (s32[1]{0:T(128)}, s32[1]{0:T(128)}, s32[1]{0:T(128)}, s32[1]{0:T(128)}) fusion(s32[4]{0:T(128)S(1)} %copy-done.2, s32[]{:T(128)S(6)} %select_n.186, s32[]{:T(128)S(6)} %select_n.178, s32[]{:T(128)S(6)} %select_n.168, s32[]{:T(128)S(6)} %select_n.182), kind=kLoop, calls=%fused_computation.33 | loop fusion | bytes 48 | tf_op jit(solution)/shard_map/dynamic_slice | solution.py:69
  23.0 1.6 %collective-permute-start.10 = (bf16[1536]{0:T(1024)(128)(2,1)S(1)}, bf16[1536]{0:T(1024)(128)(2,1)S(1)}, u32[]{:S(2)}, u32[]{:S(2)}) collective-permute-start(bf16[1536]{0:T(1024)(128)(2,1)S(1)} %maximum_select_fusion.2), channel_id=1, source_target_pairs={{0,2},{1,3},{2,0},{3,1},{4,6},{5,7},{6,4},{7,5},{8,10},{9,11},{10,... | collective-permute-start | bytes 9224 | tf_op jit(solution)/shard_map/ppermute | solution.py:45
  24.9 0.6 collective-permute-start.2
  25.5 0.4 collective-permute-start.3
  26.0 0.7 %collective-permute-done.10 = bf16[1536]{0:T(1024)(128)(2,1)S(1)} collective-permute-done((bf16[1536]{0:T(1024)(128)(2,1)S(1)}, bf16[1536]{0:T(1024)(128)(2,1)S(1)}, u32[]{:S(2)}, u32[]{:S(2)}) %collective-permute-start.10) | collective-permute-done | bytes 3104 | tf_op jit(solution)/shard_map/ppermute | solution.py:45
  26.7 2.6 %collective-permute-start.11 = (bf16[3072]{0:T(1024)(128)(2,1)S(1)}, bf16[3072]{0:T(1024)(128)(2,1)S(1)}, u32[]{:S(2)}, u32[]{:S(2)}) collective-permute-start(bf16[3072]{0:T(1024)(128)(2,1)S(1)} %maximum_select_fusion.1), channel_id=1, source_target_pairs={{0,4},{1,5},{2,6},{3,7},{4,0},{5,1},{6,2},{7,3},{8,12},{9,13},{10,... | collective-permute-start | bytes 18440 | tf_op jit(solution)/shard_map/ppermute | solution.py:45
  31.2 1.2 %collective-permute-done.11 = bf16[3072]{0:T(1024)(128)(2,1)S(1)} collective-permute-done((bf16[3072]{0:T(1024)(128)(2,1)S(1)}, bf16[3072]{0:T(1024)(128)(2,1)S(1)}, u32[]{:S(2)}, u32[]{:S(2)}) %collective-permute-start.11) | collective-permute-done | bytes 6176 | tf_op jit(solution)/shard_map/ppermute | solution.py:45
  32.5 1.6 %collective-permute-start.4 = (bf16[128,768]{1,0:T(8,128)(2,1)S(1)}, bf16[128,768]{1,0:T(8,128)(2,1)S(1)}, u32[]{:S(2)}, u32[]{:S(2)}) collective-permute-start(bf16[128,768]{1,0:T(8,128)(2,1)S(1)} %collective-permute-done.3), channel_id=1, source_target_pairs={{0,1},{1,0},{2,3},{3,2},{4,5},{5,4},{6,7},{7,6},{8,9},{9,8},{10,11... | collective-permute-start | bytes 589832 | tf_op jit(solution)/shard_map/ppermute | solution.py:77
  34.0 1.6 %collective-permute-start.5 = (bf16[128,768]{1,0:T(8,128)(2,1)S(1)}, bf16[128,768]{1,0:T(8,128)(2,1)S(1)}, u32[]{:S(2)}, u32[]{:S(2)}) collective-permute-start(bf16[128,768]{1,0:T(8,128)(2,1)S(1)} %collective-permute-done.3), channel_id=1, source_target_pairs={{0,2},{1,3},{2,6},{3,7},{4,0},{5,1},{6,4},{7,5},{8,10},{9,11},{10,... | collective-permute-start | bytes 589832 | tf_op jit(solution)/shard_map/ppermute | solution.py:72
  35.7 4.9 %collective-permute-done.5 = bf16[128,768]{1,0:T(8,128)(2,1)S(1)} collective-permute-done((bf16[128,768]{1,0:T(8,128)(2,1)S(1)}, bf16[128,768]{1,0:T(8,128)(2,1)S(1)}, u32[]{:S(2)}, u32[]{:S(2)}) %collective-permute-start.5) | collective-permute-done | bytes 196640 | tf_op jit(solution)/shard_map/ppermute | solution.py:72
  40.6 0.5 collective-permute-start.6
  41.1 0.9 %collective-permute-start.7 = (bf16[128,768]{1,0:T(8,128)(2,1)S(1)}, bf16[128,768]{1,0:T(8,128)(2,1)S(1)}, u32[]{:S(2)}, u32[]{:S(2)}) collective-permute-start(bf16[128,768]{1,0:T(8,128)(2,1)S(1)} %collective-permute-done.5), channel_id=1, source_target_pairs={{0,2},{1,3},{2,6},{3,7},{4,0},{5,1},{6,4},{7,5},{8,10},{9,11},{10,... | collective-permute-start | bytes 589832 | tf_op jit(solution)/shard_map/ppermute | solution.py:72
  42.1 5.6 %collective-permute-done.7 = bf16[128,768]{1,0:T(8,128)(2,1)S(1)} collective-permute-done((bf16[128,768]{1,0:T(8,128)(2,1)S(1)}, bf16[128,768]{1,0:T(8,128)(2,1)S(1)}, u32[]{:S(2)}, u32[]{:S(2)}) %collective-permute-start.7) | collective-permute-done | bytes 196640 | tf_op jit(solution)/shard_map/ppermute | solution.py:72
  47.7 1.5 %collective-permute-start.8 = (bf16[128,768]{1,0:T(8,128)(2,1)S(1)}, bf16[128,768]{1,0:T(8,128)(2,1)S(1)}, u32[]{:S(2)}, u32[]{:S(2)}) collective-permute-start(bf16[128,768]{1,0:T(8,128)(2,1)S(1)} %collective-permute-done.7), channel_id=1, source_target_pairs={{0,1},{1,0},{2,3},{3,2},{4,5},{5,4},{6,7},{7,6},{8,9},{9,8},{10,11... | collective-permute-start | bytes 589832 | tf_op jit(solution)/shard_map/ppermute | solution.py:77
  49.2 4.1 %collective-permute-done.8 = bf16[128,768]{1,0:T(8,128)(2,1)S(1)} collective-permute-done((bf16[128,768]{1,0:T(8,128)(2,1)S(1)}, bf16[128,768]{1,0:T(8,128)(2,1)S(1)}, u32[]{:S(2)}, u32[]{:S(2)}) %collective-permute-start.8) | collective-permute-done | bytes 196640 | tf_op jit(solution)/shard_map/ppermute | solution.py:77
  53.4 0.3 convert_reduce_fusion
  53.7 0.6 fusion.2
  54.3 9.8 %convolution_convert_fusion = bf16[128,1536]{1,0:T(8,128)(2,1)} fusion(bf16[6144,1536]{1,0:T(8,128)(2,1)} %param.13, bf16[128,6144]{1,0:T(8,128)(2,1)S(1)} %constant_dynamic-update-slice_fusion, f32[6144]{0:T(1024)S(1)} %fusion.12, f32[128]{0:T(128)S(1)} %add_sqrt_fusion, f32[128]{0:T(128)S(1)} %broadcast_multiply_fusion), kind=kOutput, calls=%fused_computation.7 | convolution fusion | flops 2420047872 | bytes 20866048 | tf_op jit(solution)/shard_map/dot_general | solution.py:84
  (31 shorter events, 0.6 us)
Async XLA Ops:
  10.6 5.0 %copy-start.3 = (bf16[768]{0:T(1024)(128)(2,1)S(1)}, bf16[768]{0:T(1024)(128)(2,1)}, u32[]{:S(2)}) copy-start(bf16[768]{0:T(1024)(128)(2,1)} %param.12) | copy-start | bytes 4612
  10.6 6.5 %copy-start.2 = (s32[4]{0:T(128)S(1)}, s32[4]{0:T(128)}, u32[]{:S(2)}) copy-start(s32[4]{0:T(128)} %constant.144.clone) | copy-start | bytes 52
  10.7 1.9 %collective-permute-start = (bf16[2,128,768]{2,1,0:T(8,128)(2,1)S(1)}, bf16[2,128,768]{2,1,0:T(8,128)(2,1)S(1)}, u32[]{:S(2)}, u32[]{:S(2)}) collective-permute-start(bf16[2,128,768]{2,1,0:T(8,128)(2,1)S(1)} %dynamic-slice_bitcast_fusion), channel_id=1, source_target_pairs={{0,8},{8,0},{16,24},{24,16},{1,9},{9,1},{17,25},{25,17},{2,10},{10... | collective-permute-start | bytes 1179656 | tf_op jit(solution)/shard_map/ppermute | solution.py:53
  11.2 13.7 %copy-start = (bf16[128,768]{1,0:T(8,128)(2,1)S(1)}, bf16[128,768]{1,0:T(8,128)(2,1)}, u32[]{:S(2)}) copy-start(bf16[128,768]{1,0:T(8,128)(2,1)} %param.11) | copy-start | bytes 589828
  12.7 12.0 %collective-permute-start.1 = (bf16[128,768]{1,0:T(8,128)(2,1)S(1)}, bf16[128,768]{1,0:T(8,128)(2,1)S(1)}, u32[]{:S(2)}, u32[]{:S(2)}) collective-permute-start(bf16[128,768]{1,0:T(8,128)(2,1)S(1)} %fusion.11), channel_id=1, source_target_pairs={{0,16},{8,24},{16,0},{24,8},{1,17},{9,25},{17,1},{25,9},{2,18},{10... | collective-permute-start | bytes 589832 | tf_op jit(solution)/shard_map/ppermute | solution.py:60
  15.6 7.4 %collective-permute-start.9 = (bf16[768]{0:T(1024)(128)(2,1)S(1)}, bf16[768]{0:T(1024)(128)(2,1)S(1)}, u32[]{:S(2)}, u32[]{:S(2)}) collective-permute-start(bf16[768]{0:T(1024)(128)(2,1)S(1)} %copy-done.3), channel_id=1, source_target_pairs={{0,1},{1,0},{2,3},{3,2},{4,5},{5,4},{6,7},{7,6},{8,9},{9,8},{10,11... | collective-permute-start | bytes 4616 | tf_op jit(solution)/shard_map/ppermute | solution.py:45
  23.0 3.7 %collective-permute-start.10 = (bf16[1536]{0:T(1024)(128)(2,1)S(1)}, bf16[1536]{0:T(1024)(128)(2,1)S(1)}, u32[]{:S(2)}, u32[]{:S(2)}) collective-permute-start(bf16[1536]{0:T(1024)(128)(2,1)S(1)} %maximum_select_fusion.2), channel_id=1, source_target_pairs={{0,2},{1,3},{2,0},{3,1},{4,6},{5,7},{6,4},{7,5},{8,10},{9,11},{10,... | collective-permute-start | bytes 9224 | tf_op jit(solution)/shard_map/ppermute | solution.py:45
  24.9 28.7 %copy-start.1 = (bf16[128,768]{1,0:T(8,128)(2,1)}, bf16[128,768]{1,0:T(8,128)(2,1)S(1)}, u32[]{:S(2)}) copy-start(bf16[128,768]{1,0:T(8,128)(2,1)S(1)} %get-tuple-element.3) | copy-start | bytes 589828
  24.9 10.7 %collective-permute-start.2 = (bf16[128,768]{1,0:T(8,128)(2,1)S(1)}, bf16[128,768]{1,0:T(8,128)(2,1)S(1)}, u32[]{:S(2)}, u32[]{:S(2)}) collective-permute-start(bf16[128,768]{1,0:T(8,128)(2,1)S(1)} %get-tuple-element.3), channel_id=1, source_target_pairs={{0,1},{1,0},{2,3},{3,2},{4,5},{5,4},{6,7},{7,6},{8,9},{9,8},{10,11... | collective-permute-start | bytes 589832 | tf_op jit(solution)/shard_map/ppermute | solution.py:77
  25.5 6.9 %collective-permute-start.3 = (bf16[128,768]{1,0:T(8,128)(2,1)S(1)}, bf16[128,768]{1,0:T(8,128)(2,1)S(1)}, u32[]{:S(2)}, u32[]{:S(2)}) collective-permute-start(bf16[128,768]{1,0:T(8,128)(2,1)S(1)} %get-tuple-element.3), channel_id=1, source_target_pairs={{0,2},{1,3},{2,6},{3,7},{4,0},{5,1},{6,4},{7,5},{8,10},{9,11},{10,... | collective-permute-start | bytes 589832 | tf_op jit(solution)/shard_map/ppermute | solution.py:72
  26.7 5.7 %collective-permute-start.11 = (bf16[3072]{0:T(1024)(128)(2,1)S(1)}, bf16[3072]{0:T(1024)(128)(2,1)S(1)}, u32[]{:S(2)}, u32[]{:S(2)}) collective-permute-start(bf16[3072]{0:T(1024)(128)(2,1)S(1)} %maximum_select_fusion.1), channel_id=1, source_target_pairs={{0,4},{1,5},{2,6},{3,7},{4,0},{5,1},{6,2},{7,3},{8,12},{9,13},{10,... | collective-permute-start | bytes 18440 | tf_op jit(solution)/shard_map/ppermute | solution.py:45
  32.5 9.5 %collective-permute-start.4 = (bf16[128,768]{1,0:T(8,128)(2,1)S(1)}, bf16[128,768]{1,0:T(8,128)(2,1)S(1)}, u32[]{:S(2)}, u32[]{:S(2)}) collective-permute-start(bf16[128,768]{1,0:T(8,128)(2,1)S(1)} %collective-permute-done.3), channel_id=1, source_target_pairs={{0,1},{1,0},{2,3},{3,2},{4,5},{5,4},{6,7},{7,6},{8,9},{9,8},{10,11... | collective-permute-start | bytes 589832 | tf_op jit(solution)/shard_map/ppermute | solution.py:77
  34.0 6.6 %collective-permute-start.5 = (bf16[128,768]{1,0:T(8,128)(2,1)S(1)}, bf16[128,768]{1,0:T(8,128)(2,1)S(1)}, u32[]{:S(2)}, u32[]{:S(2)}) collective-permute-start(bf16[128,768]{1,0:T(8,128)(2,1)S(1)} %collective-permute-done.3), channel_id=1, source_target_pairs={{0,2},{1,3},{2,6},{3,7},{4,0},{5,1},{6,4},{7,5},{8,10},{9,11},{10,... | collective-permute-start | bytes 589832 | tf_op jit(solution)/shard_map/ppermute | solution.py:72
  40.6 8.6 %collective-permute-start.6 = (bf16[128,768]{1,0:T(8,128)(2,1)S(1)}, bf16[128,768]{1,0:T(8,128)(2,1)S(1)}, u32[]{:S(2)}, u32[]{:S(2)}) collective-permute-start(bf16[128,768]{1,0:T(8,128)(2,1)S(1)} %collective-permute-done.5), channel_id=1, source_target_pairs={{0,1},{1,0},{2,3},{3,2},{4,5},{5,4},{6,7},{7,6},{8,9},{9,8},{10,11... | collective-permute-start | bytes 589832 | tf_op jit(solution)/shard_map/ppermute | solution.py:77
  41.1 6.6 %collective-permute-start.7 = (bf16[128,768]{1,0:T(8,128)(2,1)S(1)}, bf16[128,768]{1,0:T(8,128)(2,1)S(1)}, u32[]{:S(2)}, u32[]{:S(2)}) collective-permute-start(bf16[128,768]{1,0:T(8,128)(2,1)S(1)} %collective-permute-done.5), channel_id=1, source_target_pairs={{0,2},{1,3},{2,6},{3,7},{4,0},{5,1},{6,4},{7,5},{8,10},{9,11},{10,... | collective-permute-start | bytes 589832 | tf_op jit(solution)/shard_map/ppermute | solution.py:72
  47.7 5.7 %collective-permute-start.8 = (bf16[128,768]{1,0:T(8,128)(2,1)S(1)}, bf16[128,768]{1,0:T(8,128)(2,1)S(1)}, u32[]{:S(2)}, u32[]{:S(2)}) collective-permute-start(bf16[128,768]{1,0:T(8,128)(2,1)S(1)} %collective-permute-done.7), channel_id=1, source_target_pairs={{0,1},{1,0},{2,3},{3,2},{4,5},{5,4},{6,7},{7,6},{8,9},{9,8},{10,11... | collective-permute-start | bytes 589832 | tf_op jit(solution)/shard_map/ppermute | solution.py:77

commit v2 on v1

v2 whole, which is shorter than its diff:
```python
import functools

import jax
import jax.numpy as jnp
from jax import lax
from jax.experimental import pallas as pl
from jax.experimental.pallas import tpu as pltpu
from jax.sharding import PartitionSpec as P

CORES = 2
EXTRA = 16
LIMIT = 48 * 1024 * 1024
HBM = pl.BlockSpec(memory_space=pl.ANY)
VMEM = pl.BlockSpec(memory_space=pltpu.VMEM)


def grid_of(count):
    x = 1
    while (2 * x) * (2 * x) <= count:
        x *= 2
    return count // x, x


def cycle_of(count):
    z, x = grid_of(count)
    walk = [0]
    for i in range(z):
        line = list(range(1, x))
        walk += [i * x + j for j in (line if i % 2 == 0 else line[::-1])]
    return walk + [i * x for i in range(z - 1, 0, -1)]


def pick(index, table):
    value = jnp.int32(table[0])
    for i in range(1, len(table)):
        value = jnp.where(index == i, jnp.int32(table[i]), value)
    return value


def halves(size, most):
    while size > most and size % 2 == 0 and (size // 2) % 128 == 0:
        size //= 2
    return size


def down_kernel(chips_y, tok, hidden, weight, give, keep, h_buf, w_buf, total, sems):
    parts, _, depth = h_buf.shape

    def copies(k):
        span = pl.ds(pl.multiple_of(k * depth, depth), depth)
        return (
            pltpu.make_async_copy(hidden.at[:, span], h_buf.at[k], sems.at[0, k]),
            pltpu.make_async_copy(weight.at[span, :], w_buf.at[k], sems.at[1, k]),
        )

    for k in range(parts):
        for copy in copies(k):
            copy.start()
    for copy in copies(0):
        copy.wait()
    total[...] = jnp.dot(h_buf[0], w_buf[0], preferred_element_type=jnp.float32)

    def body(k, _):
        for copy in copies(k):
            copy.wait()
        total[...] += jnp.dot(h_buf[k], w_buf[k], preferred_element_type=jnp.float32)
        return _

    lax.fori_loop(1, parts, body, 0)
    me = lax.axis_index("row")
    chip, core = me // CORES, me % CORES
    for i in range(chips_y):
        other = lax.rem(chip + i, chips_y)
        for out, which in ((give, 1 - core), (keep, core)):
            first = pl.multiple_of((other * CORES + which) * tok, tok)
            out[i] = total[pl.ds(first, tok), :].astype(out.dtype)


def down(hidden, weight, tok, chips_y):
    tokens, inner = hidden.shape
    width = weight.shape[1]
    depth = halves(inner, 512)
    parts = inner // depth
    block = pltpu.VMEM((chips_y, tok, width), jnp.bfloat16)
    return pl.pallas_call(
        functools.partial(down_kernel, chips_y, tok),
        out_shape=(block, block),
        in_specs=[HBM, HBM],
        out_specs=(VMEM, VMEM),
        scratch_shapes=[
            pltpu.VMEM((parts, tokens, depth), jnp.bfloat16),
            pltpu.VMEM((parts, depth, width), jnp.bfloat16),
            pltpu.VMEM((tokens, width), jnp.float32),
            pltpu.SemaphoreType.DMA((2, parts)),
        ],
        compiler_params=pltpu.CompilerParams(vmem_limit_bytes=LIMIT),
        cost_estimate=pl.CostEstimate(
            flops=2 * tokens * inner * width, bytes_accessed=2 * inner * (tokens + width), transcendentals=0
        ),
        name="down",
    )(hidden, weight)


def project_kernel(cycle, hops, shapes, first, last, *refs):
    count = len(cycle)
    refs = list(refs)
    take = lambda n: [refs.pop(0) for _ in range(n)]
    pieces = [take(n) for n in shapes]
    gains, weight = take(2)
    shift_in, sums_in, total_in = [None] * 3 if first else take(3)
    if last:
        (out,) = take(1)
    elif first:
        shift_out, sums_out, total_out = take(3)
    else:
        sums_out, total_out = take(2)
    w_buf, lhs, sems = take(3)
    total = total_in if last else total_out
    tok = shift_in.shape[0] if not first else shift_out.shape[0]
    width = w_buf.shape[1]
    columns = weight.shape[1]
    strip = halves(columns, 512)
    strips = columns // strip

    me = lax.axis_index("col")
    place = pick(me, [cycle.index(c) for c in range(count)])
    ids = [pick(lax.rem(place + hop + count, count), cycle) for hop in hops]

    def copy(i, n):
        rows = pl.ds(pl.multiple_of(ids[i] * width, width), width)
        span = pl.ds(n * strip, strip)
        return pltpu.make_async_copy(weight.at[rows, span], w_buf.at[i, :, span], sems.at[i, n])

    for i in range(len(hops)):
        for n in range(strips):
            copy(i, n).start()

    if not first:
        shift = shift_in[...]
        one, two = sums_in[0], sums_in[1]
    for i, parts in enumerate(pieces):
        values = jnp.concatenate([part[...] for part in parts], axis=0).astype(jnp.float32)
        if first:
            shift = jnp.mean(values, axis=1, keepdims=True)
            shift_out[...] = shift
            one = two = jnp.zeros_like(shift)
        dev = values - shift
        one = one + jnp.sum(dev, axis=1, keepdims=True)
        two = two + jnp.sum(dev * dev, axis=1, keepdims=True)
        row = gains[pl.ds(me ^ ids[i], 1), :]
        lhs[i, 0:tok, :] = (dev * row).astype(lhs.dtype)
        lhs[i, tok : tok + EXTRA, :] = jnp.broadcast_to(row, (EXTRA, width)).astype(lhs.dtype)
    if not last:
        sums_out[0] = one
        sums_out[1] = two
    else:
        off = one / (width * count)
        var = jnp.maximum(two / (width * count) - off * off, 0.0)
        scale = 1.0 / jnp.sqrt(var + 1e-06)

    for n in range(strips):
        span = pl.ds(n * strip, strip)
        for i in range(len(hops)):
            copy(i, n).wait()
            product = jnp.dot(lhs[i], w_buf[i, :, span], preferred_element_type=jnp.float32)
            if i == 0:
                value = product if first else total_in[:, span] + product
            else:
                value = value + product
        if last:
            out[:, span] = ((value[0:tok] - off * value[tok : tok + 1]) * scale).astype(out.dtype)
        else:
            total[:, span] = value


def project(pieces, hops, gains, weight, state, cycle, last):
    first = state is None
    tok = sum(part.shape[0] for part in pieces[0])
    width = pieces[0][0].shape[1]
    columns = weight.shape[1]
    strips = columns // halves(columns, 512)
    shift = pltpu.VMEM((tok, 1), jnp.float32)
    sums = pltpu.VMEM((2, tok, 1), jnp.float32)
    total = pltpu.VMEM((tok + EXTRA, columns), jnp.float32)
    flat = [part for parts in pieces for part in parts]
    base = len(flat) + 2
    state = () if first else state
    if last:
        out_shape, aliases = jax.ShapeDtypeStruct((tok, columns), jnp.bfloat16), {}
    elif first:
        out_shape, aliases = (shift, sums, total), {}
    else:
        out_shape, aliases = (sums, total), {base + 1: 0, base + 2: 1}
    got = pl.pallas_call(
        functools.partial(project_kernel, cycle, hops, [len(parts) for parts in pieces], first, last),
        out_shape=out_shape,
        in_specs=[VMEM] * len(flat) + [VMEM, HBM] + [VMEM] * len(state),
        out_specs=jax.tree.map(lambda _: VMEM, out_shape),
        scratch_shapes=[
            pltpu.VMEM((len(hops), width, columns), jnp.bfloat16),
            pltpu.VMEM((len(hops), tok + EXTRA, width), jnp.bfloat16),
            pltpu.SemaphoreType.DMA((len(hops), strips)),
        ],
        input_output_aliases=aliases,
        compiler_params=pltpu.CompilerParams(vmem_limit_bytes=LIMIT),
        cost_estimate=pl.CostEstimate(
            flops=2 * len(hops) * (tok + EXTRA) * width * columns,
            bytes_accessed=2 * len(hops) * width * columns,
            transcendentals=0,
        ),
        name="project",
    )(*flat, gains, weight, *state)
    if last:
        return got
    return got if first else (state[0], *got)


def solution(mesh):
    rows, cols = mesh.shape["row"], mesh.shape["col"]
    chips_y = rows // CORES
    cycle = cycle_of(cols)
    half = cols // 2

    sibling = [(r, r ^ 1) for r in range(rows)]
    ahead = [(cycle[i], cycle[(i + 1) % cols]) for i in range(cols)]
    behind = [(cycle[(i + 1) % cols], cycle[i]) for i in range(cols)]

    def double(gains, bit):
        other = lax.ppermute(gains, "col", [(c, c ^ bit) for c in range(cols)])
        return jnp.concatenate([gains, other])

    def per_device(hidden, down_weight, residual, gain, qk_weight):
        tok = residual.shape[0]
        gains = gain[None, :]
        bits = [1 << i for i in range(cols.bit_length() - 1)]

        give, keep = down(hidden, down_weight, tok, chips_y)
        gains = double(gains, bits[0])
        got = lax.ppermute(give, "row", sibling)
        got, gains = lax.optimization_barrier((got, gains))
        both = keep.astype(jnp.float32) + got.astype(jnp.float32)
        gains = double(gains, bits[1])
        total = residual.astype(jnp.float32) + both[0]
        for step in range(1, chips_y):
            move = [(r, (r + CORES * step) % rows) for r in range(rows)]
            total = total + lax.ppermute(both[step].astype(jnp.bfloat16), "row", move).astype(jnp.float32)
        stream = total.astype(jnp.bfloat16)
        stream, gains = lax.optimization_barrier((stream, gains))
        for bit in bits[2:]:
            gains = double(gains, bit)
        gains = gains.astype(jnp.float32)

        up, down_ = stream, stream
        pieces, hops = [[stream]], [0]
        state = None
        for step in range(1, half + 1):
            if step == half:
                up, down_ = up[: tok // 2], down_[tok // 2 :]
            up, down_ = lax.ppermute(up, "col", ahead), lax.ppermute(down_, "col", behind)
            known = gain[None, :].astype(jnp.float32) if step == 1 else gains
            state = project(pieces, hops, known, qk_weight, state, cycle, False)
            up, down_, state = lax.optimization_barrier((up, down_, state))
            if step < half:
                pieces, hops = [[up], [down_]], [-step, step]
            else:
                pieces, hops = [[up, down_]], [half]
        return stream, project(pieces, hops, gains, qk_weight, state, cycle, True)

    placed = (P(None, "row"), P("row", "col"), P("row", "col"), P("col"), P(None, "col"))
    return jax.shard_map(
        per_device,
        mesh=mesh,
        in_specs=placed,
        out_specs=(P("row", "col"), P("row", "col")),
        check_vma=False,
    )
```

time: 64.3 us -> 59.6 us (0.927)
  Pallas kernels: 0 us -> 28.1 us
  matrix products: 19.7 us -> 0 us
  between operations: 7.36 us -> 0.79 us
  waiting for transfers between devices: 18 us -> 12.4 us
  local copies, waits for them, and re-layouts: 1.6 us -> 0.06 us
  starting transfers between devices: 16.4 us -> 17.8 us
  other arithmetic: 1.04 us -> 0.19 us
    pallas_call x0 -> x6, Pallas kernels: none -> 28.1 us  [the longest x5 17.4 us: project(): pl.pallas_call(functools.partial(project_kernel, cycle, hops, [len(parts)...]
    dot_general x2 -> x0, matrix products: 19.7 us -> none  [the longest x1 9.93 us: per_device(): jnp.dot(hidden, down_weight, preferred_element_type=jnp.float32)]
    ppermute x11 -> x12, waiting for transfers between devices: 16.6 us -> 12.4 us  [the longest x3 5.73 us: double(): other = lax.ppermute(gains, 'col', [(c, c ^ bit) for c in range(cols)])]
    ppermute x11 -> x12, starting transfers between devices: 15.8 us -> 17.3 us  [the longest x3 6.75 us: double(): other = lax.ppermute(gains, 'col', [(c, c ^ bit) for c in range(cols)])]
    ppermute x1, waiting for transfers between devices: 1.35 us -> 0.01 us  [per_device(): got = lax.ppermute(give, 'row', sibling)]
    dynamic_slice x2 -> x0, local copies, waits for them, and re-layouts: 1.24 us -> none  [the longest x1 0.66 us: per_device(): z = order_z[(place_z - hop_z) % chips_z]]
    reduce_sum x2 -> x0, other arithmetic: 0.85 us -> none  [the longest x1 0.57 us: per_device(): var = jnp.mean(dev * dev, axis=1, keepdims=True)]
  transfers between devices with their start and end apart: 12 -> 13, of which waited for: 6 -> 8; matrix products, arithmetic and copies ran while one was open for 2% -> 0% of each run, Pallas kernels for 0% -> 24%
where the time goes in v2:
time: 59.6 us; the launch traced here: 59.4 us
  Pallas kernels  28.1 us (47%)
  starting transfers between devices  17.8 us (30%)
  waiting for transfers between devices  12.4 us (21%)
  between operations  0.79 us (1%)
    pallas_call x5, Pallas kernels, project(): pl.pallas_call(functools.partial(project_kernel, cycle, hops, [len(parts)...  17.4 us
    pallas_call x1, Pallas kernels, down(): pl.pallas_call(functools.partial(down_kernel, chips_y, tok), out_shape=(b...  10.8 us
    ppermute x3, starting transfers between devices, double(): other = lax.ppermute(gains, 'col', [(c, c ^ bit) for c in range(cols)])  6.75 us
    ppermute x3, waiting for transfers between devices, double(): other = lax.ppermute(gains, 'col', [(c, c ^ bit) for c in range(cols)])  5.73 us
    ppermute x4, starting transfers between devices, per_device(): lax.ppermute(down_, 'col', behind)  4.51 us
    ppermute x4, starting transfers between devices, per_device(): lax.ppermute(up, 'col', ahead)  3.96 us
    ppermute x4, waiting for transfers between devices, per_device(): lax.ppermute(down_, 'col', behind)  3.45 us
    ppermute x4, waiting for transfers between devices, per_device(): lax.ppermute(up, 'col', ahead)  2.4 us
  transfers between devices with their start and end apart: 13, of which 8 were waited for; matrix products, arithmetic and copies ran while one was open for 0% of the time, Pallas kernels for 24%

profile of v2, /device:TPU:0, one launch (start us, length us, event | category | flops | bytes accessed | tf_op | source)
XLA Modules:
  0.0 59.4 jit_solution(16956731811463581309)
XLA Ops:
  0.7 10.8 %down.1 = (bf16[2,128,768]{2,1,0:T(8,128)(2,1)S(1)}, bf16[2,128,768]{2,1,0:T(8,128)(2,1)S(1)}) custom-call(bf16[512,6144]{1,0:T(8,128)(2,1)} %hidden.1, bf16[6144,768]{1,0:T(8,128)(2,1)} %weight.1), custom_call_target="tpu_custom_call" | custom-call | flops 4831838208 | bytes 15728640 | tf_op jit(solution)/shard_map/down/pallas_call | solution.py:85
  11.4 0.5 collective-permute-start
  12.0 2.6 %collective-permute-start.1 = (bf16[1,768]{1,0:T(2,128)(2,1)S(1)}, bf16[1,768]{1,0:T(2,128)(2,1)S(1)}, u32[]{:S(2)}, u32[]{:S(2)}) collective-permute-start(bf16[1,768]{1,0:T(2,128)(2,1)S(1)} %broadcast_in_dim.4), channel_id=1, source_target_pairs={{0,1},{1,0},{2,3},{3,2},{4,5},{5,4},{6,7},{7,6},{8,9},{9,8},{10,11... | collective-permute-start | bytes 4616 | tf_op jit(solution)/shard_map/ppermute | solution.py:229
  14.5 1.6 %collective-permute-done.1 = bf16[1,768]{1,0:T(2,128)(2,1)S(1)} collective-permute-done((bf16[1,768]{1,0:T(2,128)(2,1)S(1)}, bf16[1,768]{1,0:T(2,128)(2,1)S(1)}, u32[]{:S(2)}, u32[]{:S(2)}) %collective-permute-start.1) | collective-permute-done | bytes 1568 | tf_op jit(solution)/shard_map/ppermute | solution.py:229
  16.3 2.1 %collective-permute-start.2 = (bf16[128,768]{1,0:T(8,128)(2,1)S(1)}, bf16[128,768]{1,0:T(8,128)(2,1)S(1)}, u32[]{:S(2)}, u32[]{:S(2)}) collective-permute-start(bf16[128,768]{1,0:T(8,128)(2,1)S(1)} %fusion.3), channel_id=1, source_target_pairs={{0,16},{8,24},{16,0},{24,8},{1,17},{9,25},{17,1},{25,9},{2,18},{10... | collective-permute-start | bytes 589832 | tf_op jit(solution)/shard_map/ppermute | solution.py:246
  18.4 1.6 %collective-permute-start.3 = (bf16[2,768]{1,0:T(2,128)(2,1)S(1)}, bf16[2,768]{1,0:T(2,128)(2,1)S(1)}, u32[]{:S(2)}, u32[]{:S(2)}) collective-permute-start(bf16[2,768]{1,0:T(2,128)(2,1)S(1)} %pad_maximum_fusion.1), channel_id=1, source_target_pairs={{0,2},{1,3},{2,0},{3,1},{4,6},{5,7},{6,4},{7,5},{8,10},{9,11},{10,... | collective-permute-start | bytes 9224 | tf_op jit(solution)/shard_map/ppermute | solution.py:229
  19.9 2.0 %collective-permute-done.3 = bf16[2,768]{1,0:T(2,128)(2,1)S(1)} collective-permute-done((bf16[2,768]{1,0:T(2,128)(2,1)S(1)}, bf16[2,768]{1,0:T(2,128)(2,1)S(1)}, u32[]{:S(2)}, u32[]{:S(2)}) %collective-permute-start.3) | collective-permute-done | bytes 3104 | tf_op jit(solution)/shard_map/ppermute | solution.py:229
  22.0 0.8 %collective-permute-done.2 = bf16[128,768]{1,0:T(8,128)(2,1)S(1)} collective-permute-done((bf16[128,768]{1,0:T(8,128)(2,1)S(1)}, bf16[128,768]{1,0:T(8,128)(2,1)S(1)}, u32[]{:S(2)}, u32[]{:S(2)}) %collective-permute-start.2) | collective-permute-done | bytes 196640 | tf_op jit(solution)/shard_map/ppermute | solution.py:246
  22.9 1.8 %collective-permute-start.5 = (bf16[128,768]{1,0:T(8,128)(2,1)S(1)}, bf16[128,768]{1,0:T(8,128)(2,1)S(1)}, u32[]{:S(2)}, u32[]{:S(2)}) collective-permute-start(bf16[128,768]{1,0:T(8,128)(2,1)S(1)} %fusion.2.refs_0_), channel_id=1, source_target_pairs={{1,0},{3,1},{5,3},{7,5},{6,7},{4,6},{2,4},{0,2},{9,8},{11,9},{13,1... | collective-permute-start | bytes 589832 | tf_op jit(solution)/shard_map/ppermute | solution.py:259
  24.9 2.4 %project.5 = (f32[128,1]{1,0:T(8,128)S(1)}, f32[2,128,1]{2,1,0:T(8,128)S(1)}, f32[144,1536]{1,0:T(8,128)S(1)}) custom-call(bf16[128,768]{1,0:T(8,128)(2,1)S(1)} %fusion.2.refs_0_, f32[1,768]{1,0:T(1,128)S(1)} %reshape_convert_fusion.refs_1_, bf16[6144,1536]{1,0:T(8,128)(2,1)} %refs_3_.7), custom_call_target="tpu_custom_call" | custom-call | flops 339738624 | bytes 2359296 | tf_op jit(solution)/shard_map/project/pallas_call | solution.py:194
  27.3 1.3 %collective-permute-done.5.refs_1_ = bf16[128,768]{1,0:T(8,128)(2,1)S(1)} collective-permute-done((bf16[128,768]{1,0:T(8,128)(2,1)S(1)}, bf16[128,768]{1,0:T(8,128)(2,1)S(1)}, u32[]{:S(2)}, u32[]{:S(2)}) %collective-permute-start.5) | collective-permute-done | bytes 196640 | tf_op jit(solution)/shard_map/ppermute | solution.py:259
  28.6 1.9 %collective-permute-done.4.refs_0_ = bf16[128,768]{1,0:T(8,128)(2,1)S(1)} collective-permute-done((bf16[128,768]{1,0:T(8,128)(2,1)S(1)}, bf16[128,768]{1,0:T(8,128)(2,1)S(1)}, u32[]{:S(2)}, u32[]{:S(2)}) %collective-permute-start.4) | collective-permute-done | bytes 196640 | tf_op jit(solution)/shard_map/ppermute | solution.py:259
  30.6 1.9 %collective-permute-start.7 = (bf16[128,768]{1,0:T(8,128)(2,1)S(1)}, bf16[128,768]{1,0:T(8,128)(2,1)S(1)}, u32[]{:S(2)}, u32[]{:S(2)}) collective-permute-start(bf16[128,768]{1,0:T(8,128)(2,1)S(1)} %collective-permute-done.5.refs_1_), channel_id=1, source_target_pairs={{1,0},{3,1},{5,3},{7,5},{6,7},{4,6},{2,4},{0,2},{9,8},{11,9},{13,1... | collective-permute-start | bytes 589832 | tf_op jit(solution)/shard_map/ppermute | solution.py:259
  32.5 2.6 %collective-permute-start.8 = (bf16[4,768]{1,0:T(4,128)(2,1)S(1)}, bf16[4,768]{1,0:T(4,128)(2,1)S(1)}, u32[]{:S(2)}, u32[]{:S(2)}) collective-permute-start(bf16[4,768]{1,0:T(4,128)(2,1)S(1)} %pad_maximum_fusion), channel_id=1, source_target_pairs={{0,4},{1,5},{2,6},{3,7},{4,0},{5,1},{6,2},{7,3},{8,12},{9,13},{10,... | collective-permute-start | bytes 18440 | tf_op jit(solution)/shard_map/ppermute | solution.py:229
  35.1 2.1 %collective-permute-done.8 = bf16[4,768]{1,0:T(4,128)(2,1)S(1)} collective-permute-done((bf16[4,768]{1,0:T(4,128)(2,1)S(1)}, bf16[4,768]{1,0:T(4,128)(2,1)S(1)}, u32[]{:S(2)}, u32[]{:S(2)}) %collective-permute-start.8) | collective-permute-done | bytes 6176 | tf_op jit(solution)/shard_map/ppermute | solution.py:229
  37.2 4.0 %project.6 = (f32[2,128,1]{2,1,0:T(8,128)S(1)}, f32[144,1536]{1,0:T(8,128)S(1)}) custom-call(bf16[128,768]{1,0:T(8,128)(2,1)S(1)} %collective-permute-done.4.refs_0_, bf16[128,768]{1,0:T(8,128)(2,1)S(1)} %collective-permute-done.5.refs_1_, f32[8,768]{1,0:T(8,128)S(1)} %maximum_convert_fusion.refs_2_, ...), custom_call_target="tpu_custom_call", output_to_operand_aliasing={{0}: (5, {}), {1}: (6, {})} | custom-call | flops 679477248 | bytes 4718592 | tf_op jit(solution)/shard_map/project/pallas_call | solution.py:194
  41.2 2.3 %collective-permute-start.9 = (bf16[128,768]{1,0:T(8,128)(2,1)S(1)}, bf16[128,768]{1,0:T(8,128)(2,1)S(1)}, u32[]{:S(2)}, u32[]{:S(2)}) collective-permute-start(bf16[128,768]{1,0:T(8,128)(2,1)S(1)} %collective-permute-done.6.refs_0_), channel_id=1, source_target_pairs={{0,1},{1,3},{3,5},{5,7},{7,6},{6,4},{4,2},{2,0},{8,9},{9,11},{11,1... | collective-permute-start | bytes 589832 | tf_op jit(solution)/shard_map/ppermute | solution.py:259
  43.5 4.0 %project.7 = (f32[2,128,1]{2,1,0:T(8,128)S(1)}, f32[144,1536]{1,0:T(8,128)S(1)}) custom-call(bf16[128,768]{1,0:T(8,128)(2,1)S(1)} %collective-permute-done.6.refs_0_, bf16[128,768]{1,0:T(8,128)(2,1)S(1)} %collective-permute-done.7.refs_1_, f32[8,768]{1,0:T(8,128)S(1)} %maximum_convert_fusion.refs_2_, ...), custom_call_target="tpu_custom_call", output_to_operand_aliasing={{0}: (5, {}), {1}: (6, {})} | custom-call | flops 679477248 | bytes 4718592 | tf_op jit(solution)/shard_map/project/pallas_call | solution.py:194
  47.5 0.5 collective-permute-done.9.refs_0_
  48.0 2.2 %collective-permute-done.10.refs_1_ = bf16[128,768]{1,0:T(8,128)(2,1)S(1)} collective-permute-done((bf16[128,768]{1,0:T(8,128)(2,1)S(1)}, bf16[128,768]{1,0:T(8,128)(2,1)S(1)}, u32[]{:S(2)}, u32[]{:S(2)}) %collective-permute-start.10) | collective-permute-done | bytes 196640 | tf_op jit(solution)/shard_map/ppermute | solution.py:259
  50.2 1.3 %collective-permute-start.11 = (bf16[64,768]{1,0:T(8,128)(2,1)S(1)}, bf16[64,768]{1,0:T(8,128)(2,1)S(1)}, u32[]{:S(2)}, u32[]{:S(2)}) collective-permute-start(bf16[64,768]{1,0:T(8,128)(2,1)S(1)} %slice.15), channel_id=1, source_target_pairs={{0,1},{1,3},{3,5},{5,7},{7,6},{6,4},{4,2},{2,0},{8,9},{9,11},{11,1... | collective-permute-start | bytes 294920 | tf_op jit(solution)/shard_map/ppermute | solution.py:259
  51.5 0.8 %collective-permute-start.12 = (bf16[64,768]{1,0:T(8,128)(2,1)S(1)}, bf16[64,768]{1,0:T(8,128)(2,1)S(1)}, u32[]{:S(2)}, u32[]{:S(2)}) collective-permute-start(bf16[64,768]{1,0:T(8,128)(2,1)S(1)} %slice.16), channel_id=1, source_target_pairs={{1,0},{3,1},{5,3},{7,5},{6,7},{4,6},{2,4},{0,2},{9,8},{11,9},{13,1... | collective-permute-start | bytes 294920 | tf_op jit(solution)/shard_map/ppermute | solution.py:259
  52.3 4.0 %project.8 = (f32[2,128,1]{2,1,0:T(8,128)S(1)}, f32[144,1536]{1,0:T(8,128)S(1)}) custom-call(bf16[128,768]{1,0:T(8,128)(2,1)S(1)} %collective-permute-done.9.refs_0_, bf16[128,768]{1,0:T(8,128)(2,1)S(1)} %collective-permute-done.10.refs_1_, f32[8,768]{1,0:T(8,128)S(1)} %maximum_convert_fusion.refs_2_, ...), custom_call_target="tpu_custom_call", output_to_operand_aliasing={{0}: (5, {}), {1}: (6, {})} | custom-call | flops 679477248 | bytes 4718592 | tf_op jit(solution)/shard_map/project/pallas_call | solution.py:194
  56.3 3.1 %project.9 = bf16[128,1536]{1,0:T(8,128)(2,1)} custom-call(bf16[64,768]{1,0:T(8,128)(2,1)S(1)} %collective-permute-done.11.refs_0_, bf16[64,768]{1,0:T(8,128)(2,1)S(1)} %collective-permute-done.12.refs_1_, f32[8,768]{1,0:T(8,128)S(1)} %maximum_convert_fusion.refs_2_, bf16[6144,1536]{1,0:T(8,128)(2,1)} %refs_3_.7, f32[128,1]{1,0:T(8,128)S(1)} %get-tuple-element.69.refs_4_, ...), custom_call_target="tpu_custom_call" | custom-call | flops 339738624 | bytes 2359296 | tf_op jit(solution)/shard_map/project/pallas_call | solution.py:194
  (24 shorter events, 0.7 us)
Async XLA Ops:
  0.6 11.3 %copy-start.2 = (bf16[768]{0:T(1024)(128)(2,1)S(1)}, bf16[768]{0:T(1024)(128)(2,1)}, u32[]{:S(2)}) copy-start(bf16[768]{0:T(1024)(128)(2,1)} %param.8) | copy-start | bytes 4612
  0.6 22.1 %copy-start.1 = (bf16[128,768]{1,0:T(8,128)(2,1)S(1)}, bf16[128,768]{1,0:T(8,128)(2,1)}, u32[]{:S(2)}) copy-start(bf16[128,768]{1,0:T(8,128)(2,1)} %param.7) | copy-start | bytes 589828
  11.4 4.7 %collective-permute-start = (bf16[2,128,768]{2,1,0:T(8,128)(2,1)S(1)}, bf16[2,128,768]{2,1,0:T(8,128)(2,1)S(1)}, u32[]{:S(2)}, u32[]{:S(2)}) collective-permute-start(bf16[2,128,768]{2,1,0:T(8,128)(2,1)S(1)} %get-tuple-element.38), channel_id=1, source_target_pairs={{0,8},{8,0},{16,24},{24,16},{1,9},{9,1},{17,25},{25,17},{2,10},{10... | collective-permute-start | bytes 1179656 | tf_op jit(solution)/shard_map/ppermute | solution.py:239
  12.0 4.2 %collective-permute-start.1 = (bf16[1,768]{1,0:T(2,128)(2,1)S(1)}, bf16[1,768]{1,0:T(2,128)(2,1)S(1)}, u32[]{:S(2)}, u32[]{:S(2)}) collective-permute-start(bf16[1,768]{1,0:T(2,128)(2,1)S(1)} %broadcast_in_dim.4), channel_id=1, source_target_pairs={{0,1},{1,0},{2,3},{3,2},{4,5},{5,4},{6,7},{7,6},{8,9},{9,8},{10,11... | collective-permute-start | bytes 4616 | tf_op jit(solution)/shard_map/ppermute | solution.py:229
  16.3 6.5 %collective-permute-start.2 = (bf16[128,768]{1,0:T(8,128)(2,1)S(1)}, bf16[128,768]{1,0:T(8,128)(2,1)S(1)}, u32[]{:S(2)}, u32[]{:S(2)}) collective-permute-start(bf16[128,768]{1,0:T(8,128)(2,1)S(1)} %fusion.3), channel_id=1, source_target_pairs={{0,16},{8,24},{16,0},{24,8},{1,17},{9,25},{17,1},{25,9},{2,18},{10... | collective-permute-start | bytes 589832 | tf_op jit(solution)/shard_map/ppermute | solution.py:246
  18.4 3.6 %collective-permute-start.3 = (bf16[2,768]{1,0:T(2,128)(2,1)S(1)}, bf16[2,768]{1,0:T(2,128)(2,1)S(1)}, u32[]{:S(2)}, u32[]{:S(2)}) collective-permute-start(bf16[2,768]{1,0:T(2,128)(2,1)S(1)} %pad_maximum_fusion.1), channel_id=1, source_target_pairs={{0,2},{1,3},{2,0},{3,1},{4,6},{5,7},{6,4},{7,5},{8,10},{9,11},{10,... | collective-permute-start | bytes 9224 | tf_op jit(solution)/shard_map/ppermute | solution.py:229
  22.8 4.5 %copy-start = (bf16[128,768]{1,0:T(8,128)(2,1)}, bf16[128,768]{1,0:T(8,128)(2,1)S(1)}, u32[]{:S(2)}) copy-start(bf16[128,768]{1,0:T(8,128)(2,1)S(1)} %fusion.2.refs_0_) | copy-start | bytes 589828
  22.9 5.7 %collective-permute-start.5 = (bf16[128,768]{1,0:T(8,128)(2,1)S(1)}, bf16[128,768]{1,0:T(8,128)(2,1)S(1)}, u32[]{:S(2)}, u32[]{:S(2)}) collective-permute-start(bf16[128,768]{1,0:T(8,128)(2,1)S(1)} %fusion.2.refs_0_), channel_id=1, source_target_pairs={{1,0},{3,1},{5,3},{7,5},{6,7},{4,6},{2,4},{0,2},{9,8},{11,9},{13,1... | collective-permute-start | bytes 589832 | tf_op jit(solution)/shard_map/ppermute | solution.py:259
  24.7 5.7 %collective-permute-start.4 = (bf16[128,768]{1,0:T(8,128)(2,1)S(1)}, bf16[128,768]{1,0:T(8,128)(2,1)S(1)}, u32[]{:S(2)}, u32[]{:S(2)}) collective-permute-start(bf16[128,768]{1,0:T(8,128)(2,1)S(1)} %fusion.2.refs_0_), channel_id=1, source_target_pairs={{0,1},{1,3},{3,5},{5,7},{7,6},{6,4},{4,2},{2,0},{8,9},{9,11},{11,1... | collective-permute-start | bytes 589832 | tf_op jit(solution)/shard_map/ppermute | solution.py:259
  30.4 10.7 %collective-permute-start.6 = (bf16[128,768]{1,0:T(8,128)(2,1)S(1)}, bf16[128,768]{1,0:T(8,128)(2,1)S(1)}, u32[]{:S(2)}, u32[]{:S(2)}) collective-permute-start(bf16[128,768]{1,0:T(8,128)(2,1)S(1)} %collective-permute-done.4.refs_0_), channel_id=1, source_target_pairs={{0,1},{1,3},{3,5},{5,7},{7,6},{6,4},{4,2},{2,0},{8,9},{9,11},{11,1... | collective-permute-start | bytes 589832 | tf_op jit(solution)/shard_map/ppermute | solution.py:259
  30.6 10.6 %collective-permute-start.7 = (bf16[128,768]{1,0:T(8,128)(2,1)S(1)}, bf16[128,768]{1,0:T(8,128)(2,1)S(1)}, u32[]{:S(2)}, u32[]{:S(2)}) collective-permute-start(bf16[128,768]{1,0:T(8,128)(2,1)S(1)} %collective-permute-done.5.refs_1_), channel_id=1, source_target_pairs={{1,0},{3,1},{5,3},{7,5},{6,7},{4,6},{2,4},{0,2},{9,8},{11,9},{13,1... | collective-permute-start | bytes 589832 | tf_op jit(solution)/shard_map/ppermute | solution.py:259
  32.5 4.7 %collective-permute-start.8 = (bf16[4,768]{1,0:T(4,128)(2,1)S(1)}, bf16[4,768]{1,0:T(4,128)(2,1)S(1)}, u32[]{:S(2)}, u32[]{:S(2)}) collective-permute-start(bf16[4,768]{1,0:T(4,128)(2,1)S(1)} %pad_maximum_fusion), channel_id=1, source_target_pairs={{0,4},{1,5},{2,6},{3,7},{4,0},{5,1},{6,2},{7,3},{8,12},{9,13},{10,... | collective-permute-start | bytes 18440 | tf_op jit(solution)/shard_map/ppermute | solution.py:229
  41.2 6.8 %collective-permute-start.9 = (bf16[128,768]{1,0:T(8,128)(2,1)S(1)}, bf16[128,768]{1,0:T(8,128)(2,1)S(1)}, u32[]{:S(2)}, u32[]{:S(2)}) collective-permute-start(bf16[128,768]{1,0:T(8,128)(2,1)S(1)} %collective-permute-done.6.refs_0_), channel_id=1, source_target_pairs={{0,1},{1,3},{3,5},{5,7},{7,6},{6,4},{4,2},{2,0},{8,9},{9,11},{11,1... | collective-permute-start | bytes 589832 | tf_op jit(solution)/shard_map/ppermute | solution.py:259
  43.5 6.7 %collective-permute-start.10 = (bf16[128,768]{1,0:T(8,128)(2,1)S(1)}, bf16[128,768]{1,0:T(8,128)(2,1)S(1)}, u32[]{:S(2)}, u32[]{:S(2)}) collective-permute-start(bf16[128,768]{1,0:T(8,128)(2,1)S(1)} %collective-permute-done.7.refs_1_), channel_id=1, source_target_pairs={{1,0},{3,1},{5,3},{7,5},{6,7},{4,6},{2,4},{0,2},{9,8},{11,9},{13,1... | collective-permute-start | bytes 589832 | tf_op jit(solution)/shard_map/ppermute | solution.py:259
  50.2 6.1 %collective-permute-start.11 = (bf16[64,768]{1,0:T(8,128)(2,1)S(1)}, bf16[64,768]{1,0:T(8,128)(2,1)S(1)}, u32[]{:S(2)}, u32[]{:S(2)}) collective-permute-start(bf16[64,768]{1,0:T(8,128)(2,1)S(1)} %slice.15), channel_id=1, source_target_pairs={{0,1},{1,3},{3,5},{5,7},{7,6},{6,4},{4,2},{2,0},{8,9},{9,11},{11,1... | collective-permute-start | bytes 294920 | tf_op jit(solution)/shard_map/ppermute | solution.py:259
  51.5 4.8 %collective-permute-start.12 = (bf16[64,768]{1,0:T(8,128)(2,1)S(1)}, bf16[64,768]{1,0:T(8,128)(2,1)S(1)}, u32[]{:S(2)}, u32[]{:S(2)}) collective-permute-start(bf16[64,768]{1,0:T(8,128)(2,1)S(1)} %slice.16), channel_id=1, source_target_pairs={{1,0},{3,1},{5,3},{7,5},{6,7},{4,6},{2,4},{0,2},{9,8},{11,9},{13,1... | collective-permute-start | bytes 294920 | tf_op jit(solution)/shard_map/ppermute | solution.py:259

commit v3 on v2

--- a/solution.py
+++ b/solution.py
@@ -9,7 +9,7 @@
 
 CORES = 2
 EXTRA = 16
-LIMIT = 48 * 1024 * 1024
+MIB = 1024 * 1024
 HBM = pl.BlockSpec(memory_space=pl.ANY)
 VMEM = pl.BlockSpec(memory_space=pltpu.VMEM)
 
@@ -54,8 +54,8 @@
         )
 
     for k in range(parts):
-        for copy in copies(k):
-            copy.start()
+        for priority, copy in enumerate(copies(k)):
+            copy.start(priority=priority)
     for copy in copies(0):
         copy.wait()
     total[...] = jnp.dot(h_buf[0], w_buf[0], preferred_element_type=jnp.float32)
@@ -93,12 +93,12 @@
             pltpu.VMEM((tokens, width), jnp.float32),
             pltpu.SemaphoreType.DMA((2, parts)),
         ],
-        compiler_params=pltpu.CompilerParams(vmem_limit_bytes=LIMIT),
+        compiler_params=pltpu.CompilerParams(vmem_limit_bytes=24 * MIB),
         cost_estimate=pl.CostEstimate(
             flops=2 * tokens * inner * width, bytes_accessed=2 * inner * (tokens + width), transcendentals=0
         ),
         name="down",
-    )(hidden, weight)
+    )(*[pltpu.with_memory_space_constraint(x, pltpu.HBM) for x in (hidden, weight)])
 
 
 def project_kernel(cycle, hops, shapes, first, last, *refs):
@@ -114,10 +114,10 @@
         shift_out, sums_out, total_out = take(3)
     else:
         sums_out, total_out = take(2)
-    w_buf, lhs, sems = take(3)
+    (lhs,) = take(1)
     total = total_in if last else total_out
     tok = shift_in.shape[0] if not first else shift_out.shape[0]
-    width = w_buf.shape[1]
+    width = lhs.shape[2]
     columns = weight.shape[1]
     strip = halves(columns, 512)
     strips = columns // strip
@@ -125,15 +125,6 @@
     me = lax.axis_index("col")
     place = pick(me, [cycle.index(c) for c in range(count)])
     ids = [pick(lax.rem(place + hop + count, count), cycle) for hop in hops]
-
-    def copy(i, n):
-        rows = pl.ds(pl.multiple_of(ids[i] * width, width), width)
-        span = pl.ds(n * strip, strip)
-        return pltpu.make_async_copy(weight.at[rows, span], w_buf.at[i, :, span], sems.at[i, n])
-
-    for i in range(len(hops)):
-        for n in range(strips):
-            copy(i, n).start()
 
     if not first:
         shift = shift_in[...]
@@ -161,8 +152,8 @@
     for n in range(strips):
         span = pl.ds(n * strip, strip)
         for i in range(len(hops)):
-            copy(i, n).wait()
-            product = jnp.dot(lhs[i], w_buf[i, :, span], preferred_element_type=jnp.float32)
+            rows = pl.ds(pl.multiple_of(ids[i] * width, width), width)
+            product = jnp.dot(lhs[i], weight[rows, span], preferred_element_type=jnp.float32)
             if i == 0:
                 value = product if first else total_in[:, span] + product
             else:
@@ -178,7 +169,6 @@
     tok = sum(part.shape[0] for part in pieces[0])
     width = pieces[0][0].shape[1]
     columns = weight.shape[1]
-    strips = columns // halves(columns, 512)
     shift = pltpu.VMEM((tok, 1), jnp.float32)
     sums = pltpu.VMEM((2, tok, 1), jnp.float32)
     total = pltpu.VMEM((tok + EXTRA, columns), jnp.float32)
@@ -194,22 +184,20 @@
     got = pl.pallas_call(
         functools.partial(project_kernel, cycle, hops, [len(parts) for parts in pieces], first, last),
         out_shape=out_shape,
-        in_specs=[VMEM] * len(flat) + [VMEM, HBM] + [VMEM] * len(state),
+        in_specs=[VMEM] * (base + len(state)),
         out_specs=jax.tree.map(lambda _: VMEM, out_shape),
         scratch_shapes=[
-            pltpu.VMEM((len(hops), width, columns), jnp.bfloat16),
             pltpu.VMEM((len(hops), tok + EXTRA, width), jnp.bfloat16),
-            pltpu.SemaphoreType.DMA((len(hops), strips)),
         ],
         input_output_aliases=aliases,
-        compiler_params=pltpu.CompilerParams(vmem_limit_bytes=LIMIT),
+        compiler_params=pltpu.CompilerParams(vmem_limit_bytes=12 * MIB),
         cost_estimate=pl.CostEstimate(
             flops=2 * len(hops) * (tok + EXTRA) * width * columns,
-            bytes_accessed=2 * len(hops) * width * columns,
+            bytes_accessed=0,
             transcendentals=0,
         ),
         name="project",
-    )(*flat, gains, weight, *state)
+    )(*flat, gains, pltpu.with_memory_space_constraint(weight, pltpu.VMEM), *state)
     if last:
         return got
     return got if first else (state[0], *got)
@@ -234,10 +222,10 @@
         gains = gain[None, :]
         bits = [1 << i for i in range(cols.bit_length() - 1)]
 
+        gains = double(gains, bits[0])
         give, keep = down(hidden, down_weight, tok, chips_y)
-        gains = double(gains, bits[0])
+        give, gains = lax.optimization_barrier((give, gains))
         got = lax.ppermute(give, "row", sibling)
-        got, gains = lax.optimization_barrier((got, gains))
         both = keep.astype(jnp.float32) + got.astype(jnp.float32)
         gains = double(gains, bits[1])
         total = residual.astype(jnp.float32) + both[0]
@@ -248,7 +236,7 @@
         stream, gains = lax.optimization_barrier((stream, gains))
         for bit in bits[2:]:
             gains = double(gains, bit)
-        gains = gains.astype(jnp.float32)
+        known = gain[None, :].astype(jnp.float32)
 
         up, down_ = stream, stream
         pieces, hops = [[stream]], [0]
@@ -257,14 +245,15 @@
             if step == half:
                 up, down_ = up[: tok // 2], down_[tok // 2 :]
             up, down_ = lax.ppermute(up, "col", ahead), lax.ppermute(down_, "col", behind)
-            known = gain[None, :].astype(jnp.float32) if step == 1 else gains
             state = project(pieces, hops, known, qk_weight, state, cycle, False)
-            up, down_, state = lax.optimization_barrier((up, down_, state))
+            up, down_, state, gains = lax.optimization_barrier((up, down_, state, gains))
+            if step == 1:
+                known = gains.astype(jnp.float32)
             if step < half:
                 pieces, hops = [[up], [down_]], [-step, step]
             else:
                 pieces, hops = [[up, down_]], [half]
-        return stream, project(pieces, hops, gains, qk_weight, state, cycle, True)
+        return stream, project(pieces, hops, known, qk_weight, state, cycle, True)
 
     placed = (P(None, "row"), P("row", "col"), P("row", "col"), P("col"), P(None, "col"))
     return jax.shard_map(

time: 59.6 us -> 55.3 us (0.928)
  Pallas kernels: 28.1 us -> 20.1 us
  waiting for transfers between devices: 12.4 us -> 16 us
  local copies, waits for them, and re-layouts: 0.06 us -> 0.74 us
    pallas_call x5, Pallas kernels: 17.4 us -> 6.79 us  [project(): pl.pallas_call(functools.partial(project_kernel, cycle, hops, [len(parts)...]
    ppermute x4, waiting for transfers between devices: 2.4 us -> 7.07 us  [per_device(): lax.ppermute(up, 'col', ahead)]
    ppermute x4, starting transfers between devices: 4.51 us -> 7.96 us  [per_device(): lax.ppermute(down_, 'col', behind)]
    ppermute x4, starting transfers between devices: 3.96 us -> 0.62 us  [per_device(): lax.ppermute(up, 'col', ahead)]
    ppermute x4, waiting for transfers between devices: 3.45 us -> 0.12 us  [per_device(): lax.ppermute(down_, 'col', behind)]
    pallas_call x1, Pallas kernels: 10.8 us -> 13.3 us  [down(): pl.pallas_call(functools.partial(down_kernel, chips_y, tok), out_shape=(b...]
    ppermute x1, waiting for transfers between devices: 0.01 us -> 1.71 us  [per_device(): got = lax.ppermute(give, 'row', sibling)]
    ppermute x1, waiting for transfers between devices: 0.78 us -> 1.86 us  [per_device(): lax.ppermute(both[step].astype(jnp.bfloat16), 'row', move)]
  transfers between devices with their start and end apart: 13 -> 13, of which waited for: 8 -> 9; matrix products, arithmetic and copies ran while one was open for 0% -> 0% of each run, Pallas kernels for 24% -> 34%
where the time goes in v3:
time: 55.3 us; the launch traced here: 55.1 us
  Pallas kernels  20.1 us (36%)
  starting transfers between devices  17.3 us (31%)
  waiting for transfers between devices  16 us (29%)
  between operations  0.79 us (1%)
  local copies, waits for them, and re-layouts  0.74 us (1%)
    pallas_call x1, Pallas kernels, down(): pl.pallas_call(functools.partial(down_kernel, chips_y, tok), out_shape=(b...  13.3 us
    ppermute x4, starting transfers between devices, per_device(): lax.ppermute(down_, 'col', behind)  7.96 us
    ppermute x3, starting transfers between devices, double(): other = lax.ppermute(gains, 'col', [(c, c ^ bit) for c in range(cols)])  7.12 us
    ppermute x4, waiting for transfers between devices, per_device(): lax.ppermute(up, 'col', ahead)  7.07 us
    pallas_call x5, Pallas kernels, project(): pl.pallas_call(functools.partial(project_kernel, cycle, hops, [len(parts)...  6.79 us
    ppermute x3, waiting for transfers between devices, double(): other = lax.ppermute(gains, 'col', [(c, c ^ bit) for c in range(cols)])  5.25 us
    ppermute x1, waiting for transfers between devices, per_device(): lax.ppermute(both[step].astype(jnp.bfloat16), 'row', move)  1.86 us
    ppermute x1, waiting for transfers between devices, per_device(): got = lax.ppermute(give, 'row', sibling)  1.71 us
  transfers between devices with their start and end apart: 13, of which 9 were waited for; matrix products, arithmetic and copies ran while one was open for 0% of the time, Pallas kernels for 34%

profile of v3, /device:TPU:0, one launch (start us, length us, event | category | flops | bytes accessed | tf_op | source)
XLA Modules:
  0.0 55.1 jit_solution(3314492893908479192)
XLA Ops:
  0.6 0.7 %broadcast_in_dim.4 = bf16[1,768]{1,0:T(2,128)(2,1)S(1)} reshape(bf16[768]{0:T(1024)(128)(2,1)} %param.8) | data formatting | bytes 3072 | tf_op jit(solution)/shard_map/broadcast_in_dim | solution.py:222
  1.3 3.0 %collective-permute-start = (bf16[1,768]{1,0:T(2,128)(2,1)S(1)}, bf16[1,768]{1,0:T(2,128)(2,1)S(1)}, u32[]{:S(2)}, u32[]{:S(2)}) collective-permute-start(bf16[1,768]{1,0:T(2,128)(2,1)S(1)} %broadcast_in_dim.4), channel_id=1, source_target_pairs={{0,1},{1,0},{2,3},{3,2},{4,5},{5,4},{6,7},{7,6},{8,9},{9,8},{10,11... | collective-permute-start | bytes 4616 | tf_op jit(solution)/shard_map/ppermute | solution.py:217
  4.3 13.3 %down.1 = (bf16[2,128,768]{2,1,0:T(8,128)(2,1)S(1)}, bf16[2,128,768]{2,1,0:T(8,128)(2,1)S(1)}) custom-call(bf16[512,6144]{1,0:T(8,128)(2,1)} %hidden.1, bf16[6144,768]{1,0:T(8,128)(2,1)} %weight.1), custom_call_target="tpu_custom_call" | custom-call | flops 4831838208 | bytes 15728640 | tf_op jit(solution)/shard_map/down/pallas_call | solution.py:85
  17.7 1.7 %collective-permute-done.1 = bf16[2,128,768]{2,1,0:T(8,128)(2,1)S(1)} collective-permute-done((bf16[2,128,768]{2,1,0:T(8,128)(2,1)S(1)}, bf16[2,128,768]{2,1,0:T(8,128)(2,1)S(1)}, u32[]{:S(2)}, u32[]{:S(2)}) %collective-permute-start.1) | collective-permute-done | bytes 393248 | tf_op jit(solution)/shard_map/ppermute | solution.py:228
  19.5 0.1 convert_add_fusion
  19.6 1.5 %collective-permute-start.2 = (bf16[128,768]{1,0:T(8,128)(2,1)S(1)}, bf16[128,768]{1,0:T(8,128)(2,1)S(1)}, u32[]{:S(2)}, u32[]{:S(2)}) collective-permute-start(bf16[128,768]{1,0:T(8,128)(2,1)S(1)} %fusion.3), channel_id=1, source_target_pairs={{0,16},{8,24},{16,0},{24,8},{1,17},{9,25},{17,1},{25,9},{2,18},{10... | collective-permute-start | bytes 589832 | tf_op jit(solution)/shard_map/ppermute | solution.py:234
  21.1 1.6 %collective-permute-start.3 = (bf16[2,768]{1,0:T(2,128)(2,1)S(1)}, bf16[2,768]{1,0:T(2,128)(2,1)S(1)}, u32[]{:S(2)}, u32[]{:S(2)}) collective-permute-start(bf16[2,768]{1,0:T(2,128)(2,1)S(1)} %pad_maximum_fusion.2), channel_id=1, source_target_pairs={{0,2},{1,3},{2,0},{3,1},{4,6},{5,7},{6,4},{7,5},{8,10},{9,11},{10,... | collective-permute-start | bytes 9224 | tf_op jit(solution)/shard_map/ppermute | solution.py:217
  22.7 2.0 %collective-permute-done.3 = bf16[2,768]{1,0:T(2,128)(2,1)S(1)} collective-permute-done((bf16[2,768]{1,0:T(2,128)(2,1)S(1)}, bf16[2,768]{1,0:T(2,128)(2,1)S(1)}, u32[]{:S(2)}, u32[]{:S(2)}) %collective-permute-start.3) | collective-permute-done | bytes 3104 | tf_op jit(solution)/shard_map/ppermute | solution.py:217
  24.7 1.9 %collective-permute-done.2 = bf16[128,768]{1,0:T(8,128)(2,1)S(1)} collective-permute-done((bf16[128,768]{1,0:T(8,128)(2,1)S(1)}, bf16[128,768]{1,0:T(8,128)(2,1)S(1)}, u32[]{:S(2)}, u32[]{:S(2)}) %collective-permute-start.2) | collective-permute-done | bytes 196640 | tf_op jit(solution)/shard_map/ppermute | solution.py:234
  26.7 1.6 %collective-permute-start.5 = (bf16[128,768]{1,0:T(8,128)(2,1)S(1)}, bf16[128,768]{1,0:T(8,128)(2,1)S(1)}, u32[]{:S(2)}, u32[]{:S(2)}) collective-permute-start(bf16[128,768]{1,0:T(8,128)(2,1)S(1)} %fusion.2.refs_0_), channel_id=1, source_target_pairs={{1,0},{3,1},{5,3},{7,5},{6,7},{4,6},{2,4},{0,2},{9,8},{11,9},{13,1... | collective-permute-start | bytes 589832 | tf_op jit(solution)/shard_map/ppermute | solution.py:247
  28.2 0.5 collective-permute-start.4
  28.8 2.5 %collective-permute-start.6 = (bf16[4,768]{1,0:T(4,128)(2,1)S(1)}, bf16[4,768]{1,0:T(4,128)(2,1)S(1)}, u32[]{:S(2)}, u32[]{:S(2)}) collective-permute-start(bf16[4,768]{1,0:T(4,128)(2,1)S(1)} %pad_maximum_fusion.1), channel_id=1, source_target_pairs={{0,4},{1,5},{2,6},{3,7},{4,0},{5,1},{6,2},{7,3},{8,12},{9,13},{10,... | collective-permute-start | bytes 18440 | tf_op jit(solution)/shard_map/ppermute | solution.py:217
  31.3 0.8 %project.5 = (f32[128,1]{1,0:T(8,128)S(1)}, f32[2,128,1]{2,1,0:T(8,128)S(1)}, f32[144,1536]{1,0:T(8,128)S(1)}) custom-call(bf16[128,768]{1,0:T(8,128)(2,1)S(1)} %fusion.2.refs_0_, f32[1,768]{1,0:T(1,128)S(1)} %reshape_convert_fusion.refs_1_, bf16[6144,1536]{1,0:T(8,128)(2,1)S(1)} %copy-done), custom_call_target="tpu_custom_call" | custom-call | flops 339738624 | tf_op jit(solution)/shard_map/project/pallas_call | solution.py:184
  32.1 3.2 %collective-permute-done.6 = bf16[4,768]{1,0:T(4,128)(2,1)S(1)} collective-permute-done((bf16[4,768]{1,0:T(4,128)(2,1)S(1)}, bf16[4,768]{1,0:T(4,128)(2,1)S(1)}, u32[]{:S(2)}, u32[]{:S(2)}) %collective-permute-start.6) | collective-permute-done | bytes 6176 | tf_op jit(solution)/shard_map/ppermute | solution.py:217
  35.4 2.0 %collective-permute-start.8 = (bf16[128,768]{1,0:T(8,128)(2,1)S(1)}, bf16[128,768]{1,0:T(8,128)(2,1)S(1)}, u32[]{:S(2)}, u32[]{:S(2)}) collective-permute-start(bf16[128,768]{1,0:T(8,128)(2,1)S(1)} %collective-permute-done.5.refs_1_), channel_id=1, source_target_pairs={{1,0},{3,1},{5,3},{7,5},{6,7},{4,6},{2,4},{0,2},{9,8},{11,9},{13,1... | collective-permute-start | bytes 589832 | tf_op jit(solution)/shard_map/ppermute | solution.py:247
  37.4 1.5 %project.6 = (f32[2,128,1]{2,1,0:T(8,128)S(1)}, f32[144,1536]{1,0:T(8,128)S(1)}) custom-call(bf16[128,768]{1,0:T(8,128)(2,1)S(1)} %collective-permute-done.4.refs_0_, bf16[128,768]{1,0:T(8,128)(2,1)S(1)} %collective-permute-done.5.refs_1_, f32[8,768]{1,0:T(8,128)S(1)} %convert_element_type.32.refs_2_, ...), custom_call_target="tpu_custom_call", output_to_operand_aliasing={{0}: (5, {}), {1}: (6, {})} | custom-call | flops 679477248 | tf_op jit(solution)/shard_map/project/pallas_call | solution.py:184
  38.9 2.8 %collective-permute-done.7.refs_0_ = bf16[128,768]{1,0:T(8,128)(2,1)S(1)} collective-permute-done((bf16[128,768]{1,0:T(8,128)(2,1)S(1)}, bf16[128,768]{1,0:T(8,128)(2,1)S(1)}, u32[]{:S(2)}, u32[]{:S(2)}) %collective-permute-start.7) | collective-permute-done | bytes 196640 | tf_op jit(solution)/shard_map/ppermute | solution.py:247
  41.8 2.3 %collective-permute-start.10 = (bf16[128,768]{1,0:T(8,128)(2,1)S(1)}, bf16[128,768]{1,0:T(8,128)(2,1)S(1)}, u32[]{:S(2)}, u32[]{:S(2)}) collective-permute-start(bf16[128,768]{1,0:T(8,128)(2,1)S(1)} %collective-permute-done.8.refs_1_), channel_id=1, source_target_pairs={{1,0},{3,1},{5,3},{7,5},{6,7},{4,6},{2,4},{0,2},{9,8},{11,9},{13,1... | collective-permute-start | bytes 589832 | tf_op jit(solution)/shard_map/ppermute | solution.py:247
  44.1 1.5 %project.7 = (f32[2,128,1]{2,1,0:T(8,128)S(1)}, f32[144,1536]{1,0:T(8,128)S(1)}) custom-call(bf16[128,768]{1,0:T(8,128)(2,1)S(1)} %collective-permute-done.7.refs_0_, bf16[128,768]{1,0:T(8,128)(2,1)S(1)} %collective-permute-done.8.refs_1_, f32[8,768]{1,0:T(8,128)S(1)} %convert_element_type.32.refs_2_, ...), custom_call_target="tpu_custom_call", output_to_operand_aliasing={{0}: (5, {}), {1}: (6, {})} | custom-call | flops 679477248 | tf_op jit(solution)/shard_map/project/pallas_call | solution.py:184
  45.6 3.2 %collective-permute-done.9.refs_0_ = bf16[128,768]{1,0:T(8,128)(2,1)S(1)} collective-permute-done((bf16[128,768]{1,0:T(8,128)(2,1)S(1)}, bf16[128,768]{1,0:T(8,128)(2,1)S(1)}, u32[]{:S(2)}, u32[]{:S(2)}) %collective-permute-start.9) | collective-permute-done | bytes 196640 | tf_op jit(solution)/shard_map/ppermute | solution.py:247
  48.9 2.1 %collective-permute-start.12 = (bf16[64,768]{1,0:T(8,128)(2,1)S(1)}, bf16[64,768]{1,0:T(8,128)(2,1)S(1)}, u32[]{:S(2)}, u32[]{:S(2)}) collective-permute-start(bf16[64,768]{1,0:T(8,128)(2,1)S(1)} %slice.16), channel_id=1, source_target_pairs={{1,0},{3,1},{5,3},{7,5},{6,7},{4,6},{2,4},{0,2},{9,8},{11,9},{13,1... | collective-permute-start | bytes 294920 | tf_op jit(solution)/shard_map/ppermute | solution.py:247
  51.0 1.5 %project.8 = (f32[2,128,1]{2,1,0:T(8,128)S(1)}, f32[144,1536]{1,0:T(8,128)S(1)}) custom-call(bf16[128,768]{1,0:T(8,128)(2,1)S(1)} %collective-permute-done.9.refs_0_, bf16[128,768]{1,0:T(8,128)(2,1)S(1)} %collective-permute-done.10.refs_1_, f32[8,768]{1,0:T(8,128)S(1)} %convert_element_type.32.refs_2_, ...), custom_call_target="tpu_custom_call", output_to_operand_aliasing={{0}: (5, {}), {1}: (6, {})} | custom-call | flops 679477248 | tf_op jit(solution)/shard_map/project/pallas_call | solution.py:184
  52.4 1.0 %collective-permute-done.11.refs_0_ = bf16[64,768]{1,0:T(8,128)(2,1)S(1)} collective-permute-done((bf16[64,768]{1,0:T(8,128)(2,1)S(1)}, bf16[64,768]{1,0:T(8,128)(2,1)S(1)}, u32[]{:S(2)}, u32[]{:S(2)}) %collective-permute-start.11) | collective-permute-done | bytes 98336 | tf_op jit(solution)/shard_map/ppermute | solution.py:247
  53.5 1.6 %project.9 = bf16[128,1536]{1,0:T(8,128)(2,1)} custom-call(bf16[64,768]{1,0:T(8,128)(2,1)S(1)} %collective-permute-done.11.refs_0_, bf16[64,768]{1,0:T(8,128)(2,1)S(1)} %collective-permute-done.12.refs_1_, f32[8,768]{1,0:T(8,128)S(1)} %convert_element_type.32.refs_2_, bf16[6144,1536]{1,0:T(8,128)(2,1)S(1)} %copy-done, ...), custom_call_target="tpu_custom_call" | custom-call | flops 339738624 | tf_op jit(solution)/shard_map/project/pallas_call | solution.py:184
  (27 shorter events, 0.5 us)
Async XLA Ops:
  1.3 25.3 %copy-start.2 = (bf16[128,768]{1,0:T(8,128)(2,1)S(1)}, bf16[128,768]{1,0:T(8,128)(2,1)}, u32[]{:S(2)}) copy-start(bf16[128,768]{1,0:T(8,128)(2,1)} %param.7) | copy-start | bytes 589828
  1.3 27.4 %copy-start.3 = (bf16[768]{0:T(1024)(128)(2,1)S(1)}, bf16[768]{0:T(1024)(128)(2,1)}, u32[]{:S(2)}) copy-start(bf16[768]{0:T(1024)(128)(2,1)} %param.8) | copy-start | bytes 4612
  1.3 30.0 %copy-start = (bf16[6144,1536]{1,0:T(8,128)(2,1)S(1)}, bf16[6144,1536]{1,0:T(8,128)(2,1)}, u32[]{:S(2)}) copy-start(bf16[6144,1536]{1,0:T(8,128)(2,1)} %refs_3_.7) | copy-start | bytes 56623108
  1.3 16.3 %collective-permute-start = (bf16[1,768]{1,0:T(2,128)(2,1)S(1)}, bf16[1,768]{1,0:T(2,128)(2,1)S(1)}, u32[]{:S(2)}, u32[]{:S(2)}) collective-permute-start(bf16[1,768]{1,0:T(2,128)(2,1)S(1)} %broadcast_in_dim.4), channel_id=1, source_target_pairs={{0,1},{1,0},{2,3},{3,2},{4,5},{5,4},{6,7},{7,6},{8,9},{9,8},{10,11... | collective-permute-start | bytes 4616 | tf_op jit(solution)/shard_map/ppermute | solution.py:217
  17.7 1.8 %collective-permute-start.1 = (bf16[2,128,768]{2,1,0:T(8,128)(2,1)S(1)}, bf16[2,128,768]{2,1,0:T(8,128)(2,1)S(1)}, u32[]{:S(2)}, u32[]{:S(2)}) collective-permute-start(bf16[2,128,768]{2,1,0:T(8,128)(2,1)S(1)} %get-tuple-element.40), channel_id=1, source_target_pairs={{0,8},{8,0},{16,24},{24,16},{1,9},{9,1},{17,25},{25,17},{2,10},{10... | collective-permute-start | bytes 1179656 | tf_op jit(solution)/shard_map/ppermute | solution.py:228
  19.6 7.0 %collective-permute-start.2 = (bf16[128,768]{1,0:T(8,128)(2,1)S(1)}, bf16[128,768]{1,0:T(8,128)(2,1)S(1)}, u32[]{:S(2)}, u32[]{:S(2)}) collective-permute-start(bf16[128,768]{1,0:T(8,128)(2,1)S(1)} %fusion.3), channel_id=1, source_target_pairs={{0,16},{8,24},{16,0},{24,8},{1,17},{9,25},{17,1},{25,9},{2,18},{10... | collective-permute-start | bytes 589832 | tf_op jit(solution)/shard_map/ppermute | solution.py:234
  21.1 3.6 %collective-permute-start.3 = (bf16[2,768]{1,0:T(2,128)(2,1)S(1)}, bf16[2,768]{1,0:T(2,128)(2,1)S(1)}, u32[]{:S(2)}, u32[]{:S(2)}) collective-permute-start(bf16[2,768]{1,0:T(2,128)(2,1)S(1)} %pad_maximum_fusion.2), channel_id=1, source_target_pairs={{0,2},{1,3},{2,0},{3,1},{4,6},{5,7},{6,4},{7,5},{8,10},{9,11},{10,... | collective-permute-start | bytes 9224 | tf_op jit(solution)/shard_map/ppermute | solution.py:217
  26.7 5.4 %copy-start.1 = (bf16[128,768]{1,0:T(8,128)(2,1)}, bf16[128,768]{1,0:T(8,128)(2,1)S(1)}, u32[]{:S(2)}) copy-start(bf16[128,768]{1,0:T(8,128)(2,1)S(1)} %fusion.2.refs_0_) | copy-start | bytes 589828
  26.7 8.6 %collective-permute-start.5 = (bf16[128,768]{1,0:T(8,128)(2,1)S(1)}, bf16[128,768]{1,0:T(8,128)(2,1)S(1)}, u32[]{:S(2)}, u32[]{:S(2)}) collective-permute-start(bf16[128,768]{1,0:T(8,128)(2,1)S(1)} %fusion.2.refs_0_), channel_id=1, source_target_pairs={{1,0},{3,1},{5,3},{7,5},{6,7},{4,6},{2,4},{0,2},{9,8},{11,9},{13,1... | collective-permute-start | bytes 589832 | tf_op jit(solution)/shard_map/ppermute | solution.py:247
  28.2 7.1 %collective-permute-start.4 = (bf16[128,768]{1,0:T(8,128)(2,1)S(1)}, bf16[128,768]{1,0:T(8,128)(2,1)S(1)}, u32[]{:S(2)}, u32[]{:S(2)}) collective-permute-start(bf16[128,768]{1,0:T(8,128)(2,1)S(1)} %fusion.2.refs_0_), channel_id=1, source_target_pairs={{0,1},{1,3},{3,5},{5,7},{7,6},{6,4},{4,2},{2,0},{8,9},{9,11},{11,1... | collective-permute-start | bytes 589832 | tf_op jit(solution)/shard_map/ppermute | solution.py:247
  28.8 6.5 %collective-permute-start.6 = (bf16[4,768]{1,0:T(4,128)(2,1)S(1)}, bf16[4,768]{1,0:T(4,128)(2,1)S(1)}, u32[]{:S(2)}, u32[]{:S(2)}) collective-permute-start(bf16[4,768]{1,0:T(4,128)(2,1)S(1)} %pad_maximum_fusion.1), channel_id=1, source_target_pairs={{0,4},{1,5},{2,6},{3,7},{4,0},{5,1},{6,2},{7,3},{8,12},{9,13},{10,... | collective-permute-start | bytes 18440 | tf_op jit(solution)/shard_map/ppermute | solution.py:217
  35.3 6.4 %collective-permute-start.7 = (bf16[128,768]{1,0:T(8,128)(2,1)S(1)}, bf16[128,768]{1,0:T(8,128)(2,1)S(1)}, u32[]{:S(2)}, u32[]{:S(2)}) collective-permute-start(bf16[128,768]{1,0:T(8,128)(2,1)S(1)} %collective-permute-done.4.refs_0_), channel_id=1, source_target_pairs={{0,1},{1,3},{3,5},{5,7},{7,6},{6,4},{4,2},{2,0},{8,9},{9,11},{11,1... | collective-permute-start | bytes 589832 | tf_op jit(solution)/shard_map/ppermute | solution.py:247
  35.4 6.4 %collective-permute-start.8 = (bf16[128,768]{1,0:T(8,128)(2,1)S(1)}, bf16[128,768]{1,0:T(8,128)(2,1)S(1)}, u32[]{:S(2)}, u32[]{:S(2)}) collective-permute-start(bf16[128,768]{1,0:T(8,128)(2,1)S(1)} %collective-permute-done.5.refs_1_), channel_id=1, source_target_pairs={{1,0},{3,1},{5,3},{7,5},{6,7},{4,6},{2,4},{0,2},{9,8},{11,9},{13,1... | collective-permute-start | bytes 589832 | tf_op jit(solution)/shard_map/ppermute | solution.py:247
  41.8 7.0 %collective-permute-start.9 = (bf16[128,768]{1,0:T(8,128)(2,1)S(1)}, bf16[128,768]{1,0:T(8,128)(2,1)S(1)}, u32[]{:S(2)}, u32[]{:S(2)}) collective-permute-start(bf16[128,768]{1,0:T(8,128)(2,1)S(1)} %collective-permute-done.7.refs_0_), channel_id=1, source_target_pairs={{0,1},{1,3},{3,5},{5,7},{7,6},{6,4},{4,2},{2,0},{8,9},{9,11},{11,1... | collective-permute-start | bytes 589832 | tf_op jit(solution)/shard_map/ppermute | solution.py:247
  41.8 7.0 %collective-permute-start.10 = (bf16[128,768]{1,0:T(8,128)(2,1)S(1)}, bf16[128,768]{1,0:T(8,128)(2,1)S(1)}, u32[]{:S(2)}, u32[]{:S(2)}) collective-permute-start(bf16[128,768]{1,0:T(8,128)(2,1)S(1)} %collective-permute-done.8.refs_1_), channel_id=1, source_target_pairs={{1,0},{3,1},{5,3},{7,5},{6,7},{4,6},{2,4},{0,2},{9,8},{11,9},{13,1... | collective-permute-start | bytes 589832 | tf_op jit(solution)/shard_map/ppermute | solution.py:247
  48.8 4.7 %collective-permute-start.11 = (bf16[64,768]{1,0:T(8,128)(2,1)S(1)}, bf16[64,768]{1,0:T(8,128)(2,1)S(1)}, u32[]{:S(2)}, u32[]{:S(2)}) collective-permute-start(bf16[64,768]{1,0:T(8,128)(2,1)S(1)} %slice.15), channel_id=1, source_target_pairs={{0,1},{1,3},{3,5},{5,7},{7,6},{6,4},{4,2},{2,0},{8,9},{9,11},{11,1... | collective-permute-start | bytes 294920 | tf_op jit(solution)/shard_map/ppermute | solution.py:247
  48.9 4.7 %collective-permute-start.12 = (bf16[64,768]{1,0:T(8,128)(2,1)S(1)}, bf16[64,768]{1,0:T(8,128)(2,1)S(1)}, u32[]{:S(2)}, u32[]{:S(2)}) collective-permute-start(bf16[64,768]{1,0:T(8,128)(2,1)S(1)} %slice.16), channel_id=1, source_target_pairs={{1,0},{3,1},{5,3},{7,5},{6,7},{4,6},{2,4},{0,2},{9,8},{11,9},{13,1... | collective-permute-start | bytes 294920 | tf_op jit(solution)/shard_map/ppermute | solution.py:247

commit v4 on v3

v4 whole, which is shorter than its diff:
```python
import functools

import jax
import jax.numpy as jnp
from jax import lax
from jax.experimental import pallas as pl
from jax.experimental.pallas import tpu as pltpu
from jax.sharding import PartitionSpec as P

CORES = 2
EXTRA = 16
GAIN = 8
MIB = 1024 * 1024
HBM = pl.BlockSpec(memory_space=pl.ANY)
VMEM = pl.BlockSpec(memory_space=pltpu.VMEM)


def grid_of(count):
    x = 1
    while (2 * x) * (2 * x) <= count:
        x *= 2
    return count // x, x


def cycle_of(count):
    z, x = grid_of(count)
    walk = [0]
    for i in range(z):
        line = list(range(1, x))
        walk += [i * x + j for j in (line if i % 2 == 0 else line[::-1])]
    return walk + [i * x for i in range(z - 1, 0, -1)]


def pick(index, table):
    value = jnp.int32(table[0])
    for i in range(1, len(table)):
        value = jnp.where(index == i, jnp.int32(table[i]), value)
    return value


def cut(size, most):
    fits = [part for part in range(256, most + 1, 256) if size % part == 0]
    return fits[-1] if fits else size


def down_kernel(chips_y, tok, first, kept, *refs):
    refs = list(refs)
    hidden, weight, give, keep = refs[:4]
    held = refs.pop(4) if not kept else hidden
    w_buf, total, sems = refs[4:]
    parts, _, depth = held.shape
    columns = pl.ds(first, w_buf.shape[2])

    def copies(k):
        span = pl.ds(pl.multiple_of(k * depth, depth), depth)
        both = [pltpu.make_async_copy(weight.at[span, columns], w_buf.at[k], sems.at[1, k])]
        if not kept:
            both.append(pltpu.make_async_copy(hidden.at[:, span], held.at[k], sems.at[0, k]))
        return both

    for k in range(parts):
        for priority, copy in enumerate(copies(k)):
            copy.start(priority=priority)
    for copy in copies(0):
        copy.wait()
    total[...] = jnp.dot(held[0], w_buf[0], preferred_element_type=jnp.float32)

    def body(k, _):
        for copy in copies(k):
            copy.wait()
        total[...] += jnp.dot(held[k], w_buf[k], preferred_element_type=jnp.float32)
        return _

    lax.fori_loop(1, parts, body, 0)
    me = lax.axis_index("row")
    chip, core = me // CORES, me % CORES
    for i in range(chips_y):
        other = lax.rem(chip + i, chips_y)
        for out, which in ((give, 1 - core), (keep, core)):
            start = pl.multiple_of((other * CORES + which) * tok, tok)
            out[i] = total[pl.ds(start, tok), :].astype(out.dtype)


def down(hidden, weight, tok, chips_y, first, width):
    kept = hidden.ndim == 3
    if kept:
        parts, tokens, depth = hidden.shape
    else:
        tokens, inner = hidden.shape
        depth = cut(inner, 512)
        parts = inner // depth
    held = pltpu.VMEM((parts, tokens, depth), jnp.bfloat16)
    block = pltpu.VMEM((chips_y, tok, width), jnp.bfloat16)
    out_shape = (block, block) if kept else (block, block, held)
    got = pl.pallas_call(
        functools.partial(down_kernel, chips_y, tok, first, kept),
        out_shape=out_shape,
        in_specs=[VMEM if kept else HBM, HBM],
        out_specs=(VMEM,) * len(out_shape),
        scratch_shapes=[
            pltpu.VMEM((parts, depth, width), jnp.bfloat16),
            pltpu.VMEM((tokens, width), jnp.float32),
            pltpu.SemaphoreType.DMA((2, parts)),
        ],
        compiler_params=pltpu.CompilerParams(vmem_limit_bytes=24 * MIB),
        cost_estimate=pl.CostEstimate(
            flops=2 * tokens * parts * depth * width,
            bytes_accessed=2 * parts * depth * (width if kept else width + tokens),
            transcendentals=0,
        ),
        name="down",
    )(
        pltpu.with_memory_space_constraint(hidden, pltpu.VMEM if kept else pltpu.HBM),
        pltpu.with_memory_space_constraint(weight, pltpu.HBM),
    )
    return (*got, hidden) if kept else got


def merge_kernel(counts, *refs):
    refs = list(refs)
    *refs, residual, gain, stream, piece = refs
    tok = residual.shape[0]
    start = 0
    for count in counts:
        keep, got, *others = refs[:count]
        refs = refs[count:]
        span = pl.ds(start, keep.shape[2])
        start += keep.shape[2]
        value = keep[0].astype(jnp.float32) + got[0].astype(jnp.float32)
        for other in others:
            value = value + other[...].astype(jnp.float32)
        value = (residual[:, span].astype(jnp.float32) + value).astype(stream.dtype)
        stream[:, span] = value
        piece[0:tok, span] = value
    rows = jnp.broadcast_to(gain[...].astype(jnp.float32), (GAIN, gain.shape[1]))
    piece[tok : tok + GAIN, :] = rows.astype(piece.dtype)


def merge(groups, residual, gain):
    tok, width = residual.shape
    flat = [x for group in groups for x in group]
    return pl.pallas_call(
        functools.partial(merge_kernel, [len(group) for group in groups]),
        out_shape=(
            jax.ShapeDtypeStruct((tok, width), jnp.bfloat16),
            pltpu.VMEM((tok + GAIN, width), jnp.bfloat16),
        ),
        in_specs=[VMEM] * (len(flat) + 2),
        out_specs=(VMEM, VMEM),
        compiler_params=pltpu.CompilerParams(vmem_limit_bytes=8 * MIB),
        name="merge",
    )(*flat, residual, gain)


def project_kernel(cycle, hops, shapes, first, last, *refs):
    count = len(cycle)
    refs = list(refs)
    take = lambda n: [refs.pop(0) for _ in range(n)]
    pieces = [take(n) for n in shapes]
    (weight,) = take(1)
    shift_in, sums_in, total_in = [None] * 3 if first else take(3)
    if last:
        (out,) = take(1)
    elif first:
        shift_out, sums_out, total_out = take(3)
    else:
        sums_out, total_out = take(2)
    (lhs,) = take(1)
    total = total_in if last else total_out
    tok = shift_in.shape[0] if not first else shift_out.shape[0]
    width = lhs.shape[2]
    columns = weight.shape[1]
    strip = cut(columns, 512)
    strips = columns // strip

    me = lax.axis_index("col")
    place = pick(me, [cycle.index(c) for c in range(count)])
    ids = [pick(lax.rem(place + hop + count, count), cycle) for hop in hops]

    if not first:
        shift = shift_in[...]
        one, two = sums_in[0], sums_in[1]
    for i, parts in enumerate(pieces):
        whole = jnp.concatenate([part[...].astype(jnp.float32) for part in parts], axis=0)
        values, row = whole[0:tok], whole[tok : tok + 1]
        if first and i == 0:
            shift = jnp.mean(values, axis=1, keepdims=True)
            shift_out[...] = shift
            one = two = jnp.zeros_like(shift)
        dev = values - shift
        one = one + jnp.sum(dev, axis=1, keepdims=True)
        two = two + jnp.sum(dev * dev, axis=1, keepdims=True)
        lhs[i, 0:tok, :] = (dev * row).astype(lhs.dtype)
        lhs[i, tok : tok + EXTRA, :] = jnp.broadcast_to(row, (EXTRA, width)).astype(lhs.dtype)
    if not last:
        sums_out[0] = one
        sums_out[1] = two
    else:
        off = one / (width * count)
        var = jnp.maximum(two / (width * count) - off * off, 0.0)
        scale = 1.0 / jnp.sqrt(var + 1e-06)

    for n in range(strips):
        span = pl.ds(n * strip, strip)
        for i in range(len(hops)):
            rows = pl.ds(pl.multiple_of(ids[i] * width, width), width)
            product = jnp.dot(lhs[i], weight[rows, span], preferred_element_type=jnp.float32)
            if i == 0:
                value = product if first else total_in[:, span] + product
            else:
                value = value + product
        if last:
            out[:, span] = ((value[0:tok] - off * value[tok : tok + 1]) * scale).astype(out.dtype)
        else:
            total[:, span] = value


def project(pieces, hops, weight, state, cycle, last):
    first = state is None
    tok = sum(part.shape[0] for part in pieces[0]) - GAIN
    width = pieces[0][0].shape[1]
    columns = weight.shape[1]
    shift = pltpu.VMEM((tok, 1), jnp.float32)
    sums = pltpu.VMEM((2, tok, 1), jnp.float32)
    total = pltpu.VMEM((tok + EXTRA, columns), jnp.float32)
    flat = [part for parts in pieces for part in parts]
    base = len(flat) + 1
    state = () if first else state
    if last:
        out_shape, aliases = jax.ShapeDtypeStruct((tok, columns), jnp.bfloat16), {}
    elif first:
        out_shape, aliases = (shift, sums, total), {}
    else:
        out_shape, aliases = (sums, total), {base + 1: 0, base + 2: 1}
    got = pl.pallas_call(
        functools.partial(project_kernel, cycle, hops, [len(parts) for parts in pieces], first, last),
        out_shape=out_shape,
        in_specs=[VMEM] * (base + len(state)),
        out_specs=jax.tree.map(lambda _: VMEM, out_shape),
        scratch_shapes=[
            pltpu.VMEM((len(hops), tok + EXTRA, width), jnp.bfloat16),
        ],
        input_output_aliases=aliases,
        compiler_params=pltpu.CompilerParams(vmem_limit_bytes=12 * MIB),
        cost_estimate=pl.CostEstimate(
            flops=2 * len(hops) * (tok + EXTRA) * width * columns,
            bytes_accessed=0,
            transcendentals=0,
        ),
        name="project",
    )(*flat, pltpu.with_memory_space_constraint(weight, pltpu.VMEM), *state)
    if last:
        return got
    return got if first else (state[0], *got)


def solution(mesh):
    rows, cols = mesh.shape["row"], mesh.shape["col"]
    chips_y = rows // CORES
    cycle = cycle_of(cols)
    half = cols // 2

    sibling = [(r, r ^ 1) for r in range(rows)]
    ahead = [(cycle[i], cycle[(i + 1) % cols]) for i in range(cols)]
    behind = [(cycle[(i + 1) % cols], cycle[i]) for i in range(cols)]

    def per_device(hidden, down_weight, residual, gain, qk_weight):
        tok, width = residual.shape
        wide = width * 2 // 3 // 128 * 128 or width
        spans = [(0, wide), (wide, width - wide)] if wide < width else [(0, width)]

        sums = []
        for first, count in spans:
            give, keep, hidden = down(hidden, down_weight, tok, chips_y, first, count)
            sums.append((keep, lax.ppermute(give, "row", sibling)))
        groups = []
        for keep, got in sums:
            others = []
            for step in range(1, chips_y):
                move = [(r, (r + CORES * step) % rows) for r in range(rows)]
                both = keep[step].astype(jnp.float32) + got[step].astype(jnp.float32)
                others.append(lax.ppermute(both.astype(jnp.bfloat16), "row", move))
            groups.append((keep, got, *others))
        stream, piece = merge(groups, residual, gain[None, :])

        up, back = piece, piece
        pieces, hops, state = [], [], None
        for step in range(1, half + 1):
            if step == half:
                up, back = up[: tok // 2], back[tok // 2 :]
            up, back = lax.ppermute(up, "col", ahead), lax.ppermute(back, "col", behind)
            if pieces:
                state = project(pieces, hops, qk_weight, state, cycle, False)
                up, back, state = lax.optimization_barrier((up, back, state))
            if step < half:
                pieces, hops = [[up], [back]], [-step, step]
                if step == 1:
                    pieces, hops = [[piece]] + pieces, [0] + hops
            else:
                pieces, hops = [[up, back]], [half]
        return stream, project(pieces, hops, qk_weight, state, cycle, True)

    placed = (P(None, "row"), P("row", "col"), P("row", "col"), P("col"), P(None, "col"))
    return jax.shard_map(
        per_device,
        mesh=mesh,
        in_specs=placed,
        out_specs=(P("row", "col"), P("row", "col")),
        check_vma=False,
    )
```

time: 55.3 us -> 53.3 us (0.964)
  starting transfers between devices: 17.3 us -> 13 us
  waiting for transfers between devices: 16 us -> 19.9 us
  local copies, waits for them, and re-layouts: 0.74 us -> 0.04 us
  Pallas kernels: 20.1 us -> 19.5 us
    ppermute x9 -> x8, starting transfers between devices: 16.7 us -> 6.55 us  [the longest x2 3.88 us: per_device(): others.append(lax.ppermute(both.astype(jnp.bfloat16), 'row', move))]
    ppermute x4, starting transfers between devices: 0.62 us -> 6.46 us  [per_device(): lax.ppermute(up, 'col', ahead)]
    ppermute x4, waiting for transfers between devices: 7.07 us -> 12 us  [per_device(): lax.ppermute(up, 'col', ahead)]
    pallas_call x5 -> x4, Pallas kernels: 6.79 us -> 5.16 us  [project(): pl.pallas_call(functools.partial(project_kernel, cycle, hops, [len(parts)...]
    pallas_call x1 -> x3, Pallas kernels: 13.3 us -> 14.3 us  [the longest x2 13.5 us: down(): pl.pallas_call(functools.partial(down_kernel, chips_y, tok, first, kept),...]
    ppermute x9 -> x8, waiting for transfers between devices: 8.94 us -> 7.95 us  [the longest x2 4.24 us: per_device(): others.append(lax.ppermute(both.astype(jnp.bfloat16), 'row', move))]
    broadcast_in_dim x1, local copies, waits for them, and re-layouts: 0.69 us -> 0.01 us  [per_device(): stream, piece = merge(groups, residual, gain[None, :])]
  transfers between devices with their start and end apart: 13 -> 12, of which waited for: 9 -> 7; matrix products, arithmetic and copies ran while one was open for 0% -> 0% of each run, Pallas kernels for 34% -> 16%
where the time goes in v4:
time: 53.3 us; the launch traced here: 53.2 us
  waiting for transfers between devices  19.9 us (37%)
  Pallas kernels  19.5 us (37%)
  starting transfers between devices  13 us (24%)
  between operations  0.72 us (1%)
    pallas_call x2, Pallas kernels, down(): pl.pallas_call(functools.partial(down_kernel, chips_y, tok, first, kept),...  13.5 us
    ppermute x4, waiting for transfers between devices, per_device(): lax.ppermute(up, 'col', ahead)  12 us
    ppermute x4, starting transfers between devices, per_device(): lax.ppermute(up, 'col', ahead)  6.46 us
    pallas_call x4, Pallas kernels, project(): pl.pallas_call(functools.partial(project_kernel, cycle, hops, [len(parts)...  5.16 us
    ppermute x2, waiting for transfers between devices, per_device(): others.append(lax.ppermute(both.astype(jnp.bfloat16), 'row', move))  4.24 us
    ppermute x2, starting transfers between devices, per_device(): others.append(lax.ppermute(both.astype(jnp.bfloat16), 'row', move))  3.88 us
    ppermute x4, waiting for transfers between devices, per_device(): lax.ppermute(back, 'col', behind)  3.71 us
    ppermute x4, starting transfers between devices, per_device(): lax.ppermute(back, 'col', behind)  1.74 us
  transfers between devices with their start and end apart: 12, of which 7 were waited for; matrix products, arithmetic and copies ran while one was open for 0% of the time, Pallas kernels for 16%

profile of v4, /device:TPU:0, one launch (start us, length us, event | category | flops | bytes accessed | tf_op | source)
XLA Modules:
  0.0 53.2 jit_solution(9593314927804447931)
XLA Ops:
  0.6 8.7 %down.2 = (bf16[2,128,512]{2,1,0:T(8,128)(2,1)S(1)}, bf16[2,128,512]{2,1,0:T(8,128)(2,1)S(1)}, bf16[12,512,512]{2,1,0:T(8,128)(2,1)S(1)}) custom-call(bf16[512,6144]{1,0:T(8,128)(2,1)} %refs_0_.1, bf16[6144,768]{1,0:T(8,128)(2,1)} %refs_1_.3), custom_call_target="tpu_custom_call" | custom-call | flops 3221225472 | bytes 12582912 | tf_op jit(solution)/shard_map/down/pallas_call | solution.py:95
  9.3 0.5 collective-permute-start
  9.8 4.9 %down.3 = (bf16[2,128,256]{2,1,0:T(8,128)(2,1)S(1)}, bf16[2,128,256]{2,1,0:T(8,128)(2,1)S(1)}) custom-call(bf16[12,512,512]{2,1,0:T(8,128)(2,1)S(1)} %get-tuple-element.33.refs_0_, bf16[6144,768]{1,0:T(8,128)(2,1)} %refs_1_.3), custom_call_target="tpu_custom_call" | custom-call | flops 1610612736 | bytes 3145728 | tf_op jit(solution)/shard_map/down/pallas_call | solution.py:95
  15.2 2.7 %collective-permute-start.1 = (bf16[128,512]{1,0:T(8,128)(2,1)S(1)}, bf16[128,512]{1,0:T(8,128)(2,1)S(1)}, u32[]{:S(2)}, u32[]{:S(2)}) collective-permute-start(bf16[128,512]{1,0:T(8,128)(2,1)S(1)} %fusion), channel_id=1, source_target_pairs={{0,16},{8,24},{16,0},{24,8},{1,17},{9,25},{17,1},{25,9},{2,18},{10... | collective-permute-start | bytes 393224 | tf_op jit(solution)/shard_map/ppermute | solution.py:282
  17.9 1.2 %collective-permute-start.3 = (bf16[128,256]{1,0:T(8,128)(2,1)S(1)}, bf16[128,256]{1,0:T(8,128)(2,1)S(1)}, u32[]{:S(2)}, u32[]{:S(2)}) collective-permute-start(bf16[128,256]{1,0:T(8,128)(2,1)S(1)} %fusion.1), channel_id=1, source_target_pairs={{0,16},{8,24},{16,0},{24,8},{1,17},{9,25},{17,1},{25,9},{2,18},{10... | collective-permute-start | bytes 196616 | tf_op jit(solution)/shard_map/ppermute | solution.py:282
  19.1 4.2 %collective-permute-done.3.refs_5_ = bf16[128,256]{1,0:T(8,128)(2,1)S(1)} collective-permute-done((bf16[128,256]{1,0:T(8,128)(2,1)S(1)}, bf16[128,256]{1,0:T(8,128)(2,1)S(1)}, u32[]{:S(2)}, u32[]{:S(2)}) %collective-permute-start.3) | collective-permute-done | bytes 65568 | tf_op jit(solution)/shard_map/ppermute | solution.py:282
  23.3 0.8 %merge.1 = (bf16[128,768]{1,0:T(8,128)(2,1)}, bf16[136,768]{1,0:T(8,128)(2,1)S(1)}) custom-call(bf16[2,128,512]{2,1,0:T(8,128)(2,1)S(1)} %get-tuple-element.31.refs_0_, bf16[2,128,512]{2,1,0:T(8,128)(2,1)S(1)} %collective-permute-done.refs_1_, bf16[128,512]{1,0:T(8,128)(2,1)S(1)} %collective-permute-done.1.refs_2_, ...), custom_call_target="tpu_custom_call" | custom-call | tf_op jit(solution)/shard_map/merge/pallas_call | solution.py:142
  24.1 1.7 %collective-permute-start.4 = (bf16[136,768]{1,0:T(8,128)(2,1)S(1)}, bf16[136,768]{1,0:T(8,128)(2,1)S(1)}, u32[]{:S(2)}, u32[]{:S(2)}) collective-permute-start(bf16[136,768]{1,0:T(8,128)(2,1)S(1)} %get-tuple-element.37.refs_0_), channel_id=1, source_target_pairs={{0,1},{1,3},{3,5},{5,7},{7,6},{6,4},{4,2},{2,0},{8,9},{9,11},{11,1... | collective-permute-start | bytes 626696 | tf_op jit(solution)/shard_map/ppermute | solution.py:291
  26.1 4.9 %collective-permute-done.4.refs_1_ = bf16[136,768]{1,0:T(8,128)(2,1)S(1)} collective-permute-done((bf16[136,768]{1,0:T(8,128)(2,1)S(1)}, bf16[136,768]{1,0:T(8,128)(2,1)S(1)}, u32[]{:S(2)}, u32[]{:S(2)}) %collective-permute-start.4) | collective-permute-done | bytes 208928 | tf_op jit(solution)/shard_map/ppermute | solution.py:291
  31.0 1.5 %collective-permute-start.5 = (bf16[136,768]{1,0:T(8,128)(2,1)S(1)}, bf16[136,768]{1,0:T(8,128)(2,1)S(1)}, u32[]{:S(2)}, u32[]{:S(2)}) collective-permute-start(bf16[136,768]{1,0:T(8,128)(2,1)S(1)} %collective-permute-done.4.refs_1_), channel_id=1, source_target_pairs={{0,1},{1,3},{3,5},{5,7},{7,6},{6,4},{4,2},{2,0},{8,9},{9,11},{11,1... | collective-permute-start | bytes 626696 | tf_op jit(solution)/shard_map/ppermute | solution.py:291
  32.5 0.5 collective-permute-start.7
  33.0 1.5 %project.4 = (f32[128,1]{1,0:T(8,128)S(1)}, f32[2,128,1]{2,1,0:T(8,128)S(1)}, f32[144,1536]{1,0:T(8,128)S(1)}) custom-call(bf16[136,768]{1,0:T(8,128)(2,1)S(1)} %get-tuple-element.37.refs_0_, bf16[136,768]{1,0:T(8,128)(2,1)S(1)} %collective-permute-done.4.refs_1_, bf16[136,768]{1,0:T(8,128)(2,1)S(1)} %collective-permute-done.6.refs_2_, ...), custom_call_target="tpu_custom_call" | custom-call | flops 1019215872 | tf_op jit(solution)/shard_map/project/pallas_call | solution.py:235
  34.5 2.5 %collective-permute-done.5.refs_0_ = bf16[136,768]{1,0:T(8,128)(2,1)S(1)} collective-permute-done((bf16[136,768]{1,0:T(8,128)(2,1)S(1)}, bf16[136,768]{1,0:T(8,128)(2,1)S(1)}, u32[]{:S(2)}, u32[]{:S(2)}) %collective-permute-start.5) | collective-permute-done | bytes 208928 | tf_op jit(solution)/shard_map/ppermute | solution.py:291
  37.0 1.3 %collective-permute-done.7.refs_1_ = bf16[136,768]{1,0:T(8,128)(2,1)S(1)} collective-permute-done((bf16[136,768]{1,0:T(8,128)(2,1)S(1)}, bf16[136,768]{1,0:T(8,128)(2,1)S(1)}, u32[]{:S(2)}, u32[]{:S(2)}) %collective-permute-start.7) | collective-permute-done | bytes 208928 | tf_op jit(solution)/shard_map/ppermute | solution.py:291
  38.3 1.6 %collective-permute-start.8 = (bf16[136,768]{1,0:T(8,128)(2,1)S(1)}, bf16[136,768]{1,0:T(8,128)(2,1)S(1)}, u32[]{:S(2)}, u32[]{:S(2)}) collective-permute-start(bf16[136,768]{1,0:T(8,128)(2,1)S(1)} %collective-permute-done.5.refs_0_), channel_id=1, source_target_pairs={{0,1},{1,3},{3,5},{5,7},{7,6},{6,4},{4,2},{2,0},{8,9},{9,11},{11,1... | collective-permute-start | bytes 626696 | tf_op jit(solution)/shard_map/ppermute | solution.py:291
  39.9 0.4 collective-permute-start.9
  40.4 1.1 %project.5 = (f32[2,128,1]{2,1,0:T(8,128)S(1)}, f32[144,1536]{1,0:T(8,128)S(1)}) custom-call(bf16[136,768]{1,0:T(8,128)(2,1)S(1)} %collective-permute-done.5.refs_0_, bf16[136,768]{1,0:T(8,128)(2,1)S(1)} %collective-permute-done.7.refs_1_, bf16[6144,1536]{1,0:T(8,128)(2,1)S(1)} %copy-done, ...), custom_call_target="tpu_custom_call", output_to_operand_aliasing={{0}: (4, {}), {1}: (5, {})} | custom-call | flops 679477248 | tf_op jit(solution)/shard_map/project/pallas_call | solution.py:235
  41.5 2.7 %collective-permute-done.8.refs_0_ = bf16[136,768]{1,0:T(8,128)(2,1)S(1)} collective-permute-done((bf16[136,768]{1,0:T(8,128)(2,1)S(1)}, bf16[136,768]{1,0:T(8,128)(2,1)S(1)}, u32[]{:S(2)}, u32[]{:S(2)}) %collective-permute-start.8) | collective-permute-done | bytes 208928 | tf_op jit(solution)/shard_map/ppermute | solution.py:291
  44.1 2.4 %collective-permute-done.9.refs_1_ = bf16[136,768]{1,0:T(8,128)(2,1)S(1)} collective-permute-done((bf16[136,768]{1,0:T(8,128)(2,1)S(1)}, bf16[136,768]{1,0:T(8,128)(2,1)S(1)}, u32[]{:S(2)}, u32[]{:S(2)}) %collective-permute-start.9) | collective-permute-done | bytes 208928 | tf_op jit(solution)/shard_map/ppermute | solution.py:291
  46.6 0.5 collective-permute-start.11
  47.1 1.6 %collective-permute-start.10 = (bf16[64,768]{1,0:T(8,128)(2,1)S(1)}, bf16[64,768]{1,0:T(8,128)(2,1)S(1)}, u32[]{:S(2)}, u32[]{:S(2)}) collective-permute-start(bf16[64,768]{1,0:T(8,128)(2,1)S(1)} %slice.22), channel_id=1, source_target_pairs={{0,1},{1,3},{3,5},{5,7},{7,6},{6,4},{4,2},{2,0},{8,9},{9,11},{11,1... | collective-permute-start | bytes 294920 | tf_op jit(solution)/shard_map/ppermute | solution.py:291
  48.7 1.1 %project.6 = (f32[2,128,1]{2,1,0:T(8,128)S(1)}, f32[144,1536]{1,0:T(8,128)S(1)}) custom-call(bf16[136,768]{1,0:T(8,128)(2,1)S(1)} %collective-permute-done.8.refs_0_, bf16[136,768]{1,0:T(8,128)(2,1)S(1)} %collective-permute-done.9.refs_1_, bf16[6144,1536]{1,0:T(8,128)(2,1)S(1)} %copy-done, ...), custom_call_target="tpu_custom_call", output_to_operand_aliasing={{0}: (4, {}), {1}: (5, {})} | custom-call | flops 679477248 | tf_op jit(solution)/shard_map/project/pallas_call | solution.py:235
  49.8 1.9 %collective-permute-done.10.refs_0_ = bf16[64,768]{1,0:T(8,128)(2,1)S(1)} collective-permute-done((bf16[64,768]{1,0:T(8,128)(2,1)S(1)}, bf16[64,768]{1,0:T(8,128)(2,1)S(1)}, u32[]{:S(2)}, u32[]{:S(2)}) %collective-permute-start.10) | collective-permute-done | bytes 98336 | tf_op jit(solution)/shard_map/ppermute | solution.py:291
  51.7 1.5 %project.7 = bf16[128,1536]{1,0:T(8,128)(2,1)} custom-call(bf16[64,768]{1,0:T(8,128)(2,1)S(1)} %collective-permute-done.10.refs_0_, bf16[72,768]{1,0:T(8,128)(2,1)S(1)} %collective-permute-done.11.refs_1_, bf16[6144,1536]{1,0:T(8,128)(2,1)S(1)} %copy-done, f32[128,1]{1,0:T(8,128)S(1)} %get-tuple-element.57.refs_3_, ...), custom_call_target="tpu_custom_call" | custom-call | flops 339738624 | tf_op jit(solution)/shard_map/project/pallas_call | solution.py:235
  (18 shorter events, 0.8 us)
Async XLA Ops:
  0.6 32.4 %copy-start = (bf16[6144,1536]{1,0:T(8,128)(2,1)S(1)}, bf16[6144,1536]{1,0:T(8,128)(2,1)}, u32[]{:S(2)}) copy-start(bf16[6144,1536]{1,0:T(8,128)(2,1)} %refs_2_.5) | copy-start | bytes 56623108
  9.3 9.8 %copy-start.2 = (bf16[768]{0:T(1024)(128)(2,1)S(1)}, bf16[768]{0:T(1024)(128)(2,1)}, u32[]{:S(2)}) copy-start(bf16[768]{0:T(1024)(128)(2,1)} %param.8) | copy-start | bytes 4612
  9.3 14.0 %copy-start.1 = (bf16[128,768]{1,0:T(8,128)(2,1)S(1)}, bf16[128,768]{1,0:T(8,128)(2,1)}, u32[]{:S(2)}) copy-start(bf16[128,768]{1,0:T(8,128)(2,1)} %refs_6_.1) | copy-start | bytes 589828
  9.3 5.8 %collective-permute-start = (bf16[2,128,512]{2,1,0:T(8,128)(2,1)S(1)}, bf16[2,128,512]{2,1,0:T(8,128)(2,1)S(1)}, u32[]{:S(2)}, u32[]{:S(2)}) collective-permute-start(bf16[2,128,512]{2,1,0:T(8,128)(2,1)S(1)} %get-tuple-element.32), channel_id=1, source_target_pairs={{0,8},{8,0},{16,24},{24,16},{1,9},{9,1},{17,25},{25,17},{2,10},{10... | collective-permute-start | bytes 786440 | tf_op jit(solution)/shard_map/ppermute | solution.py:275
  14.7 3.1 %collective-permute-start.2 = (bf16[2,128,256]{2,1,0:T(8,128)(2,1)S(1)}, bf16[2,128,256]{2,1,0:T(8,128)(2,1)S(1)}, u32[]{:S(2)}, u32[]{:S(2)}) collective-permute-start(bf16[2,128,256]{2,1,0:T(8,128)(2,1)S(1)} %get-tuple-element.35), channel_id=1, source_target_pairs={{0,8},{8,0},{16,24},{24,16},{1,9},{9,1},{17,25},{25,17},{2,10},{10... | collective-permute-start | bytes 393224 | tf_op jit(solution)/shard_map/ppermute | solution.py:275
  15.2 8.2 %collective-permute-start.1 = (bf16[128,512]{1,0:T(8,128)(2,1)S(1)}, bf16[128,512]{1,0:T(8,128)(2,1)S(1)}, u32[]{:S(2)}, u32[]{:S(2)}) collective-permute-start(bf16[128,512]{1,0:T(8,128)(2,1)S(1)} %fusion), channel_id=1, source_target_pairs={{0,16},{8,24},{16,0},{24,8},{1,17},{9,25},{17,1},{25,9},{2,18},{10... | collective-permute-start | bytes 393224 | tf_op jit(solution)/shard_map/ppermute | solution.py:282
  17.9 5.5 %collective-permute-start.3 = (bf16[128,256]{1,0:T(8,128)(2,1)S(1)}, bf16[128,256]{1,0:T(8,128)(2,1)S(1)}, u32[]{:S(2)}, u32[]{:S(2)}) collective-permute-start(bf16[128,256]{1,0:T(8,128)(2,1)S(1)} %fusion.1), channel_id=1, source_target_pairs={{0,16},{8,24},{16,0},{24,8},{1,17},{9,25},{17,1},{25,9},{2,18},{10... | collective-permute-start | bytes 196616 | tf_op jit(solution)/shard_map/ppermute | solution.py:282
  24.1 6.9 %collective-permute-start.4 = (bf16[136,768]{1,0:T(8,128)(2,1)S(1)}, bf16[136,768]{1,0:T(8,128)(2,1)S(1)}, u32[]{:S(2)}, u32[]{:S(2)}) collective-permute-start(bf16[136,768]{1,0:T(8,128)(2,1)S(1)} %get-tuple-element.37.refs_0_), channel_id=1, source_target_pairs={{0,1},{1,3},{3,5},{5,7},{7,6},{6,4},{4,2},{2,0},{8,9},{9,11},{11,1... | collective-permute-start | bytes 626696 | tf_op jit(solution)/shard_map/ppermute | solution.py:291
  25.8 6.7 %collective-permute-start.6 = (bf16[136,768]{1,0:T(8,128)(2,1)S(1)}, bf16[136,768]{1,0:T(8,128)(2,1)S(1)}, u32[]{:S(2)}, u32[]{:S(2)}) collective-permute-start(bf16[136,768]{1,0:T(8,128)(2,1)S(1)} %get-tuple-element.37.refs_0_), channel_id=1, source_target_pairs={{1,0},{3,1},{5,3},{7,5},{6,7},{4,6},{2,4},{0,2},{9,8},{11,9},{13,1... | collective-permute-start | bytes 626696 | tf_op jit(solution)/shard_map/ppermute | solution.py:291
  31.0 6.0 %collective-permute-start.5 = (bf16[136,768]{1,0:T(8,128)(2,1)S(1)}, bf16[136,768]{1,0:T(8,128)(2,1)S(1)}, u32[]{:S(2)}, u32[]{:S(2)}) collective-permute-start(bf16[136,768]{1,0:T(8,128)(2,1)S(1)} %collective-permute-done.4.refs_1_), channel_id=1, source_target_pairs={{0,1},{1,3},{3,5},{5,7},{7,6},{6,4},{4,2},{2,0},{8,9},{9,11},{11,1... | collective-permute-start | bytes 626696 | tf_op jit(solution)/shard_map/ppermute | solution.py:291
  32.5 5.8 %collective-permute-start.7 = (bf16[136,768]{1,0:T(8,128)(2,1)S(1)}, bf16[136,768]{1,0:T(8,128)(2,1)S(1)}, u32[]{:S(2)}, u32[]{:S(2)}) collective-permute-start(bf16[136,768]{1,0:T(8,128)(2,1)S(1)} %collective-permute-done.6.refs_2_), channel_id=1, source_target_pairs={{1,0},{3,1},{5,3},{7,5},{6,7},{4,6},{2,4},{0,2},{9,8},{11,9},{13,1... | collective-permute-start | bytes 626696 | tf_op jit(solution)/shard_map/ppermute | solution.py:291
  38.3 5.8 %collective-permute-start.8 = (bf16[136,768]{1,0:T(8,128)(2,1)S(1)}, bf16[136,768]{1,0:T(8,128)(2,1)S(1)}, u32[]{:S(2)}, u32[]{:S(2)}) collective-permute-start(bf16[136,768]{1,0:T(8,128)(2,1)S(1)} %collective-permute-done.5.refs_0_), channel_id=1, source_target_pairs={{0,1},{1,3},{3,5},{5,7},{7,6},{6,4},{4,2},{2,0},{8,9},{9,11},{11,1... | collective-permute-start | bytes 626696 | tf_op jit(solution)/shard_map/ppermute | solution.py:291
  39.9 6.6 %collective-permute-start.9 = (bf16[136,768]{1,0:T(8,128)(2,1)S(1)}, bf16[136,768]{1,0:T(8,128)(2,1)S(1)}, u32[]{:S(2)}, u32[]{:S(2)}) collective-permute-start(bf16[136,768]{1,0:T(8,128)(2,1)S(1)} %collective-permute-done.7.refs_1_), channel_id=1, source_target_pairs={{1,0},{3,1},{5,3},{7,5},{6,7},{4,6},{2,4},{0,2},{9,8},{11,9},{13,1... | collective-permute-start | bytes 626696 | tf_op jit(solution)/shard_map/ppermute | solution.py:291
  46.6 5.2 %collective-permute-start.11 = (bf16[72,768]{1,0:T(8,128)(2,1)S(1)}, bf16[72,768]{1,0:T(8,128)(2,1)S(1)}, u32[]{:S(2)}, u32[]{:S(2)}) collective-permute-start(bf16[72,768]{1,0:T(8,128)(2,1)S(1)} %slice.23), channel_id=1, source_target_pairs={{1,0},{3,1},{5,3},{7,5},{6,7},{4,6},{2,4},{0,2},{9,8},{11,9},{13,1... | collective-permute-start | bytes 331784 | tf_op jit(solution)/shard_map/ppermute | solution.py:291
  47.1 4.7 %collective-permute-start.10 = (bf16[64,768]{1,0:T(8,128)(2,1)S(1)}, bf16[64,768]{1,0:T(8,128)(2,1)S(1)}, u32[]{:S(2)}, u32[]{:S(2)}) collective-permute-start(bf16[64,768]{1,0:T(8,128)(2,1)S(1)} %slice.22), channel_id=1, source_target_pairs={{0,1},{1,3},{3,5},{5,7},{7,6},{6,4},{4,2},{2,0},{8,9},{9,11},{11,1... | collective-permute-start | bytes 294920 | tf_op jit(solution)/shard_map/ppermute | solution.py:291

commit v5 on v4

--- a/solution.py
+++ b/solution.py
@@ -43,113 +43,109 @@
     return fits[-1] if fits else size
 
 
-def down_kernel(chips_y, tok, first, kept, *refs):
-    refs = list(refs)
-    hidden, weight, give, keep = refs[:4]
-    held = refs.pop(4) if not kept else hidden
-    w_buf, total, sems = refs[4:]
-    parts, _, depth = held.shape
-    columns = pl.ds(first, w_buf.shape[2])
+def down_kernel(chips_y, tok, own, hidden, weight, *refs):
+    if own:
+        (give, keep), held = refs[:2], weight
+    else:
+        give, keep, held = refs[:3]
+    h_buf, total, sems = refs[-3:]
+    parts, depth, _ = held.shape
+    me = lax.axis_index("row")
+    chip, core = me // CORES, me % CORES
+    chips = [0] if own else list(range(1, chips_y))
+    block = CORES * tok
 
     def copies(k):
         span = pl.ds(pl.multiple_of(k * depth, depth), depth)
-        both = [pltpu.make_async_copy(weight.at[span, columns], w_buf.at[k], sems.at[1, k])]
-        if not kept:
-            both.append(pltpu.make_async_copy(hidden.at[:, span], held.at[k], sems.at[0, k]))
-        return both
+        for i, step in enumerate(chips):
+            start = pl.multiple_of(lax.rem(chip + step, chips_y) * block, block)
+            yield pltpu.make_async_copy(
+                hidden.at[pl.ds(start, block), span], h_buf.at[k, pl.ds(i * block, block)], sems.at[1 + i, k]
+            )
+        if not own:
+            yield pltpu.make_async_copy(weight.at[span, :], held.at[k], sems.at[0, k])
 
     for k in range(parts):
-        for priority, copy in enumerate(copies(k)):
-            copy.start(priority=priority)
+        for copy in copies(k):
+            copy.start()
     for copy in copies(0):
         copy.wait()
-    total[...] = jnp.dot(held[0], w_buf[0], preferred_element_type=jnp.float32)
+    total[...] = jnp.dot(h_buf[0], held[0], preferred_element_type=jnp.float32)
 
     def body(k, _):
         for copy in copies(k):
             copy.wait()
-        total[...] += jnp.dot(held[k], w_buf[k], preferred_element_type=jnp.float32)
+        total[...] += jnp.dot(h_buf[k], held[k], preferred_element_type=jnp.float32)
         return _
 
     lax.fori_loop(1, parts, body, 0)
-    me = lax.axis_index("row")
-    chip, core = me // CORES, me % CORES
-    for i in range(chips_y):
-        other = lax.rem(chip + i, chips_y)
+    for i in range(len(chips)):
         for out, which in ((give, 1 - core), (keep, core)):
-            start = pl.multiple_of((other * CORES + which) * tok, tok)
+            start = pl.multiple_of((i * CORES + which) * tok, tok)
             out[i] = total[pl.ds(start, tok), :].astype(out.dtype)
 
 
-def down(hidden, weight, tok, chips_y, first, width):
-    kept = hidden.ndim == 3
-    if kept:
-        parts, tokens, depth = hidden.shape
-    else:
-        tokens, inner = hidden.shape
-        depth = cut(inner, 512)
+def down(hidden, weight, tok, chips_y, own):
+    inner = hidden.shape[1]
+    if own:
+        parts, depth, width = weight.shape
+    else:
+        width = weight.shape[1]
+        depth = cut(inner, 768)
         parts = inner // depth
-    held = pltpu.VMEM((parts, tokens, depth), jnp.bfloat16)
-    block = pltpu.VMEM((chips_y, tok, width), jnp.bfloat16)
-    out_shape = (block, block) if kept else (block, block, held)
-    got = pl.pallas_call(
-        functools.partial(down_kernel, chips_y, tok, first, kept),
+    chips = 1 if own else chips_y - 1
+    tokens = chips * CORES * tok
+    block = pltpu.VMEM((chips, tok, width), jnp.bfloat16)
+    out_shape = (block, block) if own else (block, block, pltpu.VMEM((parts, depth, width), jnp.bfloat16))
+    return pl.pallas_call(
+        functools.partial(down_kernel, chips_y, tok, own),
         out_shape=out_shape,
-        in_specs=[VMEM if kept else HBM, HBM],
+        in_specs=[HBM, VMEM if own else HBM],
         out_specs=(VMEM,) * len(out_shape),
         scratch_shapes=[
-            pltpu.VMEM((parts, depth, width), jnp.bfloat16),
+            pltpu.VMEM((parts, tokens, depth), jnp.bfloat16),
             pltpu.VMEM((tokens, width), jnp.float32),
-            pltpu.SemaphoreType.DMA((2, parts)),
+            pltpu.SemaphoreType.DMA((1 + chips, parts)),
         ],
         compiler_params=pltpu.CompilerParams(vmem_limit_bytes=24 * MIB),
         cost_estimate=pl.CostEstimate(
-            flops=2 * tokens * parts * depth * width,
-            bytes_accessed=2 * parts * depth * (width if kept else width + tokens),
+            flops=2 * tokens * inner * width,
+            bytes_accessed=2 * inner * (tokens if own else width + tokens),
             transcendentals=0,
         ),
         name="down",
     )(
-        pltpu.with_memory_space_constraint(hidden, pltpu.VMEM if kept else pltpu.HBM),
-        pltpu.with_memory_space_constraint(weight, pltpu.HBM),
+        pltpu.with_memory_space_constraint(hidden, pltpu.HBM),
+        pltpu.with_memory_space_constraint(weight, pltpu.VMEM if own else pltpu.HBM),
     )
-    return (*got, hidden) if kept else got
-
-
-def merge_kernel(counts, *refs):
-    refs = list(refs)
-    *refs, residual, gain, stream, piece = refs
-    tok = residual.shape[0]
-    start = 0
-    for count in counts:
-        keep, got, *others = refs[:count]
-        refs = refs[count:]
-        span = pl.ds(start, keep.shape[2])
-        start += keep.shape[2]
-        value = keep[0].astype(jnp.float32) + got[0].astype(jnp.float32)
-        for other in others:
-            value = value + other[...].astype(jnp.float32)
-        value = (residual[:, span].astype(jnp.float32) + value).astype(stream.dtype)
-        stream[:, span] = value
-        piece[0:tok, span] = value
-    rows = jnp.broadcast_to(gain[...].astype(jnp.float32), (GAIN, gain.shape[1]))
+
+
+def merge_kernel(*refs):
+    *parts, residual, gain, stream, piece = refs
+    tok, width = residual.shape
+    total = parts[0][...].astype(jnp.float32)
+    for part in parts[1:]:
+        total = total + part[...].astype(jnp.float32)
+    value = (residual[...].astype(jnp.float32) + total).astype(stream.dtype)
+    stream[...] = value
+    piece[0:tok, :] = value
+    rows = jnp.broadcast_to(gain[...].astype(jnp.float32), (GAIN, width))
     piece[tok : tok + GAIN, :] = rows.astype(piece.dtype)
 
 
-def merge(groups, residual, gain):
+def merge(parts, residual, gain):
     tok, width = residual.shape
-    flat = [x for group in groups for x in group]
     return pl.pallas_call(
-        functools.partial(merge_kernel, [len(group) for group in groups]),
+        merge_kernel,
         out_shape=(
             jax.ShapeDtypeStruct((tok, width), jnp.bfloat16),
             pltpu.VMEM((tok + GAIN, width), jnp.bfloat16),
         ),
-        in_specs=[VMEM] * (len(flat) + 2),
+        in_specs=[VMEM] * (len(parts) + 2),
         out_specs=(VMEM, VMEM),
         compiler_params=pltpu.CompilerParams(vmem_limit_bytes=8 * MIB),
         name="merge",
-    )(*flat, residual, gain)
+    )(*parts, residual, gain)
 
 
 def project_kernel(cycle, hops, shapes, first, last, *refs):
@@ -265,23 +261,17 @@
     behind = [(cycle[(i + 1) % cols], cycle[i]) for i in range(cols)]
 
     def per_device(hidden, down_weight, residual, gain, qk_weight):
-        tok, width = residual.shape
-        wide = width * 2 // 3 // 128 * 128 or width
-        spans = [(0, wide), (wide, width - wide)] if wide < width else [(0, width)]
-
-        sums = []
-        for first, count in spans:
-            give, keep, hidden = down(hidden, down_weight, tok, chips_y, first, count)
-            sums.append((keep, lax.ppermute(give, "row", sibling)))
-        groups = []
-        for keep, got in sums:
-            others = []
-            for step in range(1, chips_y):
-                move = [(r, (r + CORES * step) % rows) for r in range(rows)]
-                both = keep[step].astype(jnp.float32) + got[step].astype(jnp.float32)
-                others.append(lax.ppermute(both.astype(jnp.bfloat16), "row", move))
-            groups.append((keep, got, *others))
-        stream, piece = merge(groups, residual, gain[None, :])
+        tok = residual.shape[0]
+
+        cross, same, down_weight = down(hidden, down_weight, tok, chips_y, False)
+        parts = []
+        for step in range(1, chips_y):
+            for blocks, flip in ((same, 0), (cross, 1)):
+                move = [(r, ((r + CORES * step) % rows) ^ flip) for r in range(rows)]
+                parts.append(lax.ppermute(blocks[step - 1], "row", move))
+        give, keep = down(hidden, down_weight, tok, chips_y, True)
+        parts += [keep[0], lax.ppermute(give[0], "row", sibling)]
+        stream, piece = merge(parts, residual, gain[None, :])
 
         up, back = piece, piece
         pieces, hops, state = [], [], None

time: 53.3 us -> 48.7 us (0.914)
  Pallas kernels: 19.5 us -> 16.9 us
  starting transfers between devices: 13 us -> 11.8 us
  waiting for transfers between devices: 19.9 us -> 19.1 us
    pallas_call x3, Pallas kernels: 14.3 us -> 11.9 us  [the longest x2 11.1 us: down(): pl.pallas_call(functools.partial(down_kernel, chips_y, tok, own), out_sha...]
    ppermute x4 -> x3, waiting for transfers between devices: 4.25 us -> 2.33 us  [the longest x2 2.32 us: per_device(): parts.append(lax.ppermute(blocks[step - 1], 'row', move))]
    ppermute x4, waiting for transfers between devices: 12 us -> 13.8 us  [per_device(): lax.ppermute(up, 'col', ahead)]
    ppermute x4 -> x3, starting transfers between devices: 4.81 us -> 3.55 us  [the longest x2 3.03 us: per_device(): parts.append(lax.ppermute(blocks[step - 1], 'row', move))]
    ppermute x4, waiting for transfers between devices: 3.71 us -> 2.95 us  [per_device(): lax.ppermute(back, 'col', behind)]
  transfers between devices with their start and end apart: 12 -> 11, of which waited for: 7 -> 7; matrix products, arithmetic and copies ran while one was open for 0% -> 0% of each run, Pallas kernels for 16% -> 19%
where the time goes in v5:
time: 48.7 us; the launch traced here: 48.5 us
  waiting for transfers between devices  19.1 us (39%)
  Pallas kernels  16.9 us (35%)
  starting transfers between devices  11.8 us (24%)
  between operations  0.71 us (1%)
    ppermute x4, waiting for transfers between devices, per_device(): lax.ppermute(up, 'col', ahead)  13.8 us
    pallas_call x2, Pallas kernels, down(): pl.pallas_call(functools.partial(down_kernel, chips_y, tok, own), out_sha...  11.1 us
    ppermute x4, starting transfers between devices, per_device(): lax.ppermute(up, 'col', ahead)  6.36 us
    pallas_call x4, Pallas kernels, project(): pl.pallas_call(functools.partial(project_kernel, cycle, hops, [len(parts)...  5.03 us
    ppermute x2, starting transfers between devices, per_device(): parts.append(lax.ppermute(blocks[step - 1], 'row', move))  3.03 us
    ppermute x4, waiting for transfers between devices, per_device(): lax.ppermute(back, 'col', behind)  2.95 us
    ppermute x2, waiting for transfers between devices, per_device(): parts.append(lax.ppermute(blocks[step - 1], 'row', move))  2.32 us
    ppermute x4, starting transfers between devices, per_device(): lax.ppermute(back, 'col', behind)  1.85 us
  transfers between devices with their start and end apart: 11, of which 7 were waited for; matrix products, arithmetic and copies ran while one was open for 0% of the time, Pallas kernels for 19%

profile of v5, /device:TPU:0, one launch (start us, length us, event | category | flops | bytes accessed | tf_op | source)
XLA Modules:
  0.0 48.5 jit_solution(12664457562856959215)
XLA Ops:
  0.6 5.6 %down.2 = (bf16[1,128,768]{2,1,0:T(8,128)(2,1)S(1)}, bf16[1,128,768]{2,1,0:T(8,128)(2,1)S(1)}, bf16[8,768,768]{2,1,0:T(8,128)(2,1)S(1)}) custom-call(bf16[512,6144]{1,0:T(8,128)(2,1)} %hidden.3, bf16[6144,768]{1,0:T(8,128)(2,1)} %weight.1), custom_call_target="tpu_custom_call" | custom-call | flops 2415919104 | bytes 12582912 | tf_op jit(solution)/shard_map/down/pallas_call | solution.py:100
  6.3 3.0 %collective-permute-start = (bf16[128,768]{1,0:T(8,128)(2,1)S(1)}, bf16[128,768]{1,0:T(8,128)(2,1)S(1)}, u32[]{:S(2)}, u32[]{:S(2)}) collective-permute-start(bf16[128,768]{1,0:T(8,128)(2,1)S(1)} %bitcast.6), channel_id=1, source_target_pairs={{0,16},{8,24},{16,0},{24,8},{1,17},{9,25},{17,1},{25,9},{2,18},{10... | collective-permute-start | bytes 589832 | tf_op jit(solution)/shard_map/ppermute | solution.py:271
  9.3 5.5 %down.3 = (bf16[1,128,768]{2,1,0:T(8,128)(2,1)S(1)}, bf16[1,128,768]{2,1,0:T(8,128)(2,1)S(1)}) custom-call(bf16[512,6144]{1,0:T(8,128)(2,1)} %hidden.3, bf16[8,768,768]{2,1,0:T(8,128)(2,1)S(1)} %get-tuple-element.33.weight), custom_call_target="tpu_custom_call" | custom-call | flops 2415919104 | bytes 3145728 | tf_op jit(solution)/shard_map/down/pallas_call | solution.py:100
  14.8 0.5 %collective-permute-start.2 = (bf16[128,768]{1,0:T(8,128)(2,1)S(1)}, bf16[128,768]{1,0:T(8,128)(2,1)S(1)}, u32[]{:S(2)}, u32[]{:S(2)}) collective-permute-start(bf16[128,768]{1,0:T(8,128)(2,1)S(1)} %bitcast.7), channel_id=1, source_target_pairs={{0,8},{8,0},{16,24},{24,16},{1,9},{9,1},{17,25},{25,17},{2,10},{10... | collective-permute-start | bytes 589832 | tf_op jit(solution)/shard_map/ppermute | solution.py:273
  15.4 2.3 %collective-permute-done.1.refs_1_ = bf16[128,768]{1,0:T(8,128)(2,1)S(1)} collective-permute-done((bf16[128,768]{1,0:T(8,128)(2,1)S(1)}, bf16[128,768]{1,0:T(8,128)(2,1)S(1)}, u32[]{:S(2)}, u32[]{:S(2)}) %collective-permute-start.1) | collective-permute-done | bytes 196640 | tf_op jit(solution)/shard_map/ppermute | solution.py:271
  17.7 0.8 %merge.1 = (bf16[128,768]{1,0:T(8,128)(2,1)}, bf16[136,768]{1,0:T(8,128)(2,1)S(1)}) custom-call(bf16[128,768]{1,0:T(8,128)(2,1)S(1)} %collective-permute-done.refs_0_, bf16[128,768]{1,0:T(8,128)(2,1)S(1)} %collective-permute-done.1.refs_1_, bf16[128,768]{1,0:T(8,128)(2,1)S(1)} %bitcast.4, bf16[128,768]{1,0:T(8,128)(2,1)S(1)} %collective-permute-done.2.refs_3_, ...), custom_call_target="tpu_custom_call" | custom-call | tf_op jit(solution)/shard_map/merge/pallas_call | solution.py:138
  18.5 1.5 %collective-permute-start.3 = (bf16[136,768]{1,0:T(8,128)(2,1)S(1)}, bf16[136,768]{1,0:T(8,128)(2,1)S(1)}, u32[]{:S(2)}, u32[]{:S(2)}) collective-permute-start(bf16[136,768]{1,0:T(8,128)(2,1)S(1)} %get-tuple-element.37.refs_0_), channel_id=1, source_target_pairs={{0,1},{1,3},{3,5},{5,7},{7,6},{6,4},{4,2},{2,0},{8,9},{9,11},{11,1... | collective-permute-start | bytes 626696 | tf_op jit(solution)/shard_map/ppermute | solution.py:281
  20.0 0.5 %collective-permute-start.5 = (bf16[136,768]{1,0:T(8,128)(2,1)S(1)}, bf16[136,768]{1,0:T(8,128)(2,1)S(1)}, u32[]{:S(2)}, u32[]{:S(2)}) collective-permute-start(bf16[136,768]{1,0:T(8,128)(2,1)S(1)} %get-tuple-element.37.refs_0_), channel_id=1, source_target_pairs={{1,0},{3,1},{5,3},{7,5},{6,7},{4,6},{2,4},{0,2},{9,8},{11,9},{13,1... | collective-permute-start | bytes 626696 | tf_op jit(solution)/shard_map/ppermute | solution.py:281
  20.5 5.7 %collective-permute-done.3.refs_1_ = bf16[136,768]{1,0:T(8,128)(2,1)S(1)} collective-permute-done((bf16[136,768]{1,0:T(8,128)(2,1)S(1)}, bf16[136,768]{1,0:T(8,128)(2,1)S(1)}, u32[]{:S(2)}, u32[]{:S(2)}) %collective-permute-start.3) | collective-permute-done | bytes 208928 | tf_op jit(solution)/shard_map/ppermute | solution.py:281
  26.2 1.7 %collective-permute-start.4 = (bf16[136,768]{1,0:T(8,128)(2,1)S(1)}, bf16[136,768]{1,0:T(8,128)(2,1)S(1)}, u32[]{:S(2)}, u32[]{:S(2)}) collective-permute-start(bf16[136,768]{1,0:T(8,128)(2,1)S(1)} %collective-permute-done.3.refs_1_), channel_id=1, source_target_pairs={{0,1},{1,3},{3,5},{5,7},{7,6},{6,4},{4,2},{2,0},{8,9},{9,11},{11,1... | collective-permute-start | bytes 626696 | tf_op jit(solution)/shard_map/ppermute | solution.py:281
  27.8 0.4 collective-permute-start.6
  28.2 1.4 %project.4 = (f32[128,1]{1,0:T(8,128)S(1)}, f32[2,128,1]{2,1,0:T(8,128)S(1)}, f32[144,1536]{1,0:T(8,128)S(1)}) custom-call(bf16[136,768]{1,0:T(8,128)(2,1)S(1)} %get-tuple-element.37.refs_0_, bf16[136,768]{1,0:T(8,128)(2,1)S(1)} %collective-permute-done.3.refs_1_, bf16[136,768]{1,0:T(8,128)(2,1)S(1)} %collective-permute-done.5.refs_2_, ...), custom_call_target="tpu_custom_call" | custom-call | flops 1019215872 | tf_op jit(solution)/shard_map/project/pallas_call | solution.py:231
  29.6 3.5 %collective-permute-done.4.refs_0_ = bf16[136,768]{1,0:T(8,128)(2,1)S(1)} collective-permute-done((bf16[136,768]{1,0:T(8,128)(2,1)S(1)}, bf16[136,768]{1,0:T(8,128)(2,1)S(1)}, u32[]{:S(2)}, u32[]{:S(2)}) %collective-permute-start.4) | collective-permute-done | bytes 208928 | tf_op jit(solution)/shard_map/ppermute | solution.py:281
  33.2 1.4 %collective-permute-done.6.refs_1_ = bf16[136,768]{1,0:T(8,128)(2,1)S(1)} collective-permute-done((bf16[136,768]{1,0:T(8,128)(2,1)S(1)}, bf16[136,768]{1,0:T(8,128)(2,1)S(1)}, u32[]{:S(2)}, u32[]{:S(2)}) %collective-permute-start.6) | collective-permute-done | bytes 208928 | tf_op jit(solution)/shard_map/ppermute | solution.py:281
  34.5 1.6 %collective-permute-start.7 = (bf16[136,768]{1,0:T(8,128)(2,1)S(1)}, bf16[136,768]{1,0:T(8,128)(2,1)S(1)}, u32[]{:S(2)}, u32[]{:S(2)}) collective-permute-start(bf16[136,768]{1,0:T(8,128)(2,1)S(1)} %collective-permute-done.4.refs_0_), channel_id=1, source_target_pairs={{0,1},{1,3},{3,5},{5,7},{7,6},{6,4},{4,2},{2,0},{8,9},{9,11},{11,1... | collective-permute-start | bytes 626696 | tf_op jit(solution)/shard_map/ppermute | solution.py:281
  36.1 0.4 collective-permute-start.8
  36.6 1.1 %project.5 = (f32[2,128,1]{2,1,0:T(8,128)S(1)}, f32[144,1536]{1,0:T(8,128)S(1)}) custom-call(bf16[136,768]{1,0:T(8,128)(2,1)S(1)} %collective-permute-done.4.refs_0_, bf16[136,768]{1,0:T(8,128)(2,1)S(1)} %collective-permute-done.6.refs_1_, bf16[6144,1536]{1,0:T(8,128)(2,1)S(1)} %copy-done, ...), custom_call_target="tpu_custom_call", output_to_operand_aliasing={{0}: (4, {}), {1}: (5, {})} | custom-call | flops 679477248 | tf_op jit(solution)/shard_map/project/pallas_call | solution.py:231
  37.7 2.7 %collective-permute-done.7.refs_0_ = bf16[136,768]{1,0:T(8,128)(2,1)S(1)} collective-permute-done((bf16[136,768]{1,0:T(8,128)(2,1)S(1)}, bf16[136,768]{1,0:T(8,128)(2,1)S(1)}, u32[]{:S(2)}, u32[]{:S(2)}) %collective-permute-start.7) | collective-permute-done | bytes 208928 | tf_op jit(solution)/shard_map/ppermute | solution.py:281
  40.4 1.6 %collective-permute-done.8.refs_1_ = bf16[136,768]{1,0:T(8,128)(2,1)S(1)} collective-permute-done((bf16[136,768]{1,0:T(8,128)(2,1)S(1)}, bf16[136,768]{1,0:T(8,128)(2,1)S(1)}, u32[]{:S(2)}, u32[]{:S(2)}) %collective-permute-start.8) | collective-permute-done | bytes 208928 | tf_op jit(solution)/shard_map/ppermute | solution.py:281
  41.9 0.5 %collective-permute-start.10 = (bf16[72,768]{1,0:T(8,128)(2,1)S(1)}, bf16[72,768]{1,0:T(8,128)(2,1)S(1)}, u32[]{:S(2)}, u32[]{:S(2)}) collective-permute-start(bf16[72,768]{1,0:T(8,128)(2,1)S(1)} %slice.7), channel_id=1, source_target_pairs={{1,0},{3,1},{5,3},{7,5},{6,7},{4,6},{2,4},{0,2},{9,8},{11,9},{13,1... | collective-permute-start | bytes 331784 | tf_op jit(solution)/shard_map/ppermute | solution.py:281
  42.4 1.6 %collective-permute-start.9 = (bf16[64,768]{1,0:T(8,128)(2,1)S(1)}, bf16[64,768]{1,0:T(8,128)(2,1)S(1)}, u32[]{:S(2)}, u32[]{:S(2)}) collective-permute-start(bf16[64,768]{1,0:T(8,128)(2,1)S(1)} %slice.6), channel_id=1, source_target_pairs={{0,1},{1,3},{3,5},{5,7},{7,6},{6,4},{4,2},{2,0},{8,9},{9,11},{11,1... | collective-permute-start | bytes 294920 | tf_op jit(solution)/shard_map/ppermute | solution.py:281
  44.1 1.1 %project.6 = (f32[2,128,1]{2,1,0:T(8,128)S(1)}, f32[144,1536]{1,0:T(8,128)S(1)}) custom-call(bf16[136,768]{1,0:T(8,128)(2,1)S(1)} %collective-permute-done.7.refs_0_, bf16[136,768]{1,0:T(8,128)(2,1)S(1)} %collective-permute-done.8.refs_1_, bf16[6144,1536]{1,0:T(8,128)(2,1)S(1)} %copy-done, ...), custom_call_target="tpu_custom_call", output_to_operand_aliasing={{0}: (4, {}), {1}: (5, {})} | custom-call | flops 679477248 | tf_op jit(solution)/shard_map/project/pallas_call | solution.py:231
  45.2 1.9 %collective-permute-done.9.refs_0_ = bf16[64,768]{1,0:T(8,128)(2,1)S(1)} collective-permute-done((bf16[64,768]{1,0:T(8,128)(2,1)S(1)}, bf16[64,768]{1,0:T(8,128)(2,1)S(1)}, u32[]{:S(2)}, u32[]{:S(2)}) %collective-permute-start.9) | collective-permute-done | bytes 98336 | tf_op jit(solution)/shard_map/ppermute | solution.py:281
  47.1 1.4 %project.7 = bf16[128,1536]{1,0:T(8,128)(2,1)} custom-call(bf16[64,768]{1,0:T(8,128)(2,1)S(1)} %collective-permute-done.9.refs_0_, bf16[72,768]{1,0:T(8,128)(2,1)S(1)} %collective-permute-done.10.refs_1_, bf16[6144,1536]{1,0:T(8,128)(2,1)S(1)} %copy-done, f32[128,1]{1,0:T(8,128)S(1)} %get-tuple-element.57.refs_3_, ...), custom_call_target="tpu_custom_call" | custom-call | flops 339738624 | tf_op jit(solution)/shard_map/project/pallas_call | solution.py:231
  (14 shorter events, 0.1 us)
Async XLA Ops:
  0.6 27.6 %copy-start = (bf16[6144,1536]{1,0:T(8,128)(2,1)S(1)}, bf16[6144,1536]{1,0:T(8,128)(2,1)}, u32[]{:S(2)}) copy-start(bf16[6144,1536]{1,0:T(8,128)(2,1)} %refs_2_.5) | copy-start | bytes 56623108
  6.2 9.1 %copy-start.2 = (bf16[768]{0:T(1024)(128)(2,1)S(1)}, bf16[768]{0:T(1024)(128)(2,1)}, u32[]{:S(2)}) copy-start(bf16[768]{0:T(1024)(128)(2,1)} %param.8) | copy-start | bytes 4612
  6.3 11.4 %copy-start.1 = (bf16[128,768]{1,0:T(8,128)(2,1)S(1)}, bf16[128,768]{1,0:T(8,128)(2,1)}, u32[]{:S(2)}) copy-start(bf16[128,768]{1,0:T(8,128)(2,1)} %refs_4_.1) | copy-start | bytes 589828
  6.3 9.1 %collective-permute-start = (bf16[128,768]{1,0:T(8,128)(2,1)S(1)}, bf16[128,768]{1,0:T(8,128)(2,1)S(1)}, u32[]{:S(2)}, u32[]{:S(2)}) collective-permute-start(bf16[128,768]{1,0:T(8,128)(2,1)S(1)} %bitcast.6), channel_id=1, source_target_pairs={{0,16},{8,24},{16,0},{24,8},{1,17},{9,25},{17,1},{25,9},{2,18},{10... | collective-permute-start | bytes 589832 | tf_op jit(solution)/shard_map/ppermute | solution.py:271
  9.3 8.4 %collective-permute-start.1 = (bf16[128,768]{1,0:T(8,128)(2,1)S(1)}, bf16[128,768]{1,0:T(8,128)(2,1)S(1)}, u32[]{:S(2)}, u32[]{:S(2)}) collective-permute-start(bf16[128,768]{1,0:T(8,128)(2,1)S(1)} %bitcast.5), channel_id=1, source_target_pairs={{0,24},{8,16},{16,8},{24,0},{1,25},{9,17},{17,9},{25,1},{2,26},{10... | collective-permute-start | bytes 589832 | tf_op jit(solution)/shard_map/ppermute | solution.py:271
  14.8 2.9 %collective-permute-start.2 = (bf16[128,768]{1,0:T(8,128)(2,1)S(1)}, bf16[128,768]{1,0:T(8,128)(2,1)S(1)}, u32[]{:S(2)}, u32[]{:S(2)}) collective-permute-start(bf16[128,768]{1,0:T(8,128)(2,1)S(1)} %bitcast.7), channel_id=1, source_target_pairs={{0,8},{8,0},{16,24},{24,16},{1,9},{9,1},{17,25},{25,17},{2,10},{10... | collective-permute-start | bytes 589832 | tf_op jit(solution)/shard_map/ppermute | solution.py:273
  18.5 7.7 %collective-permute-start.3 = (bf16[136,768]{1,0:T(8,128)(2,1)S(1)}, bf16[136,768]{1,0:T(8,128)(2,1)S(1)}, u32[]{:S(2)}, u32[]{:S(2)}) collective-permute-start(bf16[136,768]{1,0:T(8,128)(2,1)S(1)} %get-tuple-element.37.refs_0_), channel_id=1, source_target_pairs={{0,1},{1,3},{3,5},{5,7},{7,6},{6,4},{4,2},{2,0},{8,9},{9,11},{11,1... | collective-permute-start | bytes 626696 | tf_op jit(solution)/shard_map/ppermute | solution.py:281
  20.0 7.9 %collective-permute-start.5 = (bf16[136,768]{1,0:T(8,128)(2,1)S(1)}, bf16[136,768]{1,0:T(8,128)(2,1)S(1)}, u32[]{:S(2)}, u32[]{:S(2)}) collective-permute-start(bf16[136,768]{1,0:T(8,128)(2,1)S(1)} %get-tuple-element.37.refs_0_), channel_id=1, source_target_pairs={{1,0},{3,1},{5,3},{7,5},{6,7},{4,6},{2,4},{0,2},{9,8},{11,9},{13,1... | collective-permute-start | bytes 626696 | tf_op jit(solution)/shard_map/ppermute | solution.py:281
  26.2 7.0 %collective-permute-start.4 = (bf16[136,768]{1,0:T(8,128)(2,1)S(1)}, bf16[136,768]{1,0:T(8,128)(2,1)S(1)}, u32[]{:S(2)}, u32[]{:S(2)}) collective-permute-start(bf16[136,768]{1,0:T(8,128)(2,1)S(1)} %collective-permute-done.3.refs_1_), channel_id=1, source_target_pairs={{0,1},{1,3},{3,5},{5,7},{7,6},{6,4},{4,2},{2,0},{8,9},{9,11},{11,1... | collective-permute-start | bytes 626696 | tf_op jit(solution)/shard_map/ppermute | solution.py:281
  27.8 6.7 %collective-permute-start.6 = (bf16[136,768]{1,0:T(8,128)(2,1)S(1)}, bf16[136,768]{1,0:T(8,128)(2,1)S(1)}, u32[]{:S(2)}, u32[]{:S(2)}) collective-permute-start(bf16[136,768]{1,0:T(8,128)(2,1)S(1)} %collective-permute-done.5.refs_2_), channel_id=1, source_target_pairs={{1,0},{3,1},{5,3},{7,5},{6,7},{4,6},{2,4},{0,2},{9,8},{11,9},{13,1... | collective-permute-start | bytes 626696 | tf_op jit(solution)/shard_map/ppermute | solution.py:281
  34.5 5.8 %collective-permute-start.7 = (bf16[136,768]{1,0:T(8,128)(2,1)S(1)}, bf16[136,768]{1,0:T(8,128)(2,1)S(1)}, u32[]{:S(2)}, u32[]{:S(2)}) collective-permute-start(bf16[136,768]{1,0:T(8,128)(2,1)S(1)} %collective-permute-done.4.refs_0_), channel_id=1, source_target_pairs={{0,1},{1,3},{3,5},{5,7},{7,6},{6,4},{4,2},{2,0},{8,9},{9,11},{11,1... | collective-permute-start | bytes 626696 | tf_op jit(solution)/shard_map/ppermute | solution.py:281
  36.1 5.8 %collective-permute-start.8 = (bf16[136,768]{1,0:T(8,128)(2,1)S(1)}, bf16[136,768]{1,0:T(8,128)(2,1)S(1)}, u32[]{:S(2)}, u32[]{:S(2)}) collective-permute-start(bf16[136,768]{1,0:T(8,128)(2,1)S(1)} %collective-permute-done.6.refs_1_), channel_id=1, source_target_pairs={{1,0},{3,1},{5,3},{7,5},{6,7},{4,6},{2,4},{0,2},{9,8},{11,9},{13,1... | collective-permute-start | bytes 626696 | tf_op jit(solution)/shard_map/ppermute | solution.py:281
  41.9 5.2 %collective-permute-start.10 = (bf16[72,768]{1,0:T(8,128)(2,1)S(1)}, bf16[72,768]{1,0:T(8,128)(2,1)S(1)}, u32[]{:S(2)}, u32[]{:S(2)}) collective-permute-start(bf16[72,768]{1,0:T(8,128)(2,1)S(1)} %slice.7), channel_id=1, source_target_pairs={{1,0},{3,1},{5,3},{7,5},{6,7},{4,6},{2,4},{0,2},{9,8},{11,9},{13,1... | collective-permute-start | bytes 331784 | tf_op jit(solution)/shard_map/ppermute | solution.py:281
  42.4 4.7 %collective-permute-start.9 = (bf16[64,768]{1,0:T(8,128)(2,1)S(1)}, bf16[64,768]{1,0:T(8,128)(2,1)S(1)}, u32[]{:S(2)}, u32[]{:S(2)}) collective-permute-start(bf16[64,768]{1,0:T(8,128)(2,1)S(1)} %slice.6), channel_id=1, source_target_pairs={{0,1},{1,3},{3,5},{5,7},{7,6},{6,4},{4,2},{2,0},{8,9},{9,11},{11,1... | collective-permute-start | bytes 294920 | tf_op jit(solution)/shard_map/ppermute | solution.py:281

commit v6 on v5

--- a/solution.py
+++ b/solution.py
@@ -56,7 +56,7 @@
     block = CORES * tok
 
     def copies(k):
-        span = pl.ds(pl.multiple_of(k * depth, depth), depth)
+        span = pl.ds(k * depth, depth)
         for i, step in enumerate(chips):
             start = pl.multiple_of(lax.rem(chip + step, chips_y) * block, block)
             yield pltpu.make_async_copy(
@@ -68,17 +68,15 @@
     for k in range(parts):
         for copy in copies(k):
             copy.start()
-    for copy in copies(0):
-        copy.wait()
-    total[...] = jnp.dot(h_buf[0], held[0], preferred_element_type=jnp.float32)
-
-    def body(k, _):
+    width = held.shape[2]
+    strip = cut(width, 256)
+    for k in range(parts):
         for copy in copies(k):
             copy.wait()
-        total[...] += jnp.dot(h_buf[k], held[k], preferred_element_type=jnp.float32)
-        return _
-
-    lax.fori_loop(1, parts, body, 0)
+        for n in range(0, width, strip):
+            span = pl.ds(n, strip)
+            product = jnp.dot(h_buf[k], held[k, :, span], preferred_element_type=jnp.float32)
+            total[:, span] = product if k == 0 else total[:, span] + product
     for i in range(len(chips)):
         for out, which in ((give, 1 - core), (keep, core)):
             start = pl.multiple_of((i * CORES + which) * tok, tok)
@@ -121,28 +119,26 @@
 
 
 def merge_kernel(*refs):
-    *parts, residual, gain, stream, piece = refs
+    *parts, residual, gain, stream, upper, lower = refs
     tok, width = residual.shape
     total = parts[0][...].astype(jnp.float32)
     for part in parts[1:]:
         total = total + part[...].astype(jnp.float32)
     value = (residual[...].astype(jnp.float32) + total).astype(stream.dtype)
     stream[...] = value
-    piece[0:tok, :] = value
+    upper[...] = value[: tok // 2]
+    lower[0 : tok // 2, :] = value[tok // 2 :]
     rows = jnp.broadcast_to(gain[...].astype(jnp.float32), (GAIN, width))
-    piece[tok : tok + GAIN, :] = rows.astype(piece.dtype)
+    lower[tok // 2 : tok // 2 + GAIN, :] = rows.astype(lower.dtype)
 
 
 def merge(parts, residual, gain):
     tok, width = residual.shape
     return pl.pallas_call(
         merge_kernel,
-        out_shape=(
-            jax.ShapeDtypeStruct((tok, width), jnp.bfloat16),
-            pltpu.VMEM((tok + GAIN, width), jnp.bfloat16),
-        ),
+        out_shape=[pltpu.VMEM((n, width), jnp.bfloat16) for n in (tok, tok // 2, tok // 2 + GAIN)],
         in_specs=[VMEM] * (len(parts) + 2),
-        out_specs=(VMEM, VMEM),
+        out_specs=[VMEM] * 3,
         compiler_params=pltpu.CompilerParams(vmem_limit_bytes=8 * MIB),
         name="merge",
     )(*parts, residual, gain)
@@ -263,32 +259,33 @@
     def per_device(hidden, down_weight, residual, gain, qk_weight):
         tok = residual.shape[0]
 
-        cross, same, down_weight = down(hidden, down_weight, tok, chips_y, False)
+        give, keep, down_weight = down(hidden, down_weight, tok, chips_y, False)
+        got = lax.ppermute(give, "row", sibling)
+        both = (keep.astype(jnp.float32) + got.astype(jnp.float32)).astype(jnp.bfloat16)
+        both, hidden = lax.optimization_barrier((both, hidden))
         parts = []
         for step in range(1, chips_y):
-            for blocks, flip in ((same, 0), (cross, 1)):
-                move = [(r, ((r + CORES * step) % rows) ^ flip) for r in range(rows)]
-                parts.append(lax.ppermute(blocks[step - 1], "row", move))
+            move = [(r, (r + CORES * step) % rows) for r in range(rows)]
+            parts.append(lax.ppermute(both[step - 1], "row", move))
         give, keep = down(hidden, down_weight, tok, chips_y, True)
         parts += [keep[0], lax.ppermute(give[0], "row", sibling)]
-        stream, piece = merge(parts, residual, gain[None, :])
-
-        up, back = piece, piece
+        stream, upper, lower = merge(parts, residual, gain[None, :])
+
+        up, back = [upper, lower], [upper, lower]
         pieces, hops, state = [], [], None
-        for step in range(1, half + 1):
-            if step == half:
-                up, back = up[: tok // 2], back[tok // 2 :]
-            up, back = lax.ppermute(up, "col", ahead), lax.ppermute(back, "col", behind)
+        for step in range(1, half):
+            for i in range(2):
+                up[i], back[i] = lax.ppermute(up[i], "col", ahead), lax.ppermute(back[i], "col", behind)
             if pieces:
                 state = project(pieces, hops, qk_weight, state, cycle, False)
-                up, back, state = lax.optimization_barrier((up, back, state))
-            if step < half:
-                pieces, hops = [[up], [back]], [-step, step]
-                if step == 1:
-                    pieces, hops = [[piece]] + pieces, [0] + hops
-            else:
-                pieces, hops = [[up, back]], [half]
-        return stream, project(pieces, hops, qk_weight, state, cycle, True)
+                up[1], back[1], state = lax.optimization_barrier((up[1], back[1], state))
+            pieces, hops = [list(up), list(back)], [-step, step]
+            if step == 1:
+                pieces, hops = [[upper, lower]] + pieces, [0] + hops
+        opposite = [lax.ppermute(up[0], "col", ahead), lax.ppermute(back[1], "col", behind)]
+        state = project(pieces, hops, qk_weight, state, cycle, False)
+        opposite, state = lax.optimization_barrier((opposite, state))
+        return stream, project([opposite], [half], qk_weight, state, cycle, True)
 
     placed = (P(None, "row"), P("row", "col"), P("row", "col"), P("col"), P(None, "col"))
     return jax.shard_map(

time: 48.7 us -> 49.1 us (level)
  waiting for transfers between devices: 19.1 us -> 12.6 us
  starting transfers between devices: 11.8 us -> 18 us
  local copies, waits for them, and re-layouts: 0.04 us -> 0.7 us
    ppermute x10 -> x16, waiting for transfers between devices: 19.1 us -> 12.6 us  [the longest x1 5.31 us: per_device(): parts.append(lax.ppermute(both[step - 1], 'row', move))]
    ppermute x10 -> x16, starting transfers between devices: 11.2 us -> 17.6 us  [the longest x6 10.6 us: per_device(): lax.ppermute(back[i], 'col', behind)]
    pallas_call x1, Pallas kernels: 0.81 us -> 0.1 us  [merge(): pl.pallas_call(merge_kernel, out_shape=[pltpu.VMEM((n, width), jnp.bfloat...]
    pallas_call x2, Pallas kernels: 11.1 us -> 11.8 us  [down(): pl.pallas_call(functools.partial(down_kernel, chips_y, tok, own), out_sha...]
    unnamed x6 -> x7, local copies, waits for them, and re-layouts: 0.02 us -> 0.69 us
  transfers between devices with their start and end apart: 11 -> 17, of which waited for: 7 -> 7; matrix products, arithmetic and copies ran while one was open for 0% -> 1% of each run, Pallas kernels for 19% -> 7%
where the time goes in v6:
time: 49.1 us; the launch traced here: 49 us
  starting transfers between devices  18 us (37%)
  Pallas kernels  16.9 us (34%)
  waiting for transfers between devices  12.6 us (26%)
  between operations  0.74 us (2%)
  local copies, waits for them, and re-layouts  0.7 us (1%)
    pallas_call x2, Pallas kernels, down(): pl.pallas_call(functools.partial(down_kernel, chips_y, tok, own), out_sha...  11.8 us
    ppermute x6, starting transfers between devices, per_device(): lax.ppermute(back[i], 'col', behind)  10.6 us
    ppermute x1, waiting for transfers between devices, per_device(): parts.append(lax.ppermute(both[step - 1], 'row', move))  5.31 us
    pallas_call x4, Pallas kernels, project(): pl.pallas_call(functools.partial(project_kernel, cycle, hops, [len(parts)...  5.02 us
    ppermute x1, starting transfers between devices, per_device(): parts.append(lax.ppermute(both[step - 1], 'row', move))  2.78 us
    ppermute x6, waiting for transfers between devices, per_device(): lax.ppermute(up[i], 'col', ahead)  2.08 us
    ppermute x1, waiting for transfers between devices, per_device(): lax.ppermute(up[0], 'col', ahead)  2.06 us
    ppermute x6, waiting for transfers between devices, per_device(): lax.ppermute(back[i], 'col', behind)  2.04 us
  transfers between devices with their start and end apart: 17, of which 7 were waited for; matrix products, arithmetic and copies ran while one was open for 1% of the time, Pallas kernels for 7%

profile of v6, /device:TPU:0, one launch (start us, length us, event | category | flops | bytes accessed | tf_op | source)
XLA Modules:
  0.0 49.0 jit_solution(17022479142490664741)
XLA Ops:
  0.6 6.0 %down.2 = (bf16[1,128,768]{2,1,0:T(8,128)(2,1)S(1)}, bf16[1,128,768]{2,1,0:T(8,128)(2,1)S(1)}, bf16[8,768,768]{2,1,0:T(8,128)(2,1)S(1)}) custom-call(bf16[512,6144]{1,0:T(8,128)(2,1)} %hidden.2, bf16[6144,768]{1,0:T(8,128)(2,1)} %weight.1), custom_call_target="tpu_custom_call" | custom-call | flops 2415919104 | bytes 12582912 | tf_op jit(solution)/shard_map/down/pallas_call | solution.py:98
  6.7 0.5 %collective-permute-start = (bf16[1,128,768]{2,1,0:T(8,128)(2,1)S(1)}, bf16[1,128,768]{2,1,0:T(8,128)(2,1)S(1)}, u32[]{:S(2)}, u32[]{:S(2)}) collective-permute-start(bf16[1,128,768]{2,1,0:T(8,128)(2,1)S(1)} %get-tuple-element.35), channel_id=1, source_target_pairs={{0,8},{8,0},{16,24},{24,16},{1,9},{9,1},{17,25},{25,17},{2,10},{10... | collective-permute-start | bytes 589832 | tf_op jit(solution)/shard_map/ppermute | solution.py:263
  7.2 1.1 %collective-permute-done = bf16[1,128,768]{2,1,0:T(8,128)(2,1)S(1)} collective-permute-done((bf16[1,128,768]{2,1,0:T(8,128)(2,1)S(1)}, bf16[1,128,768]{2,1,0:T(8,128)(2,1)S(1)}, u32[]{:S(2)}, u32[]{:S(2)}) %collective-permute-start) | collective-permute-done | bytes 196640 | tf_op jit(solution)/shard_map/ppermute | solution.py:263
  8.3 5.8 %down.3 = (bf16[1,128,768]{2,1,0:T(8,128)(2,1)S(1)}, bf16[1,128,768]{2,1,0:T(8,128)(2,1)S(1)}) custom-call(bf16[512,6144]{1,0:T(8,128)(2,1)} %hidden.2, bf16[8,768,768]{2,1,0:T(8,128)(2,1)S(1)} %get-tuple-element.38.weight), custom_call_target="tpu_custom_call" | custom-call | flops 2415919104 | bytes 3145728 | tf_op jit(solution)/shard_map/down/pallas_call | solution.py:98
  14.5 2.8 %collective-permute-start.1 = (bf16[128,768]{1,0:T(8,128)(2,1)S(1)}, bf16[128,768]{1,0:T(8,128)(2,1)S(1)}, u32[]{:S(2)}, u32[]{:S(2)}) collective-permute-start(bf16[128,768]{1,0:T(8,128)(2,1)S(1)} %bitcast.5), channel_id=1, source_target_pairs={{0,16},{8,24},{16,0},{24,8},{1,17},{9,25},{17,1},{25,9},{2,18},{10... | collective-permute-start | bytes 589832 | tf_op jit(solution)/shard_map/ppermute | solution.py:269
  17.3 5.3 %collective-permute-done.1.refs_0_ = bf16[128,768]{1,0:T(8,128)(2,1)S(1)} collective-permute-done((bf16[128,768]{1,0:T(8,128)(2,1)S(1)}, bf16[128,768]{1,0:T(8,128)(2,1)S(1)}, u32[]{:S(2)}, u32[]{:S(2)}) %collective-permute-start.1) | collective-permute-done | bytes 196640 | tf_op jit(solution)/shard_map/ppermute | solution.py:269
  22.7 1.9 %collective-permute-start.9 = (bf16[72,768]{1,0:T(8,128)(2,1)S(1)}, bf16[72,768]{1,0:T(8,128)(2,1)S(1)}, u32[]{:S(2)}, u32[]{:S(2)}) collective-permute-start(bf16[72,768]{1,0:T(8,128)(2,1)S(1)} %get-tuple-element.43.refs_1_), channel_id=1, source_target_pairs={{1,0},{3,1},{5,3},{7,5},{6,7},{4,6},{2,4},{0,2},{9,8},{11,9},{13,1... | collective-permute-start | bytes 331784 | tf_op jit(solution)/shard_map/ppermute | solution.py:278
  24.8 1.8 %collective-permute-start.11 = (bf16[64,768]{1,0:T(8,128)(2,1)S(1)}, bf16[64,768]{1,0:T(8,128)(2,1)S(1)}, u32[]{:S(2)}, u32[]{:S(2)}) collective-permute-start(bf16[64,768]{1,0:T(8,128)(2,1)S(1)} %get-tuple-element.42.refs_0_), channel_id=1, source_target_pairs={{1,0},{3,1},{5,3},{7,5},{6,7},{4,6},{2,4},{0,2},{9,8},{11,9},{13,1... | collective-permute-start | bytes 294920 | tf_op jit(solution)/shard_map/ppermute | solution.py:278
  26.8 1.6 %collective-permute-done.9.refs_5_ = bf16[72,768]{1,0:T(8,128)(2,1)S(1)} collective-permute-done((bf16[72,768]{1,0:T(8,128)(2,1)S(1)}, bf16[72,768]{1,0:T(8,128)(2,1)S(1)}, u32[]{:S(2)}, u32[]{:S(2)}) %collective-permute-start.9) | collective-permute-done | bytes 110624 | tf_op jit(solution)/shard_map/ppermute | solution.py:278
  28.4 1.9 %collective-permute-start.10 = (bf16[72,768]{1,0:T(8,128)(2,1)S(1)}, bf16[72,768]{1,0:T(8,128)(2,1)S(1)}, u32[]{:S(2)}, u32[]{:S(2)}) collective-permute-start(bf16[72,768]{1,0:T(8,128)(2,1)S(1)} %collective-permute-done.9.refs_5_), channel_id=1, source_target_pairs={{1,0},{3,1},{5,3},{7,5},{6,7},{4,6},{2,4},{0,2},{9,8},{11,9},{13,1... | collective-permute-start | bytes 331784 | tf_op jit(solution)/shard_map/ppermute | solution.py:278
  30.6 1.9 %collective-permute-start.14 = (bf16[64,768]{1,0:T(8,128)(2,1)S(1)}, bf16[64,768]{1,0:T(8,128)(2,1)S(1)}, u32[]{:S(2)}, u32[]{:S(2)}) collective-permute-start(bf16[64,768]{1,0:T(8,128)(2,1)S(1)} %collective-permute-done.11.refs_4_), channel_id=1, source_target_pairs={{1,0},{3,1},{5,3},{7,5},{6,7},{4,6},{2,4},{0,2},{9,8},{11,9},{13,1... | collective-permute-start | bytes 294920 | tf_op jit(solution)/shard_map/ppermute | solution.py:278
  32.6 1.4 %project.4 = (f32[128,1]{1,0:T(8,128)S(1)}, f32[2,128,1]{2,1,0:T(8,128)S(1)}, f32[144,1536]{1,0:T(8,128)S(1)}) custom-call(bf16[64,768]{1,0:T(8,128)(2,1)S(1)} %get-tuple-element.42.refs_0_, bf16[72,768]{1,0:T(8,128)(2,1)S(1)} %get-tuple-element.43.refs_1_, bf16[64,768]{1,0:T(8,128)(2,1)S(1)} %collective-permute-done.3.refs_2_, ...), custom_call_target="tpu_custom_call" | custom-call | flops 1019215872 | tf_op jit(solution)/shard_map/project/pallas_call | solution.py:227
  34.0 1.1 %collective-permute-done.8.refs_1_ = bf16[72,768]{1,0:T(8,128)(2,1)S(1)} collective-permute-done((bf16[72,768]{1,0:T(8,128)(2,1)S(1)}, bf16[72,768]{1,0:T(8,128)(2,1)S(1)}, u32[]{:S(2)}, u32[]{:S(2)}) %collective-permute-start.8) | collective-permute-done | bytes 110624 | tf_op jit(solution)/shard_map/ppermute | solution.py:278
  35.1 0.8 %collective-permute-start.12 = (bf16[72,768]{1,0:T(8,128)(2,1)S(1)}, bf16[72,768]{1,0:T(8,128)(2,1)S(1)}, u32[]{:S(2)}, u32[]{:S(2)}) collective-permute-start(bf16[72,768]{1,0:T(8,128)(2,1)S(1)} %collective-permute-done.8.refs_1_), channel_id=1, source_target_pairs={{0,1},{1,3},{3,5},{5,7},{7,6},{6,4},{4,2},{2,0},{8,9},{9,11},{11,1... | collective-permute-start | bytes 331784 | tf_op jit(solution)/shard_map/ppermute | solution.py:278
  35.9 1.2 %collective-permute-start.13 = (bf16[72,768]{1,0:T(8,128)(2,1)S(1)}, bf16[72,768]{1,0:T(8,128)(2,1)S(1)}, u32[]{:S(2)}, u32[]{:S(2)}) collective-permute-start(bf16[72,768]{1,0:T(8,128)(2,1)S(1)} %collective-permute-done.10.refs_3_), channel_id=1, source_target_pairs={{1,0},{3,1},{5,3},{7,5},{6,7},{4,6},{2,4},{0,2},{9,8},{11,9},{13,1... | collective-permute-start | bytes 331784 | tf_op jit(solution)/shard_map/ppermute | solution.py:278
  37.1 1.0 %collective-permute-done.4.refs_0_ = bf16[64,768]{1,0:T(8,128)(2,1)S(1)} collective-permute-done((bf16[64,768]{1,0:T(8,128)(2,1)S(1)}, bf16[64,768]{1,0:T(8,128)(2,1)S(1)}, u32[]{:S(2)}, u32[]{:S(2)}) %collective-permute-start.4) | collective-permute-done | bytes 98336 | tf_op jit(solution)/shard_map/ppermute | solution.py:278
  38.2 1.9 %collective-permute-start.16 = (bf16[64,768]{1,0:T(8,128)(2,1)S(1)}, bf16[64,768]{1,0:T(8,128)(2,1)S(1)}, u32[]{:S(2)}, u32[]{:S(2)}) collective-permute-start(bf16[64,768]{1,0:T(8,128)(2,1)S(1)} %collective-permute-done.14.refs_2_), channel_id=1, source_target_pairs={{1,0},{3,1},{5,3},{7,5},{6,7},{4,6},{2,4},{0,2},{9,8},{11,9},{13,1... | collective-permute-start | bytes 294920 | tf_op jit(solution)/shard_map/ppermute | solution.py:278
  40.1 1.1 %project.5 = (f32[2,128,1]{2,1,0:T(8,128)S(1)}, f32[144,1536]{1,0:T(8,128)S(1)}) custom-call(bf16[64,768]{1,0:T(8,128)(2,1)S(1)} %collective-permute-done.4.refs_0_, bf16[72,768]{1,0:T(8,128)(2,1)S(1)} %collective-permute-done.8.refs_1_, bf16[64,768]{1,0:T(8,128)(2,1)S(1)} %collective-permute-done.14.refs_2_, ...), custom_call_target="tpu_custom_call", output_to_operand_aliasing={{0}: (6, {}), {1}: (7, {})} | custom-call | flops 679477248 | tf_op jit(solution)/shard_map/project/pallas_call | solution.py:227
  41.7 1.2 %collective-permute-start.15 = (bf16[72,768]{1,0:T(8,128)(2,1)S(1)}, bf16[72,768]{1,0:T(8,128)(2,1)S(1)}, u32[]{:S(2)}, u32[]{:S(2)}) collective-permute-start(bf16[72,768]{1,0:T(8,128)(2,1)S(1)} %collective-permute-done.13.refs_3_), channel_id=1, source_target_pairs={{1,0},{3,1},{5,3},{7,5},{6,7},{4,6},{2,4},{0,2},{9,8},{11,9},{13,1... | collective-permute-start | bytes 331784 | tf_op jit(solution)/shard_map/ppermute | solution.py:285
  42.9 0.8 %collective-permute-start.6 = (bf16[64,768]{1,0:T(8,128)(2,1)S(1)}, bf16[64,768]{1,0:T(8,128)(2,1)S(1)}, u32[]{:S(2)}, u32[]{:S(2)}) collective-permute-start(bf16[64,768]{1,0:T(8,128)(2,1)S(1)} %collective-permute-done.5.refs_0_), channel_id=1, source_target_pairs={{0,1},{1,3},{3,5},{5,7},{7,6},{6,4},{4,2},{2,0},{8,9},{9,11},{11,1... | collective-permute-start | bytes 294920 | tf_op jit(solution)/shard_map/ppermute | solution.py:285
  43.7 0.7 %copy.15 = bf16[128,768]{1,0:T(8,128)(2,1)} copy(bf16[128,768]{1,0:T(8,128)(2,1)S(1)} %get-tuple-element.66) | data formatting | bytes 393216
  44.4 1.1 %project.6 = (f32[2,128,1]{2,1,0:T(8,128)S(1)}, f32[144,1536]{1,0:T(8,128)S(1)}) custom-call(bf16[64,768]{1,0:T(8,128)(2,1)S(1)} %collective-permute-done.5.refs_0_, bf16[72,768]{1,0:T(8,128)(2,1)S(1)} %collective-permute-done.12.refs_1_, bf16[64,768]{1,0:T(8,128)(2,1)S(1)} %collective-permute-done.16.refs_2_, ...), custom_call_target="tpu_custom_call", output_to_operand_aliasing={{0}: (6, {}), {1}: (7, {})} | custom-call | flops 679477248 | tf_op jit(solution)/shard_map/project/pallas_call | solution.py:227
  45.5 2.1 %collective-permute-done.6.refs_0_ = bf16[64,768]{1,0:T(8,128)(2,1)S(1)} collective-permute-done((bf16[64,768]{1,0:T(8,128)(2,1)S(1)}, bf16[64,768]{1,0:T(8,128)(2,1)S(1)}, u32[]{:S(2)}, u32[]{:S(2)}) %collective-permute-start.6) | collective-permute-done | bytes 98336 | tf_op jit(solution)/shard_map/ppermute | solution.py:285
  47.5 1.4 %project.7 = bf16[128,1536]{1,0:T(8,128)(2,1)} custom-call(bf16[64,768]{1,0:T(8,128)(2,1)S(1)} %collective-permute-done.6.refs_0_, bf16[72,768]{1,0:T(8,128)(2,1)S(1)} %collective-permute-done.15.refs_1_, bf16[6144,1536]{1,0:T(8,128)(2,1)S(1)} %copy-done, f32[128,1]{1,0:T(8,128)S(1)} %get-tuple-element.63.refs_5_.refs_3_, ...), custom_call_target="tpu_custom_call" | custom-call | flops 339738624 | tf_op jit(solution)/shard_map/project/pallas_call | solution.py:227
  (26 shorter events, 2.0 us)
Async XLA Ops:
  0.6 32.0 %copy-start = (bf16[6144,1536]{1,0:T(8,128)(2,1)S(1)}, bf16[6144,1536]{1,0:T(8,128)(2,1)}, u32[]{:S(2)}) copy-start(bf16[6144,1536]{1,0:T(8,128)(2,1)} %refs_2_.1) | copy-start | bytes 56623108
  6.7 10.6 %copy-start.2 = (bf16[768]{0:T(1024)(128)(2,1)S(1)}, bf16[768]{0:T(1024)(128)(2,1)}, u32[]{:S(2)}) copy-start(bf16[768]{0:T(1024)(128)(2,1)} %param.8) | copy-start | bytes 4612
  6.7 15.9 %copy-start.1 = (bf16[128,768]{1,0:T(8,128)(2,1)S(1)}, bf16[128,768]{1,0:T(8,128)(2,1)}, u32[]{:S(2)}) copy-start(bf16[128,768]{1,0:T(8,128)(2,1)} %refs_3_.1) | copy-start | bytes 589828
  6.7 1.6 %collective-permute-start = (bf16[1,128,768]{2,1,0:T(8,128)(2,1)S(1)}, bf16[1,128,768]{2,1,0:T(8,128)(2,1)S(1)}, u32[]{:S(2)}, u32[]{:S(2)}) collective-permute-start(bf16[1,128,768]{2,1,0:T(8,128)(2,1)S(1)} %get-tuple-element.35), channel_id=1, source_target_pairs={{0,8},{8,0},{16,24},{24,16},{1,9},{9,1},{17,25},{25,17},{2,10},{10... | collective-permute-start | bytes 589832 | tf_op jit(solution)/shard_map/ppermute | solution.py:263
  14.1 3.2 %collective-permute-start.2 = (bf16[128,768]{1,0:T(8,128)(2,1)S(1)}, bf16[128,768]{1,0:T(8,128)(2,1)S(1)}, u32[]{:S(2)}, u32[]{:S(2)}) collective-permute-start(bf16[128,768]{1,0:T(8,128)(2,1)S(1)} %bitcast.4), channel_id=1, source_target_pairs={{0,8},{8,0},{16,24},{24,16},{1,9},{9,1},{17,25},{25,17},{2,10},{10... | collective-permute-start | bytes 589832 | tf_op jit(solution)/shard_map/ppermute | solution.py:271
  14.5 8.1 %collective-permute-start.1 = (bf16[128,768]{1,0:T(8,128)(2,1)S(1)}, bf16[128,768]{1,0:T(8,128)(2,1)S(1)}, u32[]{:S(2)}, u32[]{:S(2)}) collective-permute-start(bf16[128,768]{1,0:T(8,128)(2,1)S(1)} %bitcast.5), channel_id=1, source_target_pairs={{0,16},{8,24},{16,0},{24,8},{1,17},{9,25},{17,1},{25,9},{2,18},{10... | collective-permute-start | bytes 589832 | tf_op jit(solution)/shard_map/ppermute | solution.py:269
  22.7 5.7 %collective-permute-start.9 = (bf16[72,768]{1,0:T(8,128)(2,1)S(1)}, bf16[72,768]{1,0:T(8,128)(2,1)S(1)}, u32[]{:S(2)}, u32[]{:S(2)}) collective-permute-start(bf16[72,768]{1,0:T(8,128)(2,1)S(1)} %get-tuple-element.43.refs_1_), channel_id=1, source_target_pairs={{1,0},{3,1},{5,3},{7,5},{6,7},{4,6},{2,4},{0,2},{9,8},{11,9},{13,1... | collective-permute-start | bytes 331784 | tf_op jit(solution)/shard_map/ppermute | solution.py:278
  24.6 5.8 %collective-permute-start.7 = (bf16[72,768]{1,0:T(8,128)(2,1)S(1)}, bf16[72,768]{1,0:T(8,128)(2,1)S(1)}, u32[]{:S(2)}, u32[]{:S(2)}) collective-permute-start(bf16[72,768]{1,0:T(8,128)(2,1)S(1)} %get-tuple-element.43.refs_1_), channel_id=1, source_target_pairs={{0,1},{1,3},{3,5},{5,7},{7,6},{6,4},{4,2},{2,0},{8,9},{9,11},{11,1... | collective-permute-start | bytes 331784 | tf_op jit(solution)/shard_map/ppermute | solution.py:278
  24.8 5.8 %collective-permute-start.11 = (bf16[64,768]{1,0:T(8,128)(2,1)S(1)}, bf16[64,768]{1,0:T(8,128)(2,1)S(1)}, u32[]{:S(2)}, u32[]{:S(2)}) collective-permute-start(bf16[64,768]{1,0:T(8,128)(2,1)S(1)} %get-tuple-element.42.refs_0_), channel_id=1, source_target_pairs={{1,0},{3,1},{5,3},{7,5},{6,7},{4,6},{2,4},{0,2},{9,8},{11,9},{13,1... | collective-permute-start | bytes 294920 | tf_op jit(solution)/shard_map/ppermute | solution.py:278
  26.6 5.9 %collective-permute-start.3 = (bf16[64,768]{1,0:T(8,128)(2,1)S(1)}, bf16[64,768]{1,0:T(8,128)(2,1)S(1)}, u32[]{:S(2)}, u32[]{:S(2)}) collective-permute-start(bf16[64,768]{1,0:T(8,128)(2,1)S(1)} %get-tuple-element.42.refs_0_), channel_id=1, source_target_pairs={{0,1},{1,3},{3,5},{5,7},{7,6},{6,4},{4,2},{2,0},{8,9},{9,11},{11,1... | collective-permute-start | bytes 294920 | tf_op jit(solution)/shard_map/ppermute | solution.py:278
  28.4 5.6 %collective-permute-start.10 = (bf16[72,768]{1,0:T(8,128)(2,1)S(1)}, bf16[72,768]{1,0:T(8,128)(2,1)S(1)}, u32[]{:S(2)}, u32[]{:S(2)}) collective-permute-start(bf16[72,768]{1,0:T(8,128)(2,1)S(1)} %collective-permute-done.9.refs_5_), channel_id=1, source_target_pairs={{1,0},{3,1},{5,3},{7,5},{6,7},{4,6},{2,4},{0,2},{9,8},{11,9},{13,1... | collective-permute-start | bytes 331784 | tf_op jit(solution)/shard_map/ppermute | solution.py:278
  30.4 4.7 %collective-permute-start.8 = (bf16[72,768]{1,0:T(8,128)(2,1)S(1)}, bf16[72,768]{1,0:T(8,128)(2,1)S(1)}, u32[]{:S(2)}, u32[]{:S(2)}) collective-permute-start(bf16[72,768]{1,0:T(8,128)(2,1)S(1)} %collective-permute-done.7.refs_3_), channel_id=1, source_target_pairs={{0,1},{1,3},{3,5},{5,7},{7,6},{6,4},{4,2},{2,0},{8,9},{9,11},{11,1... | collective-permute-start | bytes 331784 | tf_op jit(solution)/shard_map/ppermute | solution.py:278
  30.6 7.6 %collective-permute-start.14 = (bf16[64,768]{1,0:T(8,128)(2,1)S(1)}, bf16[64,768]{1,0:T(8,128)(2,1)S(1)}, u32[]{:S(2)}, u32[]{:S(2)}) collective-permute-start(bf16[64,768]{1,0:T(8,128)(2,1)S(1)} %collective-permute-done.11.refs_4_), channel_id=1, source_target_pairs={{1,0},{3,1},{5,3},{7,5},{6,7},{4,6},{2,4},{0,2},{9,8},{11,9},{13,1... | collective-permute-start | bytes 294920 | tf_op jit(solution)/shard_map/ppermute | solution.py:278
  32.5 5.7 %collective-permute-start.4 = (bf16[64,768]{1,0:T(8,128)(2,1)S(1)}, bf16[64,768]{1,0:T(8,128)(2,1)S(1)}, u32[]{:S(2)}, u32[]{:S(2)}) collective-permute-start(bf16[64,768]{1,0:T(8,128)(2,1)S(1)} %collective-permute-done.3.refs_2_), channel_id=1, source_target_pairs={{0,1},{1,3},{3,5},{5,7},{7,6},{6,4},{4,2},{2,0},{8,9},{9,11},{11,1... | collective-permute-start | bytes 294920 | tf_op jit(solution)/shard_map/ppermute | solution.py:278
  35.1 6.1 %collective-permute-start.12 = (bf16[72,768]{1,0:T(8,128)(2,1)S(1)}, bf16[72,768]{1,0:T(8,128)(2,1)S(1)}, u32[]{:S(2)}, u32[]{:S(2)}) collective-permute-start(bf16[72,768]{1,0:T(8,128)(2,1)S(1)} %collective-permute-done.8.refs_1_), channel_id=1, source_target_pairs={{0,1},{1,3},{3,5},{5,7},{7,6},{6,4},{4,2},{2,0},{8,9},{9,11},{11,1... | collective-permute-start | bytes 331784 | tf_op jit(solution)/shard_map/ppermute | solution.py:278
  35.9 5.8 %collective-permute-start.13 = (bf16[72,768]{1,0:T(8,128)(2,1)S(1)}, bf16[72,768]{1,0:T(8,128)(2,1)S(1)}, u32[]{:S(2)}, u32[]{:S(2)}) collective-permute-start(bf16[72,768]{1,0:T(8,128)(2,1)S(1)} %collective-permute-done.10.refs_3_), channel_id=1, source_target_pairs={{1,0},{3,1},{5,3},{7,5},{6,7},{4,6},{2,4},{0,2},{9,8},{11,9},{13,1... | collective-permute-start | bytes 331784 | tf_op jit(solution)/shard_map/ppermute | solution.py:278
  38.1 4.8 %collective-permute-start.5 = (bf16[64,768]{1,0:T(8,128)(2,1)S(1)}, bf16[64,768]{1,0:T(8,128)(2,1)S(1)}, u32[]{:S(2)}, u32[]{:S(2)}) collective-permute-start(bf16[64,768]{1,0:T(8,128)(2,1)S(1)} %collective-permute-done.4.refs_0_), channel_id=1, source_target_pairs={{0,1},{1,3},{3,5},{5,7},{7,6},{6,4},{4,2},{2,0},{8,9},{9,11},{11,1... | collective-permute-start | bytes 294920 | tf_op jit(solution)/shard_map/ppermute | solution.py:278
  38.2 6.2 %collective-permute-start.16 = (bf16[64,768]{1,0:T(8,128)(2,1)S(1)}, bf16[64,768]{1,0:T(8,128)(2,1)S(1)}, u32[]{:S(2)}, u32[]{:S(2)}) collective-permute-start(bf16[64,768]{1,0:T(8,128)(2,1)S(1)} %collective-permute-done.14.refs_2_), channel_id=1, source_target_pairs={{1,0},{3,1},{5,3},{7,5},{6,7},{4,6},{2,4},{0,2},{9,8},{11,9},{13,1... | collective-permute-start | bytes 294920 | tf_op jit(solution)/shard_map/ppermute | solution.py:278
  41.7 5.9 %collective-permute-start.15 = (bf16[72,768]{1,0:T(8,128)(2,1)S(1)}, bf16[72,768]{1,0:T(8,128)(2,1)S(1)}, u32[]{:S(2)}, u32[]{:S(2)}) collective-permute-start(bf16[72,768]{1,0:T(8,128)(2,1)S(1)} %collective-permute-done.13.refs_3_), channel_id=1, source_target_pairs={{1,0},{3,1},{5,3},{7,5},{6,7},{4,6},{2,4},{0,2},{9,8},{11,9},{13,1... | collective-permute-start | bytes 331784 | tf_op jit(solution)/shard_map/ppermute | solution.py:285
  42.9 4.6 %collective-permute-start.6 = (bf16[64,768]{1,0:T(8,128)(2,1)S(1)}, bf16[64,768]{1,0:T(8,128)(2,1)S(1)}, u32[]{:S(2)}, u32[]{:S(2)}) collective-permute-start(bf16[64,768]{1,0:T(8,128)(2,1)S(1)} %collective-permute-done.5.refs_0_), channel_id=1, source_target_pairs={{0,1},{1,3},{3,5},{5,7},{7,6},{6,4},{4,2},{2,0},{8,9},{9,11},{11,1... | collective-permute-start | bytes 294920 | tf_op jit(solution)/shard_map/ppermute | solution.py:285

commit v7 on v6

--- a/solution.py
+++ b/solution.py
@@ -118,13 +118,10 @@
     )
 
 
-def merge_kernel(*refs):
-    *parts, residual, gain, stream, upper, lower = refs
-    tok, width = residual.shape
-    total = parts[0][...].astype(jnp.float32)
-    for part in parts[1:]:
-        total = total + part[...].astype(jnp.float32)
-    value = (residual[...].astype(jnp.float32) + total).astype(stream.dtype)
+def merge_kernel(others, keep, got, gain, stream, upper, lower):
+    tok, width = others.shape
+    own = keep[...].astype(jnp.float32) + got[...].astype(jnp.float32)
+    value = (others[...] + own).astype(stream.dtype)
     stream[...] = value
     upper[...] = value[: tok // 2]
     lower[0 : tok // 2, :] = value[tok // 2 :]
@@ -132,16 +129,16 @@
     lower[tok // 2 : tok // 2 + GAIN, :] = rows.astype(lower.dtype)
 
 
-def merge(parts, residual, gain):
-    tok, width = residual.shape
+def merge(others, keep, got, gain):
+    tok, width = others.shape
     return pl.pallas_call(
         merge_kernel,
         out_shape=[pltpu.VMEM((n, width), jnp.bfloat16) for n in (tok, tok // 2, tok // 2 + GAIN)],
-        in_specs=[VMEM] * (len(parts) + 2),
+        in_specs=[VMEM] * 4,
         out_specs=[VMEM] * 3,
         compiler_params=pltpu.CompilerParams(vmem_limit_bytes=8 * MIB),
         name="merge",
-    )(*parts, residual, gain)
+    )(others, keep, got, gain)
 
 
 def project_kernel(cycle, hops, shapes, first, last, *refs):
@@ -263,13 +260,13 @@
         got = lax.ppermute(give, "row", sibling)
         both = (keep.astype(jnp.float32) + got.astype(jnp.float32)).astype(jnp.bfloat16)
         both, hidden = lax.optimization_barrier((both, hidden))
-        parts = []
+        others = residual.astype(jnp.float32)
         for step in range(1, chips_y):
             move = [(r, (r + CORES * step) % rows) for r in range(rows)]
-            parts.append(lax.ppermute(both[step - 1], "row", move))
+            others = others + lax.ppermute(both[step - 1], "row", move).astype(jnp.float32)
         give, keep = down(hidden, down_weight, tok, chips_y, True)
-        parts += [keep[0], lax.ppermute(give[0], "row", sibling)]
-        stream, upper, lower = merge(parts, residual, gain[None, :])
+        got = lax.ppermute(give[0], "row", sibling)
+        stream, upper, lower = merge(others, keep[0], got, gain[None, :])
 
         up, back = [upper, lower], [upper, lower]
         pieces, hops, state = [], [], None

time: 49.1 us -> 45.3 us (0.923)
  waiting for transfers between devices: 12.6 us -> 9.1 us
    ppermute x2, waiting for transfers between devices: 5.31 us -> 1.36 us  [the longest x1 1.36 us: per_device(): got = lax.ppermute(give[0], 'row', sibling)]
    ppermute x6, starting transfers between devices: 10.6 us -> 9.63 us  [per_device(): lax.ppermute(back[i], 'col', behind)]
    ppermute x6, starting transfers between devices: 1.75 us -> 2.58 us  [per_device(): lax.ppermute(up[i], 'col', ahead)]
    ppermute x1, starting transfers between devices: 1.22 us -> 2 us  [per_device(): lax.ppermute(back[1], 'col', behind)]
    ppermute x1, waiting for transfers between devices: 2.06 us -> 2.66 us  [per_device(): lax.ppermute(up[0], 'col', ahead)]
    ppermute x1, starting transfers between devices: 0.78 us -> 0.18 us  [per_device(): lax.ppermute(up[0], 'col', ahead)]
  transfers between devices with their start and end apart: 17 -> 17, of which waited for: 7 -> 8; matrix products, arithmetic and copies ran while one was open for 1% -> 2% of each run, Pallas kernels for 7% -> 20%
where the time goes in v7:
time: 45.3 us; the launch traced here: 45.1 us
  starting transfers between devices  17.9 us (40%)
  Pallas kernels  16.5 us (36%)
  waiting for transfers between devices  9.1 us (20%)
  between operations  0.76 us (2%)
  local copies, waits for them, and re-layouts  0.7 us (2%)
    pallas_call x2, Pallas kernels, down(): pl.pallas_call(functools.partial(down_kernel, chips_y, tok, own), out_sha...  11.4 us
    ppermute x6, starting transfers between devices, per_device(): lax.ppermute(back[i], 'col', behind)  9.63 us
    pallas_call x4, Pallas kernels, project(): pl.pallas_call(functools.partial(project_kernel, cycle, hops, [len(parts)...  5.02 us
    ppermute x1, starting transfers between devices, per_device(): lax.ppermute(both[step - 1], 'row', move).astype(jnp.float32)  2.95 us
    ppermute x1, waiting for transfers between devices, per_device(): lax.ppermute(up[0], 'col', ahead)  2.66 us
    ppermute x6, starting transfers between devices, per_device(): lax.ppermute(up[i], 'col', ahead)  2.58 us
    ppermute x6, waiting for transfers between devices, per_device(): lax.ppermute(back[i], 'col', behind)  2.04 us
    ppermute x1, starting transfers between devices, per_device(): lax.ppermute(back[1], 'col', behind)  2 us
  transfers between devices with their start and end apart: 17, of which 8 were waited for; matrix products, arithmetic and copies ran while one was open for 2% of the time, Pallas kernels for 20%

profile of v7, /device:TPU:0, one launch (start us, length us, event | category | flops | bytes accessed | tf_op | source)
XLA Modules:
  0.0 45.1 jit_solution(15498621401473557730)
XLA Ops:
  0.7 6.0 %down.2 = (bf16[1,128,768]{2,1,0:T(8,128)(2,1)S(1)}, bf16[1,128,768]{2,1,0:T(8,128)(2,1)S(1)}, bf16[8,768,768]{2,1,0:T(8,128)(2,1)S(1)}) custom-call(bf16[512,6144]{1,0:T(8,128)(2,1)} %hidden.2, bf16[6144,768]{1,0:T(8,128)(2,1)} %weight.1), custom_call_target="tpu_custom_call" | custom-call | flops 2415919104 | bytes 12582912 | tf_op jit(solution)/shard_map/down/pallas_call | solution.py:98
  6.7 0.5 %collective-permute-start = (bf16[1,128,768]{2,1,0:T(8,128)(2,1)S(1)}, bf16[1,128,768]{2,1,0:T(8,128)(2,1)S(1)}, u32[]{:S(2)}, u32[]{:S(2)}) collective-permute-start(bf16[1,128,768]{2,1,0:T(8,128)(2,1)S(1)} %get-tuple-element.35), channel_id=1, source_target_pairs={{0,8},{8,0},{16,24},{24,16},{1,9},{9,1},{17,25},{25,17},{2,10},{10... | collective-permute-start | bytes 589832 | tf_op jit(solution)/shard_map/ppermute | solution.py:260
  7.2 1.1 %collective-permute-done = bf16[1,128,768]{2,1,0:T(8,128)(2,1)S(1)} collective-permute-done((bf16[1,128,768]{2,1,0:T(8,128)(2,1)S(1)}, bf16[1,128,768]{2,1,0:T(8,128)(2,1)S(1)}, u32[]{:S(2)}, u32[]{:S(2)}) %collective-permute-start) | collective-permute-done | bytes 196640 | tf_op jit(solution)/shard_map/ppermute | solution.py:260
  8.3 3.0 %collective-permute-start.1 = (bf16[128,768]{1,0:T(8,128)(2,1)S(1)}, bf16[128,768]{1,0:T(8,128)(2,1)S(1)}, u32[]{:S(2)}, u32[]{:S(2)}) collective-permute-start(bf16[128,768]{1,0:T(8,128)(2,1)S(1)} %bitcast.5), channel_id=1, source_target_pairs={{0,16},{8,24},{16,0},{24,8},{1,17},{9,25},{17,1},{25,9},{2,18},{10... | collective-permute-start | bytes 589832 | tf_op jit(solution)/shard_map/ppermute | solution.py:266
  11.3 5.4 %down.3 = (bf16[1,128,768]{2,1,0:T(8,128)(2,1)S(1)}, bf16[1,128,768]{2,1,0:T(8,128)(2,1)S(1)}) custom-call(bf16[512,6144]{1,0:T(8,128)(2,1)} %hidden.2, bf16[8,768,768]{2,1,0:T(8,128)(2,1)S(1)} %get-tuple-element.38.weight), custom_call_target="tpu_custom_call" | custom-call | flops 2415919104 | bytes 3145728 | tf_op jit(solution)/shard_map/down/pallas_call | solution.py:98
  16.9 1.4 %collective-permute-done.2.got = bf16[128,768]{1,0:T(8,128)(2,1)S(1)} collective-permute-done((bf16[128,768]{1,0:T(8,128)(2,1)S(1)}, bf16[128,768]{1,0:T(8,128)(2,1)S(1)}, u32[]{:S(2)}, u32[]{:S(2)}) %collective-permute-start.2) | collective-permute-done | bytes 196640 | tf_op jit(solution)/shard_map/ppermute | solution.py:268
  18.3 1.6 %collective-permute-start.9 = (bf16[72,768]{1,0:T(8,128)(2,1)S(1)}, bf16[72,768]{1,0:T(8,128)(2,1)S(1)}, u32[]{:S(2)}, u32[]{:S(2)}) collective-permute-start(bf16[72,768]{1,0:T(8,128)(2,1)S(1)} %get-tuple-element.43.refs_1_), channel_id=1, source_target_pairs={{1,0},{3,1},{5,3},{7,5},{6,7},{4,6},{2,4},{0,2},{9,8},{11,9},{13,1... | collective-permute-start | bytes 331784 | tf_op jit(solution)/shard_map/ppermute | solution.py:275
  20.4 1.6 %collective-permute-start.11 = (bf16[64,768]{1,0:T(8,128)(2,1)S(1)}, bf16[64,768]{1,0:T(8,128)(2,1)S(1)}, u32[]{:S(2)}, u32[]{:S(2)}) collective-permute-start(bf16[64,768]{1,0:T(8,128)(2,1)S(1)} %get-tuple-element.42.refs_0_), channel_id=1, source_target_pairs={{1,0},{3,1},{5,3},{7,5},{6,7},{4,6},{2,4},{0,2},{9,8},{11,9},{13,1... | collective-permute-start | bytes 294920 | tf_op jit(solution)/shard_map/ppermute | solution.py:275
  22.4 1.8 %collective-permute-done.9.refs_5_ = bf16[72,768]{1,0:T(8,128)(2,1)S(1)} collective-permute-done((bf16[72,768]{1,0:T(8,128)(2,1)S(1)}, bf16[72,768]{1,0:T(8,128)(2,1)S(1)}, u32[]{:S(2)}, u32[]{:S(2)}) %collective-permute-start.9) | collective-permute-done | bytes 110624 | tf_op jit(solution)/shard_map/ppermute | solution.py:275
  24.3 1.6 %collective-permute-start.10 = (bf16[72,768]{1,0:T(8,128)(2,1)S(1)}, bf16[72,768]{1,0:T(8,128)(2,1)S(1)}, u32[]{:S(2)}, u32[]{:S(2)}) collective-permute-start(bf16[72,768]{1,0:T(8,128)(2,1)S(1)} %collective-permute-done.9.refs_5_), channel_id=1, source_target_pairs={{1,0},{3,1},{5,3},{7,5},{6,7},{4,6},{2,4},{0,2},{9,8},{11,9},{13,1... | collective-permute-start | bytes 331784 | tf_op jit(solution)/shard_map/ppermute | solution.py:275
  25.8 0.4 collective-permute-start.8
  26.3 1.6 %collective-permute-start.14 = (bf16[64,768]{1,0:T(8,128)(2,1)S(1)}, bf16[64,768]{1,0:T(8,128)(2,1)S(1)}, u32[]{:S(2)}, u32[]{:S(2)}) collective-permute-start(bf16[64,768]{1,0:T(8,128)(2,1)S(1)} %collective-permute-done.11.refs_4_), channel_id=1, source_target_pairs={{1,0},{3,1},{5,3},{7,5},{6,7},{4,6},{2,4},{0,2},{9,8},{11,9},{13,1... | collective-permute-start | bytes 294920 | tf_op jit(solution)/shard_map/ppermute | solution.py:275
  27.9 0.4 collective-permute-start.4
  28.3 1.4 %project.4 = (f32[128,1]{1,0:T(8,128)S(1)}, f32[2,128,1]{2,1,0:T(8,128)S(1)}, f32[144,1536]{1,0:T(8,128)S(1)}) custom-call(bf16[64,768]{1,0:T(8,128)(2,1)S(1)} %get-tuple-element.42.refs_0_, bf16[72,768]{1,0:T(8,128)(2,1)S(1)} %get-tuple-element.43.refs_1_, bf16[64,768]{1,0:T(8,128)(2,1)S(1)} %collective-permute-done.3.refs_2_, ...), custom_call_target="tpu_custom_call" | custom-call | flops 1019215872 | tf_op jit(solution)/shard_map/project/pallas_call | solution.py:224
  29.7 1.5 %collective-permute-done.8.refs_1_ = bf16[72,768]{1,0:T(8,128)(2,1)S(1)} collective-permute-done((bf16[72,768]{1,0:T(8,128)(2,1)S(1)}, bf16[72,768]{1,0:T(8,128)(2,1)S(1)}, u32[]{:S(2)}, u32[]{:S(2)}) %collective-permute-start.8) | collective-permute-done | bytes 110624 | tf_op jit(solution)/shard_map/ppermute | solution.py:275
  31.4 1.8 %collective-permute-start.13 = (bf16[72,768]{1,0:T(8,128)(2,1)S(1)}, bf16[72,768]{1,0:T(8,128)(2,1)S(1)}, u32[]{:S(2)}, u32[]{:S(2)}) collective-permute-start(bf16[72,768]{1,0:T(8,128)(2,1)S(1)} %collective-permute-done.10.refs_3_), channel_id=1, source_target_pairs={{1,0},{3,1},{5,3},{7,5},{6,7},{4,6},{2,4},{0,2},{9,8},{11,9},{13,1... | collective-permute-start | bytes 331784 | tf_op jit(solution)/shard_map/ppermute | solution.py:275
  33.4 0.5 %collective-permute-start.5 = (bf16[64,768]{1,0:T(8,128)(2,1)S(1)}, bf16[64,768]{1,0:T(8,128)(2,1)S(1)}, u32[]{:S(2)}, u32[]{:S(2)}) collective-permute-start(bf16[64,768]{1,0:T(8,128)(2,1)S(1)} %collective-permute-done.4.refs_0_), channel_id=1, source_target_pairs={{0,1},{1,3},{3,5},{5,7},{7,6},{6,4},{4,2},{2,0},{8,9},{9,11},{11,1... | collective-permute-start | bytes 294920 | tf_op jit(solution)/shard_map/ppermute | solution.py:275
  34.0 1.5 %collective-permute-start.16 = (bf16[64,768]{1,0:T(8,128)(2,1)S(1)}, bf16[64,768]{1,0:T(8,128)(2,1)S(1)}, u32[]{:S(2)}, u32[]{:S(2)}) collective-permute-start(bf16[64,768]{1,0:T(8,128)(2,1)S(1)} %collective-permute-done.14.refs_2_), channel_id=1, source_target_pairs={{1,0},{3,1},{5,3},{7,5},{6,7},{4,6},{2,4},{0,2},{9,8},{11,9},{13,1... | collective-permute-start | bytes 294920 | tf_op jit(solution)/shard_map/ppermute | solution.py:275
  35.4 1.1 %project.5 = (f32[2,128,1]{2,1,0:T(8,128)S(1)}, f32[144,1536]{1,0:T(8,128)S(1)}) custom-call(bf16[64,768]{1,0:T(8,128)(2,1)S(1)} %collective-permute-done.4.refs_0_, bf16[72,768]{1,0:T(8,128)(2,1)S(1)} %collective-permute-done.8.refs_1_, bf16[64,768]{1,0:T(8,128)(2,1)S(1)} %collective-permute-done.14.refs_2_, ...), custom_call_target="tpu_custom_call", output_to_operand_aliasing={{0}: (6, {}), {1}: (7, {})} | custom-call | flops 679477248 | tf_op jit(solution)/shard_map/project/pallas_call | solution.py:224
  36.7 2.0 %collective-permute-start.15 = (bf16[72,768]{1,0:T(8,128)(2,1)S(1)}, bf16[72,768]{1,0:T(8,128)(2,1)S(1)}, u32[]{:S(2)}, u32[]{:S(2)}) collective-permute-start(bf16[72,768]{1,0:T(8,128)(2,1)S(1)} %collective-permute-done.13.refs_3_), channel_id=1, source_target_pairs={{1,0},{3,1},{5,3},{7,5},{6,7},{4,6},{2,4},{0,2},{9,8},{11,9},{13,1... | collective-permute-start | bytes 331784 | tf_op jit(solution)/shard_map/ppermute | solution.py:282
  39.2 0.7 %copy.15 = bf16[128,768]{1,0:T(8,128)(2,1)} copy(bf16[128,768]{1,0:T(8,128)(2,1)S(1)} %get-tuple-element.66) | data formatting | bytes 393216
  39.9 1.1 %project.6 = (f32[2,128,1]{2,1,0:T(8,128)S(1)}, f32[144,1536]{1,0:T(8,128)S(1)}) custom-call(bf16[64,768]{1,0:T(8,128)(2,1)S(1)} %collective-permute-done.5.refs_0_, bf16[72,768]{1,0:T(8,128)(2,1)S(1)} %collective-permute-done.12.refs_1_, bf16[64,768]{1,0:T(8,128)(2,1)S(1)} %collective-permute-done.16.refs_2_, ...), custom_call_target="tpu_custom_call", output_to_operand_aliasing={{0}: (6, {}), {1}: (7, {})} | custom-call | flops 679477248 | tf_op jit(solution)/shard_map/project/pallas_call | solution.py:224
  41.0 2.7 %collective-permute-done.6.refs_0_ = bf16[64,768]{1,0:T(8,128)(2,1)S(1)} collective-permute-done((bf16[64,768]{1,0:T(8,128)(2,1)S(1)}, bf16[64,768]{1,0:T(8,128)(2,1)S(1)}, u32[]{:S(2)}, u32[]{:S(2)}) %collective-permute-start.6) | collective-permute-done | bytes 98336 | tf_op jit(solution)/shard_map/ppermute | solution.py:282
  43.7 1.4 %project.7 = bf16[128,1536]{1,0:T(8,128)(2,1)} custom-call(bf16[64,768]{1,0:T(8,128)(2,1)S(1)} %collective-permute-done.6.refs_0_, bf16[72,768]{1,0:T(8,128)(2,1)S(1)} %collective-permute-done.15.refs_1_, bf16[6144,1536]{1,0:T(8,128)(2,1)S(1)} %copy-done, f32[128,1]{1,0:T(8,128)S(1)} %get-tuple-element.63.refs_5_.refs_3_, ...), custom_call_target="tpu_custom_call" | custom-call | flops 339738624 | tf_op jit(solution)/shard_map/project/pallas_call | solution.py:224
  (27 shorter events, 2.3 us)
Async XLA Ops:
  0.6 6.6 %copy-start.2 = (bf16[768]{0:T(1024)(128)(2,1)S(1)}, bf16[768]{0:T(1024)(128)(2,1)}, u32[]{:S(2)}) copy-start(bf16[768]{0:T(1024)(128)(2,1)} %param.8) | copy-start | bytes 4612
  0.6 27.7 %copy-start = (bf16[6144,1536]{1,0:T(8,128)(2,1)S(1)}, bf16[6144,1536]{1,0:T(8,128)(2,1)}, u32[]{:S(2)}) copy-start(bf16[6144,1536]{1,0:T(8,128)(2,1)} %refs_2_.1) | copy-start | bytes 56623108
  6.7 10.1 %copy-start.1 = (bf16[128,768]{1,0:T(8,128)(2,1)S(1)}, bf16[128,768]{1,0:T(8,128)(2,1)}, u32[]{:S(2)}) copy-start(bf16[128,768]{1,0:T(8,128)(2,1)} %param.7) | copy-start | bytes 589828
  6.7 1.6 %collective-permute-start = (bf16[1,128,768]{2,1,0:T(8,128)(2,1)S(1)}, bf16[1,128,768]{2,1,0:T(8,128)(2,1)S(1)}, u32[]{:S(2)}, u32[]{:S(2)}) collective-permute-start(bf16[1,128,768]{2,1,0:T(8,128)(2,1)S(1)} %get-tuple-element.35), channel_id=1, source_target_pairs={{0,8},{8,0},{16,24},{24,16},{1,9},{9,1},{17,25},{25,17},{2,10},{10... | collective-permute-start | bytes 589832 | tf_op jit(solution)/shard_map/ppermute | solution.py:260
  8.3 8.5 %collective-permute-start.1 = (bf16[128,768]{1,0:T(8,128)(2,1)S(1)}, bf16[128,768]{1,0:T(8,128)(2,1)S(1)}, u32[]{:S(2)}, u32[]{:S(2)}) collective-permute-start(bf16[128,768]{1,0:T(8,128)(2,1)S(1)} %bitcast.5), channel_id=1, source_target_pairs={{0,16},{8,24},{16,0},{24,8},{1,17},{9,25},{17,1},{25,9},{2,18},{10... | collective-permute-start | bytes 589832 | tf_op jit(solution)/shard_map/ppermute | solution.py:266
  16.7 1.5 %collective-permute-start.2 = (bf16[128,768]{1,0:T(8,128)(2,1)S(1)}, bf16[128,768]{1,0:T(8,128)(2,1)S(1)}, u32[]{:S(2)}, u32[]{:S(2)}) collective-permute-start(bf16[128,768]{1,0:T(8,128)(2,1)S(1)} %bitcast.4), channel_id=1, source_target_pairs={{0,8},{8,0},{16,24},{24,16},{1,9},{9,1},{17,25},{25,17},{2,10},{10... | collective-permute-start | bytes 589832 | tf_op jit(solution)/shard_map/ppermute | solution.py:268
  18.3 6.0 %collective-permute-start.9 = (bf16[72,768]{1,0:T(8,128)(2,1)S(1)}, bf16[72,768]{1,0:T(8,128)(2,1)S(1)}, u32[]{:S(2)}, u32[]{:S(2)}) collective-permute-start(bf16[72,768]{1,0:T(8,128)(2,1)S(1)} %get-tuple-element.43.refs_1_), channel_id=1, source_target_pairs={{1,0},{3,1},{5,3},{7,5},{6,7},{4,6},{2,4},{0,2},{9,8},{11,9},{13,1... | collective-permute-start | bytes 331784 | tf_op jit(solution)/shard_map/ppermute | solution.py:275
  19.9 5.9 %collective-permute-start.7 = (bf16[72,768]{1,0:T(8,128)(2,1)S(1)}, bf16[72,768]{1,0:T(8,128)(2,1)S(1)}, u32[]{:S(2)}, u32[]{:S(2)}) collective-permute-start(bf16[72,768]{1,0:T(8,128)(2,1)S(1)} %get-tuple-element.43.refs_1_), channel_id=1, source_target_pairs={{0,1},{1,3},{3,5},{5,7},{7,6},{6,4},{4,2},{2,0},{8,9},{9,11},{11,1... | collective-permute-start | bytes 331784 | tf_op jit(solution)/shard_map/ppermute | solution.py:275
  20.4 5.9 %collective-permute-start.11 = (bf16[64,768]{1,0:T(8,128)(2,1)S(1)}, bf16[64,768]{1,0:T(8,128)(2,1)S(1)}, u32[]{:S(2)}, u32[]{:S(2)}) collective-permute-start(bf16[64,768]{1,0:T(8,128)(2,1)S(1)} %get-tuple-element.42.refs_0_), channel_id=1, source_target_pairs={{1,0},{3,1},{5,3},{7,5},{6,7},{4,6},{2,4},{0,2},{9,8},{11,9},{13,1... | collective-permute-start | bytes 294920 | tf_op jit(solution)/shard_map/ppermute | solution.py:275
  22.0 5.9 %collective-permute-start.3 = (bf16[64,768]{1,0:T(8,128)(2,1)S(1)}, bf16[64,768]{1,0:T(8,128)(2,1)S(1)}, u32[]{:S(2)}, u32[]{:S(2)}) collective-permute-start(bf16[64,768]{1,0:T(8,128)(2,1)S(1)} %get-tuple-element.42.refs_0_), channel_id=1, source_target_pairs={{0,1},{1,3},{3,5},{5,7},{7,6},{6,4},{4,2},{2,0},{8,9},{9,11},{11,1... | collective-permute-start | bytes 294920 | tf_op jit(solution)/shard_map/ppermute | solution.py:275
  24.3 5.5 %collective-permute-start.10 = (bf16[72,768]{1,0:T(8,128)(2,1)S(1)}, bf16[72,768]{1,0:T(8,128)(2,1)S(1)}, u32[]{:S(2)}, u32[]{:S(2)}) collective-permute-start(bf16[72,768]{1,0:T(8,128)(2,1)S(1)} %collective-permute-done.9.refs_5_), channel_id=1, source_target_pairs={{1,0},{3,1},{5,3},{7,5},{6,7},{4,6},{2,4},{0,2},{9,8},{11,9},{13,1... | collective-permute-start | bytes 331784 | tf_op jit(solution)/shard_map/ppermute | solution.py:275
  25.8 5.4 %collective-permute-start.8 = (bf16[72,768]{1,0:T(8,128)(2,1)S(1)}, bf16[72,768]{1,0:T(8,128)(2,1)S(1)}, u32[]{:S(2)}, u32[]{:S(2)}) collective-permute-start(bf16[72,768]{1,0:T(8,128)(2,1)S(1)} %collective-permute-done.7.refs_3_), channel_id=1, source_target_pairs={{0,1},{1,3},{3,5},{5,7},{7,6},{6,4},{4,2},{2,0},{8,9},{9,11},{11,1... | collective-permute-start | bytes 331784 | tf_op jit(solution)/shard_map/ppermute | solution.py:275
  26.3 7.7 %collective-permute-start.14 = (bf16[64,768]{1,0:T(8,128)(2,1)S(1)}, bf16[64,768]{1,0:T(8,128)(2,1)S(1)}, u32[]{:S(2)}, u32[]{:S(2)}) collective-permute-start(bf16[64,768]{1,0:T(8,128)(2,1)S(1)} %collective-permute-done.11.refs_4_), channel_id=1, source_target_pairs={{1,0},{3,1},{5,3},{7,5},{6,7},{4,6},{2,4},{0,2},{9,8},{11,9},{13,1... | collective-permute-start | bytes 294920 | tf_op jit(solution)/shard_map/ppermute | solution.py:275
  27.9 5.5 %collective-permute-start.4 = (bf16[64,768]{1,0:T(8,128)(2,1)S(1)}, bf16[64,768]{1,0:T(8,128)(2,1)S(1)}, u32[]{:S(2)}, u32[]{:S(2)}) collective-permute-start(bf16[64,768]{1,0:T(8,128)(2,1)S(1)} %collective-permute-done.3.refs_2_), channel_id=1, source_target_pairs={{0,1},{1,3},{3,5},{5,7},{7,6},{6,4},{4,2},{2,0},{8,9},{9,11},{11,1... | collective-permute-start | bytes 294920 | tf_op jit(solution)/shard_map/ppermute | solution.py:275
  31.2 5.4 %collective-permute-start.12 = (bf16[72,768]{1,0:T(8,128)(2,1)S(1)}, bf16[72,768]{1,0:T(8,128)(2,1)S(1)}, u32[]{:S(2)}, u32[]{:S(2)}) collective-permute-start(bf16[72,768]{1,0:T(8,128)(2,1)S(1)} %collective-permute-done.8.refs_1_), channel_id=1, source_target_pairs={{0,1},{1,3},{3,5},{5,7},{7,6},{6,4},{4,2},{2,0},{8,9},{9,11},{11,1... | collective-permute-start | bytes 331784 | tf_op jit(solution)/shard_map/ppermute | solution.py:275
  31.4 5.3 %collective-permute-start.13 = (bf16[72,768]{1,0:T(8,128)(2,1)S(1)}, bf16[72,768]{1,0:T(8,128)(2,1)S(1)}, u32[]{:S(2)}, u32[]{:S(2)}) collective-permute-start(bf16[72,768]{1,0:T(8,128)(2,1)S(1)} %collective-permute-done.10.refs_3_), channel_id=1, source_target_pairs={{1,0},{3,1},{5,3},{7,5},{6,7},{4,6},{2,4},{0,2},{9,8},{11,9},{13,1... | collective-permute-start | bytes 331784 | tf_op jit(solution)/shard_map/ppermute | solution.py:275
  33.4 5.6 %collective-permute-start.5 = (bf16[64,768]{1,0:T(8,128)(2,1)S(1)}, bf16[64,768]{1,0:T(8,128)(2,1)S(1)}, u32[]{:S(2)}, u32[]{:S(2)}) collective-permute-start(bf16[64,768]{1,0:T(8,128)(2,1)S(1)} %collective-permute-done.4.refs_0_), channel_id=1, source_target_pairs={{0,1},{1,3},{3,5},{5,7},{7,6},{6,4},{4,2},{2,0},{8,9},{9,11},{11,1... | collective-permute-start | bytes 294920 | tf_op jit(solution)/shard_map/ppermute | solution.py:275
  34.0 6.0 %collective-permute-start.16 = (bf16[64,768]{1,0:T(8,128)(2,1)S(1)}, bf16[64,768]{1,0:T(8,128)(2,1)S(1)}, u32[]{:S(2)}, u32[]{:S(2)}) collective-permute-start(bf16[64,768]{1,0:T(8,128)(2,1)S(1)} %collective-permute-done.14.refs_2_), channel_id=1, source_target_pairs={{1,0},{3,1},{5,3},{7,5},{6,7},{4,6},{2,4},{0,2},{9,8},{11,9},{13,1... | collective-permute-start | bytes 294920 | tf_op jit(solution)/shard_map/ppermute | solution.py:275
  36.7 6.9 %collective-permute-start.15 = (bf16[72,768]{1,0:T(8,128)(2,1)S(1)}, bf16[72,768]{1,0:T(8,128)(2,1)S(1)}, u32[]{:S(2)}, u32[]{:S(2)}) collective-permute-start(bf16[72,768]{1,0:T(8,128)(2,1)S(1)} %collective-permute-done.13.refs_3_), channel_id=1, source_target_pairs={{1,0},{3,1},{5,3},{7,5},{6,7},{4,6},{2,4},{0,2},{9,8},{11,9},{13,1... | collective-permute-start | bytes 331784 | tf_op jit(solution)/shard_map/ppermute | solution.py:282
  39.1 4.6 %collective-permute-start.6 = (bf16[64,768]{1,0:T(8,128)(2,1)S(1)}, bf16[64,768]{1,0:T(8,128)(2,1)S(1)}, u32[]{:S(2)}, u32[]{:S(2)}) collective-permute-start(bf16[64,768]{1,0:T(8,128)(2,1)S(1)} %collective-permute-done.5.refs_0_), channel_id=1, source_target_pairs={{0,1},{1,3},{3,5},{5,7},{7,6},{6,4},{4,2},{2,0},{8,9},{9,11},{11,1... | collective-permute-start | bytes 294920 | tf_op jit(solution)/shard_map/ppermute | solution.py:282

commit v8 on v7

--- a/solution.py
+++ b/solution.py
@@ -56,7 +56,7 @@
     block = CORES * tok
 
     def copies(k):
-        span = pl.ds(k * depth, depth)
+        span = pl.ds(pl.multiple_of(k * depth, depth), depth)
         for i, step in enumerate(chips):
             start = pl.multiple_of(lax.rem(chip + step, chips_y) * block, block)
             yield pltpu.make_async_copy(
@@ -67,16 +67,20 @@
 
     for k in range(parts):
         for copy in copies(k):
-            copy.start()
+            copy.start(priority=1)
     width = held.shape[2]
     strip = cut(width, 256)
-    for k in range(parts):
+
+    def add(k, first):
         for copy in copies(k):
             copy.wait()
         for n in range(0, width, strip):
             span = pl.ds(n, strip)
             product = jnp.dot(h_buf[k], held[k, :, span], preferred_element_type=jnp.float32)
-            total[:, span] = product if k == 0 else total[:, span] + product
+            total[:, span] = product if first else total[:, span] + product
+
+    add(0, True)
+    lax.fori_loop(1, parts, lambda k, _: add(k, False), None)
     for i in range(len(chips)):
         for out, which in ((give, 1 - core), (keep, core)):
             start = pl.multiple_of((i * CORES + which) * tok, tok)
@@ -250,8 +254,9 @@
     half = cols // 2
 
     sibling = [(r, r ^ 1) for r in range(rows)]
-    ahead = [(cycle[i], cycle[(i + 1) % cols]) for i in range(cols)]
-    behind = [(cycle[(i + 1) % cols], cycle[i]) for i in range(cols)]
+
+    def shift(hop):
+        return [(cycle[i], cycle[(i + hop) % cols]) for i in range(cols)]
 
     def per_device(hidden, down_weight, residual, gain, qk_weight):
         tok = residual.shape[0]
@@ -269,19 +274,21 @@
         stream, upper, lower = merge(others, keep[0], got, gain[None, :])
 
         up, back = [upper, lower], [upper, lower]
-        pieces, hops, state = [], [], None
+        pieces, hops, state, opposite = [], [], None, None
         for step in range(1, half):
+            if step == half - 1:
+                opposite = up[0], back[1]
             for i in range(2):
-                up[i], back[i] = lax.ppermute(up[i], "col", ahead), lax.ppermute(back[i], "col", behind)
+                up[i], back[i] = lax.ppermute(up[i], "col", shift(1)), lax.ppermute(back[i], "col", shift(-1))
+            if opposite:
+                opposite = lax.ppermute(opposite[0], "col", shift(2)), lax.ppermute(opposite[1], "col", shift(-2))
             if pieces:
                 state = project(pieces, hops, qk_weight, state, cycle, False)
                 up[1], back[1], state = lax.optimization_barrier((up[1], back[1], state))
             pieces, hops = [list(up), list(back)], [-step, step]
             if step == 1:
                 pieces, hops = [[upper, lower]] + pieces, [0] + hops
-        opposite = [lax.ppermute(up[0], "col", ahead), lax.ppermute(back[1], "col", behind)]
         state = project(pieces, hops, qk_weight, state, cycle, False)
-        opposite, state = lax.optimization_barrier((opposite, state))
         return stream, project([opposite], [half], qk_weight, state, cycle, True)
 
     placed = (P(None, "row"), P("row", "col"), P("row", "col"), P("col"), P(None, "col"))

time: 45.3 us -> 45 us (level)
  Pallas kernels: 16.5 us -> 15.7 us
  starting transfers between devices: 17.9 us -> 18.7 us
    pallas_call x2, Pallas kernels: 11.4 us -> 10.6 us  [down(): pl.pallas_call(functools.partial(down_kernel, chips_y, tok, own), out_sha...]
    ppermute x14, starting transfers between devices: 14.4 us -> 15.2 us  [the longest x6 10.7 us: per_device(): lax.ppermute(up[i], 'col', shift(1))]
  transfers between devices with their start and end apart: 17 -> 17, of which waited for: 8 -> 8; matrix products, arithmetic and copies ran while one was open for 2% -> 2% of each run, Pallas kernels for 20% -> 19%
where the time goes in v8:
time: 45 us; the launch traced here: 44.9 us
  starting transfers between devices  18.7 us (42%)
  Pallas kernels  15.7 us (35%)
  waiting for transfers between devices  8.93 us (20%)
  between operations  0.75 us (2%)
  local copies, waits for them, and re-layouts  0.7 us (2%)
    ppermute x6, starting transfers between devices, per_device(): lax.ppermute(up[i], 'col', shift(1))  10.7 us
    pallas_call x2, Pallas kernels, down(): pl.pallas_call(functools.partial(down_kernel, chips_y, tok, own), out_sha...  10.6 us
    pallas_call x4, Pallas kernels, project(): pl.pallas_call(functools.partial(project_kernel, cycle, hops, [len(parts)...  5.03 us
    ppermute x1, starting transfers between devices, per_device(): lax.ppermute(both[step - 1], 'row', move).astype(jnp.float32)  2.95 us
    ppermute x1, starting transfers between devices, per_device(): lax.ppermute(opposite[0], 'col', shift(2))  2.59 us
    ppermute x6, waiting for transfers between devices, per_device(): lax.ppermute(up[i], 'col', shift(1))  2.12 us
    ppermute x1, waiting for transfers between devices, per_device(): lax.ppermute(opposite[1], 'col', shift(-2))  1.68 us
    ppermute x6, starting transfers between devices, per_device(): lax.ppermute(back[i], 'col', shift(-1))  1.53 us
  transfers between devices with their start and end apart: 17, of which 8 were waited for; matrix products, arithmetic and copies ran while one was open for 2% of the time, Pallas kernels for 19%

profile of v8, /device:TPU:0, one launch (start us, length us, event | category | flops | bytes accessed | tf_op | source)
XLA Modules:
  0.0 44.9 jit_solution(18256940666001759200)
XLA Ops:
  0.7 5.6 %down.2 = (bf16[1,128,768]{2,1,0:T(8,128)(2,1)S(1)}, bf16[1,128,768]{2,1,0:T(8,128)(2,1)S(1)}, bf16[8,768,768]{2,1,0:T(8,128)(2,1)S(1)}) custom-call(bf16[512,6144]{1,0:T(8,128)(2,1)} %hidden.2, bf16[6144,768]{1,0:T(8,128)(2,1)} %weight.1), custom_call_target="tpu_custom_call" | custom-call | flops 2415919104 | bytes 12582912 | tf_op jit(solution)/shard_map/down/pallas_call | solution.py:102
  6.3 0.5 %collective-permute-start = (bf16[1,128,768]{2,1,0:T(8,128)(2,1)S(1)}, bf16[1,128,768]{2,1,0:T(8,128)(2,1)S(1)}, u32[]{:S(2)}, u32[]{:S(2)}) collective-permute-start(bf16[1,128,768]{2,1,0:T(8,128)(2,1)S(1)} %get-tuple-element.30), channel_id=1, source_target_pairs={{0,8},{8,0},{16,24},{24,16},{1,9},{9,1},{17,25},{25,17},{2,10},{10... | collective-permute-start | bytes 589832 | tf_op jit(solution)/shard_map/ppermute | solution.py:265
  6.8 1.1 %collective-permute-done = bf16[1,128,768]{2,1,0:T(8,128)(2,1)S(1)} collective-permute-done((bf16[1,128,768]{2,1,0:T(8,128)(2,1)S(1)}, bf16[1,128,768]{2,1,0:T(8,128)(2,1)S(1)}, u32[]{:S(2)}, u32[]{:S(2)}) %collective-permute-start) | collective-permute-done | bytes 196640 | tf_op jit(solution)/shard_map/ppermute | solution.py:265
  7.9 3.0 %collective-permute-start.1 = (bf16[128,768]{1,0:T(8,128)(2,1)S(1)}, bf16[128,768]{1,0:T(8,128)(2,1)S(1)}, u32[]{:S(2)}, u32[]{:S(2)}) collective-permute-start(bf16[128,768]{1,0:T(8,128)(2,1)S(1)} %bitcast.5), channel_id=1, source_target_pairs={{0,16},{8,24},{16,0},{24,8},{1,17},{9,25},{17,1},{25,9},{2,18},{10... | collective-permute-start | bytes 589832 | tf_op jit(solution)/shard_map/ppermute | solution.py:271
  10.9 5.0 %down.3 = (bf16[1,128,768]{2,1,0:T(8,128)(2,1)S(1)}, bf16[1,128,768]{2,1,0:T(8,128)(2,1)S(1)}) custom-call(bf16[512,6144]{1,0:T(8,128)(2,1)} %hidden.2, bf16[8,768,768]{2,1,0:T(8,128)(2,1)S(1)} %get-tuple-element.33.weight), custom_call_target="tpu_custom_call" | custom-call | flops 2415919104 | bytes 3145728 | tf_op jit(solution)/shard_map/down/pallas_call | solution.py:102
  16.1 1.3 %collective-permute-done.2.got = bf16[128,768]{1,0:T(8,128)(2,1)S(1)} collective-permute-done((bf16[128,768]{1,0:T(8,128)(2,1)S(1)}, bf16[128,768]{1,0:T(8,128)(2,1)S(1)}, u32[]{:S(2)}, u32[]{:S(2)}) %collective-permute-start.2) | collective-permute-done | bytes 196640 | tf_op jit(solution)/shard_map/ppermute | solution.py:273
  17.5 1.9 %collective-permute-start.6 = (bf16[72,768]{1,0:T(8,128)(2,1)S(1)}, bf16[72,768]{1,0:T(8,128)(2,1)S(1)}, u32[]{:S(2)}, u32[]{:S(2)}) collective-permute-start(bf16[72,768]{1,0:T(8,128)(2,1)S(1)} %get-tuple-element.38.refs_1_), channel_id=1, source_target_pairs={{0,1},{1,3},{3,5},{5,7},{7,6},{6,4},{4,2},{2,0},{8,9},{9,11},{11,1... | collective-permute-start | bytes 331784 | tf_op jit(solution)/shard_map/ppermute | solution.py:282
  19.6 1.9 %collective-permute-start.3 = (bf16[64,768]{1,0:T(8,128)(2,1)S(1)}, bf16[64,768]{1,0:T(8,128)(2,1)S(1)}, u32[]{:S(2)}, u32[]{:S(2)}) collective-permute-start(bf16[64,768]{1,0:T(8,128)(2,1)S(1)} %get-tuple-element.37.refs_0_), channel_id=1, source_target_pairs={{0,1},{1,3},{3,5},{5,7},{7,6},{6,4},{4,2},{2,0},{8,9},{9,11},{11,1... | collective-permute-start | bytes 294920 | tf_op jit(solution)/shard_map/ppermute | solution.py:282
  21.6 1.8 %collective-permute-done.6.refs_3_ = bf16[72,768]{1,0:T(8,128)(2,1)S(1)} collective-permute-done((bf16[72,768]{1,0:T(8,128)(2,1)S(1)}, bf16[72,768]{1,0:T(8,128)(2,1)S(1)}, u32[]{:S(2)}, u32[]{:S(2)}) %collective-permute-start.6) | collective-permute-done | bytes 110624 | tf_op jit(solution)/shard_map/ppermute | solution.py:282
  23.4 1.9 %collective-permute-start.7 = (bf16[72,768]{1,0:T(8,128)(2,1)S(1)}, bf16[72,768]{1,0:T(8,128)(2,1)S(1)}, u32[]{:S(2)}, u32[]{:S(2)}) collective-permute-start(bf16[72,768]{1,0:T(8,128)(2,1)S(1)} %collective-permute-done.6.refs_3_), channel_id=1, source_target_pairs={{0,1},{1,3},{3,5},{5,7},{7,6},{6,4},{4,2},{2,0},{8,9},{9,11},{11,1... | collective-permute-start | bytes 331784 | tf_op jit(solution)/shard_map/ppermute | solution.py:282
  25.5 1.9 %collective-permute-start.4 = (bf16[64,768]{1,0:T(8,128)(2,1)S(1)}, bf16[64,768]{1,0:T(8,128)(2,1)S(1)}, u32[]{:S(2)}, u32[]{:S(2)}) collective-permute-start(bf16[64,768]{1,0:T(8,128)(2,1)S(1)} %collective-permute-done.3.refs_2_), channel_id=1, source_target_pairs={{0,1},{1,3},{3,5},{5,7},{7,6},{6,4},{4,2},{2,0},{8,9},{9,11},{11,1... | collective-permute-start | bytes 294920 | tf_op jit(solution)/shard_map/ppermute | solution.py:282
  27.5 1.4 %project.4 = (f32[128,1]{1,0:T(8,128)S(1)}, f32[2,128,1]{2,1,0:T(8,128)S(1)}, f32[144,1536]{1,0:T(8,128)S(1)}) custom-call(bf16[64,768]{1,0:T(8,128)(2,1)S(1)} %get-tuple-element.37.refs_0_, bf16[72,768]{1,0:T(8,128)(2,1)S(1)} %get-tuple-element.38.refs_1_, bf16[64,768]{1,0:T(8,128)(2,1)S(1)} %collective-permute-done.3.refs_2_, ...), custom_call_target="tpu_custom_call" | custom-call | flops 1019215872 | tf_op jit(solution)/shard_map/project/pallas_call | solution.py:228
  29.2 1.3 %collective-permute-done.9.refs_3_ = bf16[72,768]{1,0:T(8,128)(2,1)S(1)} collective-permute-done((bf16[72,768]{1,0:T(8,128)(2,1)S(1)}, bf16[72,768]{1,0:T(8,128)(2,1)S(1)}, u32[]{:S(2)}, u32[]{:S(2)}) %collective-permute-start.9) | collective-permute-done | bytes 110624 | tf_op jit(solution)/shard_map/ppermute | solution.py:282
  30.5 1.6 %collective-permute-start.12 = (bf16[72,768]{1,0:T(8,128)(2,1)S(1)}, bf16[72,768]{1,0:T(8,128)(2,1)S(1)}, u32[]{:S(2)}, u32[]{:S(2)}) collective-permute-start(bf16[72,768]{1,0:T(8,128)(2,1)S(1)} %collective-permute-done.7.refs_1_), channel_id=1, source_target_pairs={{0,1},{1,3},{3,5},{5,7},{7,6},{6,4},{4,2},{2,0},{8,9},{9,11},{11,1... | collective-permute-start | bytes 331784 | tf_op jit(solution)/shard_map/ppermute | solution.py:282
  32.1 0.4 collective-permute-start.13
  32.5 1.6 %collective-permute-start.15 = (bf16[64,768]{1,0:T(8,128)(2,1)S(1)}, bf16[64,768]{1,0:T(8,128)(2,1)S(1)}, u32[]{:S(2)}, u32[]{:S(2)}) collective-permute-start(bf16[64,768]{1,0:T(8,128)(2,1)S(1)} %collective-permute-done.4.refs_0_), channel_id=1, source_target_pairs={{0,1},{1,3},{3,5},{5,7},{7,6},{6,4},{4,2},{2,0},{8,9},{9,11},{11,1... | collective-permute-start | bytes 294920 | tf_op jit(solution)/shard_map/ppermute | solution.py:282
  34.1 0.4 collective-permute-start.16
  34.5 0.7 %copy.15 = bf16[128,768]{1,0:T(8,128)(2,1)} copy(bf16[128,768]{1,0:T(8,128)(2,1)S(1)} %get-tuple-element.56) | data formatting | bytes 393216
  35.2 2.6 %collective-permute-start.5 = (bf16[64,768]{1,0:T(8,128)(2,1)S(1)}, bf16[64,768]{1,0:T(8,128)(2,1)S(1)}, u32[]{:S(2)}, u32[]{:S(2)}) collective-permute-start(bf16[64,768]{1,0:T(8,128)(2,1)S(1)} %collective-permute-done.4.refs_0_), channel_id=1, source_target_pairs={{0,3},{1,5},{3,7},{5,6},{7,4},{6,2},{4,0},{2,1},{8,11},{9,13},{11,... | collective-permute-start | bytes 294920 | tf_op jit(solution)/shard_map/ppermute | solution.py:284
  38.1 1.1 %project.5 = (f32[2,128,1]{2,1,0:T(8,128)S(1)}, f32[144,1536]{1,0:T(8,128)S(1)}) custom-call(bf16[64,768]{1,0:T(8,128)(2,1)S(1)} %collective-permute-done.4.refs_0_, bf16[72,768]{1,0:T(8,128)(2,1)S(1)} %collective-permute-done.7.refs_1_, bf16[64,768]{1,0:T(8,128)(2,1)S(1)} %collective-permute-done.14.refs_2_, ...), custom_call_target="tpu_custom_call", output_to_operand_aliasing={{0}: (6, {}), {1}: (7, {})} | custom-call | flops 679477248 | tf_op jit(solution)/shard_map/project/pallas_call | solution.py:228
  39.3 1.1 %project.6 = (f32[2,128,1]{2,1,0:T(8,128)S(1)}, f32[144,1536]{1,0:T(8,128)S(1)}) custom-call(bf16[64,768]{1,0:T(8,128)(2,1)S(1)} %collective-permute-done.15.refs_0_, bf16[72,768]{1,0:T(8,128)(2,1)S(1)} %collective-permute-done.12.refs_1_, bf16[64,768]{1,0:T(8,128)(2,1)S(1)} %collective-permute-done.16.refs_2_, ...), custom_call_target="tpu_custom_call", output_to_operand_aliasing={{0}: (6, {}), {1}: (7, {})} | custom-call | flops 679477248 | tf_op jit(solution)/shard_map/project/pallas_call | solution.py:228
  40.4 1.4 %collective-permute-done.5.refs_0_ = bf16[64,768]{1,0:T(8,128)(2,1)S(1)} collective-permute-done((bf16[64,768]{1,0:T(8,128)(2,1)S(1)}, bf16[64,768]{1,0:T(8,128)(2,1)S(1)}, u32[]{:S(2)}, u32[]{:S(2)}) %collective-permute-start.5) | collective-permute-done | bytes 98336 | tf_op jit(solution)/shard_map/ppermute | solution.py:284
  41.8 1.7 %collective-permute-done.11.refs_1_ = bf16[72,768]{1,0:T(8,128)(2,1)S(1)} collective-permute-done((bf16[72,768]{1,0:T(8,128)(2,1)S(1)}, bf16[72,768]{1,0:T(8,128)(2,1)S(1)}, u32[]{:S(2)}, u32[]{:S(2)}) %collective-permute-start.11) | collective-permute-done | bytes 110624 | tf_op jit(solution)/shard_map/ppermute | solution.py:284
  43.5 1.4 %project.7 = bf16[128,1536]{1,0:T(8,128)(2,1)} custom-call(bf16[64,768]{1,0:T(8,128)(2,1)S(1)} %collective-permute-done.5.refs_0_, bf16[72,768]{1,0:T(8,128)(2,1)S(1)} %collective-permute-done.11.refs_1_, bf16[6144,1536]{1,0:T(8,128)(2,1)S(1)} %copy-done, f32[128,1]{1,0:T(8,128)S(1)} %get-tuple-element.49.refs_5_.refs_3_, ...), custom_call_target="tpu_custom_call" | custom-call | flops 339738624 | tf_op jit(solution)/shard_map/project/pallas_call | solution.py:228
  (27 shorter events, 1.6 us)
Async XLA Ops:
  0.6 6.2 %copy-start.2 = (bf16[768]{0:T(1024)(128)(2,1)S(1)}, bf16[768]{0:T(1024)(128)(2,1)}, u32[]{:S(2)}) copy-start(bf16[768]{0:T(1024)(128)(2,1)} %param.8) | copy-start | bytes 4612
  0.6 26.9 %copy-start = (bf16[6144,1536]{1,0:T(8,128)(2,1)S(1)}, bf16[6144,1536]{1,0:T(8,128)(2,1)}, u32[]{:S(2)}) copy-start(bf16[6144,1536]{1,0:T(8,128)(2,1)} %refs_2_.1) | copy-start | bytes 56623108
  6.2 9.8 %copy-start.1 = (bf16[128,768]{1,0:T(8,128)(2,1)S(1)}, bf16[128,768]{1,0:T(8,128)(2,1)}, u32[]{:S(2)}) copy-start(bf16[128,768]{1,0:T(8,128)(2,1)} %param.7) | copy-start | bytes 589828
  6.3 1.6 %collective-permute-start = (bf16[1,128,768]{2,1,0:T(8,128)(2,1)S(1)}, bf16[1,128,768]{2,1,0:T(8,128)(2,1)S(1)}, u32[]{:S(2)}, u32[]{:S(2)}) collective-permute-start(bf16[1,128,768]{2,1,0:T(8,128)(2,1)S(1)} %get-tuple-element.30), channel_id=1, source_target_pairs={{0,8},{8,0},{16,24},{24,16},{1,9},{9,1},{17,25},{25,17},{2,10},{10... | collective-permute-start | bytes 589832 | tf_op jit(solution)/shard_map/ppermute | solution.py:265
  7.9 8.2 %collective-permute-start.1 = (bf16[128,768]{1,0:T(8,128)(2,1)S(1)}, bf16[128,768]{1,0:T(8,128)(2,1)S(1)}, u32[]{:S(2)}, u32[]{:S(2)}) collective-permute-start(bf16[128,768]{1,0:T(8,128)(2,1)S(1)} %bitcast.5), channel_id=1, source_target_pairs={{0,16},{8,24},{16,0},{24,8},{1,17},{9,25},{17,1},{25,9},{2,18},{10... | collective-permute-start | bytes 589832 | tf_op jit(solution)/shard_map/ppermute | solution.py:271
  15.9 1.5 %collective-permute-start.2 = (bf16[128,768]{1,0:T(8,128)(2,1)S(1)}, bf16[128,768]{1,0:T(8,128)(2,1)S(1)}, u32[]{:S(2)}, u32[]{:S(2)}) collective-permute-start(bf16[128,768]{1,0:T(8,128)(2,1)S(1)} %bitcast.4), channel_id=1, source_target_pairs={{0,8},{8,0},{16,24},{24,16},{1,9},{9,1},{17,25},{25,17},{2,10},{10... | collective-permute-start | bytes 589832 | tf_op jit(solution)/shard_map/ppermute | solution.py:273
  17.5 5.9 %collective-permute-start.6 = (bf16[72,768]{1,0:T(8,128)(2,1)S(1)}, bf16[72,768]{1,0:T(8,128)(2,1)S(1)}, u32[]{:S(2)}, u32[]{:S(2)}) collective-permute-start(bf16[72,768]{1,0:T(8,128)(2,1)S(1)} %get-tuple-element.38.refs_1_), channel_id=1, source_target_pairs={{0,1},{1,3},{3,5},{5,7},{7,6},{6,4},{4,2},{2,0},{8,9},{9,11},{11,1... | collective-permute-start | bytes 331784 | tf_op jit(solution)/shard_map/ppermute | solution.py:282
  19.4 5.9 %collective-permute-start.8 = (bf16[72,768]{1,0:T(8,128)(2,1)S(1)}, bf16[72,768]{1,0:T(8,128)(2,1)S(1)}, u32[]{:S(2)}, u32[]{:S(2)}) collective-permute-start(bf16[72,768]{1,0:T(8,128)(2,1)S(1)} %get-tuple-element.38.refs_1_), channel_id=1, source_target_pairs={{0,2},{1,0},{3,1},{5,3},{7,5},{6,7},{4,6},{2,4},{8,10},{9,8},{11,9... | collective-permute-start | bytes 331784 | tf_op jit(solution)/shard_map/ppermute | solution.py:282
  19.6 5.9 %collective-permute-start.3 = (bf16[64,768]{1,0:T(8,128)(2,1)S(1)}, bf16[64,768]{1,0:T(8,128)(2,1)S(1)}, u32[]{:S(2)}, u32[]{:S(2)}) collective-permute-start(bf16[64,768]{1,0:T(8,128)(2,1)S(1)} %get-tuple-element.37.refs_0_), channel_id=1, source_target_pairs={{0,1},{1,3},{3,5},{5,7},{7,6},{6,4},{4,2},{2,0},{8,9},{9,11},{11,1... | collective-permute-start | bytes 294920 | tf_op jit(solution)/shard_map/ppermute | solution.py:282
  21.4 5.9 %collective-permute-start.10 = (bf16[64,768]{1,0:T(8,128)(2,1)S(1)}, bf16[64,768]{1,0:T(8,128)(2,1)S(1)}, u32[]{:S(2)}, u32[]{:S(2)}) collective-permute-start(bf16[64,768]{1,0:T(8,128)(2,1)S(1)} %get-tuple-element.37.refs_0_), channel_id=1, source_target_pairs={{0,2},{1,0},{3,1},{5,3},{7,5},{6,7},{4,6},{2,4},{8,10},{9,8},{11,9... | collective-permute-start | bytes 294920 | tf_op jit(solution)/shard_map/ppermute | solution.py:282
  23.4 5.8 %collective-permute-start.7 = (bf16[72,768]{1,0:T(8,128)(2,1)S(1)}, bf16[72,768]{1,0:T(8,128)(2,1)S(1)}, u32[]{:S(2)}, u32[]{:S(2)}) collective-permute-start(bf16[72,768]{1,0:T(8,128)(2,1)S(1)} %collective-permute-done.6.refs_3_), channel_id=1, source_target_pairs={{0,1},{1,3},{3,5},{5,7},{7,6},{6,4},{4,2},{2,0},{8,9},{9,11},{11,1... | collective-permute-start | bytes 331784 | tf_op jit(solution)/shard_map/ppermute | solution.py:282
  25.3 5.2 %collective-permute-start.9 = (bf16[72,768]{1,0:T(8,128)(2,1)S(1)}, bf16[72,768]{1,0:T(8,128)(2,1)S(1)}, u32[]{:S(2)}, u32[]{:S(2)}) collective-permute-start(bf16[72,768]{1,0:T(8,128)(2,1)S(1)} %collective-permute-done.8.refs_5_), channel_id=1, source_target_pairs={{0,2},{1,0},{3,1},{5,3},{7,5},{6,7},{4,6},{2,4},{8,10},{9,8},{11,9... | collective-permute-start | bytes 331784 | tf_op jit(solution)/shard_map/ppermute | solution.py:282
  25.5 7.0 %collective-permute-start.4 = (bf16[64,768]{1,0:T(8,128)(2,1)S(1)}, bf16[64,768]{1,0:T(8,128)(2,1)S(1)}, u32[]{:S(2)}, u32[]{:S(2)}) collective-permute-start(bf16[64,768]{1,0:T(8,128)(2,1)S(1)} %collective-permute-done.3.refs_2_), channel_id=1, source_target_pairs={{0,1},{1,3},{3,5},{5,7},{7,6},{6,4},{4,2},{2,0},{8,9},{9,11},{11,1... | collective-permute-start | bytes 294920 | tf_op jit(solution)/shard_map/ppermute | solution.py:282
  27.3 6.7 %collective-permute-start.14 = (bf16[64,768]{1,0:T(8,128)(2,1)S(1)}, bf16[64,768]{1,0:T(8,128)(2,1)S(1)}, u32[]{:S(2)}, u32[]{:S(2)}) collective-permute-start(bf16[64,768]{1,0:T(8,128)(2,1)S(1)} %collective-permute-done.10.refs_4_), channel_id=1, source_target_pairs={{0,2},{1,0},{3,1},{5,3},{7,5},{6,7},{4,6},{2,4},{8,10},{9,8},{11,9... | collective-permute-start | bytes 294920 | tf_op jit(solution)/shard_map/ppermute | solution.py:282
  30.5 7.3 %collective-permute-start.12 = (bf16[72,768]{1,0:T(8,128)(2,1)S(1)}, bf16[72,768]{1,0:T(8,128)(2,1)S(1)}, u32[]{:S(2)}, u32[]{:S(2)}) collective-permute-start(bf16[72,768]{1,0:T(8,128)(2,1)S(1)} %collective-permute-done.7.refs_1_), channel_id=1, source_target_pairs={{0,1},{1,3},{3,5},{5,7},{7,6},{6,4},{4,2},{2,0},{8,9},{9,11},{11,1... | collective-permute-start | bytes 331784 | tf_op jit(solution)/shard_map/ppermute | solution.py:282
  32.1 7.2 %collective-permute-start.13 = (bf16[72,768]{1,0:T(8,128)(2,1)S(1)}, bf16[72,768]{1,0:T(8,128)(2,1)S(1)}, u32[]{:S(2)}, u32[]{:S(2)}) collective-permute-start(bf16[72,768]{1,0:T(8,128)(2,1)S(1)} %collective-permute-done.9.refs_3_), channel_id=1, source_target_pairs={{0,2},{1,0},{3,1},{5,3},{7,5},{6,7},{4,6},{2,4},{8,10},{9,8},{11,9... | collective-permute-start | bytes 331784 | tf_op jit(solution)/shard_map/ppermute | solution.py:282
  32.5 6.8 %collective-permute-start.15 = (bf16[64,768]{1,0:T(8,128)(2,1)S(1)}, bf16[64,768]{1,0:T(8,128)(2,1)S(1)}, u32[]{:S(2)}, u32[]{:S(2)}) collective-permute-start(bf16[64,768]{1,0:T(8,128)(2,1)S(1)} %collective-permute-done.4.refs_0_), channel_id=1, source_target_pairs={{0,1},{1,3},{3,5},{5,7},{7,6},{6,4},{4,2},{2,0},{8,9},{9,11},{11,1... | collective-permute-start | bytes 294920 | tf_op jit(solution)/shard_map/ppermute | solution.py:282
  34.1 5.2 %collective-permute-start.16 = (bf16[64,768]{1,0:T(8,128)(2,1)S(1)}, bf16[64,768]{1,0:T(8,128)(2,1)S(1)}, u32[]{:S(2)}, u32[]{:S(2)}) collective-permute-start(bf16[64,768]{1,0:T(8,128)(2,1)S(1)} %collective-permute-done.14.refs_2_), channel_id=1, source_target_pairs={{0,2},{1,0},{3,1},{5,3},{7,5},{6,7},{4,6},{2,4},{8,10},{9,8},{11,9... | collective-permute-start | bytes 294920 | tf_op jit(solution)/shard_map/ppermute | solution.py:282
  35.2 6.6 %collective-permute-start.5 = (bf16[64,768]{1,0:T(8,128)(2,1)S(1)}, bf16[64,768]{1,0:T(8,128)(2,1)S(1)}, u32[]{:S(2)}, u32[]{:S(2)}) collective-permute-start(bf16[64,768]{1,0:T(8,128)(2,1)S(1)} %collective-permute-done.4.refs_0_), channel_id=1, source_target_pairs={{0,3},{1,5},{3,7},{5,6},{7,4},{6,2},{4,0},{2,1},{8,11},{9,13},{11,... | collective-permute-start | bytes 294920 | tf_op jit(solution)/shard_map/ppermute | solution.py:284
  37.8 5.7 %collective-permute-start.11 = (bf16[72,768]{1,0:T(8,128)(2,1)S(1)}, bf16[72,768]{1,0:T(8,128)(2,1)S(1)}, u32[]{:S(2)}, u32[]{:S(2)}) collective-permute-start(bf16[72,768]{1,0:T(8,128)(2,1)S(1)} %collective-permute-done.9.refs_3_), channel_id=1, source_target_pairs={{0,4},{1,2},{3,0},{5,1},{7,3},{6,5},{4,7},{2,6},{8,12},{9,10},{11,... | collective-permute-start | bytes 331784 | tf_op jit(solution)/shard_map/ppermute | solution.py:284

commit v9 on v8

v9 whole, which is shorter than its diff:
```python
import functools

import jax
import jax.numpy as jnp
from jax import lax
from jax.experimental import pallas as pl
from jax.experimental.pallas import tpu as pltpu
from jax.sharding import PartitionSpec as P

CORES = 2
EXTRA = 16
GAIN = 8
MIB = 1024 * 1024
HBM = pl.BlockSpec(memory_space=pl.ANY)
VMEM = pl.BlockSpec(memory_space=pltpu.VMEM)


def grid_of(count):
    x = 1
    while (2 * x) * (2 * x) <= count:
        x *= 2
    return count // x, x


def cycle_of(count):
    z, x = grid_of(count)
    walk = [0]
    for i in range(z):
        line = list(range(1, x))
        walk += [i * x + j for j in (line if i % 2 == 0 else line[::-1])]
    return walk + [i * x for i in range(z - 1, 0, -1)]


def pick(index, table):
    value = jnp.int32(table[0])
    for i in range(1, len(table)):
        value = jnp.where(index == i, jnp.int32(table[i]), value)
    return value


def cut(size, most):
    fits = [part for part in range(256, most + 1, 256) if size % part == 0]
    return fits[-1] if fits else size


def down_kernel(chips_y, tok, own, hidden, weight, *refs):
    if own:
        (give, keep), held = refs[:2], weight
    else:
        give, keep, held = refs[:3]
    h_buf, total, sems = refs[-3:]
    parts, depth, _ = held.shape
    me = lax.axis_index("row")
    chip, core = me // CORES, me % CORES
    chips = [0] if own else list(range(1, chips_y))
    block = CORES * tok

    def copies(k):
        span = pl.ds(pl.multiple_of(k * depth, depth), depth)
        for i, step in enumerate(chips):
            start = pl.multiple_of(lax.rem(chip + step, chips_y) * block, block)
            yield pltpu.make_async_copy(
                hidden.at[pl.ds(start, block), span], h_buf.at[k, pl.ds(i * block, block)], sems.at[1 + i, k]
            )
        if not own:
            yield pltpu.make_async_copy(weight.at[span, :], held.at[k], sems.at[0, k])

    for k in range(parts):
        for copy in copies(k):
            copy.start(priority=1)
    for copy in copies(0):
        copy.wait()
    total[...] = jnp.dot(h_buf[0], held[0], preferred_element_type=jnp.float32)

    def body(k, _):
        for copy in copies(k):
            copy.wait()
        total[...] += jnp.dot(h_buf[k], held[k], preferred_element_type=jnp.float32)
        return _

    lax.fori_loop(1, parts, body, 0)
    for i in range(len(chips)):
        for out, which in ((give, 1 - core), (keep, core)):
            start = pl.multiple_of((i * CORES + which) * tok, tok)
            out[i] = total[pl.ds(start, tok), :].astype(out.dtype)


def down(hidden, weight, tok, chips_y, own):
    inner = hidden.shape[1]
    if own:
        parts, depth, width = weight.shape
    else:
        width = weight.shape[1]
        depth = cut(inner, 768)
        parts = inner // depth
    chips = 1 if own else chips_y - 1
    tokens = chips * CORES * tok
    block = pltpu.VMEM((chips, tok, width), jnp.bfloat16)
    out_shape = (block, block) if own else (block, block, pltpu.VMEM((parts, depth, width), jnp.bfloat16))
    return pl.pallas_call(
        functools.partial(down_kernel, chips_y, tok, own),
        out_shape=out_shape,
        in_specs=[HBM, VMEM if own else HBM],
        out_specs=(VMEM,) * len(out_shape),
        scratch_shapes=[
            pltpu.VMEM((parts, tokens, depth), jnp.bfloat16),
            pltpu.VMEM((tokens, width), jnp.float32),
            pltpu.SemaphoreType.DMA((1 + chips, parts)),
        ],
        compiler_params=pltpu.CompilerParams(vmem_limit_bytes=24 * MIB),
        cost_estimate=pl.CostEstimate(
            flops=2 * tokens * inner * width,
            bytes_accessed=2 * inner * (tokens if own else width + tokens),
            transcendentals=0,
        ),
        name="down",
    )(
        pltpu.with_memory_space_constraint(hidden, pltpu.HBM),
        pltpu.with_memory_space_constraint(weight, pltpu.VMEM if own else pltpu.HBM),
    )


def begin(values, row, weight, lhs, shift_ref, sums_ref, total_ref):
    tok, width = values.shape
    shift = jnp.mean(values, axis=1, keepdims=True)
    dev = values - shift
    shift_ref[...] = shift
    sums_ref[0] = jnp.sum(dev, axis=1, keepdims=True)
    sums_ref[1] = jnp.sum(dev * dev, axis=1, keepdims=True)
    lhs[0:tok, :] = (dev * row).astype(lhs.dtype)
    lhs[tok : tok + EXTRA, :] = jnp.broadcast_to(row, (EXTRA, width)).astype(lhs.dtype)
    start = pl.multiple_of(lax.axis_index("col") * width, width)
    columns = weight.shape[1]
    strip = cut(columns, 512)
    for n in range(0, columns, strip):
        span = pl.ds(n, strip)
        total_ref[:, span] = jnp.dot(lhs[...], weight[pl.ds(start, width), span], preferred_element_type=jnp.float32)


def merge_kernel(others, keep, got, gain, weight, piece, shift, sums, total, lhs):
    tok, width = others.shape
    own = keep[...].astype(jnp.float32) + got[...].astype(jnp.float32)
    value = (others[...] + own).astype(piece.dtype)
    row = gain[...].astype(jnp.float32)
    piece[0:tok, :] = value
    piece[tok : tok + GAIN, :] = jnp.broadcast_to(row, (GAIN, width)).astype(piece.dtype)

    @pl.when(lax.axis_index("row") % CORES == 1)
    def _():
        begin(value.astype(jnp.float32), row, weight, lhs, shift, sums, total)


def state_of(tok, columns):
    shapes = (tok, 1), (2, tok, 1), (tok + EXTRA, columns)
    return [pltpu.VMEM(shape, jnp.float32) for shape in shapes]


def merge(others, keep, got, gain, weight):
    tok, width = others.shape
    out_shape = [pltpu.VMEM((tok + GAIN, width), jnp.bfloat16), *state_of(tok, weight.shape[1])]
    piece, *state = pl.pallas_call(
        merge_kernel,
        out_shape=out_shape,
        in_specs=[VMEM] * 5,
        out_specs=[VMEM] * 4,
        scratch_shapes=[pltpu.VMEM((tok + EXTRA, width), jnp.bfloat16)],
        compiler_params=pltpu.CompilerParams(vmem_limit_bytes=12 * MIB),
        name="merge",
    )(others, keep, got, gain, pltpu.with_memory_space_constraint(weight, pltpu.VMEM))
    return piece, state


def settle_kernel(piece, weight, _, __, ___, stream, shift, sums, total, lhs):
    tok = stream.shape[0]
    stream[...] = piece[0:tok, :]

    @pl.when(lax.axis_index("row") % CORES == 0)
    def _():
        row = piece[tok : tok + GAIN, :].astype(jnp.float32)[0:1]
        begin(piece[0:tok, :].astype(jnp.float32), row, weight, lhs, shift, sums, total)


def settle(piece, weight, state):
    tok, width = piece.shape[0] - GAIN, piece.shape[1]
    stream, *state = pl.pallas_call(
        settle_kernel,
        out_shape=[jax.ShapeDtypeStruct((tok, width), jnp.bfloat16), *state_of(tok, weight.shape[1])],
        in_specs=[VMEM] * 5,
        out_specs=[VMEM] * 4,
        scratch_shapes=[pltpu.VMEM((tok + EXTRA, width), jnp.bfloat16)],
        input_output_aliases={2: 1, 3: 2, 4: 3},
        compiler_params=pltpu.CompilerParams(vmem_limit_bytes=12 * MIB),
        cost_estimate=pl.CostEstimate(
            flops=2 * (tok + EXTRA) * width * weight.shape[1], bytes_accessed=2 * tok * width, transcendentals=0
        ),
        name="settle",
    )(piece, pltpu.with_memory_space_constraint(weight, pltpu.VMEM), *state)
    return stream, state


def project_kernel(cycle, hops, shapes, last, *refs):
    count = len(cycle)
    refs = list(refs)
    take = lambda n: [refs.pop(0) for _ in range(n)]
    pieces = [take(n) for n in shapes]
    weight, shift_in, sums_in, total_in = take(4)
    outs, lhs = refs[:-1], refs[-1]
    tok = shift_in.shape[0]
    width = lhs.shape[2]
    columns = weight.shape[1]
    strip = cut(columns, 512)

    me = lax.axis_index("col")
    place = pick(me, [cycle.index(c) for c in range(count)])
    ids = [pick(lax.rem(place + hop + count, count), cycle) for hop in hops]
    one, two = sums_in[0], sums_in[1]
    for i, parts in enumerate(pieces):
        whole = jnp.concatenate([part[...].astype(jnp.float32) for part in parts], axis=0)
        row = whole[tok : tok + 1]
        dev = whole[0:tok] - shift_in[...]
        one = one + jnp.sum(dev, axis=1, keepdims=True)
        two = two + jnp.sum(dev * dev, axis=1, keepdims=True)
        lhs[i, 0:tok, :] = (dev * row).astype(lhs.dtype)
        lhs[i, tok : tok + EXTRA, :] = jnp.broadcast_to(row, (EXTRA, width)).astype(lhs.dtype)
    if last:
        off = one / (width * count)
        var = jnp.maximum(two / (width * count) - off * off, 0.0)
        scale = 1.0 / jnp.sqrt(var + 1e-06)
    else:
        outs[0][0] = one
        outs[0][1] = two

    for n in range(0, columns, strip):
        span = pl.ds(n, strip)
        value = total_in[:, span]
        for i in range(len(hops)):
            rows = pl.ds(pl.multiple_of(ids[i] * width, width), width)
            value = value + jnp.dot(lhs[i], weight[rows, span], preferred_element_type=jnp.float32)
        if last:
            outs[0][:, span] = ((value[0:tok] - off * value[tok : tok + 1]) * scale).astype(outs[0].dtype)
        else:
            outs[1][:, span] = value


def project(pieces, hops, weight, state, cycle, last):
    tok, width = state[0].shape[0], pieces[0][0].shape[1]
    columns = weight.shape[1]
    flat = [part for parts in pieces for part in parts]
    base = len(flat) + 1
    if last:
        out_shape, aliases = [jax.ShapeDtypeStruct((tok, columns), jnp.bfloat16)], {}
    else:
        out_shape, aliases = state_of(tok, columns)[1:], {base + 1: 0, base + 2: 1}
    got = pl.pallas_call(
        functools.partial(project_kernel, cycle, hops, [len(parts) for parts in pieces], last),
        out_shape=out_shape,
        in_specs=[VMEM] * (base + 3),
        out_specs=[VMEM] * len(out_shape),
        scratch_shapes=[pltpu.VMEM((len(hops), tok + EXTRA, width), jnp.bfloat16)],
        input_output_aliases=aliases,
        compiler_params=pltpu.CompilerParams(vmem_limit_bytes=12 * MIB),
        cost_estimate=pl.CostEstimate(
            flops=2 * len(hops) * (tok + EXTRA) * width * columns, bytes_accessed=0, transcendentals=0
        ),
        name="project",
    )(*flat, pltpu.with_memory_space_constraint(weight, pltpu.VMEM), *state)
    return got[0] if last else [state[0], *got]


def solution(mesh):
    rows, cols = mesh.shape["row"], mesh.shape["col"]
    chips_y = rows // CORES
    cycle = cycle_of(cols)
    half = cols // 2

    sibling = [(r, r ^ 1) for r in range(rows)]

    def shift(hop):
        return [(cycle[i], cycle[(i + hop) % cols]) for i in range(cols)]

    def per_device(hidden, down_weight, residual, gain, qk_weight):
        tok = residual.shape[0]

        give, keep, down_weight = down(hidden, down_weight, tok, chips_y, False)
        got = lax.ppermute(give, "row", sibling)
        both = (keep.astype(jnp.float32) + got.astype(jnp.float32)).astype(jnp.bfloat16)
        both, hidden = lax.optimization_barrier((both, hidden))
        others = residual.astype(jnp.float32)
        for step in range(1, chips_y):
            move = [(r, (r + CORES * step) % rows) for r in range(rows)]
            others = others + lax.ppermute(both[step - 1], "row", move).astype(jnp.float32)
        give, keep = down(hidden, down_weight, tok, chips_y, True)
        got = lax.ppermute(give[0], "row", sibling)
        piece, state = merge(others, keep[0], got, gain[None, :], qk_weight)

        up, back, pieces = piece, piece, None
        for step in range(1, half + 1):
            if step == half:
                up, back = up[: tok // 2], back[tok // 2 :]
            up, back = lax.ppermute(up, "col", shift(1)), lax.ppermute(back, "col", shift(-1))
            if step == 1:
                stream, state = settle(piece, qk_weight, state)
            else:
                state = project(pieces, [1 - step, step - 1], qk_weight, state, cycle, False)
            back, state = lax.optimization_barrier((back, state))
            pieces = [[up], [back]]
        return stream, project([[up, back]], [half], qk_weight, state, cycle, True)

    placed = (P(None, "row"), P("row", "col"), P("row", "col"), P("col"), P(None, "col"))
    return jax.shard_map(
        per_device,
        mesh=mesh,
        in_specs=placed,
        out_specs=(P("row", "col"), P("row", "col")),
        check_vma=False,
    )
```

time: 45 us -> 46.7 us (1.038)
  waiting for transfers between devices: 8.93 us -> 17.3 us
  starting transfers between devices: 18.7 us -> 11.8 us
  Pallas kernels: 15.7 us -> 16.6 us
  local copies, waits for them, and re-layouts: 0.7 us -> 0.04 us
    ppermute x14 -> x8, waiting for transfers between devices: 6.49 us -> 14.8 us  [the longest x4 13.3 us: per_device(): lax.ppermute(back, 'col', shift(-1))]
    ppermute x14 -> x8, starting transfers between devices: 15.2 us -> 8.26 us  [the longest x4 7.15 us: per_device(): lax.ppermute(back, 'col', shift(-1))]
    pallas_call x1 -> x2, Pallas kernels: 0.08 us -> 1.38 us  [the longest x1 1.31 us: settle(): pl.pallas_call(settle_kernel, out_shape=[jax.ShapeDtypeStruct((tok, width...]
    unnamed x7 -> x6, local copies, waits for them, and re-layouts: 0.69 us -> 0.01 us
  transfers between devices with their start and end apart: 17 -> 11, of which waited for: 8 -> 8; matrix products, arithmetic and copies ran while one was open for 2% -> 0% of each run, Pallas kernels for 19% -> 21%
where the time goes in v9:
time: 46.7 us; the launch traced here: 46.5 us
  waiting for transfers between devices  17.3 us (37%)
  Pallas kernels  16.6 us (36%)
  starting transfers between devices  11.8 us (25%)
  between operations  0.73 us (2%)
    ppermute x4, waiting for transfers between devices, per_device(): lax.ppermute(back, 'col', shift(-1))  13.3 us
    pallas_call x2, Pallas kernels, down(): pl.pallas_call(functools.partial(down_kernel, chips_y, tok, own), out_sha...  10.6 us
    ppermute x4, starting transfers between devices, per_device(): lax.ppermute(back, 'col', shift(-1))  7.15 us
    pallas_call x4, Pallas kernels, project(): pl.pallas_call(functools.partial(project_kernel, cycle, hops, [len(parts)...  4.62 us
    ppermute x1, starting transfers between devices, per_device(): lax.ppermute(both[step - 1], 'row', move).astype(jnp.float32)  2.95 us
    ppermute x4, waiting for transfers between devices, per_device(): lax.ppermute(up, 'col', shift(1))  1.5 us
    pallas_call x1, Pallas kernels, settle(): pl.pallas_call(settle_kernel, out_shape=[jax.ShapeDtypeStruct((tok, width...  1.31 us
    ppermute x1, waiting for transfers between devices, per_device(): got = lax.ppermute(give[0], 'row', sibling)  1.29 us
  transfers between devices with their start and end apart: 11, of which 8 were waited for; matrix products, arithmetic and copies ran while one was open for 0% of the time, Pallas kernels for 21%

profile of v9, /device:TPU:0, one launch (start us, length us, event | category | flops | bytes accessed | tf_op | source)
XLA Modules:
  0.0 46.5 jit_solution(4818120577700154281)
XLA Ops:
  0.7 5.6 %down.2 = (bf16[1,128,768]{2,1,0:T(8,128)(2,1)S(1)}, bf16[1,128,768]{2,1,0:T(8,128)(2,1)S(1)}, bf16[8,768,768]{2,1,0:T(8,128)(2,1)S(1)}) custom-call(bf16[512,6144]{1,0:T(8,128)(2,1)} %hidden.2, bf16[6144,768]{1,0:T(8,128)(2,1)} %weight.3), custom_call_target="tpu_custom_call" | custom-call | flops 2415919104 | bytes 12582912 | tf_op jit(solution)/shard_map/down/pallas_call | solution.py:100
  6.3 0.5 %collective-permute-start = (bf16[1,128,768]{2,1,0:T(8,128)(2,1)S(1)}, bf16[1,128,768]{2,1,0:T(8,128)(2,1)S(1)}, u32[]{:S(2)}, u32[]{:S(2)}) collective-permute-start(bf16[1,128,768]{2,1,0:T(8,128)(2,1)S(1)} %get-tuple-element.40), channel_id=1, source_target_pairs={{0,8},{8,0},{16,24},{24,16},{1,9},{9,1},{17,25},{25,17},{2,10},{10... | collective-permute-start | bytes 589832 | tf_op jit(solution)/shard_map/ppermute | solution.py:285
  6.8 1.1 %collective-permute-done = bf16[1,128,768]{2,1,0:T(8,128)(2,1)S(1)} collective-permute-done((bf16[1,128,768]{2,1,0:T(8,128)(2,1)S(1)}, bf16[1,128,768]{2,1,0:T(8,128)(2,1)S(1)}, u32[]{:S(2)}, u32[]{:S(2)}) %collective-permute-start) | collective-permute-done | bytes 196640 | tf_op jit(solution)/shard_map/ppermute | solution.py:285
  7.9 3.0 %collective-permute-start.1 = (bf16[128,768]{1,0:T(8,128)(2,1)S(1)}, bf16[128,768]{1,0:T(8,128)(2,1)S(1)}, u32[]{:S(2)}, u32[]{:S(2)}) collective-permute-start(bf16[128,768]{1,0:T(8,128)(2,1)S(1)} %bitcast.5), channel_id=1, source_target_pairs={{0,16},{8,24},{16,0},{24,8},{1,17},{9,25},{17,1},{25,9},{2,18},{10... | collective-permute-start | bytes 589832 | tf_op jit(solution)/shard_map/ppermute | solution.py:291
  10.9 5.0 %down.3 = (bf16[1,128,768]{2,1,0:T(8,128)(2,1)S(1)}, bf16[1,128,768]{2,1,0:T(8,128)(2,1)S(1)}) custom-call(bf16[512,6144]{1,0:T(8,128)(2,1)} %hidden.2, bf16[8,768,768]{2,1,0:T(8,128)(2,1)S(1)} %get-tuple-element.43.weight), custom_call_target="tpu_custom_call" | custom-call | flops 2415919104 | bytes 3145728 | tf_op jit(solution)/shard_map/down/pallas_call | solution.py:100
  16.0 0.1 collective-permute-done.1
  16.1 1.3 %collective-permute-done.2.got = bf16[128,768]{1,0:T(8,128)(2,1)S(1)} collective-permute-done((bf16[128,768]{1,0:T(8,128)(2,1)S(1)}, bf16[128,768]{1,0:T(8,128)(2,1)S(1)}, u32[]{:S(2)}, u32[]{:S(2)}) %collective-permute-start.2) | collective-permute-done | bytes 196640 | tf_op jit(solution)/shard_map/ppermute | solution.py:293
  17.5 2.0 %collective-permute-start.7 = (bf16[136,768]{1,0:T(8,128)(2,1)S(1)}, bf16[136,768]{1,0:T(8,128)(2,1)S(1)}, u32[]{:S(2)}, u32[]{:S(2)}) collective-permute-start(bf16[136,768]{1,0:T(8,128)(2,1)S(1)} %get-tuple-element.46.piece), channel_id=1, source_target_pairs={{0,2},{1,0},{3,1},{5,3},{7,5},{6,7},{4,6},{2,4},{8,10},{9,8},{11,9... | collective-permute-start | bytes 626696 | tf_op jit(solution)/shard_map/ppermute | solution.py:300
  19.6 1.3 %settle.1 = (bf16[128,768]{1,0:T(8,128)(2,1)}, f32[128,1]{1,0:T(8,128)S(1)}, f32[2,128,1]{2,1,0:T(8,128)S(1)}, f32[144,1536]{1,0:T(8,128)S(1)}) custom-call(bf16[136,768]{1,0:T(8,128)(2,1)S(1)} %get-tuple-element.46.piece, bf16[6144,1536]{1,0:T(8,128)(2,1)S(1)} %copy-done, ...), custom_call_target="tpu_custom_call", output_to_operand_aliasing={{1}: (2, {}), {2}: (3, {}), {3}: (4, {})} | custom-call | flops 339738624 | bytes 196608 | tf_op jit(solution)/shard_map/settle/pallas_call | solution.py:185
  20.9 4.6 %collective-permute-done.7.refs_1_ = bf16[136,768]{1,0:T(8,128)(2,1)S(1)} collective-permute-done((bf16[136,768]{1,0:T(8,128)(2,1)S(1)}, bf16[136,768]{1,0:T(8,128)(2,1)S(1)}, u32[]{:S(2)}, u32[]{:S(2)}) %collective-permute-start.7) | collective-permute-done | bytes 208928 | tf_op jit(solution)/shard_map/ppermute | solution.py:300
  25.5 1.8 %collective-permute-start.8 = (bf16[136,768]{1,0:T(8,128)(2,1)S(1)}, bf16[136,768]{1,0:T(8,128)(2,1)S(1)}, u32[]{:S(2)}, u32[]{:S(2)}) collective-permute-start(bf16[136,768]{1,0:T(8,128)(2,1)S(1)} %collective-permute-done.7.refs_1_), channel_id=1, source_target_pairs={{0,2},{1,0},{3,1},{5,3},{7,5},{6,7},{4,6},{2,4},{8,10},{9,8},{11,9... | collective-permute-start | bytes 626696 | tf_op jit(solution)/shard_map/ppermute | solution.py:300
  27.3 0.2 collective-permute-start.4
  27.5 1.1 %project.4 = (f32[2,128,1]{2,1,0:T(8,128)S(1)}, f32[144,1536]{1,0:T(8,128)S(1)}) custom-call(bf16[136,768]{1,0:T(8,128)(2,1)S(1)} %collective-permute-done.3.refs_0_, bf16[136,768]{1,0:T(8,128)(2,1)S(1)} %collective-permute-done.7.refs_1_, bf16[6144,1536]{1,0:T(8,128)(2,1)S(1)} %copy-done, ...), custom_call_target="tpu_custom_call", output_to_operand_aliasing={{0}: (4, {}), {1}: (5, {})} | custom-call | flops 679477248 | tf_op jit(solution)/shard_map/project/pallas_call | solution.py:254
  28.6 4.0 %collective-permute-done.8.refs_1_ = bf16[136,768]{1,0:T(8,128)(2,1)S(1)} collective-permute-done((bf16[136,768]{1,0:T(8,128)(2,1)S(1)}, bf16[136,768]{1,0:T(8,128)(2,1)S(1)}, u32[]{:S(2)}, u32[]{:S(2)}) %collective-permute-start.8) | collective-permute-done | bytes 208928 | tf_op jit(solution)/shard_map/ppermute | solution.py:300
  32.6 1.7 %collective-permute-start.9 = (bf16[136,768]{1,0:T(8,128)(2,1)S(1)}, bf16[136,768]{1,0:T(8,128)(2,1)S(1)}, u32[]{:S(2)}, u32[]{:S(2)}) collective-permute-start(bf16[136,768]{1,0:T(8,128)(2,1)S(1)} %collective-permute-done.8.refs_1_), channel_id=1, source_target_pairs={{0,2},{1,0},{3,1},{5,3},{7,5},{6,7},{4,6},{2,4},{8,10},{9,8},{11,9... | collective-permute-start | bytes 626696 | tf_op jit(solution)/shard_map/ppermute | solution.py:300
  34.3 0.3 collective-permute-start.5
  34.6 1.1 %project.5 = (f32[2,128,1]{2,1,0:T(8,128)S(1)}, f32[144,1536]{1,0:T(8,128)S(1)}) custom-call(bf16[136,768]{1,0:T(8,128)(2,1)S(1)} %collective-permute-done.4.refs_0_, bf16[136,768]{1,0:T(8,128)(2,1)S(1)} %collective-permute-done.8.refs_1_, bf16[6144,1536]{1,0:T(8,128)(2,1)S(1)} %copy-done, ...), custom_call_target="tpu_custom_call", output_to_operand_aliasing={{0}: (4, {}), {1}: (5, {})} | custom-call | flops 679477248 | tf_op jit(solution)/shard_map/project/pallas_call | solution.py:254
  35.7 3.1 %collective-permute-done.9.refs_1_ = bf16[136,768]{1,0:T(8,128)(2,1)S(1)} collective-permute-done((bf16[136,768]{1,0:T(8,128)(2,1)S(1)}, bf16[136,768]{1,0:T(8,128)(2,1)S(1)}, u32[]{:S(2)}, u32[]{:S(2)}) %collective-permute-start.9) | collective-permute-done | bytes 208928 | tf_op jit(solution)/shard_map/ppermute | solution.py:300
  38.8 1.6 %collective-permute-start.10 = (bf16[72,768]{1,0:T(8,128)(2,1)S(1)}, bf16[72,768]{1,0:T(8,128)(2,1)S(1)}, u32[]{:S(2)}, u32[]{:S(2)}) collective-permute-start(bf16[72,768]{1,0:T(8,128)(2,1)S(1)} %slice.7), channel_id=1, source_target_pairs={{0,2},{1,0},{3,1},{5,3},{7,5},{6,7},{4,6},{2,4},{8,10},{9,8},{11,9... | collective-permute-start | bytes 331784 | tf_op jit(solution)/shard_map/ppermute | solution.py:300
  40.5 0.5 %collective-permute-start.6 = (bf16[64,768]{1,0:T(8,128)(2,1)S(1)}, bf16[64,768]{1,0:T(8,128)(2,1)S(1)}, u32[]{:S(2)}, u32[]{:S(2)}) collective-permute-start(bf16[64,768]{1,0:T(8,128)(2,1)S(1)} %slice.8), channel_id=1, source_target_pairs={{0,1},{1,3},{3,5},{5,7},{7,6},{6,4},{4,2},{2,0},{8,9},{9,11},{11,1... | collective-permute-start | bytes 294920 | tf_op jit(solution)/shard_map/ppermute | solution.py:300
  41.0 1.1 %project.6 = (f32[2,128,1]{2,1,0:T(8,128)S(1)}, f32[144,1536]{1,0:T(8,128)S(1)}) custom-call(bf16[136,768]{1,0:T(8,128)(2,1)S(1)} %collective-permute-done.5.refs_0_, bf16[136,768]{1,0:T(8,128)(2,1)S(1)} %collective-permute-done.9.refs_1_, bf16[6144,1536]{1,0:T(8,128)(2,1)S(1)} %copy-done, ...), custom_call_target="tpu_custom_call", output_to_operand_aliasing={{0}: (4, {}), {1}: (5, {})} | custom-call | flops 679477248 | tf_op jit(solution)/shard_map/project/pallas_call | solution.py:254
  42.1 1.6 %collective-permute-done.10.refs_1_ = bf16[72,768]{1,0:T(8,128)(2,1)S(1)} collective-permute-done((bf16[72,768]{1,0:T(8,128)(2,1)S(1)}, bf16[72,768]{1,0:T(8,128)(2,1)S(1)}, u32[]{:S(2)}, u32[]{:S(2)}) %collective-permute-start.10) | collective-permute-done | bytes 110624 | tf_op jit(solution)/shard_map/ppermute | solution.py:300
  43.6 1.5 %collective-permute-done.6.refs_0_ = bf16[64,768]{1,0:T(8,128)(2,1)S(1)} collective-permute-done((bf16[64,768]{1,0:T(8,128)(2,1)S(1)}, bf16[64,768]{1,0:T(8,128)(2,1)S(1)}, u32[]{:S(2)}, u32[]{:S(2)}) %collective-permute-start.6) | collective-permute-done | bytes 98336 | tf_op jit(solution)/shard_map/ppermute | solution.py:300
  45.1 1.4 %project.7 = bf16[128,1536]{1,0:T(8,128)(2,1)} custom-call(bf16[64,768]{1,0:T(8,128)(2,1)S(1)} %collective-permute-done.6.refs_0_, bf16[72,768]{1,0:T(8,128)(2,1)S(1)} %collective-permute-done.10.refs_1_, bf16[6144,1536]{1,0:T(8,128)(2,1)S(1)} %copy-done, f32[128,1]{1,0:T(8,128)S(1)} %get-tuple-element.73.refs_3_, ...), custom_call_target="tpu_custom_call" | custom-call | flops 339738624 | tf_op jit(solution)/shard_map/project/pallas_call | solution.py:254
  (17 shorter events, 0.3 us)
Async XLA Ops:
  0.6 6.2 %copy-start.2 = (bf16[768]{0:T(1024)(128)(2,1)S(1)}, bf16[768]{0:T(1024)(128)(2,1)}, u32[]{:S(2)}) copy-start(bf16[768]{0:T(1024)(128)(2,1)} %param.8) | copy-start | bytes 4612
  0.6 16.8 %copy-start = (bf16[6144,1536]{1,0:T(8,128)(2,1)S(1)}, bf16[6144,1536]{1,0:T(8,128)(2,1)}, u32[]{:S(2)}) copy-start(bf16[6144,1536]{1,0:T(8,128)(2,1)} %refs_2_.7) | copy-start | bytes 56623108
  6.2 9.8 %copy-start.1 = (bf16[128,768]{1,0:T(8,128)(2,1)S(1)}, bf16[128,768]{1,0:T(8,128)(2,1)}, u32[]{:S(2)}) copy-start(bf16[128,768]{1,0:T(8,128)(2,1)} %param.7) | copy-start | bytes 589828
  6.3 1.6 %collective-permute-start = (bf16[1,128,768]{2,1,0:T(8,128)(2,1)S(1)}, bf16[1,128,768]{2,1,0:T(8,128)(2,1)S(1)}, u32[]{:S(2)}, u32[]{:S(2)}) collective-permute-start(bf16[1,128,768]{2,1,0:T(8,128)(2,1)S(1)} %get-tuple-element.40), channel_id=1, source_target_pairs={{0,8},{8,0},{16,24},{24,16},{1,9},{9,1},{17,25},{25,17},{2,10},{10... | collective-permute-start | bytes 589832 | tf_op jit(solution)/shard_map/ppermute | solution.py:285
  7.9 8.2 %collective-permute-start.1 = (bf16[128,768]{1,0:T(8,128)(2,1)S(1)}, bf16[128,768]{1,0:T(8,128)(2,1)S(1)}, u32[]{:S(2)}, u32[]{:S(2)}) collective-permute-start(bf16[128,768]{1,0:T(8,128)(2,1)S(1)} %bitcast.5), channel_id=1, source_target_pairs={{0,16},{8,24},{16,0},{24,8},{1,17},{9,25},{17,1},{25,9},{2,18},{10... | collective-permute-start | bytes 589832 | tf_op jit(solution)/shard_map/ppermute | solution.py:291
  15.9 1.5 %collective-permute-start.2 = (bf16[128,768]{1,0:T(8,128)(2,1)S(1)}, bf16[128,768]{1,0:T(8,128)(2,1)S(1)}, u32[]{:S(2)}, u32[]{:S(2)}) collective-permute-start(bf16[128,768]{1,0:T(8,128)(2,1)S(1)} %bitcast.4), channel_id=1, source_target_pairs={{0,8},{8,0},{16,24},{24,16},{1,9},{9,1},{17,25},{25,17},{2,10},{10... | collective-permute-start | bytes 589832 | tf_op jit(solution)/shard_map/ppermute | solution.py:293
  17.5 8.0 %collective-permute-start.7 = (bf16[136,768]{1,0:T(8,128)(2,1)S(1)}, bf16[136,768]{1,0:T(8,128)(2,1)S(1)}, u32[]{:S(2)}, u32[]{:S(2)}) collective-permute-start(bf16[136,768]{1,0:T(8,128)(2,1)S(1)} %get-tuple-element.46.piece), channel_id=1, source_target_pairs={{0,2},{1,0},{3,1},{5,3},{7,5},{6,7},{4,6},{2,4},{8,10},{9,8},{11,9... | collective-permute-start | bytes 626696 | tf_op jit(solution)/shard_map/ppermute | solution.py:300
  19.5 7.8 %collective-permute-start.3 = (bf16[136,768]{1,0:T(8,128)(2,1)S(1)}, bf16[136,768]{1,0:T(8,128)(2,1)S(1)}, u32[]{:S(2)}, u32[]{:S(2)}) collective-permute-start(bf16[136,768]{1,0:T(8,128)(2,1)S(1)} %get-tuple-element.46.piece), channel_id=1, source_target_pairs={{0,1},{1,3},{3,5},{5,7},{7,6},{6,4},{4,2},{2,0},{8,9},{9,11},{11,1... | collective-permute-start | bytes 626696 | tf_op jit(solution)/shard_map/ppermute | solution.py:300
  25.5 7.1 %collective-permute-start.8 = (bf16[136,768]{1,0:T(8,128)(2,1)S(1)}, bf16[136,768]{1,0:T(8,128)(2,1)S(1)}, u32[]{:S(2)}, u32[]{:S(2)}) collective-permute-start(bf16[136,768]{1,0:T(8,128)(2,1)S(1)} %collective-permute-done.7.refs_1_), channel_id=1, source_target_pairs={{0,2},{1,0},{3,1},{5,3},{7,5},{6,7},{4,6},{2,4},{8,10},{9,8},{11,9... | collective-permute-start | bytes 626696 | tf_op jit(solution)/shard_map/ppermute | solution.py:300
  27.3 7.0 %collective-permute-start.4 = (bf16[136,768]{1,0:T(8,128)(2,1)S(1)}, bf16[136,768]{1,0:T(8,128)(2,1)S(1)}, u32[]{:S(2)}, u32[]{:S(2)}) collective-permute-start(bf16[136,768]{1,0:T(8,128)(2,1)S(1)} %collective-permute-done.3.refs_0_), channel_id=1, source_target_pairs={{0,1},{1,3},{3,5},{5,7},{7,6},{6,4},{4,2},{2,0},{8,9},{9,11},{11,1... | collective-permute-start | bytes 626696 | tf_op jit(solution)/shard_map/ppermute | solution.py:300
  32.6 6.2 %collective-permute-start.9 = (bf16[136,768]{1,0:T(8,128)(2,1)S(1)}, bf16[136,768]{1,0:T(8,128)(2,1)S(1)}, u32[]{:S(2)}, u32[]{:S(2)}) collective-permute-start(bf16[136,768]{1,0:T(8,128)(2,1)S(1)} %collective-permute-done.8.refs_1_), channel_id=1, source_target_pairs={{0,2},{1,0},{3,1},{5,3},{7,5},{6,7},{4,6},{2,4},{8,10},{9,8},{11,9... | collective-permute-start | bytes 626696 | tf_op jit(solution)/shard_map/ppermute | solution.py:300
  34.3 6.2 %collective-permute-start.5 = (bf16[136,768]{1,0:T(8,128)(2,1)S(1)}, bf16[136,768]{1,0:T(8,128)(2,1)S(1)}, u32[]{:S(2)}, u32[]{:S(2)}) collective-permute-start(bf16[136,768]{1,0:T(8,128)(2,1)S(1)} %collective-permute-done.4.refs_0_), channel_id=1, source_target_pairs={{0,1},{1,3},{3,5},{5,7},{7,6},{6,4},{4,2},{2,0},{8,9},{9,11},{11,1... | collective-permute-start | bytes 626696 | tf_op jit(solution)/shard_map/ppermute | solution.py:300
  38.8 4.8 %collective-permute-start.10 = (bf16[72,768]{1,0:T(8,128)(2,1)S(1)}, bf16[72,768]{1,0:T(8,128)(2,1)S(1)}, u32[]{:S(2)}, u32[]{:S(2)}) collective-permute-start(bf16[72,768]{1,0:T(8,128)(2,1)S(1)} %slice.7), channel_id=1, source_target_pairs={{0,2},{1,0},{3,1},{5,3},{7,5},{6,7},{4,6},{2,4},{8,10},{9,8},{11,9... | collective-permute-start | bytes 331784 | tf_op jit(solution)/shard_map/ppermute | solution.py:300
  40.5 4.7 %collective-permute-start.6 = (bf16[64,768]{1,0:T(8,128)(2,1)S(1)}, bf16[64,768]{1,0:T(8,128)(2,1)S(1)}, u32[]{:S(2)}, u32[]{:S(2)}) collective-permute-start(bf16[64,768]{1,0:T(8,128)(2,1)S(1)} %slice.8), channel_id=1, source_target_pairs={{0,1},{1,3},{3,5},{5,7},{7,6},{6,4},{4,2},{2,0},{8,9},{9,11},{11,1... | collective-permute-start | bytes 294920 | tf_op jit(solution)/shard_map/ppermute | solution.py:300

commit v10 on v9

--- a/solution.py
+++ b/solution.py
@@ -137,17 +137,12 @@
         total_ref[:, span] = jnp.dot(lhs[...], weight[pl.ds(start, width), span], preferred_element_type=jnp.float32)
 
 
-def merge_kernel(others, keep, got, gain, weight, piece, shift, sums, total, lhs):
+def merge_kernel(others, keep, got, gain, piece):
     tok, width = others.shape
     own = keep[...].astype(jnp.float32) + got[...].astype(jnp.float32)
-    value = (others[...] + own).astype(piece.dtype)
-    row = gain[...].astype(jnp.float32)
-    piece[0:tok, :] = value
-    piece[tok : tok + GAIN, :] = jnp.broadcast_to(row, (GAIN, width)).astype(piece.dtype)
-
-    @pl.when(lax.axis_index("row") % CORES == 1)
-    def _():
-        begin(value.astype(jnp.float32), row, weight, lhs, shift, sums, total)
+    piece[0:tok, :] = (others[...] + own).astype(piece.dtype)
+    rows = jnp.broadcast_to(gain[...].astype(jnp.float32), (GAIN, width))
+    piece[tok : tok + GAIN, :] = rows.astype(piece.dtype)
 
 
 def state_of(tok, columns):
@@ -155,56 +150,46 @@
     return [pltpu.VMEM(shape, jnp.float32) for shape in shapes]
 
 
-def merge(others, keep, got, gain, weight):
+def merge(others, keep, got, gain):
     tok, width = others.shape
-    out_shape = [pltpu.VMEM((tok + GAIN, width), jnp.bfloat16), *state_of(tok, weight.shape[1])]
-    piece, *state = pl.pallas_call(
+    return pl.pallas_call(
         merge_kernel,
-        out_shape=out_shape,
-        in_specs=[VMEM] * 5,
-        out_specs=[VMEM] * 4,
-        scratch_shapes=[pltpu.VMEM((tok + EXTRA, width), jnp.bfloat16)],
-        compiler_params=pltpu.CompilerParams(vmem_limit_bytes=12 * MIB),
+        out_shape=pltpu.VMEM((tok + GAIN, width), jnp.bfloat16),
+        in_specs=[VMEM] * 4,
+        out_specs=VMEM,
+        compiler_params=pltpu.CompilerParams(vmem_limit_bytes=8 * MIB),
         name="merge",
-    )(others, keep, got, gain, pltpu.with_memory_space_constraint(weight, pltpu.VMEM))
-    return piece, state
-
-
-def settle_kernel(piece, weight, _, __, ___, stream, shift, sums, total, lhs):
+    )(others, keep, got, gain)
+
+
+def settle_kernel(piece, weight, stream, shift, sums, total, lhs):
     tok = stream.shape[0]
     stream[...] = piece[0:tok, :]
-
-    @pl.when(lax.axis_index("row") % CORES == 0)
-    def _():
-        row = piece[tok : tok + GAIN, :].astype(jnp.float32)[0:1]
-        begin(piece[0:tok, :].astype(jnp.float32), row, weight, lhs, shift, sums, total)
-
-
-def settle(piece, weight, state):
+    row = piece[tok : tok + GAIN, :].astype(jnp.float32)[0:1]
+    begin(piece[0:tok, :].astype(jnp.float32), row, weight, lhs, shift, sums, total)
+
+
+def settle(piece, weight):
     tok, width = piece.shape[0] - GAIN, piece.shape[1]
     stream, *state = pl.pallas_call(
         settle_kernel,
         out_shape=[jax.ShapeDtypeStruct((tok, width), jnp.bfloat16), *state_of(tok, weight.shape[1])],
-        in_specs=[VMEM] * 5,
+        in_specs=[VMEM] * 2,
         out_specs=[VMEM] * 4,
         scratch_shapes=[pltpu.VMEM((tok + EXTRA, width), jnp.bfloat16)],
-        input_output_aliases={2: 1, 3: 2, 4: 3},
         compiler_params=pltpu.CompilerParams(vmem_limit_bytes=12 * MIB),
         cost_estimate=pl.CostEstimate(
             flops=2 * (tok + EXTRA) * width * weight.shape[1], bytes_accessed=2 * tok * width, transcendentals=0
         ),
         name="settle",
-    )(piece, pltpu.with_memory_space_constraint(weight, pltpu.VMEM), *state)
+    )(piece, pltpu.with_memory_space_constraint(weight, pltpu.VMEM))
     return stream, state
 
 
-def project_kernel(cycle, hops, shapes, last, *refs):
+def project_kernel(cycle, hops, last, *refs):
     count = len(cycle)
-    refs = list(refs)
-    take = lambda n: [refs.pop(0) for _ in range(n)]
-    pieces = [take(n) for n in shapes]
-    weight, shift_in, sums_in, total_in = take(4)
-    outs, lhs = refs[:-1], refs[-1]
+    pieces, refs = refs[: len(hops)], refs[len(hops) :]
+    weight, shift_in, sums_in, total_in, *outs, lhs = refs
     tok = shift_in.shape[0]
     width = lhs.shape[2]
     columns = weight.shape[1]
@@ -212,10 +197,11 @@
 
     me = lax.axis_index("col")
     place = pick(me, [cycle.index(c) for c in range(count)])
-    ids = [pick(lax.rem(place + hop + count, count), cycle) for hop in hops]
+    turn = 2 * (lax.axis_index("row") % CORES) - 1
+    ids = [pick(lax.rem(place + turn * hop + count, count), cycle) for hop in hops]
     one, two = sums_in[0], sums_in[1]
-    for i, parts in enumerate(pieces):
-        whole = jnp.concatenate([part[...].astype(jnp.float32) for part in parts], axis=0)
+    for i, piece in enumerate(pieces):
+        whole = piece[...].astype(jnp.float32)
         row = whole[tok : tok + 1]
         dev = whole[0:tok] - shift_in[...]
         one = one + jnp.sum(dev, axis=1, keepdims=True)
@@ -243,16 +229,15 @@
 
 
 def project(pieces, hops, weight, state, cycle, last):
-    tok, width = state[0].shape[0], pieces[0][0].shape[1]
+    tok, width = state[0].shape[0], pieces[0].shape[1]
     columns = weight.shape[1]
-    flat = [part for parts in pieces for part in parts]
-    base = len(flat) + 1
+    base = len(pieces) + 1
     if last:
         out_shape, aliases = [jax.ShapeDtypeStruct((tok, columns), jnp.bfloat16)], {}
     else:
         out_shape, aliases = state_of(tok, columns)[1:], {base + 1: 0, base + 2: 1}
     got = pl.pallas_call(
-        functools.partial(project_kernel, cycle, hops, [len(parts) for parts in pieces], last),
+        functools.partial(project_kernel, cycle, hops, last),
         out_shape=out_shape,
         in_specs=[VMEM] * (base + 3),
         out_specs=[VMEM] * len(out_shape),
@@ -263,7 +248,7 @@
             flops=2 * len(hops) * (tok + EXTRA) * width * columns, bytes_accessed=0, transcendentals=0
         ),
         name="project",
-    )(*flat, pltpu.with_memory_space_constraint(weight, pltpu.VMEM), *state)
+    )(*pieces, pltpu.with_memory_space_constraint(weight, pltpu.VMEM), *state)
     return got[0] if last else [state[0], *got]
 
 
@@ -276,7 +261,11 @@
     sibling = [(r, r ^ 1) for r in range(rows)]
 
     def shift(hop):
-        return [(cycle[i], cycle[(i + hop) % cols]) for i in range(cols)]
+        pairs = []
+        for r in range(rows):
+            turn = hop * (2 * (r % CORES) - 1)
+            pairs += [(r * cols + cycle[i], r * cols + cycle[(i + turn) % cols]) for i in range(cols)]
+        return pairs
 
     def per_device(hidden, down_weight, residual, gain, qk_weight):
         tok = residual.shape[0]
@@ -291,20 +280,23 @@
             others = others + lax.ppermute(both[step - 1], "row", move).astype(jnp.float32)
         give, keep = down(hidden, down_weight, tok, chips_y, True)
         got = lax.ppermute(give[0], "row", sibling)
-        piece, state = merge(others, keep[0], got, gain[None, :], qk_weight)
-
-        up, back, pieces = piece, piece, None
-        for step in range(1, half + 1):
-            if step == half:
-                up, back = up[: tok // 2], back[tok // 2 :]
-            up, back = lax.ppermute(up, "col", shift(1)), lax.ppermute(back, "col", shift(-1))
-            if step == 1:
-                stream, state = settle(piece, qk_weight, state)
-            else:
-                state = project(pieces, [1 - step, step - 1], qk_weight, state, cycle, False)
-            back, state = lax.optimization_barrier((back, state))
-            pieces = [[up], [back]]
-        return stream, project([[up, back]], [half], qk_weight, state, cycle, True)
+        piece = merge(others, keep[0], got, gain[None, :])
+
+        first = lax.ppermute(piece, ("row", "col"), shift(1))
+        stream, state = settle(piece, qk_weight)
+        piece, state = lax.optimization_barrier((piece, state))
+        second, late = lax.ppermute(piece, ("row", "col"), shift(-1)), []
+        for step in range(1, half):
+            onward = lax.ppermute(first, ("row", "col"), shift(1))
+            pieces, hops = [first, *late], [-step, step - 1][: 1 + len(late)]
+            state = project(pieces, hops, qk_weight, state, cycle, False)
+            late, first = [second], onward
+            if step + 1 < half:
+                second, state = lax.optimization_barrier((second, state))
+                late = [second]
+                second = lax.ppermute(second, ("row", "col"), shift(-1))
+        state = project(late, [half - 1], qk_weight, state, cycle, False)
+        return stream, project([first], [half], qk_weight, state, cycle, True)
 
     placed = (P(None, "row"), P("row", "col"), P("row", "col"), P("col"), P(None, "col"))
     return jax.shard_map(

time: 46.7 us -> 47.3 us (1.013)
  waiting for transfers between devices: 17.3 us -> 17.9 us
    ppermute x8 -> x7, waiting for transfers between devices: 14.8 us -> 15.5 us  [the longest x3 10.9 us: per_device(): onward = lax.ppermute(first, ('row', 'col'), shift(1))]
    pallas_call x5 -> x6, Pallas kernels: 4.69 us -> 4.88 us  [the longest x5 4.81 us: project(): pl.pallas_call(functools.partial(project_kernel, cycle, hops, last), out_...]
    ppermute x8 -> x7, starting transfers between devices: 8.26 us -> 8.14 us  [the longest x3 5.98 us: per_device(): onward = lax.ppermute(first, ('row', 'col'), shift(1))]
  transfers between devices with their start and end apart: 11 -> 10, of which waited for: 8 -> 9; matrix products, arithmetic and copies ran while one was open for 0% -> 0% of each run, Pallas kernels for 21% -> 20%
where the time goes in v10:
time: 47.3 us; the launch traced here: 47.1 us
  waiting for transfers between devices  17.9 us (38%)
  Pallas kernels  16.7 us (35%)
  starting transfers between devices  11.7 us (25%)
  between operations  0.75 us (2%)
    ppermute x3, waiting for transfers between devices, per_device(): onward = lax.ppermute(first, ('row', 'col'), shift(1))  10.9 us
    pallas_call x2, Pallas kernels, down(): pl.pallas_call(functools.partial(down_kernel, chips_y, tok, own), out_sha...  10.6 us
    ppermute x3, starting transfers between devices, per_device(): onward = lax.ppermute(first, ('row', 'col'), shift(1))  5.98 us
    pallas_call x5, Pallas kernels, project(): pl.pallas_call(functools.partial(project_kernel, cycle, hops, last), out_...  4.81 us
    ppermute x1, waiting for transfers between devices, per_device(): first = lax.ppermute(piece, ('row', 'col'), shift(1))  4 us
    ppermute x1, starting transfers between devices, per_device(): lax.ppermute(both[step - 1], 'row', move).astype(jnp.float32)  2.95 us
    ppermute x1, starting transfers between devices, per_device(): first = lax.ppermute(piece, ('row', 'col'), shift(1))  2.01 us
    ppermute x1, waiting for transfers between devices, per_device(): got = lax.ppermute(give[0], 'row', sibling)  1.29 us
  transfers between devices with their start and end apart: 10, of which 9 were waited for; matrix products, arithmetic and copies ran while one was open for 0% of the time, Pallas kernels for 20%

profile of v10, /device:TPU:0, one launch (start us, length us, event | category | flops | bytes accessed | tf_op | source)
XLA Modules:
  0.0 47.1 jit_solution(4032078342063594958)
XLA Ops:
  0.7 5.6 %down.2 = (bf16[1,128,768]{2,1,0:T(8,128)(2,1)S(1)}, bf16[1,128,768]{2,1,0:T(8,128)(2,1)S(1)}, bf16[8,768,768]{2,1,0:T(8,128)(2,1)S(1)}) custom-call(bf16[512,6144]{1,0:T(8,128)(2,1)} %hidden.2, bf16[6144,768]{1,0:T(8,128)(2,1)} %weight.2), custom_call_target="tpu_custom_call" | custom-call | flops 2415919104 | bytes 12582912 | tf_op jit(solution)/shard_map/down/pallas_call | solution.py:100
  6.3 0.5 %collective-permute-start = (bf16[1,128,768]{2,1,0:T(8,128)(2,1)S(1)}, bf16[1,128,768]{2,1,0:T(8,128)(2,1)S(1)}, u32[]{:S(2)}, u32[]{:S(2)}) collective-permute-start(bf16[1,128,768]{2,1,0:T(8,128)(2,1)S(1)} %get-tuple-element.34), channel_id=1, source_target_pairs={{0,8},{8,0},{16,24},{24,16},{1,9},{9,1},{17,25},{25,17},{2,10},{10... | collective-permute-start | bytes 589832 | tf_op jit(solution)/shard_map/ppermute | solution.py:274
  6.8 1.1 %collective-permute-done = bf16[1,128,768]{2,1,0:T(8,128)(2,1)S(1)} collective-permute-done((bf16[1,128,768]{2,1,0:T(8,128)(2,1)S(1)}, bf16[1,128,768]{2,1,0:T(8,128)(2,1)S(1)}, u32[]{:S(2)}, u32[]{:S(2)}) %collective-permute-start) | collective-permute-done | bytes 196640 | tf_op jit(solution)/shard_map/ppermute | solution.py:274
  7.9 3.0 %collective-permute-start.1 = (bf16[128,768]{1,0:T(8,128)(2,1)S(1)}, bf16[128,768]{1,0:T(8,128)(2,1)S(1)}, u32[]{:S(2)}, u32[]{:S(2)}) collective-permute-start(bf16[128,768]{1,0:T(8,128)(2,1)S(1)} %bitcast.5), channel_id=1, source_target_pairs={{0,16},{8,24},{16,0},{24,8},{1,17},{9,25},{17,1},{25,9},{2,18},{10... | collective-permute-start | bytes 589832 | tf_op jit(solution)/shard_map/ppermute | solution.py:280
  10.9 5.0 %down.3 = (bf16[1,128,768]{2,1,0:T(8,128)(2,1)S(1)}, bf16[1,128,768]{2,1,0:T(8,128)(2,1)S(1)}) custom-call(bf16[512,6144]{1,0:T(8,128)(2,1)} %hidden.2, bf16[8,768,768]{2,1,0:T(8,128)(2,1)S(1)} %get-tuple-element.37.weight), custom_call_target="tpu_custom_call" | custom-call | flops 2415919104 | bytes 3145728 | tf_op jit(solution)/shard_map/down/pallas_call | solution.py:100
  16.0 0.1 collective-permute-done.1
  16.1 1.3 %collective-permute-done.2.got = bf16[128,768]{1,0:T(8,128)(2,1)S(1)} collective-permute-done((bf16[128,768]{1,0:T(8,128)(2,1)S(1)}, bf16[128,768]{1,0:T(8,128)(2,1)S(1)}, u32[]{:S(2)}, u32[]{:S(2)}) %collective-permute-start.2) | collective-permute-done | bytes 196640 | tf_op jit(solution)/shard_map/ppermute | solution.py:282
  17.5 2.0 %collective-permute-start.3 = (bf16[136,768]{1,0:T(8,128)(2,1)S(1)}, bf16[136,768]{1,0:T(8,128)(2,1)S(1)}, u32[]{:S(2)}, u32[]{:S(2)}) collective-permute-start(bf16[136,768]{1,0:T(8,128)(2,1)S(1)} %merge.1.piece), channel_id=1, source_target_pairs={{0,2},{1,0},{3,1},{5,3},{7,5},{6,7},{4,6},{2,4},{8,9},{9,11},{11,1... | collective-permute-start | bytes 626696 | tf_op jit(solution)/shard_map/ppermute | solution.py:285
  19.5 1.2 %settle.1 = (bf16[128,768]{1,0:T(8,128)(2,1)}, f32[128,1]{1,0:T(8,128)S(1)}, f32[2,128,1]{2,1,0:T(8,128)S(1)}, f32[144,1536]{1,0:T(8,128)S(1)}) custom-call(bf16[136,768]{1,0:T(8,128)(2,1)S(1)} %merge.1.piece, bf16[6144,1536]{1,0:T(8,128)(2,1)S(1)} %copy-done), custom_call_target="tpu_custom_call" | custom-call | flops 339738624 | bytes 196608 | tf_op jit(solution)/shard_map/settle/pallas_call | solution.py:174
  20.7 0.1 collective-permute-start.7
  20.7 4.0 %collective-permute-done.3.refs_0_ = bf16[136,768]{1,0:T(8,128)(2,1)S(1)} collective-permute-done((bf16[136,768]{1,0:T(8,128)(2,1)S(1)}, bf16[136,768]{1,0:T(8,128)(2,1)S(1)}, u32[]{:S(2)}, u32[]{:S(2)}) %collective-permute-start.3) | collective-permute-done | bytes 208928 | tf_op jit(solution)/shard_map/ppermute | solution.py:285
  24.7 2.5 %collective-permute-start.4 = (bf16[136,768]{1,0:T(8,128)(2,1)S(1)}, bf16[136,768]{1,0:T(8,128)(2,1)S(1)}, u32[]{:S(2)}, u32[]{:S(2)}) collective-permute-start(bf16[136,768]{1,0:T(8,128)(2,1)S(1)} %collective-permute-done.3.refs_0_), channel_id=1, source_target_pairs={{0,2},{1,0},{3,1},{5,3},{7,5},{6,7},{4,6},{2,4},{8,9},{9,11},{11,1... | collective-permute-start | bytes 626696 | tf_op jit(solution)/shard_map/ppermute | solution.py:290
  27.2 0.6 %project.5 = (f32[2,128,1]{2,1,0:T(8,128)S(1)}, f32[144,1536]{1,0:T(8,128)S(1)}) custom-call(bf16[136,768]{1,0:T(8,128)(2,1)S(1)} %collective-permute-done.3.refs_0_, bf16[6144,1536]{1,0:T(8,128)(2,1)S(1)} %copy-done, f32[128,1]{1,0:T(8,128)S(1)} %get-tuple-element.56.refs_2_.refs_3_, ...), custom_call_target="tpu_custom_call", output_to_operand_aliasing={{0}: (3, {}), {1}: (4, {})} | custom-call | flops 339738624 | tf_op jit(solution)/shard_map/project/pallas_call | solution.py:239
  28.0 4.8 %collective-permute-done.4.refs_0_ = bf16[136,768]{1,0:T(8,128)(2,1)S(1)} collective-permute-done((bf16[136,768]{1,0:T(8,128)(2,1)S(1)}, bf16[136,768]{1,0:T(8,128)(2,1)S(1)}, u32[]{:S(2)}, u32[]{:S(2)}) %collective-permute-start.4) | collective-permute-done | bytes 208928 | tf_op jit(solution)/shard_map/ppermute | solution.py:290
  32.8 2.0 %collective-permute-start.5 = (bf16[136,768]{1,0:T(8,128)(2,1)S(1)}, bf16[136,768]{1,0:T(8,128)(2,1)S(1)}, u32[]{:S(2)}, u32[]{:S(2)}) collective-permute-start(bf16[136,768]{1,0:T(8,128)(2,1)S(1)} %collective-permute-done.4.refs_0_), channel_id=1, source_target_pairs={{0,2},{1,0},{3,1},{5,3},{7,5},{6,7},{4,6},{2,4},{8,9},{9,11},{11,1... | collective-permute-start | bytes 626696 | tf_op jit(solution)/shard_map/ppermute | solution.py:290
  34.7 1.1 %project.6 = (f32[2,128,1]{2,1,0:T(8,128)S(1)}, f32[144,1536]{1,0:T(8,128)S(1)}) custom-call(bf16[136,768]{1,0:T(8,128)(2,1)S(1)} %collective-permute-done.4.refs_0_, bf16[136,768]{1,0:T(8,128)(2,1)S(1)} %collective-permute-done.7.refs_1_, bf16[6144,1536]{1,0:T(8,128)(2,1)S(1)} %copy-done, ...), custom_call_target="tpu_custom_call", output_to_operand_aliasing={{0}: (4, {}), {1}: (5, {})} | custom-call | flops 679477248 | tf_op jit(solution)/shard_map/project/pallas_call | solution.py:239
  35.8 0.1 collective-permute-done.8.refs_1_
  35.9 4.0 %collective-permute-done.5.refs_0_ = bf16[136,768]{1,0:T(8,128)(2,1)S(1)} collective-permute-done((bf16[136,768]{1,0:T(8,128)(2,1)S(1)}, bf16[136,768]{1,0:T(8,128)(2,1)S(1)}, u32[]{:S(2)}, u32[]{:S(2)}) %collective-permute-start.5) | collective-permute-done | bytes 208928 | tf_op jit(solution)/shard_map/ppermute | solution.py:290
  39.9 1.5 %collective-permute-start.6 = (bf16[136,768]{1,0:T(8,128)(2,1)S(1)}, bf16[136,768]{1,0:T(8,128)(2,1)S(1)}, u32[]{:S(2)}, u32[]{:S(2)}) collective-permute-start(bf16[136,768]{1,0:T(8,128)(2,1)S(1)} %collective-permute-done.5.refs_0_), channel_id=1, source_target_pairs={{0,2},{1,0},{3,1},{5,3},{7,5},{6,7},{4,6},{2,4},{8,9},{9,11},{11,1... | collective-permute-start | bytes 626696 | tf_op jit(solution)/shard_map/ppermute | solution.py:290
  41.4 1.1 %project.7 = (f32[2,128,1]{2,1,0:T(8,128)S(1)}, f32[144,1536]{1,0:T(8,128)S(1)}) custom-call(bf16[136,768]{1,0:T(8,128)(2,1)S(1)} %collective-permute-done.5.refs_0_, bf16[136,768]{1,0:T(8,128)(2,1)S(1)} %collective-permute-done.8.refs_1_, bf16[6144,1536]{1,0:T(8,128)(2,1)S(1)} %copy-done, ...), custom_call_target="tpu_custom_call", output_to_operand_aliasing={{0}: (4, {}), {1}: (5, {})} | custom-call | flops 679477248 | tf_op jit(solution)/shard_map/project/pallas_call | solution.py:239
  42.5 0.5 %collective-permute-done.9.refs_0_ = bf16[136,768]{1,0:T(8,128)(2,1)S(1)} collective-permute-done((bf16[136,768]{1,0:T(8,128)(2,1)S(1)}, bf16[136,768]{1,0:T(8,128)(2,1)S(1)}, u32[]{:S(2)}, u32[]{:S(2)}) %collective-permute-start.9) | collective-permute-done | bytes 208928 | tf_op jit(solution)/shard_map/ppermute | solution.py:297
  43.0 0.6 %project.8 = (f32[2,128,1]{2,1,0:T(8,128)S(1)}, f32[144,1536]{1,0:T(8,128)S(1)}) custom-call(bf16[136,768]{1,0:T(8,128)(2,1)S(1)} %collective-permute-done.9.refs_0_, bf16[6144,1536]{1,0:T(8,128)(2,1)S(1)} %copy-done, f32[128,1]{1,0:T(8,128)S(1)} %get-tuple-element.56.refs_2_.refs_3_, ...), custom_call_target="tpu_custom_call", output_to_operand_aliasing={{0}: (3, {}), {1}: (4, {})} | custom-call | flops 339738624 | tf_op jit(solution)/shard_map/project/pallas_call | solution.py:239
  43.6 2.1 %collective-permute-done.6.refs_0_ = bf16[136,768]{1,0:T(8,128)(2,1)S(1)} collective-permute-done((bf16[136,768]{1,0:T(8,128)(2,1)S(1)}, bf16[136,768]{1,0:T(8,128)(2,1)S(1)}, u32[]{:S(2)}, u32[]{:S(2)}) %collective-permute-start.6) | collective-permute-done | bytes 208928 | tf_op jit(solution)/shard_map/ppermute | solution.py:290
  45.7 1.4 %project.9 = bf16[128,1536]{1,0:T(8,128)(2,1)} custom-call(bf16[136,768]{1,0:T(8,128)(2,1)S(1)} %collective-permute-done.6.refs_0_, bf16[6144,1536]{1,0:T(8,128)(2,1)S(1)} %copy-done, f32[128,1]{1,0:T(8,128)S(1)} %get-tuple-element.56.refs_2_.refs_3_, f32[2,128,1]{2,1,0:T(8,128)S(1)} %get-tuple-element.62.refs_3_, f32[144,1536]{1,0:T(8,128)S(1)} %get-tuple-element.63.refs_4_), custom_call_target="tpu_custom_call" | custom-call | flops 339738624 | tf_op jit(solution)/shard_map/project/pallas_call | solution.py:239
  (14 shorter events, 0.3 us)
Async XLA Ops:
  0.6 6.2 %copy-start.2 = (bf16[768]{0:T(1024)(128)(2,1)S(1)}, bf16[768]{0:T(1024)(128)(2,1)}, u32[]{:S(2)}) copy-start(bf16[768]{0:T(1024)(128)(2,1)} %param.8) | copy-start | bytes 4612
  0.6 18.8 %copy-start = (bf16[6144,1536]{1,0:T(8,128)(2,1)S(1)}, bf16[6144,1536]{1,0:T(8,128)(2,1)}, u32[]{:S(2)}) copy-start(bf16[6144,1536]{1,0:T(8,128)(2,1)} %refs_1_.5) | copy-start | bytes 56623108
  6.2 9.8 %copy-start.1 = (bf16[128,768]{1,0:T(8,128)(2,1)S(1)}, bf16[128,768]{1,0:T(8,128)(2,1)}, u32[]{:S(2)}) copy-start(bf16[128,768]{1,0:T(8,128)(2,1)} %param.7) | copy-start | bytes 589828
  6.3 1.6 %collective-permute-start = (bf16[1,128,768]{2,1,0:T(8,128)(2,1)S(1)}, bf16[1,128,768]{2,1,0:T(8,128)(2,1)S(1)}, u32[]{:S(2)}, u32[]{:S(2)}) collective-permute-start(bf16[1,128,768]{2,1,0:T(8,128)(2,1)S(1)} %get-tuple-element.34), channel_id=1, source_target_pairs={{0,8},{8,0},{16,24},{24,16},{1,9},{9,1},{17,25},{25,17},{2,10},{10... | collective-permute-start | bytes 589832 | tf_op jit(solution)/shard_map/ppermute | solution.py:274
  7.9 8.2 %collective-permute-start.1 = (bf16[128,768]{1,0:T(8,128)(2,1)S(1)}, bf16[128,768]{1,0:T(8,128)(2,1)S(1)}, u32[]{:S(2)}, u32[]{:S(2)}) collective-permute-start(bf16[128,768]{1,0:T(8,128)(2,1)S(1)} %bitcast.5), channel_id=1, source_target_pairs={{0,16},{8,24},{16,0},{24,8},{1,17},{9,25},{17,1},{25,9},{2,18},{10... | collective-permute-start | bytes 589832 | tf_op jit(solution)/shard_map/ppermute | solution.py:280
  15.9 1.5 %collective-permute-start.2 = (bf16[128,768]{1,0:T(8,128)(2,1)S(1)}, bf16[128,768]{1,0:T(8,128)(2,1)S(1)}, u32[]{:S(2)}, u32[]{:S(2)}) collective-permute-start(bf16[128,768]{1,0:T(8,128)(2,1)S(1)} %bitcast.4), channel_id=1, source_target_pairs={{0,8},{8,0},{16,24},{24,16},{1,9},{9,1},{17,25},{25,17},{2,10},{10... | collective-permute-start | bytes 589832 | tf_op jit(solution)/shard_map/ppermute | solution.py:282
  17.5 7.3 %collective-permute-start.3 = (bf16[136,768]{1,0:T(8,128)(2,1)S(1)}, bf16[136,768]{1,0:T(8,128)(2,1)S(1)}, u32[]{:S(2)}, u32[]{:S(2)}) collective-permute-start(bf16[136,768]{1,0:T(8,128)(2,1)S(1)} %merge.1.piece), channel_id=1, source_target_pairs={{0,2},{1,0},{3,1},{5,3},{7,5},{6,7},{4,6},{2,4},{8,9},{9,11},{11,1... | collective-permute-start | bytes 626696 | tf_op jit(solution)/shard_map/ppermute | solution.py:285
  20.7 7.2 %collective-permute-start.7 = (bf16[136,768]{1,0:T(8,128)(2,1)S(1)}, bf16[136,768]{1,0:T(8,128)(2,1)S(1)}, u32[]{:S(2)}, u32[]{:S(2)}) collective-permute-start(bf16[136,768]{1,0:T(8,128)(2,1)S(1)} %merge.1.piece), channel_id=1, source_target_pairs={{0,1},{1,3},{3,5},{5,7},{7,6},{6,4},{4,2},{2,0},{8,10},{9,8},{11,9... | collective-permute-start | bytes 626696 | tf_op jit(solution)/shard_map/ppermute | solution.py:288
  24.7 8.0 %collective-permute-start.4 = (bf16[136,768]{1,0:T(8,128)(2,1)S(1)}, bf16[136,768]{1,0:T(8,128)(2,1)S(1)}, u32[]{:S(2)}, u32[]{:S(2)}) collective-permute-start(bf16[136,768]{1,0:T(8,128)(2,1)S(1)} %collective-permute-done.3.refs_0_), channel_id=1, source_target_pairs={{0,2},{1,0},{3,1},{5,3},{7,5},{6,7},{4,6},{2,4},{8,9},{9,11},{11,1... | collective-permute-start | bytes 626696 | tf_op jit(solution)/shard_map/ppermute | solution.py:290
  27.9 8.0 %collective-permute-start.8 = (bf16[136,768]{1,0:T(8,128)(2,1)S(1)}, bf16[136,768]{1,0:T(8,128)(2,1)S(1)}, u32[]{:S(2)}, u32[]{:S(2)}) collective-permute-start(bf16[136,768]{1,0:T(8,128)(2,1)S(1)} %collective-permute-done.7.refs_1_), channel_id=1, source_target_pairs={{0,1},{1,3},{3,5},{5,7},{7,6},{6,4},{4,2},{2,0},{8,10},{9,8},{11,9... | collective-permute-start | bytes 626696 | tf_op jit(solution)/shard_map/ppermute | solution.py:297
  32.8 7.2 %collective-permute-start.5 = (bf16[136,768]{1,0:T(8,128)(2,1)S(1)}, bf16[136,768]{1,0:T(8,128)(2,1)S(1)}, u32[]{:S(2)}, u32[]{:S(2)}) collective-permute-start(bf16[136,768]{1,0:T(8,128)(2,1)S(1)} %collective-permute-done.4.refs_0_), channel_id=1, source_target_pairs={{0,2},{1,0},{3,1},{5,3},{7,5},{6,7},{4,6},{2,4},{8,9},{9,11},{11,1... | collective-permute-start | bytes 626696 | tf_op jit(solution)/shard_map/ppermute | solution.py:290
  35.9 7.1 %collective-permute-start.9 = (bf16[136,768]{1,0:T(8,128)(2,1)S(1)}, bf16[136,768]{1,0:T(8,128)(2,1)S(1)}, u32[]{:S(2)}, u32[]{:S(2)}) collective-permute-start(bf16[136,768]{1,0:T(8,128)(2,1)S(1)} %collective-permute-done.8.refs_1_), channel_id=1, source_target_pairs={{0,1},{1,3},{3,5},{5,7},{7,6},{6,4},{4,2},{2,0},{8,10},{9,8},{11,9... | collective-permute-start | bytes 626696 | tf_op jit(solution)/shard_map/ppermute | solution.py:297
  39.9 5.8 %collective-permute-start.6 = (bf16[136,768]{1,0:T(8,128)(2,1)S(1)}, bf16[136,768]{1,0:T(8,128)(2,1)S(1)}, u32[]{:S(2)}, u32[]{:S(2)}) collective-permute-start(bf16[136,768]{1,0:T(8,128)(2,1)S(1)} %collective-permute-done.5.refs_0_), channel_id=1, source_target_pairs={{0,2},{1,0},{3,1},{5,3},{7,5},{6,7},{4,6},{2,4},{8,9},{9,11},{11,1... | collective-permute-start | bytes 626696 | tf_op jit(solution)/shard_map/ppermute | solution.py:290

commit v11 on v8

--- a/solution.py
+++ b/solution.py
@@ -43,44 +43,44 @@
     return fits[-1] if fits else size
 
 
-def down_kernel(chips_y, tok, own, hidden, weight, *refs):
+def down_kernel(chips_y, tok, parts, own, hidden, weight, *refs):
     if own:
         (give, keep), held = refs[:2], weight
     else:
         give, keep, held = refs[:3]
     h_buf, total, sems = refs[-3:]
-    parts, depth, _ = held.shape
+    depth = held.shape[0] // parts
     me = lax.axis_index("row")
     chip, core = me // CORES, me % CORES
     chips = [0] if own else list(range(1, chips_y))
     block = CORES * tok
 
+    def span(k):
+        return pl.ds(pl.multiple_of(k * depth, depth), depth)
+
     def copies(k):
-        span = pl.ds(pl.multiple_of(k * depth, depth), depth)
         for i, step in enumerate(chips):
             start = pl.multiple_of(lax.rem(chip + step, chips_y) * block, block)
             yield pltpu.make_async_copy(
-                hidden.at[pl.ds(start, block), span], h_buf.at[k, pl.ds(i * block, block)], sems.at[1 + i, k]
+                hidden.at[pl.ds(start, block), span(k)], h_buf.at[k, pl.ds(i * block, block)], sems.at[1 + i, k]
             )
         if not own:
-            yield pltpu.make_async_copy(weight.at[span, :], held.at[k], sems.at[0, k])
+            yield pltpu.make_async_copy(weight.at[span(k), :], held.at[span(k), :], sems.at[0, k])
 
     for k in range(parts):
         for copy in copies(k):
             copy.start(priority=1)
-    width = held.shape[2]
-    strip = cut(width, 256)
-
-    def add(k, first):
+    for copy in copies(0):
+        copy.wait()
+    total[...] = jnp.dot(h_buf[0], held[span(0), :], preferred_element_type=jnp.float32)
+
+    def body(k, _):
         for copy in copies(k):
             copy.wait()
-        for n in range(0, width, strip):
-            span = pl.ds(n, strip)
-            product = jnp.dot(h_buf[k], held[k, :, span], preferred_element_type=jnp.float32)
-            total[:, span] = product if first else total[:, span] + product
-
-    add(0, True)
-    lax.fori_loop(1, parts, lambda k, _: add(k, False), None)
+        total[...] += jnp.dot(h_buf[k], held[span(k), :], preferred_element_type=jnp.float32)
+        return _
+
+    lax.fori_loop(1, parts, body, 0)
     for i in range(len(chips)):
         for out, which in ((give, 1 - core), (keep, core)):
             start = pl.multiple_of((i * CORES + which) * tok, tok)
@@ -88,19 +88,15 @@
 
 
 def down(hidden, weight, tok, chips_y, own):
-    inner = hidden.shape[1]
-    if own:
-        parts, depth, width = weight.shape
-    else:
-        width = weight.shape[1]
-        depth = cut(inner, 768)
-        parts = inner // depth
+    inner, width = weight.shape
+    depth = cut(inner, 3072 if own else 1536)
+    parts = inner // depth
     chips = 1 if own else chips_y - 1
     tokens = chips * CORES * tok
     block = pltpu.VMEM((chips, tok, width), jnp.bfloat16)
-    out_shape = (block, block) if own else (block, block, pltpu.VMEM((parts, depth, width), jnp.bfloat16))
+    out_shape = (block, block) if own else (block, block, pltpu.VMEM((inner, width), jnp.bfloat16))
     return pl.pallas_call(
-        functools.partial(down_kernel, chips_y, tok, own),
+        functools.partial(down_kernel, chips_y, tok, parts, own),
         out_shape=out_shape,
         in_specs=[HBM, VMEM if own else HBM],
         out_specs=(VMEM,) * len(out_shape),
@@ -122,11 +118,10 @@
     )
 
 
-def merge_kernel(others, keep, got, gain, stream, upper, lower):
+def merge_kernel(others, keep, got, gain, upper, lower):
     tok, width = others.shape
     own = keep[...].astype(jnp.float32) + got[...].astype(jnp.float32)
-    value = (others[...] + own).astype(stream.dtype)
-    stream[...] = value
+    value = (others[...] + own).astype(upper.dtype)
     upper[...] = value[: tok // 2]
     lower[0 : tok // 2, :] = value[tok // 2 :]
     rows = jnp.broadcast_to(gain[...].astype(jnp.float32), (GAIN, width))
@@ -137,9 +132,9 @@
     tok, width = others.shape
     return pl.pallas_call(
         merge_kernel,
-        out_shape=[pltpu.VMEM((n, width), jnp.bfloat16) for n in (tok, tok // 2, tok // 2 + GAIN)],
+        out_shape=[pltpu.VMEM((n, width), jnp.bfloat16) for n in (tok // 2, tok // 2 + GAIN)],
         in_specs=[VMEM] * 4,
-        out_specs=[VMEM] * 3,
+        out_specs=[VMEM] * 2,
         compiler_params=pltpu.CompilerParams(vmem_limit_bytes=8 * MIB),
         name="merge",
     )(others, keep, got, gain)
@@ -155,7 +150,7 @@
     if last:
         (out,) = take(1)
     elif first:
-        shift_out, sums_out, total_out = take(3)
+        stream, shift_out, sums_out, total_out = take(4)
     else:
         sums_out, total_out = take(2)
     (lhs,) = take(1)
@@ -177,6 +172,7 @@
         whole = jnp.concatenate([part[...].astype(jnp.float32) for part in parts], axis=0)
         values, row = whole[0:tok], whole[tok : tok + 1]
         if first and i == 0:
+            stream[...] = values.astype(stream.dtype)
             shift = jnp.mean(values, axis=1, keepdims=True)
             shift_out[...] = shift
             one = two = jnp.zeros_like(shift)
@@ -222,7 +218,7 @@
     if last:
         out_shape, aliases = jax.ShapeDtypeStruct((tok, columns), jnp.bfloat16), {}
     elif first:
-        out_shape, aliases = (shift, sums, total), {}
+        out_shape, aliases = (jax.ShapeDtypeStruct((tok, width), jnp.bfloat16), shift, sums, total), {}
     else:
         out_shape, aliases = (sums, total), {base + 1: 0, base + 2: 1}
     got = pl.pallas_call(
@@ -244,7 +240,7 @@
     )(*flat, pltpu.with_memory_space_constraint(weight, pltpu.VMEM), *state)
     if last:
         return got
-    return got if first else (state[0], *got)
+    return (got[0], got[1:]) if first else (state[0], *got)
 
 
 def solution(mesh):
@@ -271,7 +267,7 @@
             others = others + lax.ppermute(both[step - 1], "row", move).astype(jnp.float32)
         give, keep = down(hidden, down_weight, tok, chips_y, True)
         got = lax.ppermute(give[0], "row", sibling)
-        stream, upper, lower = merge(others, keep[0], got, gain[None, :])
+        upper, lower = merge(others, keep[0], got, gain[None, :])
 
         up, back = [upper, lower], [upper, lower]
         pieces, hops, state, opposite = [], [], None, None
@@ -284,6 +280,8 @@
                 opposite = lax.ppermute(opposite[0], "col", shift(2)), lax.ppermute(opposite[1], "col", shift(-2))
             if pieces:
                 state = project(pieces, hops, qk_weight, state, cycle, False)
+                if step == 2:
+                    stream, state = state
                 up[1], back[1], state = lax.optimization_barrier((up[1], back[1], state))
             pieces, hops = [list(up), list(back)], [-step, step]
             if step == 1:

time: 45 us -> 45.3 us (level)
  starting transfers between devices: 18.7 us -> 20 us
  waiting for transfers between devices: 8.93 us -> 7.88 us
  local copies, waits for them, and re-layouts: 0.7 us -> 0.02 us
  Pallas kernels: 15.7 us -> 16.3 us
    ppermute x6, starting transfers between devices: 1.53 us -> 8.45 us  [per_device(): lax.ppermute(back[i], 'col', shift(-1))]
    ppermute x6, starting transfers between devices: 10.7 us -> 4.41 us  [per_device(): lax.ppermute(up[i], 'col', shift(1))]
    ppermute x1, starting transfers between devices: 0.33 us -> 1.86 us  [per_device(): lax.ppermute(opposite[1], 'col', shift(-2))]
    ppermute x1, waiting for transfers between devices: 1.41 us -> 0.01 us  [per_device(): lax.ppermute(opposite[0], 'col', shift(2))]
    ppermute x1, waiting for transfers between devices: 1.68 us -> 2.62 us  [per_device(): lax.ppermute(opposite[1], 'col', shift(-2))]
    ppermute x1, starting transfers between devices: 2.59 us -> 1.79 us  [per_device(): lax.ppermute(opposite[0], 'col', shift(2))]
    unnamed x7 -> x6, local copies, waits for them, and re-layouts: 0.69 us -> 0.01 us
    pallas_call x4, Pallas kernels: 5.03 us -> 5.55 us  [project(): pl.pallas_call(functools.partial(project_kernel, cycle, hops, [len(parts)...]
  transfers between devices with their start and end apart: 17 -> 17, of which waited for: 8 -> 7; matrix products, arithmetic and copies ran while one was open for 2% -> 0% of each run, Pallas kernels for 19% -> 20%
where the time goes in v11:
time: 45.3 us; the launch traced here: 45.1 us
  starting transfers between devices  20 us (44%)
  Pallas kernels  16.3 us (36%)
  waiting for transfers between devices  7.88 us (17%)
  between operations  0.75 us (2%)
    pallas_call x2, Pallas kernels, down(): pl.pallas_call(functools.partial(down_kernel, chips_y, tok, parts, own),...  10.7 us
    ppermute x6, starting transfers between devices, per_device(): lax.ppermute(back[i], 'col', shift(-1))  8.45 us
    pallas_call x4, Pallas kernels, project(): pl.pallas_call(functools.partial(project_kernel, cycle, hops, [len(parts)...  5.55 us
    ppermute x6, starting transfers between devices, per_device(): lax.ppermute(up[i], 'col', shift(1))  4.41 us
    ppermute x1, starting transfers between devices, per_device(): lax.ppermute(both[step - 1], 'row', move).astype(jnp.float32)  2.95 us
    ppermute x1, waiting for transfers between devices, per_device(): lax.ppermute(opposite[1], 'col', shift(-2))  2.62 us
    ppermute x1, starting transfers between devices, per_device(): lax.ppermute(opposite[1], 'col', shift(-2))  1.86 us
    ppermute x1, starting transfers between devices, per_device(): lax.ppermute(opposite[0], 'col', shift(2))  1.79 us
  transfers between devices with their start and end apart: 17, of which 7 were waited for; matrix products, arithmetic and copies ran while one was open for 0% of the time, Pallas kernels for 20%

profile of v11, /device:TPU:0, one launch (start us, length us, event | category | flops | bytes accessed | tf_op | source)
XLA Modules:
  0.0 45.1 jit_solution(10095982566442170)
XLA Ops:
  0.7 5.7 %down.2 = (bf16[1,128,768]{2,1,0:T(8,128)(2,1)S(1)}, bf16[1,128,768]{2,1,0:T(8,128)(2,1)S(1)}, bf16[6144,768]{1,0:T(8,128)(2,1)S(1)}) custom-call(bf16[512,6144]{1,0:T(8,128)(2,1)} %hidden.2, bf16[6144,768]{1,0:T(8,128)(2,1)} %weight.1), custom_call_target="tpu_custom_call" | custom-call | flops 2415919104 | bytes 12582912 | tf_op jit(solution)/shard_map/down/pallas_call | solution.py:98
  6.9 1.1 %collective-permute-done = bf16[1,128,768]{2,1,0:T(8,128)(2,1)S(1)} collective-permute-done((bf16[1,128,768]{2,1,0:T(8,128)(2,1)S(1)}, bf16[1,128,768]{2,1,0:T(8,128)(2,1)S(1)}, u32[]{:S(2)}, u32[]{:S(2)}) %collective-permute-start) | collective-permute-done | bytes 196640 | tf_op jit(solution)/shard_map/ppermute | solution.py:261
  8.0 3.0 %collective-permute-start.1 = (bf16[128,768]{1,0:T(8,128)(2,1)S(1)}, bf16[128,768]{1,0:T(8,128)(2,1)S(1)}, u32[]{:S(2)}, u32[]{:S(2)}) collective-permute-start(bf16[128,768]{1,0:T(8,128)(2,1)S(1)} %bitcast.5), channel_id=1, source_target_pairs={{0,16},{8,24},{16,0},{24,8},{1,17},{9,25},{17,1},{25,9},{2,18},{10... | collective-permute-start | bytes 589832 | tf_op jit(solution)/shard_map/ppermute | solution.py:267
  11.0 5.0 %down.3 = (bf16[1,128,768]{2,1,0:T(8,128)(2,1)S(1)}, bf16[1,128,768]{2,1,0:T(8,128)(2,1)S(1)}) custom-call(bf16[512,6144]{1,0:T(8,128)(2,1)} %hidden.2, bf16[6144,768]{1,0:T(8,128)(2,1)S(1)} %get-tuple-element.33.weight), custom_call_target="tpu_custom_call" | custom-call | flops 2415919104 | bytes 3145728 | tf_op jit(solution)/shard_map/down/pallas_call | solution.py:98
  16.2 1.3 %collective-permute-done.2.got = bf16[128,768]{1,0:T(8,128)(2,1)S(1)} collective-permute-done((bf16[128,768]{1,0:T(8,128)(2,1)S(1)}, bf16[128,768]{1,0:T(8,128)(2,1)S(1)}, u32[]{:S(2)}, u32[]{:S(2)}) %collective-permute-start.2) | collective-permute-done | bytes 196640 | tf_op jit(solution)/shard_map/ppermute | solution.py:269
  17.6 1.9 %collective-permute-start.6 = (bf16[72,768]{1,0:T(8,128)(2,1)S(1)}, bf16[72,768]{1,0:T(8,128)(2,1)S(1)}, u32[]{:S(2)}, u32[]{:S(2)}) collective-permute-start(bf16[72,768]{1,0:T(8,128)(2,1)S(1)} %get-tuple-element.37.refs_1_), channel_id=1, source_target_pairs={{0,2},{1,0},{3,1},{5,3},{7,5},{6,7},{4,6},{2,4},{8,10},{9,8},{11,9... | collective-permute-start | bytes 331784 | tf_op jit(solution)/shard_map/ppermute | solution.py:278
  19.7 1.7 %collective-permute-start.3 = (bf16[64,768]{1,0:T(8,128)(2,1)S(1)}, bf16[64,768]{1,0:T(8,128)(2,1)S(1)}, u32[]{:S(2)}, u32[]{:S(2)}) collective-permute-start(bf16[64,768]{1,0:T(8,128)(2,1)S(1)} %get-tuple-element.36.refs_0_), channel_id=1, source_target_pairs={{0,1},{1,3},{3,5},{5,7},{7,6},{6,4},{4,2},{2,0},{8,9},{9,11},{11,1... | collective-permute-start | bytes 294920 | tf_op jit(solution)/shard_map/ppermute | solution.py:278
  21.7 1.2 %collective-permute-done.6.refs_5_ = bf16[72,768]{1,0:T(8,128)(2,1)S(1)} collective-permute-done((bf16[72,768]{1,0:T(8,128)(2,1)S(1)}, bf16[72,768]{1,0:T(8,128)(2,1)S(1)}, u32[]{:S(2)}, u32[]{:S(2)}) %collective-permute-start.6) | collective-permute-done | bytes 110624 | tf_op jit(solution)/shard_map/ppermute | solution.py:278
  22.9 2.5 %collective-permute-start.10 = (bf16[72,768]{1,0:T(8,128)(2,1)S(1)}, bf16[72,768]{1,0:T(8,128)(2,1)S(1)}, u32[]{:S(2)}, u32[]{:S(2)}) collective-permute-start(bf16[72,768]{1,0:T(8,128)(2,1)S(1)} %collective-permute-done.6.refs_5_), channel_id=1, source_target_pairs={{0,2},{1,0},{3,1},{5,3},{7,5},{6,7},{4,6},{2,4},{8,10},{9,8},{11,9... | collective-permute-start | bytes 331784 | tf_op jit(solution)/shard_map/ppermute | solution.py:278
  25.5 1.0 %collective-permute-done.3.refs_2_ = bf16[64,768]{1,0:T(8,128)(2,1)S(1)} collective-permute-done((bf16[64,768]{1,0:T(8,128)(2,1)S(1)}, bf16[64,768]{1,0:T(8,128)(2,1)S(1)}, u32[]{:S(2)}, u32[]{:S(2)}) %collective-permute-start.3) | collective-permute-done | bytes 98336 | tf_op jit(solution)/shard_map/ppermute | solution.py:278
  26.5 0.8 %collective-permute-start.7 = (bf16[64,768]{1,0:T(8,128)(2,1)S(1)}, bf16[64,768]{1,0:T(8,128)(2,1)S(1)}, u32[]{:S(2)}, u32[]{:S(2)}) collective-permute-start(bf16[64,768]{1,0:T(8,128)(2,1)S(1)} %collective-permute-done.3.refs_2_), channel_id=1, source_target_pairs={{0,1},{1,3},{3,5},{5,7},{7,6},{6,4},{4,2},{2,0},{8,9},{9,11},{11,1... | collective-permute-start | bytes 294920 | tf_op jit(solution)/shard_map/ppermute | solution.py:278
  27.3 1.3 %collective-permute-start.14 = (bf16[64,768]{1,0:T(8,128)(2,1)S(1)}, bf16[64,768]{1,0:T(8,128)(2,1)S(1)}, u32[]{:S(2)}, u32[]{:S(2)}) collective-permute-start(bf16[64,768]{1,0:T(8,128)(2,1)S(1)} %collective-permute-done.5.refs_4_), channel_id=1, source_target_pairs={{0,2},{1,0},{3,1},{5,3},{7,5},{6,7},{4,6},{2,4},{8,10},{9,8},{11,9... | collective-permute-start | bytes 294920 | tf_op jit(solution)/shard_map/ppermute | solution.py:278
  28.5 1.9 %project.4 = (bf16[128,768]{1,0:T(8,128)(2,1)}, f32[128,1]{1,0:T(8,128)S(1)}, f32[2,128,1]{2,1,0:T(8,128)S(1)}, f32[144,1536]{1,0:T(8,128)S(1)}) custom-call(bf16[64,768]{1,0:T(8,128)(2,1)S(1)} %get-tuple-element.36.refs_0_, bf16[72,768]{1,0:T(8,128)(2,1)S(1)} %get-tuple-element.37.refs_1_, bf16[64,768]{1,0:T(8,128)(2,1)S(1)} %collective-permute-done.3.refs_2_, ...), custom_call_target="tpu_custom_call" | custom-call | flops 1019215872 | tf_op jit(solution)/shard_map/project/pallas_call | solution.py:224
  30.5 0.8 %collective-permute-start.12 = (bf16[72,768]{1,0:T(8,128)(2,1)S(1)}, bf16[72,768]{1,0:T(8,128)(2,1)S(1)}, u32[]{:S(2)}, u32[]{:S(2)}) collective-permute-start(bf16[72,768]{1,0:T(8,128)(2,1)S(1)} %collective-permute-done.9.refs_1_), channel_id=1, source_target_pairs={{0,1},{1,3},{3,5},{5,7},{7,6},{6,4},{4,2},{2,0},{8,9},{9,11},{11,1... | collective-permute-start | bytes 331784 | tf_op jit(solution)/shard_map/ppermute | solution.py:278
  31.3 1.3 %collective-permute-start.13 = (bf16[72,768]{1,0:T(8,128)(2,1)S(1)}, bf16[72,768]{1,0:T(8,128)(2,1)S(1)}, u32[]{:S(2)}, u32[]{:S(2)}) collective-permute-start(bf16[72,768]{1,0:T(8,128)(2,1)S(1)} %collective-permute-done.10.refs_3_), channel_id=1, source_target_pairs={{0,2},{1,0},{3,1},{5,3},{7,5},{6,7},{4,6},{2,4},{8,10},{9,8},{11,9... | collective-permute-start | bytes 331784 | tf_op jit(solution)/shard_map/ppermute | solution.py:278
  32.5 0.8 %collective-permute-start.15 = (bf16[64,768]{1,0:T(8,128)(2,1)S(1)}, bf16[64,768]{1,0:T(8,128)(2,1)S(1)}, u32[]{:S(2)}, u32[]{:S(2)}) collective-permute-start(bf16[64,768]{1,0:T(8,128)(2,1)S(1)} %collective-permute-done.7.refs_0_), channel_id=1, source_target_pairs={{0,1},{1,3},{3,5},{5,7},{7,6},{6,4},{4,2},{2,0},{8,9},{9,11},{11,1... | collective-permute-start | bytes 294920 | tf_op jit(solution)/shard_map/ppermute | solution.py:278
  33.3 1.3 %collective-permute-start.16 = (bf16[64,768]{1,0:T(8,128)(2,1)S(1)}, bf16[64,768]{1,0:T(8,128)(2,1)S(1)}, u32[]{:S(2)}, u32[]{:S(2)}) collective-permute-start(bf16[64,768]{1,0:T(8,128)(2,1)S(1)} %collective-permute-done.14.refs_2_), channel_id=1, source_target_pairs={{0,2},{1,0},{3,1},{5,3},{7,5},{6,7},{4,6},{2,4},{8,10},{9,8},{11,9... | collective-permute-start | bytes 294920 | tf_op jit(solution)/shard_map/ppermute | solution.py:278
  34.6 1.8 %collective-permute-start.8 = (bf16[64,768]{1,0:T(8,128)(2,1)S(1)}, bf16[64,768]{1,0:T(8,128)(2,1)S(1)}, u32[]{:S(2)}, u32[]{:S(2)}) collective-permute-start(bf16[64,768]{1,0:T(8,128)(2,1)S(1)} %collective-permute-done.7.refs_0_), channel_id=1, source_target_pairs={{0,3},{1,5},{3,7},{5,6},{7,4},{6,2},{4,0},{2,1},{8,11},{9,13},{11,... | collective-permute-start | bytes 294920 | tf_op jit(solution)/shard_map/ppermute | solution.py:280
  36.3 0.6 %collective-permute-done.12.refs_1_ = bf16[72,768]{1,0:T(8,128)(2,1)S(1)} collective-permute-done((bf16[72,768]{1,0:T(8,128)(2,1)S(1)}, bf16[72,768]{1,0:T(8,128)(2,1)S(1)}, u32[]{:S(2)}, u32[]{:S(2)}) %collective-permute-start.12) | collective-permute-done | bytes 110624 | tf_op jit(solution)/shard_map/ppermute | solution.py:278
  37.0 1.9 %collective-permute-start.11 = (bf16[72,768]{1,0:T(8,128)(2,1)S(1)}, bf16[72,768]{1,0:T(8,128)(2,1)S(1)}, u32[]{:S(2)}, u32[]{:S(2)}) collective-permute-start(bf16[72,768]{1,0:T(8,128)(2,1)S(1)} %collective-permute-done.10.refs_3_), channel_id=1, source_target_pairs={{0,4},{1,2},{3,0},{5,1},{7,3},{6,5},{4,7},{2,6},{8,12},{9,10},{11,... | collective-permute-start | bytes 331784 | tf_op jit(solution)/shard_map/ppermute | solution.py:280
  38.8 1.1 %project.5 = (f32[2,128,1]{2,1,0:T(8,128)S(1)}, f32[144,1536]{1,0:T(8,128)S(1)}) custom-call(bf16[64,768]{1,0:T(8,128)(2,1)S(1)} %collective-permute-done.7.refs_0_, bf16[72,768]{1,0:T(8,128)(2,1)S(1)} %collective-permute-done.9.refs_1_, bf16[64,768]{1,0:T(8,128)(2,1)S(1)} %collective-permute-done.14.refs_2_, ...), custom_call_target="tpu_custom_call", output_to_operand_aliasing={{0}: (6, {}), {1}: (7, {})} | custom-call | flops 679477248 | tf_op jit(solution)/shard_map/project/pallas_call | solution.py:224
  40.0 1.1 %project.6 = (f32[2,128,1]{2,1,0:T(8,128)S(1)}, f32[144,1536]{1,0:T(8,128)S(1)}) custom-call(bf16[64,768]{1,0:T(8,128)(2,1)S(1)} %collective-permute-done.15.refs_0_, bf16[72,768]{1,0:T(8,128)(2,1)S(1)} %collective-permute-done.12.refs_1_, bf16[64,768]{1,0:T(8,128)(2,1)S(1)} %collective-permute-done.16.refs_2_, ...), custom_call_target="tpu_custom_call", output_to_operand_aliasing={{0}: (6, {}), {1}: (7, {})} | custom-call | flops 679477248 | tf_op jit(solution)/shard_map/project/pallas_call | solution.py:224
  41.1 2.6 %collective-permute-done.11.refs_1_ = bf16[72,768]{1,0:T(8,128)(2,1)S(1)} collective-permute-done((bf16[72,768]{1,0:T(8,128)(2,1)S(1)}, bf16[72,768]{1,0:T(8,128)(2,1)S(1)}, u32[]{:S(2)}, u32[]{:S(2)}) %collective-permute-start.11) | collective-permute-done | bytes 110624 | tf_op jit(solution)/shard_map/ppermute | solution.py:280
  43.7 1.4 %project.7 = bf16[128,1536]{1,0:T(8,128)(2,1)} custom-call(bf16[64,768]{1,0:T(8,128)(2,1)S(1)} %collective-permute-done.8.refs_0_, bf16[72,768]{1,0:T(8,128)(2,1)S(1)} %collective-permute-done.11.refs_1_, bf16[6144,1536]{1,0:T(8,128)(2,1)S(1)} %copy-done, f32[128,1]{1,0:T(8,128)S(1)} %get-tuple-element.49.refs_5_.refs_3_, ...), custom_call_target="tpu_custom_call" | custom-call | flops 339738624 | tf_op jit(solution)/shard_map/project/pallas_call | solution.py:224
  (26 shorter events, 1.6 us)
Async XLA Ops:
  0.6 6.3 %copy-start.2 = (bf16[768]{0:T(1024)(128)(2,1)S(1)}, bf16[768]{0:T(1024)(128)(2,1)}, u32[]{:S(2)}) copy-start(bf16[768]{0:T(1024)(128)(2,1)} %param.8) | copy-start | bytes 4612
  0.6 27.9 %copy-start = (bf16[6144,1536]{1,0:T(8,128)(2,1)S(1)}, bf16[6144,1536]{1,0:T(8,128)(2,1)}, u32[]{:S(2)}) copy-start(bf16[6144,1536]{1,0:T(8,128)(2,1)} %refs_2_.1) | copy-start | bytes 56623108
  6.4 9.8 %copy-start.1 = (bf16[128,768]{1,0:T(8,128)(2,1)S(1)}, bf16[128,768]{1,0:T(8,128)(2,1)}, u32[]{:S(2)}) copy-start(bf16[128,768]{1,0:T(8,128)(2,1)} %param.7) | copy-start | bytes 589828
  6.4 1.6 %collective-permute-start = (bf16[1,128,768]{2,1,0:T(8,128)(2,1)S(1)}, bf16[1,128,768]{2,1,0:T(8,128)(2,1)S(1)}, u32[]{:S(2)}, u32[]{:S(2)}) collective-permute-start(bf16[1,128,768]{2,1,0:T(8,128)(2,1)S(1)} %get-tuple-element.30), channel_id=1, source_target_pairs={{0,8},{8,0},{16,24},{24,16},{1,9},{9,1},{17,25},{25,17},{2,10},{10... | collective-permute-start | bytes 589832 | tf_op jit(solution)/shard_map/ppermute | solution.py:261
  8.0 8.2 %collective-permute-start.1 = (bf16[128,768]{1,0:T(8,128)(2,1)S(1)}, bf16[128,768]{1,0:T(8,128)(2,1)S(1)}, u32[]{:S(2)}, u32[]{:S(2)}) collective-permute-start(bf16[128,768]{1,0:T(8,128)(2,1)S(1)} %bitcast.5), channel_id=1, source_target_pairs={{0,16},{8,24},{16,0},{24,8},{1,17},{9,25},{17,1},{25,9},{2,18},{10... | collective-permute-start | bytes 589832 | tf_op jit(solution)/shard_map/ppermute | solution.py:267
  16.0 1.5 %collective-permute-start.2 = (bf16[128,768]{1,0:T(8,128)(2,1)S(1)}, bf16[128,768]{1,0:T(8,128)(2,1)S(1)}, u32[]{:S(2)}, u32[]{:S(2)}) collective-permute-start(bf16[128,768]{1,0:T(8,128)(2,1)S(1)} %bitcast.4), channel_id=1, source_target_pairs={{0,8},{8,0},{16,24},{24,16},{1,9},{9,1},{17,25},{25,17},{2,10},{10... | collective-permute-start | bytes 589832 | tf_op jit(solution)/shard_map/ppermute | solution.py:269
  17.6 5.3 %collective-permute-start.6 = (bf16[72,768]{1,0:T(8,128)(2,1)S(1)}, bf16[72,768]{1,0:T(8,128)(2,1)S(1)}, u32[]{:S(2)}, u32[]{:S(2)}) collective-permute-start(bf16[72,768]{1,0:T(8,128)(2,1)S(1)} %get-tuple-element.37.refs_1_), channel_id=1, source_target_pairs={{0,2},{1,0},{3,1},{5,3},{7,5},{6,7},{4,6},{2,4},{8,10},{9,8},{11,9... | collective-permute-start | bytes 331784 | tf_op jit(solution)/shard_map/ppermute | solution.py:278
  19.5 5.9 %collective-permute-start.4 = (bf16[72,768]{1,0:T(8,128)(2,1)S(1)}, bf16[72,768]{1,0:T(8,128)(2,1)S(1)}, u32[]{:S(2)}, u32[]{:S(2)}) collective-permute-start(bf16[72,768]{1,0:T(8,128)(2,1)S(1)} %get-tuple-element.37.refs_1_), channel_id=1, source_target_pairs={{0,1},{1,3},{3,5},{5,7},{7,6},{6,4},{4,2},{2,0},{8,9},{9,11},{11,1... | collective-permute-start | bytes 331784 | tf_op jit(solution)/shard_map/ppermute | solution.py:278
  19.7 6.9 %collective-permute-start.3 = (bf16[64,768]{1,0:T(8,128)(2,1)S(1)}, bf16[64,768]{1,0:T(8,128)(2,1)S(1)}, u32[]{:S(2)}, u32[]{:S(2)}) collective-permute-start(bf16[64,768]{1,0:T(8,128)(2,1)S(1)} %get-tuple-element.36.refs_0_), channel_id=1, source_target_pairs={{0,1},{1,3},{3,5},{5,7},{7,6},{6,4},{4,2},{2,0},{8,9},{9,11},{11,1... | collective-permute-start | bytes 294920 | tf_op jit(solution)/shard_map/ppermute | solution.py:278
  21.4 5.9 %collective-permute-start.5 = (bf16[64,768]{1,0:T(8,128)(2,1)S(1)}, bf16[64,768]{1,0:T(8,128)(2,1)S(1)}, u32[]{:S(2)}, u32[]{:S(2)}) collective-permute-start(bf16[64,768]{1,0:T(8,128)(2,1)S(1)} %get-tuple-element.36.refs_0_), channel_id=1, source_target_pairs={{0,2},{1,0},{3,1},{5,3},{7,5},{6,7},{4,6},{2,4},{8,10},{9,8},{11,9... | collective-permute-start | bytes 294920 | tf_op jit(solution)/shard_map/ppermute | solution.py:278
  22.9 7.6 %collective-permute-start.10 = (bf16[72,768]{1,0:T(8,128)(2,1)S(1)}, bf16[72,768]{1,0:T(8,128)(2,1)S(1)}, u32[]{:S(2)}, u32[]{:S(2)}) collective-permute-start(bf16[72,768]{1,0:T(8,128)(2,1)S(1)} %collective-permute-done.6.refs_5_), channel_id=1, source_target_pairs={{0,2},{1,0},{3,1},{5,3},{7,5},{6,7},{4,6},{2,4},{8,10},{9,8},{11,9... | collective-permute-start | bytes 331784 | tf_op jit(solution)/shard_map/ppermute | solution.py:278
  25.4 5.1 %collective-permute-start.9 = (bf16[72,768]{1,0:T(8,128)(2,1)S(1)}, bf16[72,768]{1,0:T(8,128)(2,1)S(1)}, u32[]{:S(2)}, u32[]{:S(2)}) collective-permute-start(bf16[72,768]{1,0:T(8,128)(2,1)S(1)} %collective-permute-done.4.refs_3_), channel_id=1, source_target_pairs={{0,1},{1,3},{3,5},{5,7},{7,6},{6,4},{4,2},{2,0},{8,9},{9,11},{11,1... | collective-permute-start | bytes 331784 | tf_op jit(solution)/shard_map/ppermute | solution.py:278
  26.5 6.0 %collective-permute-start.7 = (bf16[64,768]{1,0:T(8,128)(2,1)S(1)}, bf16[64,768]{1,0:T(8,128)(2,1)S(1)}, u32[]{:S(2)}, u32[]{:S(2)}) collective-permute-start(bf16[64,768]{1,0:T(8,128)(2,1)S(1)} %collective-permute-done.3.refs_2_), channel_id=1, source_target_pairs={{0,1},{1,3},{3,5},{5,7},{7,6},{6,4},{4,2},{2,0},{8,9},{9,11},{11,1... | collective-permute-start | bytes 294920 | tf_op jit(solution)/shard_map/ppermute | solution.py:278
  27.3 6.0 %collective-permute-start.14 = (bf16[64,768]{1,0:T(8,128)(2,1)S(1)}, bf16[64,768]{1,0:T(8,128)(2,1)S(1)}, u32[]{:S(2)}, u32[]{:S(2)}) collective-permute-start(bf16[64,768]{1,0:T(8,128)(2,1)S(1)} %collective-permute-done.5.refs_4_), channel_id=1, source_target_pairs={{0,2},{1,0},{3,1},{5,3},{7,5},{6,7},{4,6},{2,4},{8,10},{9,8},{11,9... | collective-permute-start | bytes 294920 | tf_op jit(solution)/shard_map/ppermute | solution.py:278
  30.5 6.5 %collective-permute-start.12 = (bf16[72,768]{1,0:T(8,128)(2,1)S(1)}, bf16[72,768]{1,0:T(8,128)(2,1)S(1)}, u32[]{:S(2)}, u32[]{:S(2)}) collective-permute-start(bf16[72,768]{1,0:T(8,128)(2,1)S(1)} %collective-permute-done.9.refs_1_), channel_id=1, source_target_pairs={{0,1},{1,3},{3,5},{5,7},{7,6},{6,4},{4,2},{2,0},{8,9},{9,11},{11,1... | collective-permute-start | bytes 331784 | tf_op jit(solution)/shard_map/ppermute | solution.py:278
  31.3 8.7 %collective-permute-start.13 = (bf16[72,768]{1,0:T(8,128)(2,1)S(1)}, bf16[72,768]{1,0:T(8,128)(2,1)S(1)}, u32[]{:S(2)}, u32[]{:S(2)}) collective-permute-start(bf16[72,768]{1,0:T(8,128)(2,1)S(1)} %collective-permute-done.10.refs_3_), channel_id=1, source_target_pairs={{0,2},{1,0},{3,1},{5,3},{7,5},{6,7},{4,6},{2,4},{8,10},{9,8},{11,9... | collective-permute-start | bytes 331784 | tf_op jit(solution)/shard_map/ppermute | solution.py:278
  32.5 7.4 %collective-permute-start.15 = (bf16[64,768]{1,0:T(8,128)(2,1)S(1)}, bf16[64,768]{1,0:T(8,128)(2,1)S(1)}, u32[]{:S(2)}, u32[]{:S(2)}) collective-permute-start(bf16[64,768]{1,0:T(8,128)(2,1)S(1)} %collective-permute-done.7.refs_0_), channel_id=1, source_target_pairs={{0,1},{1,3},{3,5},{5,7},{7,6},{6,4},{4,2},{2,0},{8,9},{9,11},{11,1... | collective-permute-start | bytes 294920 | tf_op jit(solution)/shard_map/ppermute | solution.py:278
  33.3 6.7 %collective-permute-start.16 = (bf16[64,768]{1,0:T(8,128)(2,1)S(1)}, bf16[64,768]{1,0:T(8,128)(2,1)S(1)}, u32[]{:S(2)}, u32[]{:S(2)}) collective-permute-start(bf16[64,768]{1,0:T(8,128)(2,1)S(1)} %collective-permute-done.14.refs_2_), channel_id=1, source_target_pairs={{0,2},{1,0},{3,1},{5,3},{7,5},{6,7},{4,6},{2,4},{8,10},{9,8},{11,9... | collective-permute-start | bytes 294920 | tf_op jit(solution)/shard_map/ppermute | solution.py:278
  34.6 6.5 %collective-permute-start.8 = (bf16[64,768]{1,0:T(8,128)(2,1)S(1)}, bf16[64,768]{1,0:T(8,128)(2,1)S(1)}, u32[]{:S(2)}, u32[]{:S(2)}) collective-permute-start(bf16[64,768]{1,0:T(8,128)(2,1)S(1)} %collective-permute-done.7.refs_0_), channel_id=1, source_target_pairs={{0,3},{1,5},{3,7},{5,6},{7,4},{6,2},{4,0},{2,1},{8,11},{9,13},{11,... | collective-permute-start | bytes 294920 | tf_op jit(solution)/shard_map/ppermute | solution.py:280
  37.0 6.7 %collective-permute-start.11 = (bf16[72,768]{1,0:T(8,128)(2,1)S(1)}, bf16[72,768]{1,0:T(8,128)(2,1)S(1)}, u32[]{:S(2)}, u32[]{:S(2)}) collective-permute-start(bf16[72,768]{1,0:T(8,128)(2,1)S(1)} %collective-permute-done.10.refs_3_), channel_id=1, source_target_pairs={{0,4},{1,2},{3,0},{5,1},{7,3},{6,5},{4,7},{2,6},{8,12},{9,10},{11,... | collective-permute-start | bytes 331784 | tf_op jit(solution)/shard_map/ppermute | solution.py:280

commit v12 on v11

--- a/solution.py
+++ b/solution.py
@@ -70,17 +70,19 @@
     for k in range(parts):
         for copy in copies(k):
             copy.start(priority=1)
-    for copy in copies(0):
-        copy.wait()
-    total[...] = jnp.dot(h_buf[0], held[span(0), :], preferred_element_type=jnp.float32)
+    tokens, width = total.shape
+    total[...] = jnp.zeros_like(total)
 
     def body(k, _):
         for copy in copies(k):
             copy.wait()
-        total[...] += jnp.dot(h_buf[k], held[span(k), :], preferred_element_type=jnp.float32)
+        for row in range(0, tokens, 128):
+            for column in range(0, width, 512):
+                place = pl.ds(row, 128), pl.ds(column, min(512, width - column))
+                total[place] += jnp.dot(h_buf[k, place[0], :], held[span(k), place[1]], preferred_element_type=jnp.float32)
         return _
 
-    lax.fori_loop(1, parts, body, 0)
+    lax.fori_loop(0, parts, body, 0)
     for i in range(len(chips)):
         for out, which in ((give, 1 - core), (keep, core)):
             start = pl.multiple_of((i * CORES + which) * tok, tok)
@@ -89,7 +91,7 @@
 
 def down(hidden, weight, tok, chips_y, own):
     inner, width = weight.shape
-    depth = cut(inner, 3072 if own else 1536)
+    depth = cut(inner, 1536)
     parts = inner // depth
     chips = 1 if own else chips_y - 1
     tokens = chips * CORES * tok
@@ -270,7 +272,7 @@
         upper, lower = merge(others, keep[0], got, gain[None, :])
 
         up, back = [upper, lower], [upper, lower]
-        pieces, hops, state, opposite = [], [], None, None
+        pieces, opposite = [[upper, lower]], None
         for step in range(1, half):
             if step == half - 1:
                 opposite = up[0], back[1]
@@ -278,15 +280,10 @@
                 up[i], back[i] = lax.ppermute(up[i], "col", shift(1)), lax.ppermute(back[i], "col", shift(-1))
             if opposite:
                 opposite = lax.ppermute(opposite[0], "col", shift(2)), lax.ppermute(opposite[1], "col", shift(-2))
-            if pieces:
-                state = project(pieces, hops, qk_weight, state, cycle, False)
-                if step == 2:
-                    stream, state = state
-                up[1], back[1], state = lax.optimization_barrier((up[1], back[1], state))
-            pieces, hops = [list(up), list(back)], [-step, step]
-            if step == 1:
-                pieces, hops = [[upper, lower]] + pieces, [0] + hops
-        state = project(pieces, hops, qk_weight, state, cycle, False)
+            pieces += [list(up), list(back)]
+        hops = [0] + [hop for step in range(1, half) for hop in (-step, step)]
+        stream, state = project(pieces[:-2], hops[:-2], qk_weight, None, cycle, False)
+        state = project(pieces[-2:], hops[-2:], qk_weight, state, cycle, False)
         return stream, project([opposite], [half], qk_weight, state, cycle, True)
 
     placed = (P(None, "row"), P("row", "col"), P("row", "col"), P("col"), P(None, "col"))

time: 45.3 us -> 43.6 us (0.962)
  Pallas kernels: 16.3 us -> 15.4 us
  waiting for transfers between devices: 7.88 us -> 7.14 us
    ppermute x6, starting transfers between devices: 8.45 us -> 2.42 us  [per_device(): lax.ppermute(back[i], 'col', shift(-1))]
    ppermute x6, starting transfers between devices: 4.41 us -> 9.09 us  [per_device(): lax.ppermute(up[i], 'col', shift(1))]
    ppermute x6, waiting for transfers between devices: 1.62 us -> 4.41 us  [per_device(): lax.ppermute(up[i], 'col', shift(1))]
    ppermute x1, waiting for transfers between devices: 2.62 us -> 0.08 us  [per_device(): lax.ppermute(opposite[1], 'col', shift(-2))]
    ppermute x6, waiting for transfers between devices: 1.2 us -> 0.2 us  [per_device(): lax.ppermute(back[i], 'col', shift(-1))]
    ppermute x1, starting transfers between devices: 1.79 us -> 2.59 us  [per_device(): lax.ppermute(opposite[0], 'col', shift(2))]
    ppermute x1, waiting for transfers between devices: 1.26 us -> 0.67 us  [per_device(): got = lax.ppermute(give[0], 'row', sibling)]
    ppermute x1, waiting for transfers between devices: 0.12 us -> 0.71 us  [per_device(): lax.ppermute(both[step - 1], 'row', move).astype(jnp.float32)]
  transfers between devices with their start and end apart: 17 -> 17, of which waited for: 7 -> 8; matrix products, arithmetic and copies ran while one was open for 0% -> 0% of each run, Pallas kernels for 20% -> 19%
where the time goes in v12:
time: 43.6 us; the launch traced here: 43.5 us
  starting transfers between devices  20 us (46%)
  Pallas kernels  15.4 us (35%)
  waiting for transfers between devices  7.14 us (16%)
  between operations  0.72 us (2%)
    pallas_call x2, Pallas kernels, down(): pl.pallas_call(functools.partial(down_kernel, chips_y, tok, parts, own),...  10.1 us
    ppermute x6, starting transfers between devices, per_device(): lax.ppermute(up[i], 'col', shift(1))  9.09 us
    pallas_call x3, Pallas kernels, project(): pl.pallas_call(functools.partial(project_kernel, cycle, hops, [len(parts)...  5.23 us
    ppermute x6, waiting for transfers between devices, per_device(): lax.ppermute(up[i], 'col', shift(1))  4.41 us
    ppermute x1, starting transfers between devices, per_device(): lax.ppermute(both[step - 1], 'row', move).astype(jnp.float32)  2.95 us
    ppermute x1, starting transfers between devices, per_device(): lax.ppermute(opposite[0], 'col', shift(2))  2.59 us
    ppermute x6, starting transfers between devices, per_device(): lax.ppermute(back[i], 'col', shift(-1))  2.42 us
    ppermute x1, starting transfers between devices, per_device(): lax.ppermute(opposite[1], 'col', shift(-2))  2.4 us
  transfers between devices with their start and end apart: 17, of which 8 were waited for; matrix products, arithmetic and copies ran while one was open for 0% of the time, Pallas kernels for 19%

profile of v12, /device:TPU:0, one launch (start us, length us, event | category | flops | bytes accessed | tf_op | source)
XLA Modules:
  0.0 43.5 jit_solution(8882709734789337458)
XLA Ops:
  0.7 5.7 %down.2 = (bf16[1,128,768]{2,1,0:T(8,128)(2,1)S(1)}, bf16[1,128,768]{2,1,0:T(8,128)(2,1)S(1)}, bf16[6144,768]{1,0:T(8,128)(2,1)S(1)}) custom-call(bf16[512,6144]{1,0:T(8,128)(2,1)} %hidden.2, bf16[6144,768]{1,0:T(8,128)(2,1)} %weight.1), custom_call_target="tpu_custom_call" | custom-call | flops 2415919104 | bytes 12582912 | tf_op jit(solution)/shard_map/down/pallas_call | solution.py:100
  6.4 0.5 %collective-permute-start = (bf16[1,128,768]{2,1,0:T(8,128)(2,1)S(1)}, bf16[1,128,768]{2,1,0:T(8,128)(2,1)S(1)}, u32[]{:S(2)}, u32[]{:S(2)}) collective-permute-start(bf16[1,128,768]{2,1,0:T(8,128)(2,1)S(1)} %get-tuple-element.18), channel_id=1, source_target_pairs={{0,8},{8,0},{16,24},{24,16},{1,9},{9,1},{17,25},{25,17},{2,10},{10... | collective-permute-start | bytes 589832 | tf_op jit(solution)/shard_map/ppermute | solution.py:263
  6.9 1.1 %collective-permute-done = bf16[1,128,768]{2,1,0:T(8,128)(2,1)S(1)} collective-permute-done((bf16[1,128,768]{2,1,0:T(8,128)(2,1)S(1)}, bf16[1,128,768]{2,1,0:T(8,128)(2,1)S(1)}, u32[]{:S(2)}, u32[]{:S(2)}) %collective-permute-start) | collective-permute-done | bytes 196640 | tf_op jit(solution)/shard_map/ppermute | solution.py:263
  8.0 3.0 %collective-permute-start.1 = (bf16[128,768]{1,0:T(8,128)(2,1)S(1)}, bf16[128,768]{1,0:T(8,128)(2,1)S(1)}, u32[]{:S(2)}, u32[]{:S(2)}) collective-permute-start(bf16[128,768]{1,0:T(8,128)(2,1)S(1)} %bitcast.5), channel_id=1, source_target_pairs={{0,16},{8,24},{16,0},{24,8},{1,17},{9,25},{17,1},{25,9},{2,18},{10... | collective-permute-start | bytes 589832 | tf_op jit(solution)/shard_map/ppermute | solution.py:269
  11.0 4.4 %down.3 = (bf16[1,128,768]{2,1,0:T(8,128)(2,1)S(1)}, bf16[1,128,768]{2,1,0:T(8,128)(2,1)S(1)}) custom-call(bf16[512,6144]{1,0:T(8,128)(2,1)} %hidden.2, bf16[6144,768]{1,0:T(8,128)(2,1)S(1)} %get-tuple-element.21.weight), custom_call_target="tpu_custom_call" | custom-call | flops 2415919104 | bytes 3145728 | tf_op jit(solution)/shard_map/down/pallas_call | solution.py:100
  15.5 0.7 %collective-permute-done.1 = bf16[128,768]{1,0:T(8,128)(2,1)S(1)} collective-permute-done((bf16[128,768]{1,0:T(8,128)(2,1)S(1)}, bf16[128,768]{1,0:T(8,128)(2,1)S(1)}, u32[]{:S(2)}, u32[]{:S(2)}) %collective-permute-start.1) | collective-permute-done | bytes 196640 | tf_op jit(solution)/shard_map/ppermute | solution.py:269
  16.2 0.7 %collective-permute-done.2.got = bf16[128,768]{1,0:T(8,128)(2,1)S(1)} collective-permute-done((bf16[128,768]{1,0:T(8,128)(2,1)S(1)}, bf16[128,768]{1,0:T(8,128)(2,1)S(1)}, u32[]{:S(2)}, u32[]{:S(2)}) %collective-permute-start.2) | collective-permute-done | bytes 196640 | tf_op jit(solution)/shard_map/ppermute | solution.py:271
  17.0 1.8 %collective-permute-start.3 = (bf16[64,768]{1,0:T(8,128)(2,1)S(1)}, bf16[64,768]{1,0:T(8,128)(2,1)S(1)}, u32[]{:S(2)}, u32[]{:S(2)}) collective-permute-start(bf16[64,768]{1,0:T(8,128)(2,1)S(1)} %get-tuple-element.24.refs_0_), channel_id=1, source_target_pairs={{0,1},{1,3},{3,5},{5,7},{7,6},{6,4},{4,2},{2,0},{8,9},{9,11},{11,1... | collective-permute-start | bytes 294920 | tf_op jit(solution)/shard_map/ppermute | solution.py:280
  19.1 1.7 %collective-permute-start.4 = (bf16[72,768]{1,0:T(8,128)(2,1)S(1)}, bf16[72,768]{1,0:T(8,128)(2,1)S(1)}, u32[]{:S(2)}, u32[]{:S(2)}) collective-permute-start(bf16[72,768]{1,0:T(8,128)(2,1)S(1)} %get-tuple-element.25.refs_1_), channel_id=1, source_target_pairs={{0,1},{1,3},{3,5},{5,7},{7,6},{6,4},{4,2},{2,0},{8,9},{9,11},{11,1... | collective-permute-start | bytes 331784 | tf_op jit(solution)/shard_map/ppermute | solution.py:280
  21.1 1.4 %collective-permute-done.3.refs_2_ = bf16[64,768]{1,0:T(8,128)(2,1)S(1)} collective-permute-done((bf16[64,768]{1,0:T(8,128)(2,1)S(1)}, bf16[64,768]{1,0:T(8,128)(2,1)S(1)}, u32[]{:S(2)}, u32[]{:S(2)}) %collective-permute-start.3) | collective-permute-done | bytes 98336 | tf_op jit(solution)/shard_map/ppermute | solution.py:280
  22.5 1.7 %collective-permute-start.7 = (bf16[64,768]{1,0:T(8,128)(2,1)S(1)}, bf16[64,768]{1,0:T(8,128)(2,1)S(1)}, u32[]{:S(2)}, u32[]{:S(2)}) collective-permute-start(bf16[64,768]{1,0:T(8,128)(2,1)S(1)} %collective-permute-done.3.refs_2_), channel_id=1, source_target_pairs={{0,1},{1,3},{3,5},{5,7},{7,6},{6,4},{4,2},{2,0},{8,9},{9,11},{11,1... | collective-permute-start | bytes 294920 | tf_op jit(solution)/shard_map/ppermute | solution.py:280
  24.9 1.6 %collective-permute-start.8 = (bf16[72,768]{1,0:T(8,128)(2,1)S(1)}, bf16[72,768]{1,0:T(8,128)(2,1)S(1)}, u32[]{:S(2)}, u32[]{:S(2)}) collective-permute-start(bf16[72,768]{1,0:T(8,128)(2,1)S(1)} %collective-permute-done.4.refs_3_), channel_id=1, source_target_pairs={{0,1},{1,3},{3,5},{5,7},{7,6},{6,4},{4,2},{2,0},{8,9},{9,11},{11,1... | collective-permute-start | bytes 331784 | tf_op jit(solution)/shard_map/ppermute | solution.py:280
  26.5 0.4 collective-permute-start.9
  26.9 1.1 %collective-permute-done.7.refs_6_ = bf16[64,768]{1,0:T(8,128)(2,1)S(1)} collective-permute-done((bf16[64,768]{1,0:T(8,128)(2,1)S(1)}, bf16[64,768]{1,0:T(8,128)(2,1)S(1)}, u32[]{:S(2)}, u32[]{:S(2)}) %collective-permute-start.7) | collective-permute-done | bytes 98336 | tf_op jit(solution)/shard_map/ppermute | solution.py:280
  28.1 1.9 %collective-permute-start.13 = (bf16[64,768]{1,0:T(8,128)(2,1)S(1)}, bf16[64,768]{1,0:T(8,128)(2,1)S(1)}, u32[]{:S(2)}, u32[]{:S(2)}) collective-permute-start(bf16[64,768]{1,0:T(8,128)(2,1)S(1)} %collective-permute-done.7.refs_6_), channel_id=1, source_target_pairs={{0,1},{1,3},{3,5},{5,7},{7,6},{6,4},{4,2},{2,0},{8,9},{9,11},{11,1... | collective-permute-start | bytes 294920 | tf_op jit(solution)/shard_map/ppermute | solution.py:280
  29.9 2.6 %collective-permute-start.11 = (bf16[64,768]{1,0:T(8,128)(2,1)S(1)}, bf16[64,768]{1,0:T(8,128)(2,1)S(1)}, u32[]{:S(2)}, u32[]{:S(2)}) collective-permute-start(bf16[64,768]{1,0:T(8,128)(2,1)S(1)} %collective-permute-done.7.refs_6_), channel_id=1, source_target_pairs={{0,3},{1,5},{3,7},{5,6},{7,4},{6,2},{4,0},{2,1},{8,11},{9,13},{11,... | collective-permute-start | bytes 294920 | tf_op jit(solution)/shard_map/ppermute | solution.py:282
  32.5 0.5 %collective-permute-start.15 = (bf16[64,768]{1,0:T(8,128)(2,1)S(1)}, bf16[64,768]{1,0:T(8,128)(2,1)S(1)}, u32[]{:S(2)}, u32[]{:S(2)}) collective-permute-start(bf16[64,768]{1,0:T(8,128)(2,1)S(1)} %collective-permute-done.9.refs_8_), channel_id=1, source_target_pairs={{0,2},{1,0},{3,1},{5,3},{7,5},{6,7},{4,6},{2,4},{8,10},{9,8},{11,9... | collective-permute-start | bytes 294920 | tf_op jit(solution)/shard_map/ppermute | solution.py:280
  33.0 0.4 %collective-permute-start.16 = (bf16[72,768]{1,0:T(8,128)(2,1)S(1)}, bf16[72,768]{1,0:T(8,128)(2,1)S(1)}, u32[]{:S(2)}, u32[]{:S(2)}) collective-permute-start(bf16[72,768]{1,0:T(8,128)(2,1)S(1)} %collective-permute-done.10.refs_9_), channel_id=1, source_target_pairs={{0,2},{1,0},{3,1},{5,3},{7,5},{6,7},{4,6},{2,4},{8,10},{9,8},{11,9... | collective-permute-start | bytes 331784 | tf_op jit(solution)/shard_map/ppermute | solution.py:280
  33.4 2.4 %collective-permute-start.12 = (bf16[72,768]{1,0:T(8,128)(2,1)S(1)}, bf16[72,768]{1,0:T(8,128)(2,1)S(1)}, u32[]{:S(2)}, u32[]{:S(2)}) collective-permute-start(bf16[72,768]{1,0:T(8,128)(2,1)S(1)} %collective-permute-done.10.refs_9_), channel_id=1, source_target_pairs={{0,4},{1,2},{3,0},{5,1},{7,3},{6,5},{4,7},{2,6},{8,12},{9,10},{11,... | collective-permute-start | bytes 331784 | tf_op jit(solution)/shard_map/ppermute | solution.py:282
  35.8 0.4 %collective-permute-start.14 = (bf16[72,768]{1,0:T(8,128)(2,1)S(1)}, bf16[72,768]{1,0:T(8,128)(2,1)S(1)}, u32[]{:S(2)}, u32[]{:S(2)}) collective-permute-start(bf16[72,768]{1,0:T(8,128)(2,1)S(1)} %collective-permute-done.8.refs_7_), channel_id=1, source_target_pairs={{0,1},{1,3},{3,5},{5,7},{7,6},{6,4},{4,2},{2,0},{8,9},{9,11},{11,1... | collective-permute-start | bytes 331784 | tf_op jit(solution)/shard_map/ppermute | solution.py:280
  36.3 2.7 %project.3 = (bf16[128,768]{1,0:T(8,128)(2,1)}, f32[128,1]{1,0:T(8,128)S(1)}, f32[2,128,1]{2,1,0:T(8,128)S(1)}, f32[144,1536]{1,0:T(8,128)S(1)}) custom-call(bf16[64,768]{1,0:T(8,128)(2,1)S(1)} %get-tuple-element.24.refs_0_, bf16[72,768]{1,0:T(8,128)(2,1)S(1)} %get-tuple-element.25.refs_1_, bf16[64,768]{1,0:T(8,128)(2,1)S(1)} %collective-permute-done.3.refs_2_, ...), custom_call_target="tpu_custom_call" | custom-call | flops 1698693120 | tf_op jit(solution)/shard_map/project/pallas_call | solution.py:226
  39.0 1.8 %collective-permute-done.14.refs_1_ = bf16[72,768]{1,0:T(8,128)(2,1)S(1)} collective-permute-done((bf16[72,768]{1,0:T(8,128)(2,1)S(1)}, bf16[72,768]{1,0:T(8,128)(2,1)S(1)}, u32[]{:S(2)}, u32[]{:S(2)}) %collective-permute-start.14) | collective-permute-done | bytes 110624 | tf_op jit(solution)/shard_map/ppermute | solution.py:280
  40.9 1.1 %project.4 = (f32[2,128,1]{2,1,0:T(8,128)S(1)}, f32[144,1536]{1,0:T(8,128)S(1)}) custom-call(bf16[64,768]{1,0:T(8,128)(2,1)S(1)} %collective-permute-done.13.refs_0_, bf16[72,768]{1,0:T(8,128)(2,1)S(1)} %collective-permute-done.14.refs_1_, bf16[64,768]{1,0:T(8,128)(2,1)S(1)} %collective-permute-done.15.refs_2_, ...), custom_call_target="tpu_custom_call", output_to_operand_aliasing={{0}: (6, {}), {1}: (7, {})} | custom-call | flops 679477248 | tf_op jit(solution)/shard_map/project/pallas_call | solution.py:226
  42.0 1.4 %project.5 = bf16[128,1536]{1,0:T(8,128)(2,1)} custom-call(bf16[64,768]{1,0:T(8,128)(2,1)S(1)} %collective-permute-done.11.refs_0_, bf16[72,768]{1,0:T(8,128)(2,1)S(1)} %collective-permute-done.12.refs_1_, bf16[6144,1536]{1,0:T(8,128)(2,1)S(1)} %copy-done, f32[128,1]{1,0:T(8,128)S(1)} %get-tuple-element.27.refs_5_.refs_3_, ...), custom_call_target="tpu_custom_call" | custom-call | flops 339738624 | tf_op jit(solution)/shard_map/project/pallas_call | solution.py:226
  (25 shorter events, 1.6 us)
Async XLA Ops:
  0.6 6.3 %copy-start.2 = (bf16[768]{0:T(1024)(128)(2,1)S(1)}, bf16[768]{0:T(1024)(128)(2,1)}, u32[]{:S(2)}) copy-start(bf16[768]{0:T(1024)(128)(2,1)} %param.8) | copy-start | bytes 4612
  0.6 35.6 %copy-start = (bf16[6144,1536]{1,0:T(8,128)(2,1)S(1)}, bf16[6144,1536]{1,0:T(8,128)(2,1)}, u32[]{:S(2)}) copy-start(bf16[6144,1536]{1,0:T(8,128)(2,1)} %refs_2_.1) | copy-start | bytes 56623108
  6.4 9.8 %copy-start.1 = (bf16[128,768]{1,0:T(8,128)(2,1)S(1)}, bf16[128,768]{1,0:T(8,128)(2,1)}, u32[]{:S(2)}) copy-start(bf16[128,768]{1,0:T(8,128)(2,1)} %param.7) | copy-start | bytes 589828
  6.4 1.6 %collective-permute-start = (bf16[1,128,768]{2,1,0:T(8,128)(2,1)S(1)}, bf16[1,128,768]{2,1,0:T(8,128)(2,1)S(1)}, u32[]{:S(2)}, u32[]{:S(2)}) collective-permute-start(bf16[1,128,768]{2,1,0:T(8,128)(2,1)S(1)} %get-tuple-element.18), channel_id=1, source_target_pairs={{0,8},{8,0},{16,24},{24,16},{1,9},{9,1},{17,25},{25,17},{2,10},{10... | collective-permute-start | bytes 589832 | tf_op jit(solution)/shard_map/ppermute | solution.py:263
  8.0 8.2 %collective-permute-start.1 = (bf16[128,768]{1,0:T(8,128)(2,1)S(1)}, bf16[128,768]{1,0:T(8,128)(2,1)S(1)}, u32[]{:S(2)}, u32[]{:S(2)}) collective-permute-start(bf16[128,768]{1,0:T(8,128)(2,1)S(1)} %bitcast.5), channel_id=1, source_target_pairs={{0,16},{8,24},{16,0},{24,8},{1,17},{9,25},{17,1},{25,9},{2,18},{10... | collective-permute-start | bytes 589832 | tf_op jit(solution)/shard_map/ppermute | solution.py:269
  15.4 1.5 %collective-permute-start.2 = (bf16[128,768]{1,0:T(8,128)(2,1)S(1)}, bf16[128,768]{1,0:T(8,128)(2,1)S(1)}, u32[]{:S(2)}, u32[]{:S(2)}) collective-permute-start(bf16[128,768]{1,0:T(8,128)(2,1)S(1)} %bitcast.4), channel_id=1, source_target_pairs={{0,8},{8,0},{16,24},{24,16},{1,9},{9,1},{17,25},{25,17},{2,10},{10... | collective-permute-start | bytes 589832 | tf_op jit(solution)/shard_map/ppermute | solution.py:271
  17.0 5.6 %collective-permute-start.3 = (bf16[64,768]{1,0:T(8,128)(2,1)S(1)}, bf16[64,768]{1,0:T(8,128)(2,1)S(1)}, u32[]{:S(2)}, u32[]{:S(2)}) collective-permute-start(bf16[64,768]{1,0:T(8,128)(2,1)S(1)} %get-tuple-element.24.refs_0_), channel_id=1, source_target_pairs={{0,1},{1,3},{3,5},{5,7},{7,6},{6,4},{4,2},{2,0},{8,9},{9,11},{11,1... | collective-permute-start | bytes 294920 | tf_op jit(solution)/shard_map/ppermute | solution.py:280
  18.7 5.7 %collective-permute-start.6 = (bf16[72,768]{1,0:T(8,128)(2,1)S(1)}, bf16[72,768]{1,0:T(8,128)(2,1)S(1)}, u32[]{:S(2)}, u32[]{:S(2)}) collective-permute-start(bf16[72,768]{1,0:T(8,128)(2,1)S(1)} %get-tuple-element.25.refs_1_), channel_id=1, source_target_pairs={{0,2},{1,0},{3,1},{5,3},{7,5},{6,7},{4,6},{2,4},{8,10},{9,8},{11,9... | collective-permute-start | bytes 331784 | tf_op jit(solution)/shard_map/ppermute | solution.py:280
  19.1 5.8 %collective-permute-start.4 = (bf16[72,768]{1,0:T(8,128)(2,1)S(1)}, bf16[72,768]{1,0:T(8,128)(2,1)S(1)}, u32[]{:S(2)}, u32[]{:S(2)}) collective-permute-start(bf16[72,768]{1,0:T(8,128)(2,1)S(1)} %get-tuple-element.25.refs_1_), channel_id=1, source_target_pairs={{0,1},{1,3},{3,5},{5,7},{7,6},{6,4},{4,2},{2,0},{8,9},{9,11},{11,1... | collective-permute-start | bytes 331784 | tf_op jit(solution)/shard_map/ppermute | solution.py:280
  20.8 5.7 %collective-permute-start.5 = (bf16[64,768]{1,0:T(8,128)(2,1)S(1)}, bf16[64,768]{1,0:T(8,128)(2,1)S(1)}, u32[]{:S(2)}, u32[]{:S(2)}) collective-permute-start(bf16[64,768]{1,0:T(8,128)(2,1)S(1)} %get-tuple-element.24.refs_0_), channel_id=1, source_target_pairs={{0,2},{1,0},{3,1},{5,3},{7,5},{6,7},{4,6},{2,4},{8,10},{9,8},{11,9... | collective-permute-start | bytes 294920 | tf_op jit(solution)/shard_map/ppermute | solution.py:280
  22.5 5.5 %collective-permute-start.7 = (bf16[64,768]{1,0:T(8,128)(2,1)S(1)}, bf16[64,768]{1,0:T(8,128)(2,1)S(1)}, u32[]{:S(2)}, u32[]{:S(2)}) collective-permute-start(bf16[64,768]{1,0:T(8,128)(2,1)S(1)} %collective-permute-done.3.refs_2_), channel_id=1, source_target_pairs={{0,1},{1,3},{3,5},{5,7},{7,6},{6,4},{4,2},{2,0},{8,9},{9,11},{11,1... | collective-permute-start | bytes 294920 | tf_op jit(solution)/shard_map/ppermute | solution.py:280
  24.5 8.5 %collective-permute-start.10 = (bf16[72,768]{1,0:T(8,128)(2,1)S(1)}, bf16[72,768]{1,0:T(8,128)(2,1)S(1)}, u32[]{:S(2)}, u32[]{:S(2)}) collective-permute-start(bf16[72,768]{1,0:T(8,128)(2,1)S(1)} %collective-permute-done.6.refs_5_), channel_id=1, source_target_pairs={{0,2},{1,0},{3,1},{5,3},{7,5},{6,7},{4,6},{2,4},{8,10},{9,8},{11,9... | collective-permute-start | bytes 331784 | tf_op jit(solution)/shard_map/ppermute | solution.py:280
  24.9 8.5 %collective-permute-start.8 = (bf16[72,768]{1,0:T(8,128)(2,1)S(1)}, bf16[72,768]{1,0:T(8,128)(2,1)S(1)}, u32[]{:S(2)}, u32[]{:S(2)}) collective-permute-start(bf16[72,768]{1,0:T(8,128)(2,1)S(1)} %collective-permute-done.4.refs_3_), channel_id=1, source_target_pairs={{0,1},{1,3},{3,5},{5,7},{7,6},{6,4},{4,2},{2,0},{8,9},{9,11},{11,1... | collective-permute-start | bytes 331784 | tf_op jit(solution)/shard_map/ppermute | solution.py:280
  26.5 6.0 %collective-permute-start.9 = (bf16[64,768]{1,0:T(8,128)(2,1)S(1)}, bf16[64,768]{1,0:T(8,128)(2,1)S(1)}, u32[]{:S(2)}, u32[]{:S(2)}) collective-permute-start(bf16[64,768]{1,0:T(8,128)(2,1)S(1)} %collective-permute-done.5.refs_4_), channel_id=1, source_target_pairs={{0,2},{1,0},{3,1},{5,3},{7,5},{6,7},{4,6},{2,4},{8,10},{9,8},{11,9... | collective-permute-start | bytes 294920 | tf_op jit(solution)/shard_map/ppermute | solution.py:280
  28.1 7.8 %collective-permute-start.13 = (bf16[64,768]{1,0:T(8,128)(2,1)S(1)}, bf16[64,768]{1,0:T(8,128)(2,1)S(1)}, u32[]{:S(2)}, u32[]{:S(2)}) collective-permute-start(bf16[64,768]{1,0:T(8,128)(2,1)S(1)} %collective-permute-done.7.refs_6_), channel_id=1, source_target_pairs={{0,1},{1,3},{3,5},{5,7},{7,6},{6,4},{4,2},{2,0},{8,9},{9,11},{11,1... | collective-permute-start | bytes 294920 | tf_op jit(solution)/shard_map/ppermute | solution.py:280
  29.9 12.0 %collective-permute-start.11 = (bf16[64,768]{1,0:T(8,128)(2,1)S(1)}, bf16[64,768]{1,0:T(8,128)(2,1)S(1)}, u32[]{:S(2)}, u32[]{:S(2)}) collective-permute-start(bf16[64,768]{1,0:T(8,128)(2,1)S(1)} %collective-permute-done.7.refs_6_), channel_id=1, source_target_pairs={{0,3},{1,5},{3,7},{5,6},{7,4},{6,2},{4,0},{2,1},{8,11},{9,13},{11,... | collective-permute-start | bytes 294920 | tf_op jit(solution)/shard_map/ppermute | solution.py:282
  32.5 6.5 %collective-permute-start.15 = (bf16[64,768]{1,0:T(8,128)(2,1)S(1)}, bf16[64,768]{1,0:T(8,128)(2,1)S(1)}, u32[]{:S(2)}, u32[]{:S(2)}) collective-permute-start(bf16[64,768]{1,0:T(8,128)(2,1)S(1)} %collective-permute-done.9.refs_8_), channel_id=1, source_target_pairs={{0,2},{1,0},{3,1},{5,3},{7,5},{6,7},{4,6},{2,4},{8,10},{9,8},{11,9... | collective-permute-start | bytes 294920 | tf_op jit(solution)/shard_map/ppermute | solution.py:280
  33.0 6.0 %collective-permute-start.16 = (bf16[72,768]{1,0:T(8,128)(2,1)S(1)}, bf16[72,768]{1,0:T(8,128)(2,1)S(1)}, u32[]{:S(2)}, u32[]{:S(2)}) collective-permute-start(bf16[72,768]{1,0:T(8,128)(2,1)S(1)} %collective-permute-done.10.refs_9_), channel_id=1, source_target_pairs={{0,2},{1,0},{3,1},{5,3},{7,5},{6,7},{4,6},{2,4},{8,10},{9,8},{11,9... | collective-permute-start | bytes 331784 | tf_op jit(solution)/shard_map/ppermute | solution.py:280
  33.4 8.6 %collective-permute-start.12 = (bf16[72,768]{1,0:T(8,128)(2,1)S(1)}, bf16[72,768]{1,0:T(8,128)(2,1)S(1)}, u32[]{:S(2)}, u32[]{:S(2)}) collective-permute-start(bf16[72,768]{1,0:T(8,128)(2,1)S(1)} %collective-permute-done.10.refs_9_), channel_id=1, source_target_pairs={{0,4},{1,2},{3,0},{5,1},{7,3},{6,5},{4,7},{2,6},{8,12},{9,10},{11,... | collective-permute-start | bytes 331784 | tf_op jit(solution)/shard_map/ppermute | solution.py:282
  35.8 5.0 %collective-permute-start.14 = (bf16[72,768]{1,0:T(8,128)(2,1)S(1)}, bf16[72,768]{1,0:T(8,128)(2,1)S(1)}, u32[]{:S(2)}, u32[]{:S(2)}) collective-permute-start(bf16[72,768]{1,0:T(8,128)(2,1)S(1)} %collective-permute-done.8.refs_7_), channel_id=1, source_target_pairs={{0,1},{1,3},{3,5},{5,7},{7,6},{6,4},{4,2},{2,0},{8,9},{9,11},{11,1... | collective-permute-start | bytes 331784 | tf_op jit(solution)/shard_map/ppermute | solution.py:280

commit v13 on v12

--- a/solution.py
+++ b/solution.py
@@ -91,7 +91,7 @@
 
 def down(hidden, weight, tok, chips_y, own):
     inner, width = weight.shape
-    depth = cut(inner, 1536)
+    depth = cut(inner, 1536 if own else 768)
     parts = inner // depth
     chips = 1 if own else chips_y - 1
     tokens = chips * CORES * tok
@@ -150,12 +150,11 @@
     (weight,) = take(1)
     shift_in, sums_in, total_in = [None] * 3 if first else take(3)
     if last:
-        (out,) = take(1)
+        out, lhs, block, sems = refs
     elif first:
-        stream, shift_out, sums_out, total_out = take(4)
+        stream, shift_out, sums_out, total_out, lhs = refs
     else:
-        sums_out, total_out = take(2)
-    (lhs,) = take(1)
+        sums_out, total_out, lhs = refs
     total = total_in if last else total_out
     tok = shift_in.shape[0] if not first else shift_out.shape[0]
     width = lhs.shape[2]
@@ -191,6 +190,10 @@
         var = jnp.maximum(two / (width * count) - off * off, 0.0)
         scale = 1.0 / jnp.sqrt(var + 1e-06)
 
+    def leave(n):
+        span = pl.ds(n * strip, strip)
+        return pltpu.make_async_copy(block.at[:, span], out.at[:, span], sems.at[n])
+
     for n in range(strips):
         span = pl.ds(n * strip, strip)
         for i in range(len(hops)):
@@ -201,9 +204,13 @@
             else:
                 value = value + product
         if last:
-            out[:, span] = ((value[0:tok] - off * value[tok : tok + 1]) * scale).astype(out.dtype)
+            block[:, span] = ((value[0:tok] - off * value[tok : tok + 1]) * scale).astype(block.dtype)
+            leave(n).start()
         else:
             total[:, span] = value
+    if last:
+        for n in range(strips):
+            leave(n).wait()
 
 
 def project(pieces, hops, weight, state, cycle, last):
@@ -217,8 +224,10 @@
     flat = [part for parts in pieces for part in parts]
     base = len(flat) + 1
     state = () if first else state
+    extra = []
     if last:
         out_shape, aliases = jax.ShapeDtypeStruct((tok, columns), jnp.bfloat16), {}
+        extra = [pltpu.VMEM((tok, columns), jnp.bfloat16), pltpu.SemaphoreType.DMA((columns // cut(columns, 512),))]
     elif first:
         out_shape, aliases = (jax.ShapeDtypeStruct((tok, width), jnp.bfloat16), shift, sums, total), {}
     else:
@@ -227,10 +236,8 @@
         functools.partial(project_kernel, cycle, hops, [len(parts) for parts in pieces], first, last),
         out_shape=out_shape,
         in_specs=[VMEM] * (base + len(state)),
-        out_specs=jax.tree.map(lambda _: VMEM, out_shape),
-        scratch_shapes=[
-            pltpu.VMEM((len(hops), tok + EXTRA, width), jnp.bfloat16),
-        ],
+        out_specs=jax.tree.map(lambda _: HBM if last else VMEM, out_shape),
+        scratch_shapes=[pltpu.VMEM((len(hops), tok + EXTRA, width), jnp.bfloat16), *extra],
         input_output_aliases=aliases,
         compiler_params=pltpu.CompilerParams(vmem_limit_bytes=12 * MIB),
         cost_estimate=pl.CostEstimate(
@@ -272,17 +279,15 @@
         upper, lower = merge(others, keep[0], got, gain[None, :])
 
         up, back = [upper, lower], [upper, lower]
-        pieces, opposite = [[upper, lower]], None
+        pieces, hops = [[upper, lower]], [0]
         for step in range(1, half):
-            if step == half - 1:
-                opposite = up[0], back[1]
             for i in range(2):
                 up[i], back[i] = lax.ppermute(up[i], "col", shift(1)), lax.ppermute(back[i], "col", shift(-1))
-            if opposite:
-                opposite = lax.ppermute(opposite[0], "col", shift(2)), lax.ppermute(opposite[1], "col", shift(-2))
             pieces += [list(up), list(back)]
-        hops = [0] + [hop for step in range(1, half) for hop in (-step, step)]
+            hops += [-step, step]
         stream, state = project(pieces[:-2], hops[:-2], qk_weight, None, cycle, False)
+        back[1], state = lax.optimization_barrier((back[1], state))
+        opposite = [lax.ppermute(up[0], "col", shift(1)), lax.ppermute(back[1], "col", shift(-1))]
         state = project(pieces[-2:], hops[-2:], qk_weight, state, cycle, False)
         return stream, project([opposite], [half], qk_weight, state, cycle, True)
 

time: 43.6 us -> 45.4 us (1.041)
  waiting for transfers between devices: 7.14 us -> 10.8 us
  starting transfers between devices: 20 us -> 18.4 us
    ppermute x6, starting transfers between devices: 2.42 us -> 8.88 us  [per_device(): lax.ppermute(back[i], 'col', shift(-1))]
    ppermute x6, starting transfers between devices: 9.09 us -> 3.92 us  [per_device(): lax.ppermute(up[i], 'col', shift(1))]
    ppermute x2, waiting for transfers between devices: 0.08 us -> 3.12 us  [the longest x1 3.12 us: per_device(): lax.ppermute(up[0], 'col', shift(1))]
    ppermute x2, starting transfers between devices: 5 us -> 2.03 us  [the longest x1 1.63 us: per_device(): lax.ppermute(back[1], 'col', shift(-1))]
    ppermute x6, waiting for transfers between devices: 0.2 us -> 1.54 us  [per_device(): lax.ppermute(back[i], 'col', shift(-1))]
    ppermute x6, waiting for transfers between devices: 4.41 us -> 3.74 us  [per_device(): lax.ppermute(up[i], 'col', shift(1))]
  transfers between devices with their start and end apart: 17 -> 17, of which waited for: 8 -> 8; matrix products, arithmetic and copies ran while one was open for 0% -> 0% of each run, Pallas kernels for 19% -> 18%
where the time goes in v13:
time: 45.4 us; the launch traced here: 45.3 us
  starting transfers between devices  18.4 us (41%)
  Pallas kernels  15.3 us (34%)
  waiting for transfers between devices  10.8 us (24%)
  between operations  0.72 us (2%)
    pallas_call x2, Pallas kernels, down(): pl.pallas_call(functools.partial(down_kernel, chips_y, tok, parts, own),...  10 us
    ppermute x6, starting transfers between devices, per_device(): lax.ppermute(back[i], 'col', shift(-1))  8.88 us
    pallas_call x3, Pallas kernels, project(): pl.pallas_call(functools.partial(project_kernel, cycle, hops, [len(parts)...  5.16 us
    ppermute x6, starting transfers between devices, per_device(): lax.ppermute(up[i], 'col', shift(1))  3.92 us
    ppermute x6, waiting for transfers between devices, per_device(): lax.ppermute(up[i], 'col', shift(1))  3.74 us
    ppermute x1, waiting for transfers between devices, per_device(): lax.ppermute(up[0], 'col', shift(1))  3.12 us
    ppermute x1, starting transfers between devices, per_device(): lax.ppermute(both[step - 1], 'row', move).astype(jnp.float32)  2.95 us
    ppermute x1, starting transfers between devices, per_device(): lax.ppermute(back[1], 'col', shift(-1))  1.63 us
  transfers between devices with their start and end apart: 17, of which 8 were waited for; matrix products, arithmetic and copies ran while one was open for 0% of the time, Pallas kernels for 18%

profile of v13, /device:TPU:0, one launch (start us, length us, event | category | flops | bytes accessed | tf_op | source)
XLA Modules:
  0.0 45.3 jit_solution(14021917745881209352)
XLA Ops:
  0.7 5.6 %down.2 = (bf16[1,128,768]{2,1,0:T(8,128)(2,1)S(1)}, bf16[1,128,768]{2,1,0:T(8,128)(2,1)S(1)}, bf16[6144,768]{1,0:T(8,128)(2,1)S(1)}) custom-call(bf16[512,6144]{1,0:T(8,128)(2,1)} %hidden.2, bf16[6144,768]{1,0:T(8,128)(2,1)} %weight.1), custom_call_target="tpu_custom_call" | custom-call | flops 2415919104 | bytes 12582912 | tf_op jit(solution)/shard_map/down/pallas_call | solution.py:100
  6.3 0.5 %collective-permute-start = (bf16[1,128,768]{2,1,0:T(8,128)(2,1)S(1)}, bf16[1,128,768]{2,1,0:T(8,128)(2,1)S(1)}, u32[]{:S(2)}, u32[]{:S(2)}) collective-permute-start(bf16[1,128,768]{2,1,0:T(8,128)(2,1)S(1)} %get-tuple-element.22), channel_id=1, source_target_pairs={{0,8},{8,0},{16,24},{24,16},{1,9},{9,1},{17,25},{25,17},{2,10},{10... | collective-permute-start | bytes 589832 | tf_op jit(solution)/shard_map/ppermute | solution.py:270
  6.8 1.1 %collective-permute-done = bf16[1,128,768]{2,1,0:T(8,128)(2,1)S(1)} collective-permute-done((bf16[1,128,768]{2,1,0:T(8,128)(2,1)S(1)}, bf16[1,128,768]{2,1,0:T(8,128)(2,1)S(1)}, u32[]{:S(2)}, u32[]{:S(2)}) %collective-permute-start) | collective-permute-done | bytes 196640 | tf_op jit(solution)/shard_map/ppermute | solution.py:270
  7.9 3.0 %collective-permute-start.1 = (bf16[128,768]{1,0:T(8,128)(2,1)S(1)}, bf16[128,768]{1,0:T(8,128)(2,1)S(1)}, u32[]{:S(2)}, u32[]{:S(2)}) collective-permute-start(bf16[128,768]{1,0:T(8,128)(2,1)S(1)} %bitcast.5), channel_id=1, source_target_pairs={{0,16},{8,24},{16,0},{24,8},{1,17},{9,25},{17,1},{25,9},{2,18},{10... | collective-permute-start | bytes 589832 | tf_op jit(solution)/shard_map/ppermute | solution.py:276
  10.9 4.4 %down.3 = (bf16[1,128,768]{2,1,0:T(8,128)(2,1)S(1)}, bf16[1,128,768]{2,1,0:T(8,128)(2,1)S(1)}) custom-call(bf16[512,6144]{1,0:T(8,128)(2,1)} %hidden.2, bf16[6144,768]{1,0:T(8,128)(2,1)S(1)} %get-tuple-element.25.weight), custom_call_target="tpu_custom_call" | custom-call | flops 2415919104 | bytes 3145728 | tf_op jit(solution)/shard_map/down/pallas_call | solution.py:100
  15.4 0.7 %collective-permute-done.1 = bf16[128,768]{1,0:T(8,128)(2,1)S(1)} collective-permute-done((bf16[128,768]{1,0:T(8,128)(2,1)S(1)}, bf16[128,768]{1,0:T(8,128)(2,1)S(1)}, u32[]{:S(2)}, u32[]{:S(2)}) %collective-permute-start.1) | collective-permute-done | bytes 196640 | tf_op jit(solution)/shard_map/ppermute | solution.py:276
  16.1 0.7 %collective-permute-done.2.got = bf16[128,768]{1,0:T(8,128)(2,1)S(1)} collective-permute-done((bf16[128,768]{1,0:T(8,128)(2,1)S(1)}, bf16[128,768]{1,0:T(8,128)(2,1)S(1)}, u32[]{:S(2)}, u32[]{:S(2)}) %collective-permute-start.2) | collective-permute-done | bytes 196640 | tf_op jit(solution)/shard_map/ppermute | solution.py:278
  16.9 2.0 %collective-permute-start.6 = (bf16[72,768]{1,0:T(8,128)(2,1)S(1)}, bf16[72,768]{1,0:T(8,128)(2,1)S(1)}, u32[]{:S(2)}, u32[]{:S(2)}) collective-permute-start(bf16[72,768]{1,0:T(8,128)(2,1)S(1)} %get-tuple-element.29.refs_1_), channel_id=1, source_target_pairs={{0,2},{1,0},{3,1},{5,3},{7,5},{6,7},{4,6},{2,4},{8,10},{9,8},{11,9... | collective-permute-start | bytes 331784 | tf_op jit(solution)/shard_map/ppermute | solution.py:285
  19.0 1.8 %collective-permute-start.3 = (bf16[64,768]{1,0:T(8,128)(2,1)S(1)}, bf16[64,768]{1,0:T(8,128)(2,1)S(1)}, u32[]{:S(2)}, u32[]{:S(2)}) collective-permute-start(bf16[64,768]{1,0:T(8,128)(2,1)S(1)} %get-tuple-element.28.refs_0_), channel_id=1, source_target_pairs={{0,1},{1,3},{3,5},{5,7},{7,6},{6,4},{4,2},{2,0},{8,9},{9,11},{11,1... | collective-permute-start | bytes 294920 | tf_op jit(solution)/shard_map/ppermute | solution.py:285
  21.0 1.3 %collective-permute-done.6.refs_5_ = bf16[72,768]{1,0:T(8,128)(2,1)S(1)} collective-permute-done((bf16[72,768]{1,0:T(8,128)(2,1)S(1)}, bf16[72,768]{1,0:T(8,128)(2,1)S(1)}, u32[]{:S(2)}, u32[]{:S(2)}) %collective-permute-start.6) | collective-permute-done | bytes 110624 | tf_op jit(solution)/shard_map/ppermute | solution.py:285
  22.3 2.5 %collective-permute-start.10 = (bf16[72,768]{1,0:T(8,128)(2,1)S(1)}, bf16[72,768]{1,0:T(8,128)(2,1)S(1)}, u32[]{:S(2)}, u32[]{:S(2)}) collective-permute-start(bf16[72,768]{1,0:T(8,128)(2,1)S(1)} %collective-permute-done.6.refs_5_), channel_id=1, source_target_pairs={{0,2},{1,0},{3,1},{5,3},{7,5},{6,7},{4,6},{2,4},{8,10},{9,8},{11,9... | collective-permute-start | bytes 331784 | tf_op jit(solution)/shard_map/ppermute | solution.py:285
  24.9 1.0 %collective-permute-done.3.refs_2_ = bf16[64,768]{1,0:T(8,128)(2,1)S(1)} collective-permute-done((bf16[64,768]{1,0:T(8,128)(2,1)S(1)}, bf16[64,768]{1,0:T(8,128)(2,1)S(1)}, u32[]{:S(2)}, u32[]{:S(2)}) %collective-permute-start.3) | collective-permute-done | bytes 98336 | tf_op jit(solution)/shard_map/ppermute | solution.py:285
  25.9 0.8 %collective-permute-start.7 = (bf16[64,768]{1,0:T(8,128)(2,1)S(1)}, bf16[64,768]{1,0:T(8,128)(2,1)S(1)}, u32[]{:S(2)}, u32[]{:S(2)}) collective-permute-start(bf16[64,768]{1,0:T(8,128)(2,1)S(1)} %collective-permute-done.3.refs_2_), channel_id=1, source_target_pairs={{0,1},{1,3},{3,5},{5,7},{7,6},{6,4},{4,2},{2,0},{8,9},{9,11},{11,1... | collective-permute-start | bytes 294920 | tf_op jit(solution)/shard_map/ppermute | solution.py:285
  26.7 1.3 %collective-permute-start.9 = (bf16[64,768]{1,0:T(8,128)(2,1)S(1)}, bf16[64,768]{1,0:T(8,128)(2,1)S(1)}, u32[]{:S(2)}, u32[]{:S(2)}) collective-permute-start(bf16[64,768]{1,0:T(8,128)(2,1)S(1)} %collective-permute-done.5.refs_4_), channel_id=1, source_target_pairs={{0,2},{1,0},{3,1},{5,3},{7,5},{6,7},{4,6},{2,4},{8,10},{9,8},{11,9... | collective-permute-start | bytes 294920 | tf_op jit(solution)/shard_map/ppermute | solution.py:285
  27.9 2.7 %collective-permute-done.7.refs_6_ = bf16[64,768]{1,0:T(8,128)(2,1)S(1)} collective-permute-done((bf16[64,768]{1,0:T(8,128)(2,1)S(1)}, bf16[64,768]{1,0:T(8,128)(2,1)S(1)}, u32[]{:S(2)}, u32[]{:S(2)}) %collective-permute-start.7) | collective-permute-done | bytes 98336 | tf_op jit(solution)/shard_map/ppermute | solution.py:285
  30.7 0.6 %collective-permute-start.11 = (bf16[64,768]{1,0:T(8,128)(2,1)S(1)}, bf16[64,768]{1,0:T(8,128)(2,1)S(1)}, u32[]{:S(2)}, u32[]{:S(2)}) collective-permute-start(bf16[64,768]{1,0:T(8,128)(2,1)S(1)} %collective-permute-done.7.refs_6_), channel_id=1, source_target_pairs={{0,1},{1,3},{3,5},{5,7},{7,6},{6,4},{4,2},{2,0},{8,9},{9,11},{11,1... | collective-permute-start | bytes 294920 | tf_op jit(solution)/shard_map/ppermute | solution.py:285
  31.3 1.4 %collective-permute-start.16 = (bf16[64,768]{1,0:T(8,128)(2,1)S(1)}, bf16[64,768]{1,0:T(8,128)(2,1)S(1)}, u32[]{:S(2)}, u32[]{:S(2)}) collective-permute-start(bf16[64,768]{1,0:T(8,128)(2,1)S(1)} %collective-permute-done.9.refs_8_), channel_id=1, source_target_pairs={{0,2},{1,0},{3,1},{5,3},{7,5},{6,7},{4,6},{2,4},{8,10},{9,8},{11,9... | collective-permute-start | bytes 294920 | tf_op jit(solution)/shard_map/ppermute | solution.py:285
  32.7 1.6 %collective-permute-start.13 = (bf16[72,768]{1,0:T(8,128)(2,1)S(1)}, bf16[72,768]{1,0:T(8,128)(2,1)S(1)}, u32[]{:S(2)}, u32[]{:S(2)}) collective-permute-start(bf16[72,768]{1,0:T(8,128)(2,1)S(1)} %collective-permute-done.10.refs_9_), channel_id=1, source_target_pairs={{0,2},{1,0},{3,1},{5,3},{7,5},{6,7},{4,6},{2,4},{8,10},{9,8},{11,9... | collective-permute-start | bytes 331784 | tf_op jit(solution)/shard_map/ppermute | solution.py:285
  34.3 0.4 collective-permute-start.15
  34.7 2.7 %project.3 = (bf16[128,768]{1,0:T(8,128)(2,1)}, f32[128,1]{1,0:T(8,128)S(1)}, f32[2,128,1]{2,1,0:T(8,128)S(1)}, f32[144,1536]{1,0:T(8,128)S(1)}) custom-call(bf16[64,768]{1,0:T(8,128)(2,1)S(1)} %get-tuple-element.28.refs_0_, bf16[72,768]{1,0:T(8,128)(2,1)S(1)} %get-tuple-element.29.refs_1_, bf16[64,768]{1,0:T(8,128)(2,1)S(1)} %collective-permute-done.3.refs_2_, ...), custom_call_target="tpu_custom_call" | custom-call | flops 1698693120 | tf_op jit(solution)/shard_map/project/pallas_call | solution.py:235
  37.7 1.6 %collective-permute-start.14 = (bf16[72,768]{1,0:T(8,128)(2,1)S(1)}, bf16[72,768]{1,0:T(8,128)(2,1)S(1)}, u32[]{:S(2)}, u32[]{:S(2)}) collective-permute-start(bf16[72,768]{1,0:T(8,128)(2,1)S(1)} %collective-permute-done.13.refs_3_), channel_id=1, source_target_pairs={{0,2},{1,0},{3,1},{5,3},{7,5},{6,7},{4,6},{2,4},{8,10},{9,8},{11,9... | collective-permute-start | bytes 331784 | tf_op jit(solution)/shard_map/ppermute | solution.py:290
  39.7 1.1 %project.4 = (f32[2,128,1]{2,1,0:T(8,128)S(1)}, f32[144,1536]{1,0:T(8,128)S(1)}) custom-call(bf16[64,768]{1,0:T(8,128)(2,1)S(1)} %collective-permute-done.11.refs_0_, bf16[72,768]{1,0:T(8,128)(2,1)S(1)} %collective-permute-done.15.refs_1_, bf16[64,768]{1,0:T(8,128)(2,1)S(1)} %collective-permute-done.16.refs_2_, ...), custom_call_target="tpu_custom_call", output_to_operand_aliasing={{0}: (6, {}), {1}: (7, {})} | custom-call | flops 679477248 | tf_op jit(solution)/shard_map/project/pallas_call | solution.py:235
  40.8 3.1 %collective-permute-done.12.refs_0_ = bf16[64,768]{1,0:T(8,128)(2,1)S(1)} collective-permute-done((bf16[64,768]{1,0:T(8,128)(2,1)S(1)}, bf16[64,768]{1,0:T(8,128)(2,1)S(1)}, u32[]{:S(2)}, u32[]{:S(2)}) %collective-permute-start.12) | collective-permute-done | bytes 98336 | tf_op jit(solution)/shard_map/ppermute | solution.py:290
  43.9 1.3 %project.5 = bf16[128,1536]{1,0:T(8,128)(2,1)} custom-call(bf16[64,768]{1,0:T(8,128)(2,1)S(1)} %collective-permute-done.12.refs_0_, bf16[72,768]{1,0:T(8,128)(2,1)S(1)} %collective-permute-done.14.refs_1_, bf16[6144,1536]{1,0:T(8,128)(2,1)S(1)} %copy-done, f32[128,1]{1,0:T(8,128)S(1)} %get-tuple-element.35.refs_5_.refs_3_, ...), custom_call_target="tpu_custom_call" | custom-call | flops 339738624 | tf_op jit(solution)/shard_map/project/pallas_call | solution.py:235
  (25 shorter events, 1.3 us)
Async XLA Ops:
  0.6 6.2 %copy-start.2 = (bf16[768]{0:T(1024)(128)(2,1)S(1)}, bf16[768]{0:T(1024)(128)(2,1)}, u32[]{:S(2)}) copy-start(bf16[768]{0:T(1024)(128)(2,1)} %param.8) | copy-start | bytes 4612
  0.6 34.1 %copy-start = (bf16[6144,1536]{1,0:T(8,128)(2,1)S(1)}, bf16[6144,1536]{1,0:T(8,128)(2,1)}, u32[]{:S(2)}) copy-start(bf16[6144,1536]{1,0:T(8,128)(2,1)} %refs_2_.1) | copy-start | bytes 56623108
  6.3 9.8 %copy-start.1 = (bf16[128,768]{1,0:T(8,128)(2,1)S(1)}, bf16[128,768]{1,0:T(8,128)(2,1)}, u32[]{:S(2)}) copy-start(bf16[128,768]{1,0:T(8,128)(2,1)} %param.7) | copy-start | bytes 589828
  6.3 1.6 %collective-permute-start = (bf16[1,128,768]{2,1,0:T(8,128)(2,1)S(1)}, bf16[1,128,768]{2,1,0:T(8,128)(2,1)S(1)}, u32[]{:S(2)}, u32[]{:S(2)}) collective-permute-start(bf16[1,128,768]{2,1,0:T(8,128)(2,1)S(1)} %get-tuple-element.22), channel_id=1, source_target_pairs={{0,8},{8,0},{16,24},{24,16},{1,9},{9,1},{17,25},{25,17},{2,10},{10... | collective-permute-start | bytes 589832 | tf_op jit(solution)/shard_map/ppermute | solution.py:270
  7.9 8.2 %collective-permute-start.1 = (bf16[128,768]{1,0:T(8,128)(2,1)S(1)}, bf16[128,768]{1,0:T(8,128)(2,1)S(1)}, u32[]{:S(2)}, u32[]{:S(2)}) collective-permute-start(bf16[128,768]{1,0:T(8,128)(2,1)S(1)} %bitcast.5), channel_id=1, source_target_pairs={{0,16},{8,24},{16,0},{24,8},{1,17},{9,25},{17,1},{25,9},{2,18},{10... | collective-permute-start | bytes 589832 | tf_op jit(solution)/shard_map/ppermute | solution.py:276
  15.3 1.5 %collective-permute-start.2 = (bf16[128,768]{1,0:T(8,128)(2,1)S(1)}, bf16[128,768]{1,0:T(8,128)(2,1)S(1)}, u32[]{:S(2)}, u32[]{:S(2)}) collective-permute-start(bf16[128,768]{1,0:T(8,128)(2,1)S(1)} %bitcast.4), channel_id=1, source_target_pairs={{0,8},{8,0},{16,24},{24,16},{1,9},{9,1},{17,25},{25,17},{2,10},{10... | collective-permute-start | bytes 589832 | tf_op jit(solution)/shard_map/ppermute | solution.py:278
  16.9 5.4 %collective-permute-start.6 = (bf16[72,768]{1,0:T(8,128)(2,1)S(1)}, bf16[72,768]{1,0:T(8,128)(2,1)S(1)}, u32[]{:S(2)}, u32[]{:S(2)}) collective-permute-start(bf16[72,768]{1,0:T(8,128)(2,1)S(1)} %get-tuple-element.29.refs_1_), channel_id=1, source_target_pairs={{0,2},{1,0},{3,1},{5,3},{7,5},{6,7},{4,6},{2,4},{8,10},{9,8},{11,9... | collective-permute-start | bytes 331784 | tf_op jit(solution)/shard_map/ppermute | solution.py:285
  18.9 5.9 %collective-permute-start.4 = (bf16[72,768]{1,0:T(8,128)(2,1)S(1)}, bf16[72,768]{1,0:T(8,128)(2,1)S(1)}, u32[]{:S(2)}, u32[]{:S(2)}) collective-permute-start(bf16[72,768]{1,0:T(8,128)(2,1)S(1)} %get-tuple-element.29.refs_1_), channel_id=1, source_target_pairs={{0,1},{1,3},{3,5},{5,7},{7,6},{6,4},{4,2},{2,0},{8,9},{9,11},{11,1... | collective-permute-start | bytes 331784 | tf_op jit(solution)/shard_map/ppermute | solution.py:285
  19.0 7.0 %collective-permute-start.3 = (bf16[64,768]{1,0:T(8,128)(2,1)S(1)}, bf16[64,768]{1,0:T(8,128)(2,1)S(1)}, u32[]{:S(2)}, u32[]{:S(2)}) collective-permute-start(bf16[64,768]{1,0:T(8,128)(2,1)S(1)} %get-tuple-element.28.refs_0_), channel_id=1, source_target_pairs={{0,1},{1,3},{3,5},{5,7},{7,6},{6,4},{4,2},{2,0},{8,9},{9,11},{11,1... | collective-permute-start | bytes 294920 | tf_op jit(solution)/shard_map/ppermute | solution.py:285
  20.8 5.9 %collective-permute-start.5 = (bf16[64,768]{1,0:T(8,128)(2,1)S(1)}, bf16[64,768]{1,0:T(8,128)(2,1)S(1)}, u32[]{:S(2)}, u32[]{:S(2)}) collective-permute-start(bf16[64,768]{1,0:T(8,128)(2,1)S(1)} %get-tuple-element.28.refs_0_), channel_id=1, source_target_pairs={{0,2},{1,0},{3,1},{5,3},{7,5},{6,7},{4,6},{2,4},{8,10},{9,8},{11,9... | collective-permute-start | bytes 294920 | tf_op jit(solution)/shard_map/ppermute | solution.py:285
  22.3 10.4 %collective-permute-start.10 = (bf16[72,768]{1,0:T(8,128)(2,1)S(1)}, bf16[72,768]{1,0:T(8,128)(2,1)S(1)}, u32[]{:S(2)}, u32[]{:S(2)}) collective-permute-start(bf16[72,768]{1,0:T(8,128)(2,1)S(1)} %collective-permute-done.6.refs_5_), channel_id=1, source_target_pairs={{0,2},{1,0},{3,1},{5,3},{7,5},{6,7},{4,6},{2,4},{8,10},{9,8},{11,9... | collective-permute-start | bytes 331784 | tf_op jit(solution)/shard_map/ppermute | solution.py:285
  24.8 9.5 %collective-permute-start.8 = (bf16[72,768]{1,0:T(8,128)(2,1)S(1)}, bf16[72,768]{1,0:T(8,128)(2,1)S(1)}, u32[]{:S(2)}, u32[]{:S(2)}) collective-permute-start(bf16[72,768]{1,0:T(8,128)(2,1)S(1)} %collective-permute-done.4.refs_3_), channel_id=1, source_target_pairs={{0,1},{1,3},{3,5},{5,7},{7,6},{6,4},{4,2},{2,0},{8,9},{9,11},{11,1... | collective-permute-start | bytes 331784 | tf_op jit(solution)/shard_map/ppermute | solution.py:285
  25.9 4.7 %collective-permute-start.7 = (bf16[64,768]{1,0:T(8,128)(2,1)S(1)}, bf16[64,768]{1,0:T(8,128)(2,1)S(1)}, u32[]{:S(2)}, u32[]{:S(2)}) collective-permute-start(bf16[64,768]{1,0:T(8,128)(2,1)S(1)} %collective-permute-done.3.refs_2_), channel_id=1, source_target_pairs={{0,1},{1,3},{3,5},{5,7},{7,6},{6,4},{4,2},{2,0},{8,9},{9,11},{11,1... | collective-permute-start | bytes 294920 | tf_op jit(solution)/shard_map/ppermute | solution.py:285
  26.7 4.6 %collective-permute-start.9 = (bf16[64,768]{1,0:T(8,128)(2,1)S(1)}, bf16[64,768]{1,0:T(8,128)(2,1)S(1)}, u32[]{:S(2)}, u32[]{:S(2)}) collective-permute-start(bf16[64,768]{1,0:T(8,128)(2,1)S(1)} %collective-permute-done.5.refs_4_), channel_id=1, source_target_pairs={{0,2},{1,0},{3,1},{5,3},{7,5},{6,7},{4,6},{2,4},{8,10},{9,8},{11,9... | collective-permute-start | bytes 294920 | tf_op jit(solution)/shard_map/ppermute | solution.py:285
  30.7 8.7 %collective-permute-start.11 = (bf16[64,768]{1,0:T(8,128)(2,1)S(1)}, bf16[64,768]{1,0:T(8,128)(2,1)S(1)}, u32[]{:S(2)}, u32[]{:S(2)}) collective-permute-start(bf16[64,768]{1,0:T(8,128)(2,1)S(1)} %collective-permute-done.7.refs_6_), channel_id=1, source_target_pairs={{0,1},{1,3},{3,5},{5,7},{7,6},{6,4},{4,2},{2,0},{8,9},{9,11},{11,1... | collective-permute-start | bytes 294920 | tf_op jit(solution)/shard_map/ppermute | solution.py:285
  31.3 8.4 %collective-permute-start.16 = (bf16[64,768]{1,0:T(8,128)(2,1)S(1)}, bf16[64,768]{1,0:T(8,128)(2,1)S(1)}, u32[]{:S(2)}, u32[]{:S(2)}) collective-permute-start(bf16[64,768]{1,0:T(8,128)(2,1)S(1)} %collective-permute-done.9.refs_8_), channel_id=1, source_target_pairs={{0,2},{1,0},{3,1},{5,3},{7,5},{6,7},{4,6},{2,4},{8,10},{9,8},{11,9... | collective-permute-start | bytes 294920 | tf_op jit(solution)/shard_map/ppermute | solution.py:285
  32.7 5.0 %collective-permute-start.13 = (bf16[72,768]{1,0:T(8,128)(2,1)S(1)}, bf16[72,768]{1,0:T(8,128)(2,1)S(1)}, u32[]{:S(2)}, u32[]{:S(2)}) collective-permute-start(bf16[72,768]{1,0:T(8,128)(2,1)S(1)} %collective-permute-done.10.refs_9_), channel_id=1, source_target_pairs={{0,2},{1,0},{3,1},{5,3},{7,5},{6,7},{4,6},{2,4},{8,10},{9,8},{11,9... | collective-permute-start | bytes 331784 | tf_op jit(solution)/shard_map/ppermute | solution.py:285
  34.3 5.5 %collective-permute-start.15 = (bf16[72,768]{1,0:T(8,128)(2,1)S(1)}, bf16[72,768]{1,0:T(8,128)(2,1)S(1)}, u32[]{:S(2)}, u32[]{:S(2)}) collective-permute-start(bf16[72,768]{1,0:T(8,128)(2,1)S(1)} %collective-permute-done.8.refs_7_), channel_id=1, source_target_pairs={{0,1},{1,3},{3,5},{5,7},{7,6},{6,4},{4,2},{2,0},{8,9},{9,11},{11,1... | collective-permute-start | bytes 331784 | tf_op jit(solution)/shard_map/ppermute | solution.py:285
  37.7 6.3 %collective-permute-start.14 = (bf16[72,768]{1,0:T(8,128)(2,1)S(1)}, bf16[72,768]{1,0:T(8,128)(2,1)S(1)}, u32[]{:S(2)}, u32[]{:S(2)}) collective-permute-start(bf16[72,768]{1,0:T(8,128)(2,1)S(1)} %collective-permute-done.13.refs_3_), channel_id=1, source_target_pairs={{0,2},{1,0},{3,1},{5,3},{7,5},{6,7},{4,6},{2,4},{8,10},{9,8},{11,9... | collective-permute-start | bytes 331784 | tf_op jit(solution)/shard_map/ppermute | solution.py:290
  39.3 4.6 %collective-permute-start.12 = (bf16[64,768]{1,0:T(8,128)(2,1)S(1)}, bf16[64,768]{1,0:T(8,128)(2,1)S(1)}, u32[]{:S(2)}, u32[]{:S(2)}) collective-permute-start(bf16[64,768]{1,0:T(8,128)(2,1)S(1)} %collective-permute-done.11.refs_0_), channel_id=1, source_target_pairs={{0,1},{1,3},{3,5},{5,7},{7,6},{6,4},{4,2},{2,0},{8,9},{9,11},{11,1... | collective-permute-start | bytes 294920 | tf_op jit(solution)/shard_map/ppermute | solution.py:290

commit v14 on v13

--- a/solution.py
+++ b/solution.py
@@ -279,17 +279,19 @@
         upper, lower = merge(others, keep[0], got, gain[None, :])
 
         up, back = [upper, lower], [upper, lower]
-        pieces, hops = [[upper, lower]], [0]
+        pieces, hops, opposite = [[upper, lower]], [0], None
         for step in range(1, half):
+            if step == half - 1:
+                opposite = up[0], back[1]
             for i in range(2):
                 up[i], back[i] = lax.ppermute(up[i], "col", shift(1)), lax.ppermute(back[i], "col", shift(-1))
+            if opposite:
+                opposite = lax.ppermute(opposite[0], "col", shift(2)), lax.ppermute(opposite[1], "col", shift(-2))
             pieces += [list(up), list(back)]
             hops += [-step, step]
         stream, state = project(pieces[:-2], hops[:-2], qk_weight, None, cycle, False)
-        back[1], state = lax.optimization_barrier((back[1], state))
-        opposite = [lax.ppermute(up[0], "col", shift(1)), lax.ppermute(back[1], "col", shift(-1))]
-        state = project(pieces[-2:], hops[-2:], qk_weight, state, cycle, False)
-        return stream, project([opposite], [half], qk_weight, state, cycle, True)
+        state = project([opposite], [half], qk_weight, state, cycle, False)
+        return stream, project(pieces[-2:], hops[-2:], qk_weight, state, cycle, True)
 
     placed = (P(None, "row"), P("row", "col"), P("row", "col"), P("col"), P(None, "col"))
     return jax.shard_map(

time: 45.4 us -> 43.4 us (0.956)
  waiting for transfers between devices: 10.8 us -> 7.31 us
  starting transfers between devices: 18.4 us -> 19.9 us
    ppermute x6, starting transfers between devices: 8.88 us -> 3.19 us  [per_device(): lax.ppermute(back[i], 'col', shift(-1))]
    ppermute x6, starting transfers between devices: 3.92 us -> 8.82 us  [per_device(): lax.ppermute(up[i], 'col', shift(1))]
    ppermute x2, starting transfers between devices: 2.03 us -> 4.34 us  [the longest x1 3.06 us: per_device(): lax.ppermute(opposite[0], 'col', shift(2))]
    ppermute x6, waiting for transfers between devices: 1.54 us -> 0.2 us  [per_device(): lax.ppermute(back[i], 'col', shift(-1))]
    ppermute x6, waiting for transfers between devices: 3.74 us -> 2.57 us  [per_device(): lax.ppermute(up[i], 'col', shift(1))]
    ppermute x2, waiting for transfers between devices: 3.12 us -> 2.1 us  [the longest x1 1.79 us: per_device(): lax.ppermute(opposite[1], 'col', shift(-2))]
where the time goes in v14:
time: 43.4 us; the launch traced here: 43.3 us
  starting transfers between devices  19.9 us (46%)
  Pallas kernels  15.2 us (35%)
  waiting for transfers between devices  7.31 us (17%)
  between operations  0.75 us (2%)
    pallas_call x2, Pallas kernels, down(): pl.pallas_call(functools.partial(down_kernel, chips_y, tok, parts, own),...  10 us
    ppermute x6, starting transfers between devices, per_device(): lax.ppermute(up[i], 'col', shift(1))  8.82 us
    pallas_call x3, Pallas kernels, project(): pl.pallas_call(functools.partial(project_kernel, cycle, hops, [len(parts)...  5.14 us
    ppermute x6, starting transfers between devices, per_device(): lax.ppermute(back[i], 'col', shift(-1))  3.19 us
    ppermute x1, starting transfers between devices, per_device(): lax.ppermute(opposite[0], 'col', shift(2))  3.06 us
    ppermute x1, starting transfers between devices, per_device(): lax.ppermute(both[step - 1], 'row', move).astype(jnp.float32)  2.95 us
    ppermute x6, waiting for transfers between devices, per_device(): lax.ppermute(up[i], 'col', shift(1))  2.57 us
    ppermute x1, waiting for transfers between devices, per_device(): lax.ppermute(opposite[1], 'col', shift(-2))  1.79 us
  transfers between devices with their start and end apart: 17, of which 8 were waited for; matrix products, arithmetic and copies ran while one was open for 0% of the time, Pallas kernels for 18%

profile of v14, /device:TPU:0, one launch (start us, length us, event | category | flops | bytes accessed | tf_op | source)
XLA Modules:
  0.0 43.3 jit_solution(5976901484666172708)
XLA Ops:
  0.7 5.6 %down.2 = (bf16[1,128,768]{2,1,0:T(8,128)(2,1)S(1)}, bf16[1,128,768]{2,1,0:T(8,128)(2,1)S(1)}, bf16[6144,768]{1,0:T(8,128)(2,1)S(1)}) custom-call(bf16[512,6144]{1,0:T(8,128)(2,1)} %hidden.2, bf16[6144,768]{1,0:T(8,128)(2,1)} %weight.1), custom_call_target="tpu_custom_call" | custom-call | flops 2415919104 | bytes 12582912 | tf_op jit(solution)/shard_map/down/pallas_call | solution.py:100
  6.3 0.5 %collective-permute-start = (bf16[1,128,768]{2,1,0:T(8,128)(2,1)S(1)}, bf16[1,128,768]{2,1,0:T(8,128)(2,1)S(1)}, u32[]{:S(2)}, u32[]{:S(2)}) collective-permute-start(bf16[1,128,768]{2,1,0:T(8,128)(2,1)S(1)} %get-tuple-element.18), channel_id=1, source_target_pairs={{0,8},{8,0},{16,24},{24,16},{1,9},{9,1},{17,25},{25,17},{2,10},{10... | collective-permute-start | bytes 589832 | tf_op jit(solution)/shard_map/ppermute | solution.py:270
  6.8 1.1 %collective-permute-done = bf16[1,128,768]{2,1,0:T(8,128)(2,1)S(1)} collective-permute-done((bf16[1,128,768]{2,1,0:T(8,128)(2,1)S(1)}, bf16[1,128,768]{2,1,0:T(8,128)(2,1)S(1)}, u32[]{:S(2)}, u32[]{:S(2)}) %collective-permute-start) | collective-permute-done | bytes 196640 | tf_op jit(solution)/shard_map/ppermute | solution.py:270
  7.9 3.0 %collective-permute-start.1 = (bf16[128,768]{1,0:T(8,128)(2,1)S(1)}, bf16[128,768]{1,0:T(8,128)(2,1)S(1)}, u32[]{:S(2)}, u32[]{:S(2)}) collective-permute-start(bf16[128,768]{1,0:T(8,128)(2,1)S(1)} %bitcast.5), channel_id=1, source_target_pairs={{0,16},{8,24},{16,0},{24,8},{1,17},{9,25},{17,1},{25,9},{2,18},{10... | collective-permute-start | bytes 589832 | tf_op jit(solution)/shard_map/ppermute | solution.py:276
  10.9 4.4 %down.3 = (bf16[1,128,768]{2,1,0:T(8,128)(2,1)S(1)}, bf16[1,128,768]{2,1,0:T(8,128)(2,1)S(1)}) custom-call(bf16[512,6144]{1,0:T(8,128)(2,1)} %hidden.2, bf16[6144,768]{1,0:T(8,128)(2,1)S(1)} %get-tuple-element.21.weight), custom_call_target="tpu_custom_call" | custom-call | flops 2415919104 | bytes 3145728 | tf_op jit(solution)/shard_map/down/pallas_call | solution.py:100
  15.4 0.7 %collective-permute-done.1 = bf16[128,768]{1,0:T(8,128)(2,1)S(1)} collective-permute-done((bf16[128,768]{1,0:T(8,128)(2,1)S(1)}, bf16[128,768]{1,0:T(8,128)(2,1)S(1)}, u32[]{:S(2)}, u32[]{:S(2)}) %collective-permute-start.1) | collective-permute-done | bytes 196640 | tf_op jit(solution)/shard_map/ppermute | solution.py:276
  16.1 0.7 %collective-permute-done.2.got = bf16[128,768]{1,0:T(8,128)(2,1)S(1)} collective-permute-done((bf16[128,768]{1,0:T(8,128)(2,1)S(1)}, bf16[128,768]{1,0:T(8,128)(2,1)S(1)}, u32[]{:S(2)}, u32[]{:S(2)}) %collective-permute-start.2) | collective-permute-done | bytes 196640 | tf_op jit(solution)/shard_map/ppermute | solution.py:278
  16.9 1.9 %collective-permute-start.3 = (bf16[64,768]{1,0:T(8,128)(2,1)S(1)}, bf16[64,768]{1,0:T(8,128)(2,1)S(1)}, u32[]{:S(2)}, u32[]{:S(2)}) collective-permute-start(bf16[64,768]{1,0:T(8,128)(2,1)S(1)} %get-tuple-element.24.refs_0_), channel_id=1, source_target_pairs={{0,1},{1,3},{3,5},{5,7},{7,6},{6,4},{4,2},{2,0},{8,9},{9,11},{11,1... | collective-permute-start | bytes 294920 | tf_op jit(solution)/shard_map/ppermute | solution.py:287
  19.0 1.8 %collective-permute-start.4 = (bf16[72,768]{1,0:T(8,128)(2,1)S(1)}, bf16[72,768]{1,0:T(8,128)(2,1)S(1)}, u32[]{:S(2)}, u32[]{:S(2)}) collective-permute-start(bf16[72,768]{1,0:T(8,128)(2,1)S(1)} %get-tuple-element.25.refs_1_), channel_id=1, source_target_pairs={{0,1},{1,3},{3,5},{5,7},{7,6},{6,4},{4,2},{2,0},{8,9},{9,11},{11,1... | collective-permute-start | bytes 331784 | tf_op jit(solution)/shard_map/ppermute | solution.py:287
  21.0 1.6 %collective-permute-done.3.refs_2_ = bf16[64,768]{1,0:T(8,128)(2,1)S(1)} collective-permute-done((bf16[64,768]{1,0:T(8,128)(2,1)S(1)}, bf16[64,768]{1,0:T(8,128)(2,1)S(1)}, u32[]{:S(2)}, u32[]{:S(2)}) %collective-permute-start.3) | collective-permute-done | bytes 98336 | tf_op jit(solution)/shard_map/ppermute | solution.py:287
  22.5 1.8 %collective-permute-start.7 = (bf16[64,768]{1,0:T(8,128)(2,1)S(1)}, bf16[64,768]{1,0:T(8,128)(2,1)S(1)}, u32[]{:S(2)}, u32[]{:S(2)}) collective-permute-start(bf16[64,768]{1,0:T(8,128)(2,1)S(1)} %collective-permute-done.3.refs_2_), channel_id=1, source_target_pairs={{0,1},{1,3},{3,5},{5,7},{7,6},{6,4},{4,2},{2,0},{8,9},{9,11},{11,1... | collective-permute-start | bytes 294920 | tf_op jit(solution)/shard_map/ppermute | solution.py:287
  24.5 0.4 collective-permute-start.10
  24.9 1.6 %collective-permute-start.8 = (bf16[72,768]{1,0:T(8,128)(2,1)S(1)}, bf16[72,768]{1,0:T(8,128)(2,1)S(1)}, u32[]{:S(2)}, u32[]{:S(2)}) collective-permute-start(bf16[72,768]{1,0:T(8,128)(2,1)S(1)} %collective-permute-done.4.refs_3_), channel_id=1, source_target_pairs={{0,1},{1,3},{3,5},{5,7},{7,6},{6,4},{4,2},{2,0},{8,9},{9,11},{11,1... | collective-permute-start | bytes 331784 | tf_op jit(solution)/shard_map/ppermute | solution.py:287
  26.5 0.4 collective-permute-start.9
  26.9 1.0 %collective-permute-done.7.refs_6_ = bf16[64,768]{1,0:T(8,128)(2,1)S(1)} collective-permute-done((bf16[64,768]{1,0:T(8,128)(2,1)S(1)}, bf16[64,768]{1,0:T(8,128)(2,1)S(1)}, u32[]{:S(2)}, u32[]{:S(2)}) %collective-permute-start.7) | collective-permute-done | bytes 98336 | tf_op jit(solution)/shard_map/ppermute | solution.py:287
  27.9 3.1 %collective-permute-start.15 = (bf16[64,768]{1,0:T(8,128)(2,1)S(1)}, bf16[64,768]{1,0:T(8,128)(2,1)S(1)}, u32[]{:S(2)}, u32[]{:S(2)}) collective-permute-start(bf16[64,768]{1,0:T(8,128)(2,1)S(1)} %collective-permute-done.7.refs_6_), channel_id=1, source_target_pairs={{0,3},{1,5},{3,7},{5,6},{7,4},{6,2},{4,0},{2,1},{8,11},{9,13},{11,... | collective-permute-start | bytes 294920 | tf_op jit(solution)/shard_map/ppermute | solution.py:289
  31.0 1.6 %collective-permute-start.11 = (bf16[64,768]{1,0:T(8,128)(2,1)S(1)}, bf16[64,768]{1,0:T(8,128)(2,1)S(1)}, u32[]{:S(2)}, u32[]{:S(2)}) collective-permute-start(bf16[64,768]{1,0:T(8,128)(2,1)S(1)} %collective-permute-done.7.refs_6_), channel_id=1, source_target_pairs={{0,1},{1,3},{3,5},{5,7},{7,6},{6,4},{4,2},{2,0},{8,9},{9,11},{11,1... | collective-permute-start | bytes 294920 | tf_op jit(solution)/shard_map/ppermute | solution.py:287
  32.5 0.4 %collective-permute-start.13 = (bf16[64,768]{1,0:T(8,128)(2,1)S(1)}, bf16[64,768]{1,0:T(8,128)(2,1)S(1)}, u32[]{:S(2)}, u32[]{:S(2)}) collective-permute-start(bf16[64,768]{1,0:T(8,128)(2,1)S(1)} %collective-permute-done.9.refs_8_), channel_id=1, source_target_pairs={{0,2},{1,0},{3,1},{5,3},{7,5},{6,7},{4,6},{2,4},{8,10},{9,8},{11,9... | collective-permute-start | bytes 294920 | tf_op jit(solution)/shard_map/ppermute | solution.py:287
  33.0 1.3 %collective-permute-start.16 = (bf16[72,768]{1,0:T(8,128)(2,1)S(1)}, bf16[72,768]{1,0:T(8,128)(2,1)S(1)}, u32[]{:S(2)}, u32[]{:S(2)}) collective-permute-start(bf16[72,768]{1,0:T(8,128)(2,1)S(1)} %collective-permute-done.10.refs_9_), channel_id=1, source_target_pairs={{0,4},{1,2},{3,0},{5,1},{7,3},{6,5},{4,7},{2,6},{8,12},{9,10},{11,... | collective-permute-start | bytes 331784 | tf_op jit(solution)/shard_map/ppermute | solution.py:289
  34.3 1.6 %collective-permute-start.14 = (bf16[72,768]{1,0:T(8,128)(2,1)S(1)}, bf16[72,768]{1,0:T(8,128)(2,1)S(1)}, u32[]{:S(2)}, u32[]{:S(2)}) collective-permute-start(bf16[72,768]{1,0:T(8,128)(2,1)S(1)} %collective-permute-done.10.refs_9_), channel_id=1, source_target_pairs={{0,2},{1,0},{3,1},{5,3},{7,5},{6,7},{4,6},{2,4},{8,10},{9,8},{11,9... | collective-permute-start | bytes 331784 | tf_op jit(solution)/shard_map/ppermute | solution.py:287
  36.3 2.7 %project.3 = (bf16[128,768]{1,0:T(8,128)(2,1)}, f32[128,1]{1,0:T(8,128)S(1)}, f32[2,128,1]{2,1,0:T(8,128)S(1)}, f32[144,1536]{1,0:T(8,128)S(1)}) custom-call(bf16[64,768]{1,0:T(8,128)(2,1)S(1)} %get-tuple-element.24.refs_0_, bf16[72,768]{1,0:T(8,128)(2,1)S(1)} %get-tuple-element.25.refs_1_, bf16[64,768]{1,0:T(8,128)(2,1)S(1)} %collective-permute-done.3.refs_2_, ...), custom_call_target="tpu_custom_call" | custom-call | flops 1698693120 | tf_op jit(solution)/shard_map/project/pallas_call | solution.py:235
  39.0 1.8 %collective-permute-done.16.refs_1_ = bf16[72,768]{1,0:T(8,128)(2,1)S(1)} collective-permute-done((bf16[72,768]{1,0:T(8,128)(2,1)S(1)}, bf16[72,768]{1,0:T(8,128)(2,1)S(1)}, u32[]{:S(2)}, u32[]{:S(2)}) %collective-permute-start.16) | collective-permute-done | bytes 110624 | tf_op jit(solution)/shard_map/ppermute | solution.py:289
  40.8 0.7 %project.4 = (f32[2,128,1]{2,1,0:T(8,128)S(1)}, f32[144,1536]{1,0:T(8,128)S(1)}) custom-call(bf16[64,768]{1,0:T(8,128)(2,1)S(1)} %collective-permute-done.15.refs_0_, bf16[72,768]{1,0:T(8,128)(2,1)S(1)} %collective-permute-done.16.refs_1_, bf16[6144,1536]{1,0:T(8,128)(2,1)S(1)} %copy-done, ...), custom_call_target="tpu_custom_call", output_to_operand_aliasing={{0}: (4, {}), {1}: (5, {})} | custom-call | flops 339738624 | tf_op jit(solution)/shard_map/project/pallas_call | solution.py:235
  41.5 1.8 %project.5 = bf16[128,1536]{1,0:T(8,128)(2,1)} custom-call(bf16[64,768]{1,0:T(8,128)(2,1)S(1)} %collective-permute-done.11.refs_0_, bf16[72,768]{1,0:T(8,128)(2,1)S(1)} %collective-permute-done.12.refs_1_, bf16[64,768]{1,0:T(8,128)(2,1)S(1)} %collective-permute-done.13.refs_2_, bf16[72,768]{1,0:T(8,128)(2,1)S(1)} %collective-permute-done.14.refs_3_, ...), custom_call_target="tpu_custom_call" | custom-call | flops 679477248 | tf_op jit(solution)/shard_map/project/pallas_call | solution.py:235
  (25 shorter events, 1.3 us)
Async XLA Ops:
  0.6 6.2 %copy-start.2 = (bf16[768]{0:T(1024)(128)(2,1)S(1)}, bf16[768]{0:T(1024)(128)(2,1)}, u32[]{:S(2)}) copy-start(bf16[768]{0:T(1024)(128)(2,1)} %param.8) | copy-start | bytes 4612
  0.6 35.7 %copy-start = (bf16[6144,1536]{1,0:T(8,128)(2,1)S(1)}, bf16[6144,1536]{1,0:T(8,128)(2,1)}, u32[]{:S(2)}) copy-start(bf16[6144,1536]{1,0:T(8,128)(2,1)} %refs_4_.1) | copy-start | bytes 56623108
  6.3 9.8 %copy-start.1 = (bf16[128,768]{1,0:T(8,128)(2,1)S(1)}, bf16[128,768]{1,0:T(8,128)(2,1)}, u32[]{:S(2)}) copy-start(bf16[128,768]{1,0:T(8,128)(2,1)} %param.7) | copy-start | bytes 589828
  6.3 1.6 %collective-permute-start = (bf16[1,128,768]{2,1,0:T(8,128)(2,1)S(1)}, bf16[1,128,768]{2,1,0:T(8,128)(2,1)S(1)}, u32[]{:S(2)}, u32[]{:S(2)}) collective-permute-start(bf16[1,128,768]{2,1,0:T(8,128)(2,1)S(1)} %get-tuple-element.18), channel_id=1, source_target_pairs={{0,8},{8,0},{16,24},{24,16},{1,9},{9,1},{17,25},{25,17},{2,10},{10... | collective-permute-start | bytes 589832 | tf_op jit(solution)/shard_map/ppermute | solution.py:270
  7.9 8.2 %collective-permute-start.1 = (bf16[128,768]{1,0:T(8,128)(2,1)S(1)}, bf16[128,768]{1,0:T(8,128)(2,1)S(1)}, u32[]{:S(2)}, u32[]{:S(2)}) collective-permute-start(bf16[128,768]{1,0:T(8,128)(2,1)S(1)} %bitcast.5), channel_id=1, source_target_pairs={{0,16},{8,24},{16,0},{24,8},{1,17},{9,25},{17,1},{25,9},{2,18},{10... | collective-permute-start | bytes 589832 | tf_op jit(solution)/shard_map/ppermute | solution.py:276
  15.3 1.5 %collective-permute-start.2 = (bf16[128,768]{1,0:T(8,128)(2,1)S(1)}, bf16[128,768]{1,0:T(8,128)(2,1)S(1)}, u32[]{:S(2)}, u32[]{:S(2)}) collective-permute-start(bf16[128,768]{1,0:T(8,128)(2,1)S(1)} %bitcast.4), channel_id=1, source_target_pairs={{0,8},{8,0},{16,24},{24,16},{1,9},{9,1},{17,25},{25,17},{2,10},{10... | collective-permute-start | bytes 589832 | tf_op jit(solution)/shard_map/ppermute | solution.py:278
  16.9 5.7 %collective-permute-start.3 = (bf16[64,768]{1,0:T(8,128)(2,1)S(1)}, bf16[64,768]{1,0:T(8,128)(2,1)S(1)}, u32[]{:S(2)}, u32[]{:S(2)}) collective-permute-start(bf16[64,768]{1,0:T(8,128)(2,1)S(1)} %get-tuple-element.24.refs_0_), channel_id=1, source_target_pairs={{0,1},{1,3},{3,5},{5,7},{7,6},{6,4},{4,2},{2,0},{8,9},{9,11},{11,1... | collective-permute-start | bytes 294920 | tf_op jit(solution)/shard_map/ppermute | solution.py:287
  18.8 5.7 %collective-permute-start.6 = (bf16[72,768]{1,0:T(8,128)(2,1)S(1)}, bf16[72,768]{1,0:T(8,128)(2,1)S(1)}, u32[]{:S(2)}, u32[]{:S(2)}) collective-permute-start(bf16[72,768]{1,0:T(8,128)(2,1)S(1)} %get-tuple-element.25.refs_1_), channel_id=1, source_target_pairs={{0,2},{1,0},{3,1},{5,3},{7,5},{6,7},{4,6},{2,4},{8,10},{9,8},{11,9... | collective-permute-start | bytes 331784 | tf_op jit(solution)/shard_map/ppermute | solution.py:287
  19.0 5.9 %collective-permute-start.4 = (bf16[72,768]{1,0:T(8,128)(2,1)S(1)}, bf16[72,768]{1,0:T(8,128)(2,1)S(1)}, u32[]{:S(2)}, u32[]{:S(2)}) collective-permute-start(bf16[72,768]{1,0:T(8,128)(2,1)S(1)} %get-tuple-element.25.refs_1_), channel_id=1, source_target_pairs={{0,1},{1,3},{3,5},{5,7},{7,6},{6,4},{4,2},{2,0},{8,9},{9,11},{11,1... | collective-permute-start | bytes 331784 | tf_op jit(solution)/shard_map/ppermute | solution.py:287
  20.8 5.7 %collective-permute-start.5 = (bf16[64,768]{1,0:T(8,128)(2,1)S(1)}, bf16[64,768]{1,0:T(8,128)(2,1)S(1)}, u32[]{:S(2)}, u32[]{:S(2)}) collective-permute-start(bf16[64,768]{1,0:T(8,128)(2,1)S(1)} %get-tuple-element.24.refs_0_), channel_id=1, source_target_pairs={{0,2},{1,0},{3,1},{5,3},{7,5},{6,7},{4,6},{2,4},{8,10},{9,8},{11,9... | collective-permute-start | bytes 294920 | tf_op jit(solution)/shard_map/ppermute | solution.py:287
  22.5 5.4 %collective-permute-start.7 = (bf16[64,768]{1,0:T(8,128)(2,1)S(1)}, bf16[64,768]{1,0:T(8,128)(2,1)S(1)}, u32[]{:S(2)}, u32[]{:S(2)}) collective-permute-start(bf16[64,768]{1,0:T(8,128)(2,1)S(1)} %collective-permute-done.3.refs_2_), channel_id=1, source_target_pairs={{0,1},{1,3},{3,5},{5,7},{7,6},{6,4},{4,2},{2,0},{8,9},{9,11},{11,1... | collective-permute-start | bytes 294920 | tf_op jit(solution)/shard_map/ppermute | solution.py:287
  24.5 8.5 %collective-permute-start.10 = (bf16[72,768]{1,0:T(8,128)(2,1)S(1)}, bf16[72,768]{1,0:T(8,128)(2,1)S(1)}, u32[]{:S(2)}, u32[]{:S(2)}) collective-permute-start(bf16[72,768]{1,0:T(8,128)(2,1)S(1)} %collective-permute-done.6.refs_5_), channel_id=1, source_target_pairs={{0,2},{1,0},{3,1},{5,3},{7,5},{6,7},{4,6},{2,4},{8,10},{9,8},{11,9... | collective-permute-start | bytes 331784 | tf_op jit(solution)/shard_map/ppermute | solution.py:287
  24.9 9.4 %collective-permute-start.8 = (bf16[72,768]{1,0:T(8,128)(2,1)S(1)}, bf16[72,768]{1,0:T(8,128)(2,1)S(1)}, u32[]{:S(2)}, u32[]{:S(2)}) collective-permute-start(bf16[72,768]{1,0:T(8,128)(2,1)S(1)} %collective-permute-done.4.refs_3_), channel_id=1, source_target_pairs={{0,1},{1,3},{3,5},{5,7},{7,6},{6,4},{4,2},{2,0},{8,9},{9,11},{11,1... | collective-permute-start | bytes 331784 | tf_op jit(solution)/shard_map/ppermute | solution.py:287
  26.5 6.0 %collective-permute-start.9 = (bf16[64,768]{1,0:T(8,128)(2,1)S(1)}, bf16[64,768]{1,0:T(8,128)(2,1)S(1)}, u32[]{:S(2)}, u32[]{:S(2)}) collective-permute-start(bf16[64,768]{1,0:T(8,128)(2,1)S(1)} %collective-permute-done.5.refs_4_), channel_id=1, source_target_pairs={{0,2},{1,0},{3,1},{5,3},{7,5},{6,7},{4,6},{2,4},{8,10},{9,8},{11,9... | collective-permute-start | bytes 294920 | tf_op jit(solution)/shard_map/ppermute | solution.py:287
  27.9 8.3 %collective-permute-start.15 = (bf16[64,768]{1,0:T(8,128)(2,1)S(1)}, bf16[64,768]{1,0:T(8,128)(2,1)S(1)}, u32[]{:S(2)}, u32[]{:S(2)}) collective-permute-start(bf16[64,768]{1,0:T(8,128)(2,1)S(1)} %collective-permute-done.7.refs_6_), channel_id=1, source_target_pairs={{0,3},{1,5},{3,7},{5,6},{7,4},{6,2},{4,0},{2,1},{8,11},{9,13},{11,... | collective-permute-start | bytes 294920 | tf_op jit(solution)/shard_map/ppermute | solution.py:289
  31.0 10.5 %collective-permute-start.11 = (bf16[64,768]{1,0:T(8,128)(2,1)S(1)}, bf16[64,768]{1,0:T(8,128)(2,1)S(1)}, u32[]{:S(2)}, u32[]{:S(2)}) collective-permute-start(bf16[64,768]{1,0:T(8,128)(2,1)S(1)} %collective-permute-done.7.refs_6_), channel_id=1, source_target_pairs={{0,1},{1,3},{3,5},{5,7},{7,6},{6,4},{4,2},{2,0},{8,9},{9,11},{11,1... | collective-permute-start | bytes 294920 | tf_op jit(solution)/shard_map/ppermute | solution.py:287
  32.5 9.0 %collective-permute-start.13 = (bf16[64,768]{1,0:T(8,128)(2,1)S(1)}, bf16[64,768]{1,0:T(8,128)(2,1)S(1)}, u32[]{:S(2)}, u32[]{:S(2)}) collective-permute-start(bf16[64,768]{1,0:T(8,128)(2,1)S(1)} %collective-permute-done.9.refs_8_), channel_id=1, source_target_pairs={{0,2},{1,0},{3,1},{5,3},{7,5},{6,7},{4,6},{2,4},{8,10},{9,8},{11,9... | collective-permute-start | bytes 294920 | tf_op jit(solution)/shard_map/ppermute | solution.py:287
  33.0 7.8 %collective-permute-start.16 = (bf16[72,768]{1,0:T(8,128)(2,1)S(1)}, bf16[72,768]{1,0:T(8,128)(2,1)S(1)}, u32[]{:S(2)}, u32[]{:S(2)}) collective-permute-start(bf16[72,768]{1,0:T(8,128)(2,1)S(1)} %collective-permute-done.10.refs_9_), channel_id=1, source_target_pairs={{0,4},{1,2},{3,0},{5,1},{7,3},{6,5},{4,7},{2,6},{8,12},{9,10},{11,... | collective-permute-start | bytes 331784 | tf_op jit(solution)/shard_map/ppermute | solution.py:289
  34.3 7.2 %collective-permute-start.14 = (bf16[72,768]{1,0:T(8,128)(2,1)S(1)}, bf16[72,768]{1,0:T(8,128)(2,1)S(1)}, u32[]{:S(2)}, u32[]{:S(2)}) collective-permute-start(bf16[72,768]{1,0:T(8,128)(2,1)S(1)} %collective-permute-done.10.refs_9_), channel_id=1, source_target_pairs={{0,2},{1,0},{3,1},{5,3},{7,5},{6,7},{4,6},{2,4},{8,10},{9,8},{11,9... | collective-permute-start | bytes 331784 | tf_op jit(solution)/shard_map/ppermute | solution.py:287
  36.2 5.4 %collective-permute-start.12 = (bf16[72,768]{1,0:T(8,128)(2,1)S(1)}, bf16[72,768]{1,0:T(8,128)(2,1)S(1)}, u32[]{:S(2)}, u32[]{:S(2)}) collective-permute-start(bf16[72,768]{1,0:T(8,128)(2,1)S(1)} %collective-permute-done.8.refs_7_), channel_id=1, source_target_pairs={{0,1},{1,3},{3,5},{5,7},{7,6},{6,4},{4,2},{2,0},{8,9},{9,11},{11,1... | collective-permute-start | bytes 331784 | tf_op jit(solution)/shard_map/ppermute | solution.py:287

commit v15 on v14

--- a/solution.py
+++ b/solution.py
@@ -43,28 +43,37 @@
     return fits[-1] if fits else size
 
 
-def down_kernel(chips_y, tok, parts, own, hidden, weight, *refs):
-    if own:
-        (give, keep), held = refs[:2], weight
-    else:
-        give, keep, held = refs[:3]
-    h_buf, total, sems = refs[-3:]
-    depth = held.shape[0] // parts
+def down_kernel(chips_y, tok, parts, hidden, weight, give, keep, held, h_buf, total, sems):
     me = lax.axis_index("row")
     chip, core = me // CORES, me % CORES
-    chips = [0] if own else list(range(1, chips_y))
     block = CORES * tok
+    starts = [pl.multiple_of(lax.rem(chip + step, chips_y) * block, block) for step in range(1, chips_y)]
+    multiply(parts, starts, block, hidden, weight, held, h_buf, total, sems)
+    for i in range(chips_y - 1):
+        for out, which in ((give, 1 - core), (keep, core)):
+            start = pl.multiple_of((i * CORES + which) * tok, tok)
+            out[i] = total[pl.ds(start, tok), :].astype(out.dtype)
+
+
+def own_kernel(tok, parts, flip, hidden, held, out, h_buf, total, sems):
+    me = lax.axis_index("row")
+    block = me // CORES * CORES + (1 - me % CORES if flip else me % CORES)
+    multiply(parts, [pl.multiple_of(block * tok, tok)], tok, hidden, None, held, h_buf, total, sems)
+    out[...] = total[...].astype(out.dtype)
+
+
+def multiply(parts, starts, block, hidden, weight, held, h_buf, total, sems):
+    depth = held.shape[0] // parts
 
     def span(k):
         return pl.ds(pl.multiple_of(k * depth, depth), depth)
 
     def copies(k):
-        for i, step in enumerate(chips):
-            start = pl.multiple_of(lax.rem(chip + step, chips_y) * block, block)
+        for i, start in enumerate(starts):
             yield pltpu.make_async_copy(
                 hidden.at[pl.ds(start, block), span(k)], h_buf.at[k, pl.ds(i * block, block)], sems.at[1 + i, k]
             )
-        if not own:
+        if weight is not None:
             yield pltpu.make_async_copy(weight.at[span(k), :], held.at[span(k), :], sems.at[0, k])
 
     for k in range(parts):
@@ -83,27 +92,28 @@
         return _
 
     lax.fori_loop(0, parts, body, 0)
-    for i in range(len(chips)):
-        for out, which in ((give, 1 - core), (keep, core)):
-            start = pl.multiple_of((i * CORES + which) * tok, tok)
-            out[i] = total[pl.ds(start, tok), :].astype(out.dtype)
-
-
-def down(hidden, weight, tok, chips_y, own):
+
+
+def down(hidden, weight, tok, chips_y, flip=None):
+    own = flip is not None
     inner, width = weight.shape
-    depth = cut(inner, 1536 if own else 768)
-    parts = inner // depth
-    chips = 1 if own else chips_y - 1
-    tokens = chips * CORES * tok
+    parts = inner // cut(inner, 1536 if own else 768)
+    chips = chips_y - 1
+    tokens = tok if own else chips * CORES * tok
     block = pltpu.VMEM((chips, tok, width), jnp.bfloat16)
-    out_shape = (block, block) if own else (block, block, pltpu.VMEM((inner, width), jnp.bfloat16))
+    if own:
+        kernel = functools.partial(own_kernel, tok, parts, flip)
+        out_shape = pltpu.VMEM((tok, width), jnp.bfloat16)
+    else:
+        kernel = functools.partial(down_kernel, chips_y, tok, parts)
+        out_shape = block, block, pltpu.VMEM((inner, width), jnp.bfloat16)
     return pl.pallas_call(
-        functools.partial(down_kernel, chips_y, tok, parts, own),
+        kernel,
         out_shape=out_shape,
         in_specs=[HBM, VMEM if own else HBM],
-        out_specs=(VMEM,) * len(out_shape),
+        out_specs=jax.tree.map(lambda _: VMEM, out_shape),
         scratch_shapes=[
-            pltpu.VMEM((parts, tokens, depth), jnp.bfloat16),
+            pltpu.VMEM((parts, tokens, inner // parts), jnp.bfloat16),
             pltpu.VMEM((tokens, width), jnp.float32),
             pltpu.SemaphoreType.DMA((1 + chips, parts)),
         ],
@@ -266,7 +276,7 @@
     def per_device(hidden, down_weight, residual, gain, qk_weight):
         tok = residual.shape[0]
 
-        give, keep, down_weight = down(hidden, down_weight, tok, chips_y, False)
+        give, keep, down_weight = down(hidden, down_weight, tok, chips_y)
         got = lax.ppermute(give, "row", sibling)
         both = (keep.astype(jnp.float32) + got.astype(jnp.float32)).astype(jnp.bfloat16)
         both, hidden = lax.optimization_barrier((both, hidden))
@@ -274,9 +284,9 @@
         for step in range(1, chips_y):
             move = [(r, (r + CORES * step) % rows) for r in range(rows)]
             others = others + lax.ppermute(both[step - 1], "row", move).astype(jnp.float32)
-        give, keep = down(hidden, down_weight, tok, chips_y, True)
-        got = lax.ppermute(give[0], "row", sibling)
-        upper, lower = merge(others, keep[0], got, gain[None, :])
+        got = lax.ppermute(down(hidden, down_weight, tok, chips_y, True), "row", sibling)
+        keep = down(hidden, down_weight, tok, chips_y, False)
+        upper, lower = merge(others, keep, got, gain[None, :])
 
         up, back = [upper, lower], [upper, lower]
         pieces, hops, opposite = [[upper, lower]], [0], None

time: 43.4 us -> 44.2 us (1.018)
  Pallas kernels: 15.2 us -> 17.1 us
  waiting for transfers between devices: 7.31 us -> 5.42 us
  starting transfers between devices: 19.9 us -> 20.6 us
    pallas_call x2 -> x3, Pallas kernels: 10 us -> 11.8 us  [down(): pl.pallas_call(kernel, out_shape=out_shape, in_specs=[HBM, VMEM if own el...]
    ppermute x6, starting transfers between devices: 3.19 us -> 4.61 us  [per_device(): lax.ppermute(back[i], 'col', shift(-1))]
    ppermute x6, starting transfers between devices: 8.82 us -> 8.01 us  [per_device(): lax.ppermute(up[i], 'col', shift(1))]
    ppermute x1, waiting for transfers between devices: 0.71 us -> 0.01 us  [per_device(): lax.ppermute(both[step - 1], 'row', move).astype(jnp.float32)]
    ppermute x1, starting transfers between devices: 1.27 us -> 1.97 us  [per_device(): lax.ppermute(opposite[1], 'col', shift(-2))]
    ppermute x1, waiting for transfers between devices: 0.67 us -> 0.01 us  [per_device(): lax.ppermute(down(hidden, down_weight, tok, chips_y, True), 'row', sibling)]
    ppermute x1, starting transfers between devices: 3.06 us -> 2.5 us  [per_device(): lax.ppermute(opposite[0], 'col', shift(2))]
    ppermute x6, waiting for transfers between devices: 2.57 us -> 2.08 us  [per_device(): lax.ppermute(up[i], 'col', shift(1))]
  transfers between devices with their start and end apart: 17 -> 17, of which waited for: 8 -> 6; matrix products, arithmetic and copies ran while one was open for 0% -> 0% of each run, Pallas kernels for 18% -> 22%
where the time goes in v15:
time: 44.2 us; the launch traced here: 44 us
  starting transfers between devices  20.6 us (47%)
  Pallas kernels  17.1 us (39%)
  waiting for transfers between devices  5.42 us (12%)
  between operations  0.81 us (2%)
    pallas_call x3, Pallas kernels, down(): pl.pallas_call(kernel, out_shape=out_shape, in_specs=[HBM, VMEM if own el...  11.8 us
    ppermute x6, starting transfers between devices, per_device(): lax.ppermute(up[i], 'col', shift(1))  8.01 us
    pallas_call x3, Pallas kernels, project(): pl.pallas_call(functools.partial(project_kernel, cycle, hops, [len(parts)...  5.15 us
    ppermute x6, starting transfers between devices, per_device(): lax.ppermute(back[i], 'col', shift(-1))  4.61 us
    ppermute x1, starting transfers between devices, per_device(): lax.ppermute(both[step - 1], 'row', move).astype(jnp.float32)  2.95 us
    ppermute x1, starting transfers between devices, per_device(): lax.ppermute(opposite[0], 'col', shift(2))  2.5 us
    ppermute x6, waiting for transfers between devices, per_device(): lax.ppermute(up[i], 'col', shift(1))  2.08 us
    ppermute x1, waiting for transfers between devices, per_device(): lax.ppermute(opposite[1], 'col', shift(-2))  2.01 us
  transfers between devices with their start and end apart: 17, of which 6 were waited for; matrix products, arithmetic and copies ran while one was open for 0% of the time, Pallas kernels for 22%

profile of v15, /device:TPU:0, one launch (start us, length us, event | category | flops | bytes accessed | tf_op | source)
XLA Modules:
  0.0 44.0 jit_solution(3032489603657835994)
XLA Ops:
  0.6 5.5 %down.3 = (bf16[1,128,768]{2,1,0:T(8,128)(2,1)S(1)}, bf16[1,128,768]{2,1,0:T(8,128)(2,1)S(1)}, bf16[6144,768]{1,0:T(8,128)(2,1)S(1)}) custom-call(bf16[512,6144]{1,0:T(8,128)(2,1)} %hidden.3, bf16[6144,768]{1,0:T(8,128)(2,1)} %weight.1), custom_call_target="tpu_custom_call" | custom-call | flops 2415919104 | bytes 12582912 | tf_op jit(solution)/shard_map/down/pallas_call | solution.py:110
  6.1 0.5 %collective-permute-start = (bf16[1,128,768]{2,1,0:T(8,128)(2,1)S(1)}, bf16[1,128,768]{2,1,0:T(8,128)(2,1)S(1)}, u32[]{:S(2)}, u32[]{:S(2)}) collective-permute-start(bf16[1,128,768]{2,1,0:T(8,128)(2,1)S(1)} %get-tuple-element.16), channel_id=1, source_target_pairs={{0,8},{8,0},{16,24},{24,16},{1,9},{9,1},{17,25},{25,17},{2,10},{10... | collective-permute-start | bytes 589832 | tf_op jit(solution)/shard_map/ppermute | solution.py:280
  6.6 1.1 %collective-permute-done = bf16[1,128,768]{2,1,0:T(8,128)(2,1)S(1)} collective-permute-done((bf16[1,128,768]{2,1,0:T(8,128)(2,1)S(1)}, bf16[1,128,768]{2,1,0:T(8,128)(2,1)S(1)}, u32[]{:S(2)}, u32[]{:S(2)}) %collective-permute-start) | collective-permute-done | bytes 196640 | tf_op jit(solution)/shard_map/ppermute | solution.py:280
  7.8 3.0 %collective-permute-start.1 = (bf16[128,768]{1,0:T(8,128)(2,1)S(1)}, bf16[128,768]{1,0:T(8,128)(2,1)S(1)}, u32[]{:S(2)}, u32[]{:S(2)}) collective-permute-start(bf16[128,768]{1,0:T(8,128)(2,1)S(1)} %bitcast.3), channel_id=1, source_target_pairs={{0,16},{8,24},{16,0},{24,8},{1,17},{9,25},{17,1},{25,9},{2,18},{10... | collective-permute-start | bytes 589832 | tf_op jit(solution)/shard_map/ppermute | solution.py:286
  10.7 3.2 %down.5 = bf16[128,768]{1,0:T(8,128)(2,1)S(1)} custom-call(bf16[512,6144]{1,0:T(8,128)(2,1)} %hidden.3, bf16[6144,768]{1,0:T(8,128)(2,1)S(1)} %get-tuple-element.19.held), custom_call_target="tpu_custom_call" | custom-call | flops 1207959552 | bytes 1572864 | tf_op jit(solution)/shard_map/down/pallas_call | solution.py:110
  14.0 3.2 %down.4.keep = bf16[128,768]{1,0:T(8,128)(2,1)S(1)} custom-call(bf16[512,6144]{1,0:T(8,128)(2,1)} %hidden.3, bf16[6144,768]{1,0:T(8,128)(2,1)S(1)} %get-tuple-element.19.held), custom_call_target="tpu_custom_call" | custom-call | flops 1207959552 | bytes 1572864 | tf_op jit(solution)/shard_map/down/pallas_call | solution.py:110
  17.4 1.5 %collective-permute-start.3 = (bf16[64,768]{1,0:T(8,128)(2,1)S(1)}, bf16[64,768]{1,0:T(8,128)(2,1)S(1)}, u32[]{:S(2)}, u32[]{:S(2)}) collective-permute-start(bf16[64,768]{1,0:T(8,128)(2,1)S(1)} %get-tuple-element.20.refs_0_), channel_id=1, source_target_pairs={{0,1},{1,3},{3,5},{5,7},{7,6},{6,4},{4,2},{2,0},{8,9},{9,11},{11,1... | collective-permute-start | bytes 294920 | tf_op jit(solution)/shard_map/ppermute | solution.py:297
  18.9 0.5 %collective-permute-start.6 = (bf16[72,768]{1,0:T(8,128)(2,1)S(1)}, bf16[72,768]{1,0:T(8,128)(2,1)S(1)}, u32[]{:S(2)}, u32[]{:S(2)}) collective-permute-start(bf16[72,768]{1,0:T(8,128)(2,1)S(1)} %get-tuple-element.21.refs_1_), channel_id=1, source_target_pairs={{0,2},{1,0},{3,1},{5,3},{7,5},{6,7},{4,6},{2,4},{8,10},{9,8},{11,9... | collective-permute-start | bytes 331784 | tf_op jit(solution)/shard_map/ppermute | solution.py:297
  19.4 1.5 %collective-permute-start.4 = (bf16[72,768]{1,0:T(8,128)(2,1)S(1)}, bf16[72,768]{1,0:T(8,128)(2,1)S(1)}, u32[]{:S(2)}, u32[]{:S(2)}) collective-permute-start(bf16[72,768]{1,0:T(8,128)(2,1)S(1)} %get-tuple-element.21.refs_1_), channel_id=1, source_target_pairs={{0,1},{1,3},{3,5},{5,7},{7,6},{6,4},{4,2},{2,0},{8,9},{9,11},{11,1... | collective-permute-start | bytes 331784 | tf_op jit(solution)/shard_map/ppermute | solution.py:297
  20.9 0.5 %collective-permute-start.5 = (bf16[64,768]{1,0:T(8,128)(2,1)S(1)}, bf16[64,768]{1,0:T(8,128)(2,1)S(1)}, u32[]{:S(2)}, u32[]{:S(2)}) collective-permute-start(bf16[64,768]{1,0:T(8,128)(2,1)S(1)} %get-tuple-element.20.refs_0_), channel_id=1, source_target_pairs={{0,2},{1,0},{3,1},{5,3},{7,5},{6,7},{4,6},{2,4},{8,10},{9,8},{11,9... | collective-permute-start | bytes 294920 | tf_op jit(solution)/shard_map/ppermute | solution.py:297
  21.5 1.6 %collective-permute-done.3.refs_2_ = bf16[64,768]{1,0:T(8,128)(2,1)S(1)} collective-permute-done((bf16[64,768]{1,0:T(8,128)(2,1)S(1)}, bf16[64,768]{1,0:T(8,128)(2,1)S(1)}, u32[]{:S(2)}, u32[]{:S(2)}) %collective-permute-start.3) | collective-permute-done | bytes 98336 | tf_op jit(solution)/shard_map/ppermute | solution.py:297
  23.1 1.5 %collective-permute-start.7 = (bf16[64,768]{1,0:T(8,128)(2,1)S(1)}, bf16[64,768]{1,0:T(8,128)(2,1)S(1)}, u32[]{:S(2)}, u32[]{:S(2)}) collective-permute-start(bf16[64,768]{1,0:T(8,128)(2,1)S(1)} %collective-permute-done.3.refs_2_), channel_id=1, source_target_pairs={{0,1},{1,3},{3,5},{5,7},{7,6},{6,4},{4,2},{2,0},{8,9},{9,11},{11,1... | collective-permute-start | bytes 294920 | tf_op jit(solution)/shard_map/ppermute | solution.py:297
  24.8 0.5 %collective-permute-start.10 = (bf16[72,768]{1,0:T(8,128)(2,1)S(1)}, bf16[72,768]{1,0:T(8,128)(2,1)S(1)}, u32[]{:S(2)}, u32[]{:S(2)}) collective-permute-start(bf16[72,768]{1,0:T(8,128)(2,1)S(1)} %collective-permute-done.6.refs_5_), channel_id=1, source_target_pairs={{0,2},{1,0},{3,1},{5,3},{7,5},{6,7},{4,6},{2,4},{8,10},{9,8},{11,9... | collective-permute-start | bytes 331784 | tf_op jit(solution)/shard_map/ppermute | solution.py:297
  25.3 1.5 %collective-permute-start.8 = (bf16[72,768]{1,0:T(8,128)(2,1)S(1)}, bf16[72,768]{1,0:T(8,128)(2,1)S(1)}, u32[]{:S(2)}, u32[]{:S(2)}) collective-permute-start(bf16[72,768]{1,0:T(8,128)(2,1)S(1)} %collective-permute-done.4.refs_3_), channel_id=1, source_target_pairs={{0,1},{1,3},{3,5},{5,7},{7,6},{6,4},{4,2},{2,0},{8,9},{9,11},{11,1... | collective-permute-start | bytes 331784 | tf_op jit(solution)/shard_map/ppermute | solution.py:297
  26.8 0.5 %collective-permute-start.9 = (bf16[64,768]{1,0:T(8,128)(2,1)S(1)}, bf16[64,768]{1,0:T(8,128)(2,1)S(1)}, u32[]{:S(2)}, u32[]{:S(2)}) collective-permute-start(bf16[64,768]{1,0:T(8,128)(2,1)S(1)} %collective-permute-done.5.refs_4_), channel_id=1, source_target_pairs={{0,2},{1,0},{3,1},{5,3},{7,5},{6,7},{4,6},{2,4},{8,10},{9,8},{11,9... | collective-permute-start | bytes 294920 | tf_op jit(solution)/shard_map/ppermute | solution.py:297
  27.8 2.5 %collective-permute-start.15 = (bf16[64,768]{1,0:T(8,128)(2,1)S(1)}, bf16[64,768]{1,0:T(8,128)(2,1)S(1)}, u32[]{:S(2)}, u32[]{:S(2)}) collective-permute-start(bf16[64,768]{1,0:T(8,128)(2,1)S(1)} %collective-permute-done.7.refs_6_), channel_id=1, source_target_pairs={{0,3},{1,5},{3,7},{5,6},{7,4},{6,2},{4,0},{2,1},{8,11},{9,13},{11,... | collective-permute-start | bytes 294920 | tf_op jit(solution)/shard_map/ppermute | solution.py:299
  30.3 1.6 %collective-permute-start.11 = (bf16[64,768]{1,0:T(8,128)(2,1)S(1)}, bf16[64,768]{1,0:T(8,128)(2,1)S(1)}, u32[]{:S(2)}, u32[]{:S(2)}) collective-permute-start(bf16[64,768]{1,0:T(8,128)(2,1)S(1)} %collective-permute-done.7.refs_6_), channel_id=1, source_target_pairs={{0,1},{1,3},{3,5},{5,7},{7,6},{6,4},{4,2},{2,0},{8,9},{9,11},{11,1... | collective-permute-start | bytes 294920 | tf_op jit(solution)/shard_map/ppermute | solution.py:297
  31.9 0.9 %collective-permute-start.13 = (bf16[64,768]{1,0:T(8,128)(2,1)S(1)}, bf16[64,768]{1,0:T(8,128)(2,1)S(1)}, u32[]{:S(2)}, u32[]{:S(2)}) collective-permute-start(bf16[64,768]{1,0:T(8,128)(2,1)S(1)} %collective-permute-done.9.refs_8_), channel_id=1, source_target_pairs={{0,2},{1,0},{3,1},{5,3},{7,5},{6,7},{4,6},{2,4},{8,10},{9,8},{11,9... | collective-permute-start | bytes 294920 | tf_op jit(solution)/shard_map/ppermute | solution.py:297
  32.8 2.0 %collective-permute-start.16 = (bf16[72,768]{1,0:T(8,128)(2,1)S(1)}, bf16[72,768]{1,0:T(8,128)(2,1)S(1)}, u32[]{:S(2)}, u32[]{:S(2)}) collective-permute-start(bf16[72,768]{1,0:T(8,128)(2,1)S(1)} %collective-permute-done.10.refs_9_), channel_id=1, source_target_pairs={{0,4},{1,2},{3,0},{5,1},{7,3},{6,5},{4,7},{2,6},{8,12},{9,10},{11,... | collective-permute-start | bytes 331784 | tf_op jit(solution)/shard_map/ppermute | solution.py:299
  34.8 1.6 %collective-permute-start.14 = (bf16[72,768]{1,0:T(8,128)(2,1)S(1)}, bf16[72,768]{1,0:T(8,128)(2,1)S(1)}, u32[]{:S(2)}, u32[]{:S(2)}) collective-permute-start(bf16[72,768]{1,0:T(8,128)(2,1)S(1)} %collective-permute-done.10.refs_9_), channel_id=1, source_target_pairs={{0,2},{1,0},{3,1},{5,3},{7,5},{6,7},{4,6},{2,4},{8,10},{9,8},{11,9... | collective-permute-start | bytes 331784 | tf_op jit(solution)/shard_map/ppermute | solution.py:297
  36.8 2.7 %project.3 = (bf16[128,768]{1,0:T(8,128)(2,1)}, f32[128,1]{1,0:T(8,128)S(1)}, f32[2,128,1]{2,1,0:T(8,128)S(1)}, f32[144,1536]{1,0:T(8,128)S(1)}) custom-call(bf16[64,768]{1,0:T(8,128)(2,1)S(1)} %get-tuple-element.20.refs_0_, bf16[72,768]{1,0:T(8,128)(2,1)S(1)} %get-tuple-element.21.refs_1_, bf16[64,768]{1,0:T(8,128)(2,1)S(1)} %collective-permute-done.3.refs_2_, ...), custom_call_target="tpu_custom_call" | custom-call | flops 1698693120 | tf_op jit(solution)/shard_map/project/pallas_call | solution.py:245
  39.6 2.0 %collective-permute-done.16.refs_1_ = bf16[72,768]{1,0:T(8,128)(2,1)S(1)} collective-permute-done((bf16[72,768]{1,0:T(8,128)(2,1)S(1)}, bf16[72,768]{1,0:T(8,128)(2,1)S(1)}, u32[]{:S(2)}, u32[]{:S(2)}) %collective-permute-start.16) | collective-permute-done | bytes 110624 | tf_op jit(solution)/shard_map/ppermute | solution.py:299
  41.6 0.7 %project.4 = (f32[2,128,1]{2,1,0:T(8,128)S(1)}, f32[144,1536]{1,0:T(8,128)S(1)}) custom-call(bf16[64,768]{1,0:T(8,128)(2,1)S(1)} %collective-permute-done.15.refs_0_, bf16[72,768]{1,0:T(8,128)(2,1)S(1)} %collective-permute-done.16.refs_1_, bf16[6144,1536]{1,0:T(8,128)(2,1)S(1)} %bitcast.2, ...), custom_call_target="tpu_custom_call", output_to_operand_aliasing={{0}: (4, {}), {1}: (5, {})} | custom-call | flops 339738624 | tf_op jit(solution)/shard_map/project/pallas_call | solution.py:245
  42.3 1.8 %project.5 = bf16[128,1536]{1,0:T(8,128)(2,1)} custom-call(bf16[64,768]{1,0:T(8,128)(2,1)S(1)} %collective-permute-done.11.refs_0_, bf16[72,768]{1,0:T(8,128)(2,1)S(1)} %collective-permute-done.12.refs_1_, bf16[64,768]{1,0:T(8,128)(2,1)S(1)} %collective-permute-done.13.refs_2_, bf16[72,768]{1,0:T(8,128)(2,1)S(1)} %collective-permute-done.14.refs_3_, ...), custom_call_target="tpu_custom_call" | custom-call | flops 679477248 | tf_op jit(solution)/shard_map/project/pallas_call | solution.py:245
  (35 shorter events, 1.4 us)
Async XLA Ops:
  0.6 6.0 %copy-start.1 = (bf16[768]{0:T(1024)(128)(2,1)S(1)}, bf16[768]{0:T(1024)(128)(2,1)}, u32[]{:S(2)}) copy-start(bf16[768]{0:T(1024)(128)(2,1)} %param.8) | copy-start | bytes 4612
  6.1 1.6 %collective-permute-start = (bf16[1,128,768]{2,1,0:T(8,128)(2,1)S(1)}, bf16[1,128,768]{2,1,0:T(8,128)(2,1)S(1)}, u32[]{:S(2)}, u32[]{:S(2)}) collective-permute-start(bf16[1,128,768]{2,1,0:T(8,128)(2,1)S(1)} %get-tuple-element.16), channel_id=1, source_target_pairs={{0,8},{8,0},{16,24},{24,16},{1,9},{9,1},{17,25},{25,17},{2,10},{10... | collective-permute-start | bytes 589832 | tf_op jit(solution)/shard_map/ppermute | solution.py:280
  7.7 29.1 %slice-start = ((s8[18874368]{0:T(1024)(128)(4,1)}), s8[4194304]{0:T(1024)(128)(4,1)S(1)}, s32[]{:S(2)}) async-start(s8[18874368]{0:T(1024)(128)(4,1)} %bitcast.1), calls=%async_computation | async-start | bytes 8388608
  7.8 9.4 %collective-permute-start.1 = (bf16[128,768]{1,0:T(8,128)(2,1)S(1)}, bf16[128,768]{1,0:T(8,128)(2,1)S(1)}, u32[]{:S(2)}, u32[]{:S(2)}) collective-permute-start(bf16[128,768]{1,0:T(8,128)(2,1)S(1)} %bitcast.3), channel_id=1, source_target_pairs={{0,16},{8,24},{16,0},{24,8},{1,17},{9,25},{17,1},{25,9},{2,18},{10... | collective-permute-start | bytes 589832 | tf_op jit(solution)/shard_map/ppermute | solution.py:286
  10.7 26.1 %slice-start.1 = ((s8[18874368]{0:T(1024)(128)(4,1)}), s8[4194304]{0:T(1024)(128)(4,1)S(1)}, s32[]{:S(2)}) async-start(s8[18874368]{0:T(1024)(128)(4,1)} %bitcast.1), calls=%async_computation.1 | async-start | bytes 8388608
  10.7 26.1 %slice-start.2 = ((s8[18874368]{0:T(1024)(128)(4,1)}), s8[4194304]{0:T(1024)(128)(4,1)S(1)}, s32[]{:S(2)}) async-start(s8[18874368]{0:T(1024)(128)(4,1)} %bitcast.1), calls=%async_computation.2 | async-start | bytes 8388608
  13.9 3.3 %copy-start = (bf16[128,768]{1,0:T(8,128)(2,1)S(1)}, bf16[128,768]{1,0:T(8,128)(2,1)}, u32[]{:S(2)}) copy-start(bf16[128,768]{1,0:T(8,128)(2,1)} %param.7) | copy-start | bytes 589828
  13.9 22.9 %slice-start.3 = ((s8[18874368]{0:T(1024)(128)(4,1)}), s8[4194304]{0:T(1024)(128)(4,1)S(1)}, s32[]{:S(2)}) async-start(s8[18874368]{0:T(1024)(128)(4,1)} %bitcast.1), calls=%async_computation.3 | async-start | bytes 8388608
  13.9 22.9 %slice-start.4 = ((s8[18874368]{0:T(1024)(128)(4,1)}), s8[2097152]{0:T(1024)(128)(4,1)S(1)}, s32[]{:S(2)}) async-start(s8[18874368]{0:T(1024)(128)(4,1)} %bitcast.1), calls=%async_computation.4 | async-start | bytes 4194304
  13.9 3.3 %collective-permute-start.2 = (bf16[128,768]{1,0:T(8,128)(2,1)S(1)}, bf16[128,768]{1,0:T(8,128)(2,1)S(1)}, u32[]{:S(2)}, u32[]{:S(2)}) collective-permute-start(bf16[128,768]{1,0:T(8,128)(2,1)S(1)} %down.5), channel_id=1, source_target_pairs={{0,8},{8,0},{16,24},{24,16},{1,9},{9,1},{17,25},{25,17},{2,10},{10... | collective-permute-start | bytes 589832 | tf_op jit(solution)/shard_map/ppermute | solution.py:287
  17.4 5.7 %collective-permute-start.3 = (bf16[64,768]{1,0:T(8,128)(2,1)S(1)}, bf16[64,768]{1,0:T(8,128)(2,1)S(1)}, u32[]{:S(2)}, u32[]{:S(2)}) collective-permute-start(bf16[64,768]{1,0:T(8,128)(2,1)S(1)} %get-tuple-element.20.refs_0_), channel_id=1, source_target_pairs={{0,1},{1,3},{3,5},{5,7},{7,6},{6,4},{4,2},{2,0},{8,9},{9,11},{11,1... | collective-permute-start | bytes 294920 | tf_op jit(solution)/shard_map/ppermute | solution.py:297
  18.9 5.9 %collective-permute-start.6 = (bf16[72,768]{1,0:T(8,128)(2,1)S(1)}, bf16[72,768]{1,0:T(8,128)(2,1)S(1)}, u32[]{:S(2)}, u32[]{:S(2)}) collective-permute-start(bf16[72,768]{1,0:T(8,128)(2,1)S(1)} %get-tuple-element.21.refs_1_), channel_id=1, source_target_pairs={{0,2},{1,0},{3,1},{5,3},{7,5},{6,7},{4,6},{2,4},{8,10},{9,8},{11,9... | collective-permute-start | bytes 331784 | tf_op jit(solution)/shard_map/ppermute | solution.py:297
  19.4 5.9 %collective-permute-start.4 = (bf16[72,768]{1,0:T(8,128)(2,1)S(1)}, bf16[72,768]{1,0:T(8,128)(2,1)S(1)}, u32[]{:S(2)}, u32[]{:S(2)}) collective-permute-start(bf16[72,768]{1,0:T(8,128)(2,1)S(1)} %get-tuple-element.21.refs_1_), channel_id=1, source_target_pairs={{0,1},{1,3},{3,5},{5,7},{7,6},{6,4},{4,2},{2,0},{8,9},{9,11},{11,1... | collective-permute-start | bytes 331784 | tf_op jit(solution)/shard_map/ppermute | solution.py:297
  20.9 5.9 %collective-permute-start.5 = (bf16[64,768]{1,0:T(8,128)(2,1)S(1)}, bf16[64,768]{1,0:T(8,128)(2,1)S(1)}, u32[]{:S(2)}, u32[]{:S(2)}) collective-permute-start(bf16[64,768]{1,0:T(8,128)(2,1)S(1)} %get-tuple-element.20.refs_0_), channel_id=1, source_target_pairs={{0,2},{1,0},{3,1},{5,3},{7,5},{6,7},{4,6},{2,4},{8,10},{9,8},{11,9... | collective-permute-start | bytes 294920 | tf_op jit(solution)/shard_map/ppermute | solution.py:297
  23.1 4.7 %collective-permute-start.7 = (bf16[64,768]{1,0:T(8,128)(2,1)S(1)}, bf16[64,768]{1,0:T(8,128)(2,1)S(1)}, u32[]{:S(2)}, u32[]{:S(2)}) collective-permute-start(bf16[64,768]{1,0:T(8,128)(2,1)S(1)} %collective-permute-done.3.refs_2_), channel_id=1, source_target_pairs={{0,1},{1,3},{3,5},{5,7},{7,6},{6,4},{4,2},{2,0},{8,9},{9,11},{11,1... | collective-permute-start | bytes 294920 | tf_op jit(solution)/shard_map/ppermute | solution.py:297
  24.8 8.0 %collective-permute-start.10 = (bf16[72,768]{1,0:T(8,128)(2,1)S(1)}, bf16[72,768]{1,0:T(8,128)(2,1)S(1)}, u32[]{:S(2)}, u32[]{:S(2)}) collective-permute-start(bf16[72,768]{1,0:T(8,128)(2,1)S(1)} %collective-permute-done.6.refs_5_), channel_id=1, source_target_pairs={{0,2},{1,0},{3,1},{5,3},{7,5},{6,7},{4,6},{2,4},{8,10},{9,8},{11,9... | collective-permute-start | bytes 331784 | tf_op jit(solution)/shard_map/ppermute | solution.py:297
  25.3 9.5 %collective-permute-start.8 = (bf16[72,768]{1,0:T(8,128)(2,1)S(1)}, bf16[72,768]{1,0:T(8,128)(2,1)S(1)}, u32[]{:S(2)}, u32[]{:S(2)}) collective-permute-start(bf16[72,768]{1,0:T(8,128)(2,1)S(1)} %collective-permute-done.4.refs_3_), channel_id=1, source_target_pairs={{0,1},{1,3},{3,5},{5,7},{7,6},{6,4},{4,2},{2,0},{8,9},{9,11},{11,1... | collective-permute-start | bytes 331784 | tf_op jit(solution)/shard_map/ppermute | solution.py:297
  26.8 5.1 %collective-permute-start.9 = (bf16[64,768]{1,0:T(8,128)(2,1)S(1)}, bf16[64,768]{1,0:T(8,128)(2,1)S(1)}, u32[]{:S(2)}, u32[]{:S(2)}) collective-permute-start(bf16[64,768]{1,0:T(8,128)(2,1)S(1)} %collective-permute-done.5.refs_4_), channel_id=1, source_target_pairs={{0,2},{1,0},{3,1},{5,3},{7,5},{6,7},{4,6},{2,4},{8,10},{9,8},{11,9... | collective-permute-start | bytes 294920 | tf_op jit(solution)/shard_map/ppermute | solution.py:297
  27.8 8.6 %collective-permute-start.15 = (bf16[64,768]{1,0:T(8,128)(2,1)S(1)}, bf16[64,768]{1,0:T(8,128)(2,1)S(1)}, u32[]{:S(2)}, u32[]{:S(2)}) collective-permute-start(bf16[64,768]{1,0:T(8,128)(2,1)S(1)} %collective-permute-done.7.refs_6_), channel_id=1, source_target_pairs={{0,3},{1,5},{3,7},{5,6},{7,4},{6,2},{4,0},{2,1},{8,11},{9,13},{11,... | collective-permute-start | bytes 294920 | tf_op jit(solution)/shard_map/ppermute | solution.py:299
  30.3 11.9 %collective-permute-start.11 = (bf16[64,768]{1,0:T(8,128)(2,1)S(1)}, bf16[64,768]{1,0:T(8,128)(2,1)S(1)}, u32[]{:S(2)}, u32[]{:S(2)}) collective-permute-start(bf16[64,768]{1,0:T(8,128)(2,1)S(1)} %collective-permute-done.7.refs_6_), channel_id=1, source_target_pairs={{0,1},{1,3},{3,5},{5,7},{7,6},{6,4},{4,2},{2,0},{8,9},{9,11},{11,1... | collective-permute-start | bytes 294920 | tf_op jit(solution)/shard_map/ppermute | solution.py:297
  31.9 10.4 %collective-permute-start.13 = (bf16[64,768]{1,0:T(8,128)(2,1)S(1)}, bf16[64,768]{1,0:T(8,128)(2,1)S(1)}, u32[]{:S(2)}, u32[]{:S(2)}) collective-permute-start(bf16[64,768]{1,0:T(8,128)(2,1)S(1)} %collective-permute-done.9.refs_8_), channel_id=1, source_target_pairs={{0,2},{1,0},{3,1},{5,3},{7,5},{6,7},{4,6},{2,4},{8,10},{9,8},{11,9... | collective-permute-start | bytes 294920 | tf_op jit(solution)/shard_map/ppermute | solution.py:297
  32.8 8.8 %collective-permute-start.16 = (bf16[72,768]{1,0:T(8,128)(2,1)S(1)}, bf16[72,768]{1,0:T(8,128)(2,1)S(1)}, u32[]{:S(2)}, u32[]{:S(2)}) collective-permute-start(bf16[72,768]{1,0:T(8,128)(2,1)S(1)} %collective-permute-done.10.refs_9_), channel_id=1, source_target_pairs={{0,4},{1,2},{3,0},{5,1},{7,3},{6,5},{4,7},{2,6},{8,12},{9,10},{11,... | collective-permute-start | bytes 331784 | tf_op jit(solution)/shard_map/ppermute | solution.py:299
  34.8 7.5 %collective-permute-start.14 = (bf16[72,768]{1,0:T(8,128)(2,1)S(1)}, bf16[72,768]{1,0:T(8,128)(2,1)S(1)}, u32[]{:S(2)}, u32[]{:S(2)}) collective-permute-start(bf16[72,768]{1,0:T(8,128)(2,1)S(1)} %collective-permute-done.10.refs_9_), channel_id=1, source_target_pairs={{0,2},{1,0},{3,1},{5,3},{7,5},{6,7},{4,6},{2,4},{8,10},{9,8},{11,9... | collective-permute-start | bytes 331784 | tf_op jit(solution)/shard_map/ppermute | solution.py:297
  36.4 5.9 %collective-permute-start.12 = (bf16[72,768]{1,0:T(8,128)(2,1)S(1)}, bf16[72,768]{1,0:T(8,128)(2,1)S(1)}, u32[]{:S(2)}, u32[]{:S(2)}) collective-permute-start(bf16[72,768]{1,0:T(8,128)(2,1)S(1)} %collective-permute-done.8.refs_7_), channel_id=1, source_target_pairs={{0,1},{1,3},{3,5},{5,7},{7,6},{6,4},{4,2},{2,0},{8,9},{9,11},{11,1... | collective-permute-start | bytes 331784 | tf_op jit(solution)/shard_map/ppermute | solution.py:297

commit v16 on v13

--- a/solution.py
+++ b/solution.py
@@ -79,7 +79,13 @@
         for row in range(0, tokens, 128):
             for column in range(0, width, 512):
                 place = pl.ds(row, 128), pl.ds(column, min(512, width - column))
-                total[place] += jnp.dot(h_buf[k, place[0], :], held[span(k), place[1]], preferred_element_type=jnp.float32)
+                cuts = [0, depth] if width - column >= 512 or depth % 512 else [0, depth // 2, depth]
+                value = total[place]
+                for low, high in zip(cuts, cuts[1:]):
+                    left = h_buf[k, place[0], low:high]
+                    right = held[pl.ds(pl.multiple_of(k * depth + low, 256), high - low), place[1]]
+                    value = value + jnp.dot(left, right, preferred_element_type=jnp.float32)
+                total[place] = value
         return _
 
     lax.fori_loop(0, parts, body, 0)
@@ -91,7 +97,7 @@
 
 def down(hidden, weight, tok, chips_y, own):
     inner, width = weight.shape
-    depth = cut(inner, 1536 if own else 768)
+    depth = cut(inner, 1536)
     parts = inner // depth
     chips = 1 if own else chips_y - 1
     tokens = chips * CORES * tok
@@ -280,16 +286,16 @@
 
         up, back = [upper, lower], [upper, lower]
         pieces, hops = [[upper, lower]], [0]
-        for step in range(1, half):
+        for step in range(1, half - 1):
             for i in range(2):
                 up[i], back[i] = lax.ppermute(up[i], "col", shift(1)), lax.ppermute(back[i], "col", shift(-1))
             pieces += [list(up), list(back)]
             hops += [-step, step]
-        stream, state = project(pieces[:-2], hops[:-2], qk_weight, None, cycle, False)
-        back[1], state = lax.optimization_barrier((back[1], state))
-        opposite = [lax.ppermute(up[0], "col", shift(1)), lax.ppermute(back[1], "col", shift(-1))]
-        state = project(pieces[-2:], hops[-2:], qk_weight, state, cycle, False)
-        return stream, project([opposite], [half], qk_weight, state, cycle, True)
+        opposite = lax.ppermute(up[0], "col", shift(2)), lax.ppermute(back[1], "col", shift(-2))
+        far = [[lax.ppermute(jnp.concatenate(way), "col", shift(hop))] for way, hop in ((up, 1), (back, -1))]
+        stream, state = project(pieces, hops, qk_weight, None, cycle, False)
+        state = project([opposite], [half], qk_weight, state, cycle, False)
+        return stream, project(far, [1 - half, half - 1], qk_weight, state, cycle, True)
 
     placed = (P(None, "row"), P("row", "col"), P("row", "col"), P("col"), P(None, "col"))
     return jax.shard_map(

time: 45.4 us -> 49.4 us (1.088)
  waiting for transfers between devices: 10.8 us -> 15.9 us
  starting transfers between devices: 18.4 us -> 16.9 us
    ppermute x6 -> x4, waiting for transfers between devices: 3.74 us -> 7.66 us  [per_device(): lax.ppermute(up[i], 'col', shift(1))]
    ppermute x6 -> x4, starting transfers between devices: 8.88 us -> 6.35 us  [per_device(): lax.ppermute(back[i], 'col', shift(-1))]
    ppermute x2 -> x4, starting transfers between devices: 2.03 us -> 4.13 us  [the longest x1 2.6 us: per_device(): lax.ppermute(up[0], 'col', shift(2))]
    ppermute x6 -> x4, starting transfers between devices: 3.92 us -> 2.84 us  [per_device(): lax.ppermute(up[i], 'col', shift(1))]
    ppermute x6 -> x4, waiting for transfers between devices: 1.54 us -> 2.31 us  [per_device(): lax.ppermute(back[i], 'col', shift(-1))]
    ppermute x2 -> x4, waiting for transfers between devices: 3.12 us -> 3.47 us  [the longest x1 1.81 us: per_device(): lax.ppermute(back[1], 'col', shift(-2))]
  transfers between devices with their start and end apart: 17 -> 15, of which waited for: 8 -> 9; matrix products, arithmetic and copies ran while one was open for 0% -> 0% of each run, Pallas kernels for 18% -> 16%
where the time goes in v16:
time: 49.4 us; the launch traced here: 49.2 us
  starting transfers between devices  16.9 us (34%)
  waiting for transfers between devices  15.9 us (32%)
  Pallas kernels  15.5 us (31%)
  between operations  0.77 us (2%)
    pallas_call x2, Pallas kernels, down(): pl.pallas_call(functools.partial(down_kernel, chips_y, tok, parts, own),...  10.3 us
    ppermute x4, waiting for transfers between devices, per_device(): lax.ppermute(up[i], 'col', shift(1))  7.66 us
    ppermute x4, starting transfers between devices, per_device(): lax.ppermute(back[i], 'col', shift(-1))  6.35 us
    pallas_call x3, Pallas kernels, project(): pl.pallas_call(functools.partial(project_kernel, cycle, hops, [len(parts)...  5.16 us
    ppermute x1, starting transfers between devices, per_device(): lax.ppermute(both[step - 1], 'row', move).astype(jnp.float32)  2.95 us
    ppermute x4, starting transfers between devices, per_device(): lax.ppermute(up[i], 'col', shift(1))  2.84 us
    ppermute x1, starting transfers between devices, per_device(): lax.ppermute(up[0], 'col', shift(2))  2.6 us
    ppermute x4, waiting for transfers between devices, per_device(): lax.ppermute(back[i], 'col', shift(-1))  2.31 us
  transfers between devices with their start and end apart: 15, of which 9 were waited for; matrix products, arithmetic and copies ran while one was open for 0% of the time, Pallas kernels for 16%

profile of v16, /device:TPU:0, one launch (start us, length us, event | category | flops | bytes accessed | tf_op | source)
XLA Modules:
  0.0 49.2 jit_solution(18014770274125448971)
XLA Ops:
  0.7 5.7 %down.2 = (bf16[1,128,768]{2,1,0:T(8,128)(2,1)S(1)}, bf16[1,128,768]{2,1,0:T(8,128)(2,1)S(1)}, bf16[6144,768]{1,0:T(8,128)(2,1)S(1)}) custom-call(bf16[512,6144]{1,0:T(8,128)(2,1)} %hidden.2, bf16[6144,768]{1,0:T(8,128)(2,1)} %weight.1), custom_call_target="tpu_custom_call" | custom-call | flops 2415919104 | bytes 12582912 | tf_op jit(solution)/shard_map/down/pallas_call | solution.py:106
  6.4 0.5 %collective-permute-start = (bf16[1,128,768]{2,1,0:T(8,128)(2,1)S(1)}, bf16[1,128,768]{2,1,0:T(8,128)(2,1)S(1)}, u32[]{:S(2)}, u32[]{:S(2)}) collective-permute-start(bf16[1,128,768]{2,1,0:T(8,128)(2,1)S(1)} %get-tuple-element.18), channel_id=1, source_target_pairs={{0,8},{8,0},{16,24},{24,16},{1,9},{9,1},{17,25},{25,17},{2,10},{10... | collective-permute-start | bytes 589832 | tf_op jit(solution)/shard_map/ppermute | solution.py:276
  6.9 1.1 %collective-permute-done = bf16[1,128,768]{2,1,0:T(8,128)(2,1)S(1)} collective-permute-done((bf16[1,128,768]{2,1,0:T(8,128)(2,1)S(1)}, bf16[1,128,768]{2,1,0:T(8,128)(2,1)S(1)}, u32[]{:S(2)}, u32[]{:S(2)}) %collective-permute-start) | collective-permute-done | bytes 196640 | tf_op jit(solution)/shard_map/ppermute | solution.py:276
  8.1 3.0 %collective-permute-start.1 = (bf16[128,768]{1,0:T(8,128)(2,1)S(1)}, bf16[128,768]{1,0:T(8,128)(2,1)S(1)}, u32[]{:S(2)}, u32[]{:S(2)}) collective-permute-start(bf16[128,768]{1,0:T(8,128)(2,1)S(1)} %bitcast.7), channel_id=1, source_target_pairs={{0,16},{8,24},{16,0},{24,8},{1,17},{9,25},{17,1},{25,9},{2,18},{10... | collective-permute-start | bytes 589832 | tf_op jit(solution)/shard_map/ppermute | solution.py:282
  11.0 4.6 %down.3 = (bf16[1,128,768]{2,1,0:T(8,128)(2,1)S(1)}, bf16[1,128,768]{2,1,0:T(8,128)(2,1)S(1)}) custom-call(bf16[512,6144]{1,0:T(8,128)(2,1)} %hidden.2, bf16[6144,768]{1,0:T(8,128)(2,1)S(1)} %get-tuple-element.21.weight), custom_call_target="tpu_custom_call" | custom-call | flops 2415919104 | bytes 3145728 | tf_op jit(solution)/shard_map/down/pallas_call | solution.py:106
  15.7 0.6 %collective-permute-done.1 = bf16[128,768]{1,0:T(8,128)(2,1)S(1)} collective-permute-done((bf16[128,768]{1,0:T(8,128)(2,1)S(1)}, bf16[128,768]{1,0:T(8,128)(2,1)S(1)}, u32[]{:S(2)}, u32[]{:S(2)}) %collective-permute-start.1) | collective-permute-done | bytes 196640 | tf_op jit(solution)/shard_map/ppermute | solution.py:282
  16.3 0.8 %collective-permute-done.2.got = bf16[128,768]{1,0:T(8,128)(2,1)S(1)} collective-permute-done((bf16[128,768]{1,0:T(8,128)(2,1)S(1)}, bf16[128,768]{1,0:T(8,128)(2,1)S(1)}, u32[]{:S(2)}, u32[]{:S(2)}) %collective-permute-start.2) | collective-permute-done | bytes 196640 | tf_op jit(solution)/shard_map/ppermute | solution.py:284
  17.2 1.6 %collective-permute-start.6 = (bf16[72,768]{1,0:T(8,128)(2,1)S(1)}, bf16[72,768]{1,0:T(8,128)(2,1)S(1)}, u32[]{:S(2)}, u32[]{:S(2)}) collective-permute-start(bf16[72,768]{1,0:T(8,128)(2,1)S(1)} %get-tuple-element.25.refs_1_), channel_id=1, source_target_pairs={{0,2},{1,0},{3,1},{5,3},{7,5},{6,7},{4,6},{2,4},{8,10},{9,8},{11,9... | collective-permute-start | bytes 331784 | tf_op jit(solution)/shard_map/ppermute | solution.py:291
  18.8 1.6 %collective-permute-start.5 = (bf16[64,768]{1,0:T(8,128)(2,1)S(1)}, bf16[64,768]{1,0:T(8,128)(2,1)S(1)}, u32[]{:S(2)}, u32[]{:S(2)}) collective-permute-start(bf16[64,768]{1,0:T(8,128)(2,1)S(1)} %get-tuple-element.24.refs_0_), channel_id=1, source_target_pairs={{0,2},{1,0},{3,1},{5,3},{7,5},{6,7},{4,6},{2,4},{8,10},{9,8},{11,9... | collective-permute-start | bytes 294920 | tf_op jit(solution)/shard_map/ppermute | solution.py:291
  20.8 2.3 %collective-permute-done.6.refs_5_ = bf16[72,768]{1,0:T(8,128)(2,1)S(1)} collective-permute-done((bf16[72,768]{1,0:T(8,128)(2,1)S(1)}, bf16[72,768]{1,0:T(8,128)(2,1)S(1)}, u32[]{:S(2)}, u32[]{:S(2)}) %collective-permute-start.6) | collective-permute-done | bytes 110624 | tf_op jit(solution)/shard_map/ppermute | solution.py:291
  23.1 1.6 %collective-permute-start.10 = (bf16[72,768]{1,0:T(8,128)(2,1)S(1)}, bf16[72,768]{1,0:T(8,128)(2,1)S(1)}, u32[]{:S(2)}, u32[]{:S(2)}) collective-permute-start(bf16[72,768]{1,0:T(8,128)(2,1)S(1)} %collective-permute-done.6.refs_5_), channel_id=1, source_target_pairs={{0,2},{1,0},{3,1},{5,3},{7,5},{6,7},{4,6},{2,4},{8,10},{9,8},{11,9... | collective-permute-start | bytes 331784 | tf_op jit(solution)/shard_map/ppermute | solution.py:291
  25.2 1.6 %collective-permute-start.9 = (bf16[64,768]{1,0:T(8,128)(2,1)S(1)}, bf16[64,768]{1,0:T(8,128)(2,1)S(1)}, u32[]{:S(2)}, u32[]{:S(2)}) collective-permute-start(bf16[64,768]{1,0:T(8,128)(2,1)S(1)} %collective-permute-done.5.refs_4_), channel_id=1, source_target_pairs={{0,2},{1,0},{3,1},{5,3},{7,5},{6,7},{4,6},{2,4},{8,10},{9,8},{11,9... | collective-permute-start | bytes 294920 | tf_op jit(solution)/shard_map/ppermute | solution.py:291
  26.7 2.9 %collective-permute-done.3.refs_2_ = bf16[64,768]{1,0:T(8,128)(2,1)S(1)} collective-permute-done((bf16[64,768]{1,0:T(8,128)(2,1)S(1)}, bf16[64,768]{1,0:T(8,128)(2,1)S(1)}, u32[]{:S(2)}, u32[]{:S(2)}) %collective-permute-start.3) | collective-permute-done | bytes 98336 | tf_op jit(solution)/shard_map/ppermute | solution.py:291
  30.1 1.5 %collective-permute-start.8 = (bf16[72,768]{1,0:T(8,128)(2,1)S(1)}, bf16[72,768]{1,0:T(8,128)(2,1)S(1)}, u32[]{:S(2)}, u32[]{:S(2)}) collective-permute-start(bf16[72,768]{1,0:T(8,128)(2,1)S(1)} %collective-permute-done.4.refs_3_), channel_id=1, source_target_pairs={{0,1},{1,3},{3,5},{5,7},{7,6},{6,4},{4,2},{2,0},{8,9},{9,11},{11,1... | collective-permute-start | bytes 331784 | tf_op jit(solution)/shard_map/ppermute | solution.py:291
  31.7 0.6 %collective-permute-start.12 = (bf16[136,768]{1,0:T(8,128)(2,1)S(1)}, bf16[136,768]{1,0:T(8,128)(2,1)S(1)}, u32[]{:S(2)}, u32[]{:S(2)}) collective-permute-start(bf16[136,768]{1,0:T(8,128)(2,1)S(1)} %pad_maximum_fusion.1), channel_id=1, source_target_pairs={{0,2},{1,0},{3,1},{5,3},{7,5},{6,7},{4,6},{2,4},{8,10},{9,8},{11,9... | collective-permute-start | bytes 626696 | tf_op jit(solution)/shard_map/ppermute | solution.py:295
  32.2 2.3 %collective-permute-done.7.refs_6_ = bf16[64,768]{1,0:T(8,128)(2,1)S(1)} collective-permute-done((bf16[64,768]{1,0:T(8,128)(2,1)S(1)}, bf16[64,768]{1,0:T(8,128)(2,1)S(1)}, u32[]{:S(2)}, u32[]{:S(2)}) %collective-permute-start.7) | collective-permute-done | bytes 98336 | tf_op jit(solution)/shard_map/ppermute | solution.py:291
  34.6 2.4 %collective-permute-done.8.refs_7_ = bf16[72,768]{1,0:T(8,128)(2,1)S(1)} collective-permute-done((bf16[72,768]{1,0:T(8,128)(2,1)S(1)}, bf16[72,768]{1,0:T(8,128)(2,1)S(1)}, u32[]{:S(2)}, u32[]{:S(2)}) %collective-permute-start.8) | collective-permute-done | bytes 110624 | tf_op jit(solution)/shard_map/ppermute | solution.py:291
  37.0 0.6 %collective-permute-start.11 = (bf16[136,768]{1,0:T(8,128)(2,1)S(1)}, bf16[136,768]{1,0:T(8,128)(2,1)S(1)}, u32[]{:S(2)}, u32[]{:S(2)}) collective-permute-start(bf16[136,768]{1,0:T(8,128)(2,1)S(1)} %pad_maximum_fusion), channel_id=1, source_target_pairs={{0,1},{1,3},{3,5},{5,7},{7,6},{6,4},{4,2},{2,0},{8,9},{9,11},{11,1... | collective-permute-start | bytes 626696 | tf_op jit(solution)/shard_map/ppermute | solution.py:295
  37.6 2.6 %collective-permute-start.13 = (bf16[64,768]{1,0:T(8,128)(2,1)S(1)}, bf16[64,768]{1,0:T(8,128)(2,1)S(1)}, u32[]{:S(2)}, u32[]{:S(2)}) collective-permute-start(bf16[64,768]{1,0:T(8,128)(2,1)S(1)} %collective-permute-done.7.refs_6_), channel_id=1, source_target_pairs={{0,3},{1,5},{3,7},{5,6},{7,4},{6,2},{4,0},{2,1},{8,11},{9,13},{11,... | collective-permute-start | bytes 294920 | tf_op jit(solution)/shard_map/ppermute | solution.py:294
  40.5 2.7 %project.3 = (bf16[128,768]{1,0:T(8,128)(2,1)}, f32[128,1]{1,0:T(8,128)S(1)}, f32[2,128,1]{2,1,0:T(8,128)S(1)}, f32[144,1536]{1,0:T(8,128)S(1)}) custom-call(bf16[64,768]{1,0:T(8,128)(2,1)S(1)} %get-tuple-element.24.refs_0_, bf16[72,768]{1,0:T(8,128)(2,1)S(1)} %get-tuple-element.25.refs_1_, bf16[64,768]{1,0:T(8,128)(2,1)S(1)} %collective-permute-done.3.refs_2_, ...), custom_call_target="tpu_custom_call" | custom-call | flops 1698693120 | tf_op jit(solution)/shard_map/project/pallas_call | solution.py:241
  43.3 1.7 %collective-permute-done.13.refs_0_ = bf16[64,768]{1,0:T(8,128)(2,1)S(1)} collective-permute-done((bf16[64,768]{1,0:T(8,128)(2,1)S(1)}, bf16[64,768]{1,0:T(8,128)(2,1)S(1)}, u32[]{:S(2)}, u32[]{:S(2)}) %collective-permute-start.13) | collective-permute-done | bytes 98336 | tf_op jit(solution)/shard_map/ppermute | solution.py:294
  44.9 1.8 %collective-permute-done.14.refs_1_ = bf16[72,768]{1,0:T(8,128)(2,1)S(1)} collective-permute-done((bf16[72,768]{1,0:T(8,128)(2,1)S(1)}, bf16[72,768]{1,0:T(8,128)(2,1)S(1)}, u32[]{:S(2)}, u32[]{:S(2)}) %collective-permute-start.14) | collective-permute-done | bytes 110624 | tf_op jit(solution)/shard_map/ppermute | solution.py:294
  46.8 0.7 %project.4 = (f32[2,128,1]{2,1,0:T(8,128)S(1)}, f32[144,1536]{1,0:T(8,128)S(1)}) custom-call(bf16[64,768]{1,0:T(8,128)(2,1)S(1)} %collective-permute-done.13.refs_0_, bf16[72,768]{1,0:T(8,128)(2,1)S(1)} %collective-permute-done.14.refs_1_, bf16[6144,1536]{1,0:T(8,128)(2,1)S(1)} %bitcast.4, ...), custom_call_target="tpu_custom_call", output_to_operand_aliasing={{0}: (4, {}), {1}: (5, {})} | custom-call | flops 339738624 | tf_op jit(solution)/shard_map/project/pallas_call | solution.py:241
  47.5 1.8 %project.5 = bf16[128,1536]{1,0:T(8,128)(2,1)} custom-call(bf16[136,768]{1,0:T(8,128)(2,1)S(1)} %collective-permute-done.11.refs_0_, bf16[136,768]{1,0:T(8,128)(2,1)S(1)} %collective-permute-done.12.refs_1_, bf16[6144,1536]{1,0:T(8,128)(2,1)S(1)} %bitcast.4, f32[128,1]{1,0:T(8,128)S(1)} %get-tuple-element.27.refs_3_, ...), custom_call_target="tpu_custom_call" | custom-call | flops 679477248 | tf_op jit(solution)/shard_map/project/pallas_call | solution.py:241
  (32 shorter events, 2.0 us)
Async XLA Ops:
  0.6 6.3 %copy-start.1 = (bf16[768]{0:T(1024)(128)(2,1)S(1)}, bf16[768]{0:T(1024)(128)(2,1)}, u32[]{:S(2)}) copy-start(bf16[768]{0:T(1024)(128)(2,1)} %param.8) | copy-start | bytes 4612
  0.6 39.9 %slice-start = ((s8[18874368]{0:T(1024)(128)(4,1)}), s8[4194304]{0:T(1024)(128)(4,1)S(1)}, s32[]{:S(2)}) async-start(s8[18874368]{0:T(1024)(128)(4,1)} %bitcast.3), calls=%async_computation | async-start | bytes 8388608
  0.7 39.9 %slice-start.1 = ((s8[18874368]{0:T(1024)(128)(4,1)}), s8[4194304]{0:T(1024)(128)(4,1)S(1)}, s32[]{:S(2)}) async-start(s8[18874368]{0:T(1024)(128)(4,1)} %bitcast.3), calls=%async_computation.1 | async-start | bytes 8388608
  0.7 39.9 %slice-start.2 = ((s8[18874368]{0:T(1024)(128)(4,1)}), s8[4194304]{0:T(1024)(128)(4,1)S(1)}, s32[]{:S(2)}) async-start(s8[18874368]{0:T(1024)(128)(4,1)} %bitcast.3), calls=%async_computation.2 | async-start | bytes 8388608
  6.4 9.8 %copy-start = (bf16[128,768]{1,0:T(8,128)(2,1)S(1)}, bf16[128,768]{1,0:T(8,128)(2,1)}, u32[]{:S(2)}) copy-start(bf16[128,768]{1,0:T(8,128)(2,1)} %param.7) | copy-start | bytes 589828
  6.4 1.6 %collective-permute-start = (bf16[1,128,768]{2,1,0:T(8,128)(2,1)S(1)}, bf16[1,128,768]{2,1,0:T(8,128)(2,1)S(1)}, u32[]{:S(2)}, u32[]{:S(2)}) collective-permute-start(bf16[1,128,768]{2,1,0:T(8,128)(2,1)S(1)} %get-tuple-element.18), channel_id=1, source_target_pairs={{0,8},{8,0},{16,24},{24,16},{1,9},{9,1},{17,25},{25,17},{2,10},{10... | collective-permute-start | bytes 589832 | tf_op jit(solution)/shard_map/ppermute | solution.py:276
  8.1 8.2 %collective-permute-start.1 = (bf16[128,768]{1,0:T(8,128)(2,1)S(1)}, bf16[128,768]{1,0:T(8,128)(2,1)S(1)}, u32[]{:S(2)}, u32[]{:S(2)}) collective-permute-start(bf16[128,768]{1,0:T(8,128)(2,1)S(1)} %bitcast.7), channel_id=1, source_target_pairs={{0,16},{8,24},{16,0},{24,8},{1,17},{9,25},{17,1},{25,9},{2,18},{10... | collective-permute-start | bytes 589832 | tf_op jit(solution)/shard_map/ppermute | solution.py:282
  11.0 29.5 %slice-start.3 = ((s8[18874368]{0:T(1024)(128)(4,1)}), s8[4194304]{0:T(1024)(128)(4,1)S(1)}, s32[]{:S(2)}) async-start(s8[18874368]{0:T(1024)(128)(4,1)} %bitcast.3), calls=%async_computation.3 | async-start | bytes 8388608
  11.0 29.5 %slice-start.4 = ((s8[18874368]{0:T(1024)(128)(4,1)}), s8[2097152]{0:T(1024)(128)(4,1)S(1)}, s32[]{:S(2)}) async-start(s8[18874368]{0:T(1024)(128)(4,1)} %bitcast.3), calls=%async_computation.4 | async-start | bytes 4194304
  15.6 1.5 %collective-permute-start.2 = (bf16[128,768]{1,0:T(8,128)(2,1)S(1)}, bf16[128,768]{1,0:T(8,128)(2,1)S(1)}, u32[]{:S(2)}, u32[]{:S(2)}) collective-permute-start(bf16[128,768]{1,0:T(8,128)(2,1)S(1)} %bitcast.6), channel_id=1, source_target_pairs={{0,8},{8,0},{16,24},{24,16},{1,9},{9,1},{17,25},{25,17},{2,10},{10... | collective-permute-start | bytes 589832 | tf_op jit(solution)/shard_map/ppermute | solution.py:284
  17.2 6.0 %collective-permute-start.6 = (bf16[72,768]{1,0:T(8,128)(2,1)S(1)}, bf16[72,768]{1,0:T(8,128)(2,1)S(1)}, u32[]{:S(2)}, u32[]{:S(2)}) collective-permute-start(bf16[72,768]{1,0:T(8,128)(2,1)S(1)} %get-tuple-element.25.refs_1_), channel_id=1, source_target_pairs={{0,2},{1,0},{3,1},{5,3},{7,5},{6,7},{4,6},{2,4},{8,10},{9,8},{11,9... | collective-permute-start | bytes 331784 | tf_op jit(solution)/shard_map/ppermute | solution.py:291
  18.8 6.4 %collective-permute-start.5 = (bf16[64,768]{1,0:T(8,128)(2,1)S(1)}, bf16[64,768]{1,0:T(8,128)(2,1)S(1)}, u32[]{:S(2)}, u32[]{:S(2)}) collective-permute-start(bf16[64,768]{1,0:T(8,128)(2,1)S(1)} %get-tuple-element.24.refs_0_), channel_id=1, source_target_pairs={{0,2},{1,0},{3,1},{5,3},{7,5},{6,7},{4,6},{2,4},{8,10},{9,8},{11,9... | collective-permute-start | bytes 294920 | tf_op jit(solution)/shard_map/ppermute | solution.py:291
  20.4 9.8 %collective-permute-start.4 = (bf16[72,768]{1,0:T(8,128)(2,1)S(1)}, bf16[72,768]{1,0:T(8,128)(2,1)S(1)}, u32[]{:S(2)}, u32[]{:S(2)}) collective-permute-start(bf16[72,768]{1,0:T(8,128)(2,1)S(1)} %get-tuple-element.25.refs_1_), channel_id=1, source_target_pairs={{0,1},{1,3},{3,5},{5,7},{7,6},{6,4},{4,2},{2,0},{8,9},{9,11},{11,1... | collective-permute-start | bytes 331784 | tf_op jit(solution)/shard_map/ppermute | solution.py:291
  23.1 8.5 %collective-permute-start.10 = (bf16[72,768]{1,0:T(8,128)(2,1)S(1)}, bf16[72,768]{1,0:T(8,128)(2,1)S(1)}, u32[]{:S(2)}, u32[]{:S(2)}) collective-permute-start(bf16[72,768]{1,0:T(8,128)(2,1)S(1)} %collective-permute-done.6.refs_5_), channel_id=1, source_target_pairs={{0,2},{1,0},{3,1},{5,3},{7,5},{6,7},{4,6},{2,4},{8,10},{9,8},{11,9... | collective-permute-start | bytes 331784 | tf_op jit(solution)/shard_map/ppermute | solution.py:291
  24.7 5.0 %collective-permute-start.3 = (bf16[64,768]{1,0:T(8,128)(2,1)S(1)}, bf16[64,768]{1,0:T(8,128)(2,1)S(1)}, u32[]{:S(2)}, u32[]{:S(2)}) collective-permute-start(bf16[64,768]{1,0:T(8,128)(2,1)S(1)} %get-tuple-element.24.refs_0_), channel_id=1, source_target_pairs={{0,1},{1,3},{3,5},{5,7},{7,6},{6,4},{4,2},{2,0},{8,9},{9,11},{11,1... | collective-permute-start | bytes 294920 | tf_op jit(solution)/shard_map/ppermute | solution.py:291
  25.2 6.5 %collective-permute-start.9 = (bf16[64,768]{1,0:T(8,128)(2,1)S(1)}, bf16[64,768]{1,0:T(8,128)(2,1)S(1)}, u32[]{:S(2)}, u32[]{:S(2)}) collective-permute-start(bf16[64,768]{1,0:T(8,128)(2,1)S(1)} %collective-permute-done.5.refs_4_), channel_id=1, source_target_pairs={{0,2},{1,0},{3,1},{5,3},{7,5},{6,7},{4,6},{2,4},{8,10},{9,8},{11,9... | collective-permute-start | bytes 294920 | tf_op jit(solution)/shard_map/ppermute | solution.py:291
  29.7 4.9 %collective-permute-start.7 = (bf16[64,768]{1,0:T(8,128)(2,1)S(1)}, bf16[64,768]{1,0:T(8,128)(2,1)S(1)}, u32[]{:S(2)}, u32[]{:S(2)}) collective-permute-start(bf16[64,768]{1,0:T(8,128)(2,1)S(1)} %collective-permute-done.3.refs_2_), channel_id=1, source_target_pairs={{0,1},{1,3},{3,5},{5,7},{7,6},{6,4},{4,2},{2,0},{8,9},{9,11},{11,1... | collective-permute-start | bytes 294920 | tf_op jit(solution)/shard_map/ppermute | solution.py:291
  30.1 6.8 %collective-permute-start.8 = (bf16[72,768]{1,0:T(8,128)(2,1)S(1)}, bf16[72,768]{1,0:T(8,128)(2,1)S(1)}, u32[]{:S(2)}, u32[]{:S(2)}) collective-permute-start(bf16[72,768]{1,0:T(8,128)(2,1)S(1)} %collective-permute-done.4.refs_3_), channel_id=1, source_target_pairs={{0,1},{1,3},{3,5},{5,7},{7,6},{6,4},{4,2},{2,0},{8,9},{9,11},{11,1... | collective-permute-start | bytes 331784 | tf_op jit(solution)/shard_map/ppermute | solution.py:291
  31.7 15.8 %collective-permute-start.12 = (bf16[136,768]{1,0:T(8,128)(2,1)S(1)}, bf16[136,768]{1,0:T(8,128)(2,1)S(1)}, u32[]{:S(2)}, u32[]{:S(2)}) collective-permute-start(bf16[136,768]{1,0:T(8,128)(2,1)S(1)} %pad_maximum_fusion.1), channel_id=1, source_target_pairs={{0,2},{1,0},{3,1},{5,3},{7,5},{6,7},{4,6},{2,4},{8,10},{9,8},{11,9... | collective-permute-start | bytes 626696 | tf_op jit(solution)/shard_map/ppermute | solution.py:295
  37.0 10.5 %collective-permute-start.11 = (bf16[136,768]{1,0:T(8,128)(2,1)S(1)}, bf16[136,768]{1,0:T(8,128)(2,1)S(1)}, u32[]{:S(2)}, u32[]{:S(2)}) collective-permute-start(bf16[136,768]{1,0:T(8,128)(2,1)S(1)} %pad_maximum_fusion), channel_id=1, source_target_pairs={{0,1},{1,3},{3,5},{5,7},{7,6},{6,4},{4,2},{2,0},{8,9},{9,11},{11,1... | collective-permute-start | bytes 626696 | tf_op jit(solution)/shard_map/ppermute | solution.py:295
  37.6 7.3 %collective-permute-start.13 = (bf16[64,768]{1,0:T(8,128)(2,1)S(1)}, bf16[64,768]{1,0:T(8,128)(2,1)S(1)}, u32[]{:S(2)}, u32[]{:S(2)}) collective-permute-start(bf16[64,768]{1,0:T(8,128)(2,1)S(1)} %collective-permute-done.7.refs_6_), channel_id=1, source_target_pairs={{0,3},{1,5},{3,7},{5,6},{7,4},{6,2},{4,0},{2,1},{8,11},{9,13},{11,... | collective-permute-start | bytes 294920 | tf_op jit(solution)/shard_map/ppermute | solution.py:294
  40.2 6.6 %collective-permute-start.14 = (bf16[72,768]{1,0:T(8,128)(2,1)S(1)}, bf16[72,768]{1,0:T(8,128)(2,1)S(1)}, u32[]{:S(2)}, u32[]{:S(2)}) collective-permute-start(bf16[72,768]{1,0:T(8,128)(2,1)S(1)} %collective-permute-done.10.refs_9_), channel_id=1, source_target_pairs={{0,4},{1,2},{3,0},{5,1},{7,3},{6,5},{4,7},{2,6},{8,12},{9,10},{11,... | collective-permute-start | bytes 331784 | tf_op jit(solution)/shard_map/ppermute | solution.py:294

commit v17 on v14

--- a/solution.py
+++ b/solution.py
@@ -77,9 +77,8 @@
         for copy in copies(k):
             copy.wait()
         for row in range(0, tokens, 128):
-            for column in range(0, width, 512):
-                place = pl.ds(row, 128), pl.ds(column, min(512, width - column))
-                total[place] += jnp.dot(h_buf[k, place[0], :], held[span(k), place[1]], preferred_element_type=jnp.float32)
+            place = pl.ds(row, 128)
+            total[place, :] += jnp.dot(h_buf[k, place, :], held[span(k), :], preferred_element_type=jnp.float32)
         return _
 
     lax.fori_loop(0, parts, body, 0)

time: 43.4 us -> 43.4 us (level)
  no operation moved by 1% of the time
where the time goes in v17:
time: 43.4 us; the launch traced here: 43.3 us
  starting transfers between devices  19.9 us (46%)
  Pallas kernels  15.2 us (35%)
  waiting for transfers between devices  7.31 us (17%)
  between operations  0.75 us (2%)
    pallas_call x2, Pallas kernels, down(): pl.pallas_call(functools.partial(down_kernel, chips_y, tok, parts, own),...  10 us
    ppermute x6, starting transfers between devices, per_device(): lax.ppermute(up[i], 'col', shift(1))  8.82 us
    pallas_call x3, Pallas kernels, project(): pl.pallas_call(functools.partial(project_kernel, cycle, hops, [len(parts)...  5.14 us
    ppermute x6, starting transfers between devices, per_device(): lax.ppermute(back[i], 'col', shift(-1))  3.19 us
    ppermute x1, starting transfers between devices, per_device(): lax.ppermute(opposite[0], 'col', shift(2))  3.06 us
    ppermute x1, starting transfers between devices, per_device(): lax.ppermute(both[step - 1], 'row', move).astype(jnp.float32)  2.95 us
    ppermute x6, waiting for transfers between devices, per_device(): lax.ppermute(up[i], 'col', shift(1))  2.57 us
    ppermute x1, waiting for transfers between devices, per_device(): lax.ppermute(opposite[1], 'col', shift(-2))  1.79 us
  transfers between devices with their start and end apart: 17, of which 8 were waited for; matrix products, arithmetic and copies ran while one was open for 0% of the time, Pallas kernels for 18%

profile of v17, /device:TPU:0, one launch (start us, length us, event | category | flops | bytes accessed | tf_op | source)
XLA Modules:
  0.0 43.3 jit_solution(7977586205312375946)
XLA Ops:
  0.7 5.6 %down.2 = (bf16[1,128,768]{2,1,0:T(8,128)(2,1)S(1)}, bf16[1,128,768]{2,1,0:T(8,128)(2,1)S(1)}, bf16[6144,768]{1,0:T(8,128)(2,1)S(1)}) custom-call(bf16[512,6144]{1,0:T(8,128)(2,1)} %hidden.2, bf16[6144,768]{1,0:T(8,128)(2,1)} %weight.1), custom_call_target="tpu_custom_call" | custom-call | flops 2415919104 | bytes 12582912 | tf_op jit(solution)/shard_map/down/pallas_call | solution.py:99
  6.3 0.5 %collective-permute-start = (bf16[1,128,768]{2,1,0:T(8,128)(2,1)S(1)}, bf16[1,128,768]{2,1,0:T(8,128)(2,1)S(1)}, u32[]{:S(2)}, u32[]{:S(2)}) collective-permute-start(bf16[1,128,768]{2,1,0:T(8,128)(2,1)S(1)} %get-tuple-element.18), channel_id=1, source_target_pairs={{0,8},{8,0},{16,24},{24,16},{1,9},{9,1},{17,25},{25,17},{2,10},{10... | collective-permute-start | bytes 589832 | tf_op jit(solution)/shard_map/ppermute | solution.py:269
  6.8 1.1 %collective-permute-done = bf16[1,128,768]{2,1,0:T(8,128)(2,1)S(1)} collective-permute-done((bf16[1,128,768]{2,1,0:T(8,128)(2,1)S(1)}, bf16[1,128,768]{2,1,0:T(8,128)(2,1)S(1)}, u32[]{:S(2)}, u32[]{:S(2)}) %collective-permute-start) | collective-permute-done | bytes 196640 | tf_op jit(solution)/shard_map/ppermute | solution.py:269
  7.9 3.0 %collective-permute-start.1 = (bf16[128,768]{1,0:T(8,128)(2,1)S(1)}, bf16[128,768]{1,0:T(8,128)(2,1)S(1)}, u32[]{:S(2)}, u32[]{:S(2)}) collective-permute-start(bf16[128,768]{1,0:T(8,128)(2,1)S(1)} %bitcast.5), channel_id=1, source_target_pairs={{0,16},{8,24},{16,0},{24,8},{1,17},{9,25},{17,1},{25,9},{2,18},{10... | collective-permute-start | bytes 589832 | tf_op jit(solution)/shard_map/ppermute | solution.py:275
  10.9 4.4 %down.3 = (bf16[1,128,768]{2,1,0:T(8,128)(2,1)S(1)}, bf16[1,128,768]{2,1,0:T(8,128)(2,1)S(1)}) custom-call(bf16[512,6144]{1,0:T(8,128)(2,1)} %hidden.2, bf16[6144,768]{1,0:T(8,128)(2,1)S(1)} %get-tuple-element.21.weight), custom_call_target="tpu_custom_call" | custom-call | flops 2415919104 | bytes 3145728 | tf_op jit(solution)/shard_map/down/pallas_call | solution.py:99
  15.4 0.7 %collective-permute-done.1 = bf16[128,768]{1,0:T(8,128)(2,1)S(1)} collective-permute-done((bf16[128,768]{1,0:T(8,128)(2,1)S(1)}, bf16[128,768]{1,0:T(8,128)(2,1)S(1)}, u32[]{:S(2)}, u32[]{:S(2)}) %collective-permute-start.1) | collective-permute-done | bytes 196640 | tf_op jit(solution)/shard_map/ppermute | solution.py:275
  16.1 0.7 %collective-permute-done.2.got = bf16[128,768]{1,0:T(8,128)(2,1)S(1)} collective-permute-done((bf16[128,768]{1,0:T(8,128)(2,1)S(1)}, bf16[128,768]{1,0:T(8,128)(2,1)S(1)}, u32[]{:S(2)}, u32[]{:S(2)}) %collective-permute-start.2) | collective-permute-done | bytes 196640 | tf_op jit(solution)/shard_map/ppermute | solution.py:277
  16.9 1.9 %collective-permute-start.3 = (bf16[64,768]{1,0:T(8,128)(2,1)S(1)}, bf16[64,768]{1,0:T(8,128)(2,1)S(1)}, u32[]{:S(2)}, u32[]{:S(2)}) collective-permute-start(bf16[64,768]{1,0:T(8,128)(2,1)S(1)} %get-tuple-element.24.refs_0_), channel_id=1, source_target_pairs={{0,1},{1,3},{3,5},{5,7},{7,6},{6,4},{4,2},{2,0},{8,9},{9,11},{11,1... | collective-permute-start | bytes 294920 | tf_op jit(solution)/shard_map/ppermute | solution.py:286
  19.0 1.8 %collective-permute-start.4 = (bf16[72,768]{1,0:T(8,128)(2,1)S(1)}, bf16[72,768]{1,0:T(8,128)(2,1)S(1)}, u32[]{:S(2)}, u32[]{:S(2)}) collective-permute-start(bf16[72,768]{1,0:T(8,128)(2,1)S(1)} %get-tuple-element.25.refs_1_), channel_id=1, source_target_pairs={{0,1},{1,3},{3,5},{5,7},{7,6},{6,4},{4,2},{2,0},{8,9},{9,11},{11,1... | collective-permute-start | bytes 331784 | tf_op jit(solution)/shard_map/ppermute | solution.py:286
  21.0 1.6 %collective-permute-done.3.refs_2_ = bf16[64,768]{1,0:T(8,128)(2,1)S(1)} collective-permute-done((bf16[64,768]{1,0:T(8,128)(2,1)S(1)}, bf16[64,768]{1,0:T(8,128)(2,1)S(1)}, u32[]{:S(2)}, u32[]{:S(2)}) %collective-permute-start.3) | collective-permute-done | bytes 98336 | tf_op jit(solution)/shard_map/ppermute | solution.py:286
  22.5 1.8 %collective-permute-start.7 = (bf16[64,768]{1,0:T(8,128)(2,1)S(1)}, bf16[64,768]{1,0:T(8,128)(2,1)S(1)}, u32[]{:S(2)}, u32[]{:S(2)}) collective-permute-start(bf16[64,768]{1,0:T(8,128)(2,1)S(1)} %collective-permute-done.3.refs_2_), channel_id=1, source_target_pairs={{0,1},{1,3},{3,5},{5,7},{7,6},{6,4},{4,2},{2,0},{8,9},{9,11},{11,1... | collective-permute-start | bytes 294920 | tf_op jit(solution)/shard_map/ppermute | solution.py:286
  24.5 0.4 collective-permute-start.10
  24.9 1.6 %collective-permute-start.8 = (bf16[72,768]{1,0:T(8,128)(2,1)S(1)}, bf16[72,768]{1,0:T(8,128)(2,1)S(1)}, u32[]{:S(2)}, u32[]{:S(2)}) collective-permute-start(bf16[72,768]{1,0:T(8,128)(2,1)S(1)} %collective-permute-done.4.refs_3_), channel_id=1, source_target_pairs={{0,1},{1,3},{3,5},{5,7},{7,6},{6,4},{4,2},{2,0},{8,9},{9,11},{11,1... | collective-permute-start | bytes 331784 | tf_op jit(solution)/shard_map/ppermute | solution.py:286
  26.5 0.4 collective-permute-start.9
  26.9 1.0 %collective-permute-done.7.refs_6_ = bf16[64,768]{1,0:T(8,128)(2,1)S(1)} collective-permute-done((bf16[64,768]{1,0:T(8,128)(2,1)S(1)}, bf16[64,768]{1,0:T(8,128)(2,1)S(1)}, u32[]{:S(2)}, u32[]{:S(2)}) %collective-permute-start.7) | collective-permute-done | bytes 98336 | tf_op jit(solution)/shard_map/ppermute | solution.py:286
  27.9 3.1 %collective-permute-start.15 = (bf16[64,768]{1,0:T(8,128)(2,1)S(1)}, bf16[64,768]{1,0:T(8,128)(2,1)S(1)}, u32[]{:S(2)}, u32[]{:S(2)}) collective-permute-start(bf16[64,768]{1,0:T(8,128)(2,1)S(1)} %collective-permute-done.7.refs_6_), channel_id=1, source_target_pairs={{0,3},{1,5},{3,7},{5,6},{7,4},{6,2},{4,0},{2,1},{8,11},{9,13},{11,... | collective-permute-start | bytes 294920 | tf_op jit(solution)/shard_map/ppermute | solution.py:288
  31.0 1.6 %collective-permute-start.11 = (bf16[64,768]{1,0:T(8,128)(2,1)S(1)}, bf16[64,768]{1,0:T(8,128)(2,1)S(1)}, u32[]{:S(2)}, u32[]{:S(2)}) collective-permute-start(bf16[64,768]{1,0:T(8,128)(2,1)S(1)} %collective-permute-done.7.refs_6_), channel_id=1, source_target_pairs={{0,1},{1,3},{3,5},{5,7},{7,6},{6,4},{4,2},{2,0},{8,9},{9,11},{11,1... | collective-permute-start | bytes 294920 | tf_op jit(solution)/shard_map/ppermute | solution.py:286
  32.5 0.4 %collective-permute-start.13 = (bf16[64,768]{1,0:T(8,128)(2,1)S(1)}, bf16[64,768]{1,0:T(8,128)(2,1)S(1)}, u32[]{:S(2)}, u32[]{:S(2)}) collective-permute-start(bf16[64,768]{1,0:T(8,128)(2,1)S(1)} %collective-permute-done.9.refs_8_), channel_id=1, source_target_pairs={{0,2},{1,0},{3,1},{5,3},{7,5},{6,7},{4,6},{2,4},{8,10},{9,8},{11,9... | collective-permute-start | bytes 294920 | tf_op jit(solution)/shard_map/ppermute | solution.py:286
  33.0 1.3 %collective-permute-start.16 = (bf16[72,768]{1,0:T(8,128)(2,1)S(1)}, bf16[72,768]{1,0:T(8,128)(2,1)S(1)}, u32[]{:S(2)}, u32[]{:S(2)}) collective-permute-start(bf16[72,768]{1,0:T(8,128)(2,1)S(1)} %collective-permute-done.10.refs_9_), channel_id=1, source_target_pairs={{0,4},{1,2},{3,0},{5,1},{7,3},{6,5},{4,7},{2,6},{8,12},{9,10},{11,... | collective-permute-start | bytes 331784 | tf_op jit(solution)/shard_map/ppermute | solution.py:288
  34.3 1.6 %collective-permute-start.14 = (bf16[72,768]{1,0:T(8,128)(2,1)S(1)}, bf16[72,768]{1,0:T(8,128)(2,1)S(1)}, u32[]{:S(2)}, u32[]{:S(2)}) collective-permute-start(bf16[72,768]{1,0:T(8,128)(2,1)S(1)} %collective-permute-done.10.refs_9_), channel_id=1, source_target_pairs={{0,2},{1,0},{3,1},{5,3},{7,5},{6,7},{4,6},{2,4},{8,10},{9,8},{11,9... | collective-permute-start | bytes 331784 | tf_op jit(solution)/shard_map/ppermute | solution.py:286
  36.3 2.7 %project.3 = (bf16[128,768]{1,0:T(8,128)(2,1)}, f32[128,1]{1,0:T(8,128)S(1)}, f32[2,128,1]{2,1,0:T(8,128)S(1)}, f32[144,1536]{1,0:T(8,128)S(1)}) custom-call(bf16[64,768]{1,0:T(8,128)(2,1)S(1)} %get-tuple-element.24.refs_0_, bf16[72,768]{1,0:T(8,128)(2,1)S(1)} %get-tuple-element.25.refs_1_, bf16[64,768]{1,0:T(8,128)(2,1)S(1)} %collective-permute-done.3.refs_2_, ...), custom_call_target="tpu_custom_call" | custom-call | flops 1698693120 | tf_op jit(solution)/shard_map/project/pallas_call | solution.py:234
  39.0 1.8 %collective-permute-done.16.refs_1_ = bf16[72,768]{1,0:T(8,128)(2,1)S(1)} collective-permute-done((bf16[72,768]{1,0:T(8,128)(2,1)S(1)}, bf16[72,768]{1,0:T(8,128)(2,1)S(1)}, u32[]{:S(2)}, u32[]{:S(2)}) %collective-permute-start.16) | collective-permute-done | bytes 110624 | tf_op jit(solution)/shard_map/ppermute | solution.py:288
  40.8 0.7 %project.4 = (f32[2,128,1]{2,1,0:T(8,128)S(1)}, f32[144,1536]{1,0:T(8,128)S(1)}) custom-call(bf16[64,768]{1,0:T(8,128)(2,1)S(1)} %collective-permute-done.15.refs_0_, bf16[72,768]{1,0:T(8,128)(2,1)S(1)} %collective-permute-done.16.refs_1_, bf16[6144,1536]{1,0:T(8,128)(2,1)S(1)} %copy-done, ...), custom_call_target="tpu_custom_call", output_to_operand_aliasing={{0}: (4, {}), {1}: (5, {})} | custom-call | flops 339738624 | tf_op jit(solution)/shard_map/project/pallas_call | solution.py:234
  41.5 1.8 %project.5 = bf16[128,1536]{1,0:T(8,128)(2,1)} custom-call(bf16[64,768]{1,0:T(8,128)(2,1)S(1)} %collective-permute-done.11.refs_0_, bf16[72,768]{1,0:T(8,128)(2,1)S(1)} %collective-permute-done.12.refs_1_, bf16[64,768]{1,0:T(8,128)(2,1)S(1)} %collective-permute-done.13.refs_2_, bf16[72,768]{1,0:T(8,128)(2,1)S(1)} %collective-permute-done.14.refs_3_, ...), custom_call_target="tpu_custom_call" | custom-call | flops 679477248 | tf_op jit(solution)/shard_map/project/pallas_call | solution.py:234
  (25 shorter events, 1.3 us)
Async XLA Ops:
  0.6 6.2 %copy-start.2 = (bf16[768]{0:T(1024)(128)(2,1)S(1)}, bf16[768]{0:T(1024)(128)(2,1)}, u32[]{:S(2)}) copy-start(bf16[768]{0:T(1024)(128)(2,1)} %param.8) | copy-start | bytes 4612
  0.6 35.7 %copy-start = (bf16[6144,1536]{1,0:T(8,128)(2,1)S(1)}, bf16[6144,1536]{1,0:T(8,128)(2,1)}, u32[]{:S(2)}) copy-start(bf16[6144,1536]{1,0:T(8,128)(2,1)} %refs_4_.1) | copy-start | bytes 56623108
  6.3 9.8 %copy-start.1 = (bf16[128,768]{1,0:T(8,128)(2,1)S(1)}, bf16[128,768]{1,0:T(8,128)(2,1)}, u32[]{:S(2)}) copy-start(bf16[128,768]{1,0:T(8,128)(2,1)} %param.7) | copy-start | bytes 589828
  6.3 1.6 %collective-permute-start = (bf16[1,128,768]{2,1,0:T(8,128)(2,1)S(1)}, bf16[1,128,768]{2,1,0:T(8,128)(2,1)S(1)}, u32[]{:S(2)}, u32[]{:S(2)}) collective-permute-start(bf16[1,128,768]{2,1,0:T(8,128)(2,1)S(1)} %get-tuple-element.18), channel_id=1, source_target_pairs={{0,8},{8,0},{16,24},{24,16},{1,9},{9,1},{17,25},{25,17},{2,10},{10... | collective-permute-start | bytes 589832 | tf_op jit(solution)/shard_map/ppermute | solution.py:269
  7.9 8.2 %collective-permute-start.1 = (bf16[128,768]{1,0:T(8,128)(2,1)S(1)}, bf16[128,768]{1,0:T(8,128)(2,1)S(1)}, u32[]{:S(2)}, u32[]{:S(2)}) collective-permute-start(bf16[128,768]{1,0:T(8,128)(2,1)S(1)} %bitcast.5), channel_id=1, source_target_pairs={{0,16},{8,24},{16,0},{24,8},{1,17},{9,25},{17,1},{25,9},{2,18},{10... | collective-permute-start | bytes 589832 | tf_op jit(solution)/shard_map/ppermute | solution.py:275
  15.3 1.5 %collective-permute-start.2 = (bf16[128,768]{1,0:T(8,128)(2,1)S(1)}, bf16[128,768]{1,0:T(8,128)(2,1)S(1)}, u32[]{:S(2)}, u32[]{:S(2)}) collective-permute-start(bf16[128,768]{1,0:T(8,128)(2,1)S(1)} %bitcast.4), channel_id=1, source_target_pairs={{0,8},{8,0},{16,24},{24,16},{1,9},{9,1},{17,25},{25,17},{2,10},{10... | collective-permute-start | bytes 589832 | tf_op jit(solution)/shard_map/ppermute | solution.py:277
  16.9 5.7 %collective-permute-start.3 = (bf16[64,768]{1,0:T(8,128)(2,1)S(1)}, bf16[64,768]{1,0:T(8,128)(2,1)S(1)}, u32[]{:S(2)}, u32[]{:S(2)}) collective-permute-start(bf16[64,768]{1,0:T(8,128)(2,1)S(1)} %get-tuple-element.24.refs_0_), channel_id=1, source_target_pairs={{0,1},{1,3},{3,5},{5,7},{7,6},{6,4},{4,2},{2,0},{8,9},{9,11},{11,1... | collective-permute-start | bytes 294920 | tf_op jit(solution)/shard_map/ppermute | solution.py:286
  18.8 5.7 %collective-permute-start.6 = (bf16[72,768]{1,0:T(8,128)(2,1)S(1)}, bf16[72,768]{1,0:T(8,128)(2,1)S(1)}, u32[]{:S(2)}, u32[]{:S(2)}) collective-permute-start(bf16[72,768]{1,0:T(8,128)(2,1)S(1)} %get-tuple-element.25.refs_1_), channel_id=1, source_target_pairs={{0,2},{1,0},{3,1},{5,3},{7,5},{6,7},{4,6},{2,4},{8,10},{9,8},{11,9... | collective-permute-start | bytes 331784 | tf_op jit(solution)/shard_map/ppermute | solution.py:286
  19.0 5.9 %collective-permute-start.4 = (bf16[72,768]{1,0:T(8,128)(2,1)S(1)}, bf16[72,768]{1,0:T(8,128)(2,1)S(1)}, u32[]{:S(2)}, u32[]{:S(2)}) collective-permute-start(bf16[72,768]{1,0:T(8,128)(2,1)S(1)} %get-tuple-element.25.refs_1_), channel_id=1, source_target_pairs={{0,1},{1,3},{3,5},{5,7},{7,6},{6,4},{4,2},{2,0},{8,9},{9,11},{11,1... | collective-permute-start | bytes 331784 | tf_op jit(solution)/shard_map/ppermute | solution.py:286
  20.8 5.7 %collective-permute-start.5 = (bf16[64,768]{1,0:T(8,128)(2,1)S(1)}, bf16[64,768]{1,0:T(8,128)(2,1)S(1)}, u32[]{:S(2)}, u32[]{:S(2)}) collective-permute-start(bf16[64,768]{1,0:T(8,128)(2,1)S(1)} %get-tuple-element.24.refs_0_), channel_id=1, source_target_pairs={{0,2},{1,0},{3,1},{5,3},{7,5},{6,7},{4,6},{2,4},{8,10},{9,8},{11,9... | collective-permute-start | bytes 294920 | tf_op jit(solution)/shard_map/ppermute | solution.py:286
  22.5 5.4 %collective-permute-start.7 = (bf16[64,768]{1,0:T(8,128)(2,1)S(1)}, bf16[64,768]{1,0:T(8,128)(2,1)S(1)}, u32[]{:S(2)}, u32[]{:S(2)}) collective-permute-start(bf16[64,768]{1,0:T(8,128)(2,1)S(1)} %collective-permute-done.3.refs_2_), channel_id=1, source_target_pairs={{0,1},{1,3},{3,5},{5,7},{7,6},{6,4},{4,2},{2,0},{8,9},{9,11},{11,1... | collective-permute-start | bytes 294920 | tf_op jit(solution)/shard_map/ppermute | solution.py:286
  24.5 8.5 %collective-permute-start.10 = (bf16[72,768]{1,0:T(8,128)(2,1)S(1)}, bf16[72,768]{1,0:T(8,128)(2,1)S(1)}, u32[]{:S(2)}, u32[]{:S(2)}) collective-permute-start(bf16[72,768]{1,0:T(8,128)(2,1)S(1)} %collective-permute-done.6.refs_5_), channel_id=1, source_target_pairs={{0,2},{1,0},{3,1},{5,3},{7,5},{6,7},{4,6},{2,4},{8,10},{9,8},{11,9... | collective-permute-start | bytes 331784 | tf_op jit(solution)/shard_map/ppermute | solution.py:286
  24.9 9.4 %collective-permute-start.8 = (bf16[72,768]{1,0:T(8,128)(2,1)S(1)}, bf16[72,768]{1,0:T(8,128)(2,1)S(1)}, u32[]{:S(2)}, u32[]{:S(2)}) collective-permute-start(bf16[72,768]{1,0:T(8,128)(2,1)S(1)} %collective-permute-done.4.refs_3_), channel_id=1, source_target_pairs={{0,1},{1,3},{3,5},{5,7},{7,6},{6,4},{4,2},{2,0},{8,9},{9,11},{11,1... | collective-permute-start | bytes 331784 | tf_op jit(solution)/shard_map/ppermute | solution.py:286
  26.5 6.0 %collective-permute-start.9 = (bf16[64,768]{1,0:T(8,128)(2,1)S(1)}, bf16[64,768]{1,0:T(8,128)(2,1)S(1)}, u32[]{:S(2)}, u32[]{:S(2)}) collective-permute-start(bf16[64,768]{1,0:T(8,128)(2,1)S(1)} %collective-permute-done.5.refs_4_), channel_id=1, source_target_pairs={{0,2},{1,0},{3,1},{5,3},{7,5},{6,7},{4,6},{2,4},{8,10},{9,8},{11,9... | collective-permute-start | bytes 294920 | tf_op jit(solution)/shard_map/ppermute | solution.py:286
  27.9 8.3 %collective-permute-start.15 = (bf16[64,768]{1,0:T(8,128)(2,1)S(1)}, bf16[64,768]{1,0:T(8,128)(2,1)S(1)}, u32[]{:S(2)}, u32[]{:S(2)}) collective-permute-start(bf16[64,768]{1,0:T(8,128)(2,1)S(1)} %collective-permute-done.7.refs_6_), channel_id=1, source_target_pairs={{0,3},{1,5},{3,7},{5,6},{7,4},{6,2},{4,0},{2,1},{8,11},{9,13},{11,... | collective-permute-start | bytes 294920 | tf_op jit(solution)/shard_map/ppermute | solution.py:288
  31.0 10.5 %collective-permute-start.11 = (bf16[64,768]{1,0:T(8,128)(2,1)S(1)}, bf16[64,768]{1,0:T(8,128)(2,1)S(1)}, u32[]{:S(2)}, u32[]{:S(2)}) collective-permute-start(bf16[64,768]{1,0:T(8,128)(2,1)S(1)} %collective-permute-done.7.refs_6_), channel_id=1, source_target_pairs={{0,1},{1,3},{3,5},{5,7},{7,6},{6,4},{4,2},{2,0},{8,9},{9,11},{11,1... | collective-permute-start | bytes 294920 | tf_op jit(solution)/shard_map/ppermute | solution.py:286
  32.5 9.0 %collective-permute-start.13 = (bf16[64,768]{1,0:T(8,128)(2,1)S(1)}, bf16[64,768]{1,0:T(8,128)(2,1)S(1)}, u32[]{:S(2)}, u32[]{:S(2)}) collective-permute-start(bf16[64,768]{1,0:T(8,128)(2,1)S(1)} %collective-permute-done.9.refs_8_), channel_id=1, source_target_pairs={{0,2},{1,0},{3,1},{5,3},{7,5},{6,7},{4,6},{2,4},{8,10},{9,8},{11,9... | collective-permute-start | bytes 294920 | tf_op jit(solution)/shard_map/ppermute | solution.py:286
  33.0 7.8 %collective-permute-start.16 = (bf16[72,768]{1,0:T(8,128)(2,1)S(1)}, bf16[72,768]{1,0:T(8,128)(2,1)S(1)}, u32[]{:S(2)}, u32[]{:S(2)}) collective-permute-start(bf16[72,768]{1,0:T(8,128)(2,1)S(1)} %collective-permute-done.10.refs_9_), channel_id=1, source_target_pairs={{0,4},{1,2},{3,0},{5,1},{7,3},{6,5},{4,7},{2,6},{8,12},{9,10},{11,... | collective-permute-start | bytes 331784 | tf_op jit(solution)/shard_map/ppermute | solution.py:288
  34.3 7.2 %collective-permute-start.14 = (bf16[72,768]{1,0:T(8,128)(2,1)S(1)}, bf16[72,768]{1,0:T(8,128)(2,1)S(1)}, u32[]{:S(2)}, u32[]{:S(2)}) collective-permute-start(bf16[72,768]{1,0:T(8,128)(2,1)S(1)} %collective-permute-done.10.refs_9_), channel_id=1, source_target_pairs={{0,2},{1,0},{3,1},{5,3},{7,5},{6,7},{4,6},{2,4},{8,10},{9,8},{11,9... | collective-permute-start | bytes 331784 | tf_op jit(solution)/shard_map/ppermute | solution.py:286
  36.2 5.4 %collective-permute-start.12 = (bf16[72,768]{1,0:T(8,128)(2,1)S(1)}, bf16[72,768]{1,0:T(8,128)(2,1)S(1)}, u32[]{:S(2)}, u32[]{:S(2)}) collective-permute-start(bf16[72,768]{1,0:T(8,128)(2,1)S(1)} %collective-permute-done.8.refs_7_), channel_id=1, source_target_pairs={{0,1},{1,3},{3,5},{5,7},{7,6},{6,4},{4,2},{2,0},{8,9},{9,11},{11,1... | collective-permute-start | bytes 331784 | tf_op jit(solution)/shard_map/ppermute | solution.py:286

commit v18 on v17

--- a/solution.py
+++ b/solution.py
@@ -289,8 +289,7 @@
             pieces += [list(up), list(back)]
             hops += [-step, step]
         stream, state = project(pieces[:-2], hops[:-2], qk_weight, None, cycle, False)
-        state = project([opposite], [half], qk_weight, state, cycle, False)
-        return stream, project(pieces[-2:], hops[-2:], qk_weight, state, cycle, True)
+        return stream, project([opposite, *pieces[-2:]], [half, *hops[-2:]], qk_weight, state, cycle, True)
 
     placed = (P(None, "row"), P("row", "col"), P("row", "col"), P("col"), P(None, "col"))
     return jax.shard_map(

time: 43.4 us -> 43.3 us (level)
    pallas_call x3 -> x2, Pallas kernels: 5.14 us -> 4.94 us  [project(): pl.pallas_call(functools.partial(project_kernel, cycle, hops, [len(parts)...]
  transfers between devices with their start and end apart: 17 -> 17, of which waited for: 8 -> 9; matrix products, arithmetic and copies ran while one was open for 0% -> 0% of each run, Pallas kernels for 18% -> 17%
where the time goes in v18:
time: 43.3 us; the launch traced here: 43.1 us
  starting transfers between devices  19.9 us (46%)
  Pallas kernels  15 us (35%)
  waiting for transfers between devices  7.38 us (17%)
  between operations  0.71 us (2%)
    pallas_call x2, Pallas kernels, down(): pl.pallas_call(functools.partial(down_kernel, chips_y, tok, parts, own),...  10 us
    ppermute x6, starting transfers between devices, per_device(): lax.ppermute(up[i], 'col', shift(1))  8.79 us
    pallas_call x2, Pallas kernels, project(): pl.pallas_call(functools.partial(project_kernel, cycle, hops, [len(parts)...  4.94 us
    ppermute x6, starting transfers between devices, per_device(): lax.ppermute(back[i], 'col', shift(-1))  3.23 us
    ppermute x1, starting transfers between devices, per_device(): lax.ppermute(opposite[0], 'col', shift(2))  3.06 us
    ppermute x1, starting transfers between devices, per_device(): lax.ppermute(both[step - 1], 'row', move).astype(jnp.float32)  2.95 us
    ppermute x6, waiting for transfers between devices, per_device(): lax.ppermute(up[i], 'col', shift(1))  2.65 us
    ppermute x1, waiting for transfers between devices, per_device(): lax.ppermute(opposite[1], 'col', shift(-2))  1.78 us
  transfers between devices with their start and end apart: 17, of which 9 were waited for; matrix products, arithmetic and copies ran while one was open for 0% of the time, Pallas kernels for 17%

profile of v18, /device:TPU:0, one launch (start us, length us, event | category | flops | bytes accessed | tf_op | source)
XLA Modules:
  0.0 43.1 jit_solution(3751764055952508938)
XLA Ops:
  0.7 5.6 %down.2 = (bf16[1,128,768]{2,1,0:T(8,128)(2,1)S(1)}, bf16[1,128,768]{2,1,0:T(8,128)(2,1)S(1)}, bf16[6144,768]{1,0:T(8,128)(2,1)S(1)}) custom-call(bf16[512,6144]{1,0:T(8,128)(2,1)} %hidden.2, bf16[6144,768]{1,0:T(8,128)(2,1)} %weight.1), custom_call_target="tpu_custom_call" | custom-call | flops 2415919104 | bytes 12582912 | tf_op jit(solution)/shard_map/down/pallas_call | solution.py:99
  6.3 0.5 %collective-permute-start = (bf16[1,128,768]{2,1,0:T(8,128)(2,1)S(1)}, bf16[1,128,768]{2,1,0:T(8,128)(2,1)S(1)}, u32[]{:S(2)}, u32[]{:S(2)}) collective-permute-start(bf16[1,128,768]{2,1,0:T(8,128)(2,1)S(1)} %get-tuple-element.16), channel_id=1, source_target_pairs={{0,8},{8,0},{16,24},{24,16},{1,9},{9,1},{17,25},{25,17},{2,10},{10... | collective-permute-start | bytes 589832 | tf_op jit(solution)/shard_map/ppermute | solution.py:269
  6.8 1.1 %collective-permute-done = bf16[1,128,768]{2,1,0:T(8,128)(2,1)S(1)} collective-permute-done((bf16[1,128,768]{2,1,0:T(8,128)(2,1)S(1)}, bf16[1,128,768]{2,1,0:T(8,128)(2,1)S(1)}, u32[]{:S(2)}, u32[]{:S(2)}) %collective-permute-start) | collective-permute-done | bytes 196640 | tf_op jit(solution)/shard_map/ppermute | solution.py:269
  7.9 3.0 %collective-permute-start.1 = (bf16[128,768]{1,0:T(8,128)(2,1)S(1)}, bf16[128,768]{1,0:T(8,128)(2,1)S(1)}, u32[]{:S(2)}, u32[]{:S(2)}) collective-permute-start(bf16[128,768]{1,0:T(8,128)(2,1)S(1)} %bitcast.5), channel_id=1, source_target_pairs={{0,16},{8,24},{16,0},{24,8},{1,17},{9,25},{17,1},{25,9},{2,18},{10... | collective-permute-start | bytes 589832 | tf_op jit(solution)/shard_map/ppermute | solution.py:275
  10.9 4.4 %down.3 = (bf16[1,128,768]{2,1,0:T(8,128)(2,1)S(1)}, bf16[1,128,768]{2,1,0:T(8,128)(2,1)S(1)}) custom-call(bf16[512,6144]{1,0:T(8,128)(2,1)} %hidden.2, bf16[6144,768]{1,0:T(8,128)(2,1)S(1)} %get-tuple-element.19.weight), custom_call_target="tpu_custom_call" | custom-call | flops 2415919104 | bytes 3145728 | tf_op jit(solution)/shard_map/down/pallas_call | solution.py:99
  15.4 0.7 %collective-permute-done.1 = bf16[128,768]{1,0:T(8,128)(2,1)S(1)} collective-permute-done((bf16[128,768]{1,0:T(8,128)(2,1)S(1)}, bf16[128,768]{1,0:T(8,128)(2,1)S(1)}, u32[]{:S(2)}, u32[]{:S(2)}) %collective-permute-start.1) | collective-permute-done | bytes 196640 | tf_op jit(solution)/shard_map/ppermute | solution.py:275
  16.1 0.7 %collective-permute-done.2.got = bf16[128,768]{1,0:T(8,128)(2,1)S(1)} collective-permute-done((bf16[128,768]{1,0:T(8,128)(2,1)S(1)}, bf16[128,768]{1,0:T(8,128)(2,1)S(1)}, u32[]{:S(2)}, u32[]{:S(2)}) %collective-permute-start.2) | collective-permute-done | bytes 196640 | tf_op jit(solution)/shard_map/ppermute | solution.py:277
  16.9 1.9 %collective-permute-start.3 = (bf16[64,768]{1,0:T(8,128)(2,1)S(1)}, bf16[64,768]{1,0:T(8,128)(2,1)S(1)}, u32[]{:S(2)}, u32[]{:S(2)}) collective-permute-start(bf16[64,768]{1,0:T(8,128)(2,1)S(1)} %get-tuple-element.22.refs_0_), channel_id=1, source_target_pairs={{0,1},{1,3},{3,5},{5,7},{7,6},{6,4},{4,2},{2,0},{8,9},{9,11},{11,1... | collective-permute-start | bytes 294920 | tf_op jit(solution)/shard_map/ppermute | solution.py:286
  19.0 1.8 %collective-permute-start.4 = (bf16[72,768]{1,0:T(8,128)(2,1)S(1)}, bf16[72,768]{1,0:T(8,128)(2,1)S(1)}, u32[]{:S(2)}, u32[]{:S(2)}) collective-permute-start(bf16[72,768]{1,0:T(8,128)(2,1)S(1)} %get-tuple-element.23.refs_1_), channel_id=1, source_target_pairs={{0,1},{1,3},{3,5},{5,7},{7,6},{6,4},{4,2},{2,0},{8,9},{9,11},{11,1... | collective-permute-start | bytes 331784 | tf_op jit(solution)/shard_map/ppermute | solution.py:286
  21.0 1.6 %collective-permute-done.3.refs_2_ = bf16[64,768]{1,0:T(8,128)(2,1)S(1)} collective-permute-done((bf16[64,768]{1,0:T(8,128)(2,1)S(1)}, bf16[64,768]{1,0:T(8,128)(2,1)S(1)}, u32[]{:S(2)}, u32[]{:S(2)}) %collective-permute-start.3) | collective-permute-done | bytes 98336 | tf_op jit(solution)/shard_map/ppermute | solution.py:286
  22.5 1.8 %collective-permute-start.7 = (bf16[64,768]{1,0:T(8,128)(2,1)S(1)}, bf16[64,768]{1,0:T(8,128)(2,1)S(1)}, u32[]{:S(2)}, u32[]{:S(2)}) collective-permute-start(bf16[64,768]{1,0:T(8,128)(2,1)S(1)} %collective-permute-done.3.refs_2_), channel_id=1, source_target_pairs={{0,1},{1,3},{3,5},{5,7},{7,6},{6,4},{4,2},{2,0},{8,9},{9,11},{11,1... | collective-permute-start | bytes 294920 | tf_op jit(solution)/shard_map/ppermute | solution.py:286
  24.5 0.4 collective-permute-start.10
  24.9 1.6 %collective-permute-start.8 = (bf16[72,768]{1,0:T(8,128)(2,1)S(1)}, bf16[72,768]{1,0:T(8,128)(2,1)S(1)}, u32[]{:S(2)}, u32[]{:S(2)}) collective-permute-start(bf16[72,768]{1,0:T(8,128)(2,1)S(1)} %collective-permute-done.4.refs_3_), channel_id=1, source_target_pairs={{0,1},{1,3},{3,5},{5,7},{7,6},{6,4},{4,2},{2,0},{8,9},{9,11},{11,1... | collective-permute-start | bytes 331784 | tf_op jit(solution)/shard_map/ppermute | solution.py:286
  26.5 0.4 collective-permute-start.9
  26.9 1.0 %collective-permute-done.7.refs_6_ = bf16[64,768]{1,0:T(8,128)(2,1)S(1)} collective-permute-done((bf16[64,768]{1,0:T(8,128)(2,1)S(1)}, bf16[64,768]{1,0:T(8,128)(2,1)S(1)}, u32[]{:S(2)}, u32[]{:S(2)}) %collective-permute-start.7) | collective-permute-done | bytes 98336 | tf_op jit(solution)/shard_map/ppermute | solution.py:286
  27.9 3.1 %collective-permute-start.11 = (bf16[64,768]{1,0:T(8,128)(2,1)S(1)}, bf16[64,768]{1,0:T(8,128)(2,1)S(1)}, u32[]{:S(2)}, u32[]{:S(2)}) collective-permute-start(bf16[64,768]{1,0:T(8,128)(2,1)S(1)} %collective-permute-done.7.refs_6_), channel_id=1, source_target_pairs={{0,3},{1,5},{3,7},{5,6},{7,4},{6,2},{4,0},{2,1},{8,11},{9,13},{11,... | collective-permute-start | bytes 294920 | tf_op jit(solution)/shard_map/ppermute | solution.py:288
  31.0 1.6 %collective-permute-start.13 = (bf16[64,768]{1,0:T(8,128)(2,1)S(1)}, bf16[64,768]{1,0:T(8,128)(2,1)S(1)}, u32[]{:S(2)}, u32[]{:S(2)}) collective-permute-start(bf16[64,768]{1,0:T(8,128)(2,1)S(1)} %collective-permute-done.7.refs_6_), channel_id=1, source_target_pairs={{0,1},{1,3},{3,5},{5,7},{7,6},{6,4},{4,2},{2,0},{8,9},{9,11},{11,1... | collective-permute-start | bytes 294920 | tf_op jit(solution)/shard_map/ppermute | solution.py:286
  32.5 0.4 %collective-permute-start.15 = (bf16[64,768]{1,0:T(8,128)(2,1)S(1)}, bf16[64,768]{1,0:T(8,128)(2,1)S(1)}, u32[]{:S(2)}, u32[]{:S(2)}) collective-permute-start(bf16[64,768]{1,0:T(8,128)(2,1)S(1)} %collective-permute-done.9.refs_8_), channel_id=1, source_target_pairs={{0,2},{1,0},{3,1},{5,3},{7,5},{6,7},{4,6},{2,4},{8,10},{9,8},{11,9... | collective-permute-start | bytes 294920 | tf_op jit(solution)/shard_map/ppermute | solution.py:286
  33.0 1.3 %collective-permute-start.12 = (bf16[72,768]{1,0:T(8,128)(2,1)S(1)}, bf16[72,768]{1,0:T(8,128)(2,1)S(1)}, u32[]{:S(2)}, u32[]{:S(2)}) collective-permute-start(bf16[72,768]{1,0:T(8,128)(2,1)S(1)} %collective-permute-done.10.refs_9_), channel_id=1, source_target_pairs={{0,4},{1,2},{3,0},{5,1},{7,3},{6,5},{4,7},{2,6},{8,12},{9,10},{11,... | collective-permute-start | bytes 331784 | tf_op jit(solution)/shard_map/ppermute | solution.py:288
  34.3 1.6 %collective-permute-start.16 = (bf16[72,768]{1,0:T(8,128)(2,1)S(1)}, bf16[72,768]{1,0:T(8,128)(2,1)S(1)}, u32[]{:S(2)}, u32[]{:S(2)}) collective-permute-start(bf16[72,768]{1,0:T(8,128)(2,1)S(1)} %collective-permute-done.10.refs_9_), channel_id=1, source_target_pairs={{0,2},{1,0},{3,1},{5,3},{7,5},{6,7},{4,6},{2,4},{8,10},{9,8},{11,9... | collective-permute-start | bytes 331784 | tf_op jit(solution)/shard_map/ppermute | solution.py:286
  35.9 0.3 collective-permute-done.11.refs_0_
  36.3 2.7 %project.2 = (bf16[128,768]{1,0:T(8,128)(2,1)}, f32[128,1]{1,0:T(8,128)S(1)}, f32[2,128,1]{2,1,0:T(8,128)S(1)}, f32[144,1536]{1,0:T(8,128)S(1)}) custom-call(bf16[64,768]{1,0:T(8,128)(2,1)S(1)} %get-tuple-element.22.refs_0_, bf16[72,768]{1,0:T(8,128)(2,1)S(1)} %get-tuple-element.23.refs_1_, bf16[64,768]{1,0:T(8,128)(2,1)S(1)} %collective-permute-done.3.refs_2_, ...), custom_call_target="tpu_custom_call" | custom-call | flops 1698693120 | tf_op jit(solution)/shard_map/project/pallas_call | solution.py:234
  39.0 1.8 %collective-permute-done.12.refs_1_ = bf16[72,768]{1,0:T(8,128)(2,1)S(1)} collective-permute-done((bf16[72,768]{1,0:T(8,128)(2,1)S(1)}, bf16[72,768]{1,0:T(8,128)(2,1)S(1)}, u32[]{:S(2)}, u32[]{:S(2)}) %collective-permute-start.12) | collective-permute-done | bytes 110624 | tf_op jit(solution)/shard_map/ppermute | solution.py:288
  40.9 2.2 %project.3 = bf16[128,1536]{1,0:T(8,128)(2,1)} custom-call(bf16[64,768]{1,0:T(8,128)(2,1)S(1)} %collective-permute-done.11.refs_0_, bf16[72,768]{1,0:T(8,128)(2,1)S(1)} %collective-permute-done.12.refs_1_, bf16[64,768]{1,0:T(8,128)(2,1)S(1)} %collective-permute-done.13.refs_2_, bf16[72,768]{1,0:T(8,128)(2,1)S(1)} %collective-permute-done.14.refs_3_, ...), custom_call_target="tpu_custom_call" | custom-call | flops 1019215872 | tf_op jit(solution)/shard_map/project/pallas_call | solution.py:234
  (24 shorter events, 1.1 us)
Async XLA Ops:
  0.6 6.2 %copy-start.2 = (bf16[768]{0:T(1024)(128)(2,1)S(1)}, bf16[768]{0:T(1024)(128)(2,1)}, u32[]{:S(2)}) copy-start(bf16[768]{0:T(1024)(128)(2,1)} %param.8) | copy-start | bytes 4612
  0.6 35.7 %copy-start = (bf16[6144,1536]{1,0:T(8,128)(2,1)S(1)}, bf16[6144,1536]{1,0:T(8,128)(2,1)}, u32[]{:S(2)}) copy-start(bf16[6144,1536]{1,0:T(8,128)(2,1)} %refs_6_.1) | copy-start | bytes 56623108
  6.3 9.8 %copy-start.1 = (bf16[128,768]{1,0:T(8,128)(2,1)S(1)}, bf16[128,768]{1,0:T(8,128)(2,1)}, u32[]{:S(2)}) copy-start(bf16[128,768]{1,0:T(8,128)(2,1)} %param.7) | copy-start | bytes 589828
  6.3 1.6 %collective-permute-start = (bf16[1,128,768]{2,1,0:T(8,128)(2,1)S(1)}, bf16[1,128,768]{2,1,0:T(8,128)(2,1)S(1)}, u32[]{:S(2)}, u32[]{:S(2)}) collective-permute-start(bf16[1,128,768]{2,1,0:T(8,128)(2,1)S(1)} %get-tuple-element.16), channel_id=1, source_target_pairs={{0,8},{8,0},{16,24},{24,16},{1,9},{9,1},{17,25},{25,17},{2,10},{10... | collective-permute-start | bytes 589832 | tf_op jit(solution)/shard_map/ppermute | solution.py:269
  7.9 8.2 %collective-permute-start.1 = (bf16[128,768]{1,0:T(8,128)(2,1)S(1)}, bf16[128,768]{1,0:T(8,128)(2,1)S(1)}, u32[]{:S(2)}, u32[]{:S(2)}) collective-permute-start(bf16[128,768]{1,0:T(8,128)(2,1)S(1)} %bitcast.5), channel_id=1, source_target_pairs={{0,16},{8,24},{16,0},{24,8},{1,17},{9,25},{17,1},{25,9},{2,18},{10... | collective-permute-start | bytes 589832 | tf_op jit(solution)/shard_map/ppermute | solution.py:275
  15.3 1.5 %collective-permute-start.2 = (bf16[128,768]{1,0:T(8,128)(2,1)S(1)}, bf16[128,768]{1,0:T(8,128)(2,1)S(1)}, u32[]{:S(2)}, u32[]{:S(2)}) collective-permute-start(bf16[128,768]{1,0:T(8,128)(2,1)S(1)} %bitcast.4), channel_id=1, source_target_pairs={{0,8},{8,0},{16,24},{24,16},{1,9},{9,1},{17,25},{25,17},{2,10},{10... | collective-permute-start | bytes 589832 | tf_op jit(solution)/shard_map/ppermute | solution.py:277
  16.9 5.7 %collective-permute-start.3 = (bf16[64,768]{1,0:T(8,128)(2,1)S(1)}, bf16[64,768]{1,0:T(8,128)(2,1)S(1)}, u32[]{:S(2)}, u32[]{:S(2)}) collective-permute-start(bf16[64,768]{1,0:T(8,128)(2,1)S(1)} %get-tuple-element.22.refs_0_), channel_id=1, source_target_pairs={{0,1},{1,3},{3,5},{5,7},{7,6},{6,4},{4,2},{2,0},{8,9},{9,11},{11,1... | collective-permute-start | bytes 294920 | tf_op jit(solution)/shard_map/ppermute | solution.py:286
  18.8 5.7 %collective-permute-start.6 = (bf16[72,768]{1,0:T(8,128)(2,1)S(1)}, bf16[72,768]{1,0:T(8,128)(2,1)S(1)}, u32[]{:S(2)}, u32[]{:S(2)}) collective-permute-start(bf16[72,768]{1,0:T(8,128)(2,1)S(1)} %get-tuple-element.23.refs_1_), channel_id=1, source_target_pairs={{0,2},{1,0},{3,1},{5,3},{7,5},{6,7},{4,6},{2,4},{8,10},{9,8},{11,9... | collective-permute-start | bytes 331784 | tf_op jit(solution)/shard_map/ppermute | solution.py:286
  19.0 5.9 %collective-permute-start.4 = (bf16[72,768]{1,0:T(8,128)(2,1)S(1)}, bf16[72,768]{1,0:T(8,128)(2,1)S(1)}, u32[]{:S(2)}, u32[]{:S(2)}) collective-permute-start(bf16[72,768]{1,0:T(8,128)(2,1)S(1)} %get-tuple-element.23.refs_1_), channel_id=1, source_target_pairs={{0,1},{1,3},{3,5},{5,7},{7,6},{6,4},{4,2},{2,0},{8,9},{9,11},{11,1... | collective-permute-start | bytes 331784 | tf_op jit(solution)/shard_map/ppermute | solution.py:286
  20.8 5.7 %collective-permute-start.5 = (bf16[64,768]{1,0:T(8,128)(2,1)S(1)}, bf16[64,768]{1,0:T(8,128)(2,1)S(1)}, u32[]{:S(2)}, u32[]{:S(2)}) collective-permute-start(bf16[64,768]{1,0:T(8,128)(2,1)S(1)} %get-tuple-element.22.refs_0_), channel_id=1, source_target_pairs={{0,2},{1,0},{3,1},{5,3},{7,5},{6,7},{4,6},{2,4},{8,10},{9,8},{11,9... | collective-permute-start | bytes 294920 | tf_op jit(solution)/shard_map/ppermute | solution.py:286
  22.5 5.4 %collective-permute-start.7 = (bf16[64,768]{1,0:T(8,128)(2,1)S(1)}, bf16[64,768]{1,0:T(8,128)(2,1)S(1)}, u32[]{:S(2)}, u32[]{:S(2)}) collective-permute-start(bf16[64,768]{1,0:T(8,128)(2,1)S(1)} %collective-permute-done.3.refs_2_), channel_id=1, source_target_pairs={{0,1},{1,3},{3,5},{5,7},{7,6},{6,4},{4,2},{2,0},{8,9},{9,11},{11,1... | collective-permute-start | bytes 294920 | tf_op jit(solution)/shard_map/ppermute | solution.py:286
  24.5 8.5 %collective-permute-start.10 = (bf16[72,768]{1,0:T(8,128)(2,1)S(1)}, bf16[72,768]{1,0:T(8,128)(2,1)S(1)}, u32[]{:S(2)}, u32[]{:S(2)}) collective-permute-start(bf16[72,768]{1,0:T(8,128)(2,1)S(1)} %collective-permute-done.6.refs_5_), channel_id=1, source_target_pairs={{0,2},{1,0},{3,1},{5,3},{7,5},{6,7},{4,6},{2,4},{8,10},{9,8},{11,9... | collective-permute-start | bytes 331784 | tf_op jit(solution)/shard_map/ppermute | solution.py:286
  24.9 9.4 %collective-permute-start.8 = (bf16[72,768]{1,0:T(8,128)(2,1)S(1)}, bf16[72,768]{1,0:T(8,128)(2,1)S(1)}, u32[]{:S(2)}, u32[]{:S(2)}) collective-permute-start(bf16[72,768]{1,0:T(8,128)(2,1)S(1)} %collective-permute-done.4.refs_3_), channel_id=1, source_target_pairs={{0,1},{1,3},{3,5},{5,7},{7,6},{6,4},{4,2},{2,0},{8,9},{9,11},{11,1... | collective-permute-start | bytes 331784 | tf_op jit(solution)/shard_map/ppermute | solution.py:286
  26.5 6.0 %collective-permute-start.9 = (bf16[64,768]{1,0:T(8,128)(2,1)S(1)}, bf16[64,768]{1,0:T(8,128)(2,1)S(1)}, u32[]{:S(2)}, u32[]{:S(2)}) collective-permute-start(bf16[64,768]{1,0:T(8,128)(2,1)S(1)} %collective-permute-done.5.refs_4_), channel_id=1, source_target_pairs={{0,2},{1,0},{3,1},{5,3},{7,5},{6,7},{4,6},{2,4},{8,10},{9,8},{11,9... | collective-permute-start | bytes 294920 | tf_op jit(solution)/shard_map/ppermute | solution.py:286
  27.9 8.3 %collective-permute-start.11 = (bf16[64,768]{1,0:T(8,128)(2,1)S(1)}, bf16[64,768]{1,0:T(8,128)(2,1)S(1)}, u32[]{:S(2)}, u32[]{:S(2)}) collective-permute-start(bf16[64,768]{1,0:T(8,128)(2,1)S(1)} %collective-permute-done.7.refs_6_), channel_id=1, source_target_pairs={{0,3},{1,5},{3,7},{5,6},{7,4},{6,2},{4,0},{2,1},{8,11},{9,13},{11,... | collective-permute-start | bytes 294920 | tf_op jit(solution)/shard_map/ppermute | solution.py:288
  31.0 8.1 %collective-permute-start.13 = (bf16[64,768]{1,0:T(8,128)(2,1)S(1)}, bf16[64,768]{1,0:T(8,128)(2,1)S(1)}, u32[]{:S(2)}, u32[]{:S(2)}) collective-permute-start(bf16[64,768]{1,0:T(8,128)(2,1)S(1)} %collective-permute-done.7.refs_6_), channel_id=1, source_target_pairs={{0,1},{1,3},{3,5},{5,7},{7,6},{6,4},{4,2},{2,0},{8,9},{9,11},{11,1... | collective-permute-start | bytes 294920 | tf_op jit(solution)/shard_map/ppermute | solution.py:286
  32.5 6.5 %collective-permute-start.15 = (bf16[64,768]{1,0:T(8,128)(2,1)S(1)}, bf16[64,768]{1,0:T(8,128)(2,1)S(1)}, u32[]{:S(2)}, u32[]{:S(2)}) collective-permute-start(bf16[64,768]{1,0:T(8,128)(2,1)S(1)} %collective-permute-done.9.refs_8_), channel_id=1, source_target_pairs={{0,2},{1,0},{3,1},{5,3},{7,5},{6,7},{4,6},{2,4},{8,10},{9,8},{11,9... | collective-permute-start | bytes 294920 | tf_op jit(solution)/shard_map/ppermute | solution.py:286
  33.0 7.8 %collective-permute-start.12 = (bf16[72,768]{1,0:T(8,128)(2,1)S(1)}, bf16[72,768]{1,0:T(8,128)(2,1)S(1)}, u32[]{:S(2)}, u32[]{:S(2)}) collective-permute-start(bf16[72,768]{1,0:T(8,128)(2,1)S(1)} %collective-permute-done.10.refs_9_), channel_id=1, source_target_pairs={{0,4},{1,2},{3,0},{5,1},{7,3},{6,5},{4,7},{2,6},{8,12},{9,10},{11,... | collective-permute-start | bytes 331784 | tf_op jit(solution)/shard_map/ppermute | solution.py:288
  34.3 6.6 %collective-permute-start.16 = (bf16[72,768]{1,0:T(8,128)(2,1)S(1)}, bf16[72,768]{1,0:T(8,128)(2,1)S(1)}, u32[]{:S(2)}, u32[]{:S(2)}) collective-permute-start(bf16[72,768]{1,0:T(8,128)(2,1)S(1)} %collective-permute-done.10.refs_9_), channel_id=1, source_target_pairs={{0,2},{1,0},{3,1},{5,3},{7,5},{6,7},{4,6},{2,4},{8,10},{9,8},{11,9... | collective-permute-start | bytes 331784 | tf_op jit(solution)/shard_map/ppermute | solution.py:286
  36.2 4.7 %collective-permute-start.14 = (bf16[72,768]{1,0:T(8,128)(2,1)S(1)}, bf16[72,768]{1,0:T(8,128)(2,1)S(1)}, u32[]{:S(2)}, u32[]{:S(2)}) collective-permute-start(bf16[72,768]{1,0:T(8,128)(2,1)S(1)} %collective-permute-done.8.refs_7_), channel_id=1, source_target_pairs={{0,1},{1,3},{3,5},{5,7},{7,6},{6,4},{4,2},{2,0},{8,9},{9,11},{11,1... | collective-permute-start | bytes 331784 | tf_op jit(solution)/shard_map/ppermute | solution.py:286

commit v19 on v17

--- a/solution.py
+++ b/solution.py
@@ -121,19 +121,20 @@
 
 def merge_kernel(others, keep, got, gain, upper, lower):
     tok, width = others.shape
+    cut_at = upper.shape[0]
     own = keep[...].astype(jnp.float32) + got[...].astype(jnp.float32)
     value = (others[...] + own).astype(upper.dtype)
-    upper[...] = value[: tok // 2]
-    lower[0 : tok // 2, :] = value[tok // 2 :]
+    upper[...] = value[:cut_at]
+    lower[0 : tok - cut_at, :] = value[cut_at:]
     rows = jnp.broadcast_to(gain[...].astype(jnp.float32), (GAIN, width))
-    lower[tok // 2 : tok // 2 + GAIN, :] = rows.astype(lower.dtype)
+    lower[tok - cut_at : tok - cut_at + GAIN, :] = rows.astype(lower.dtype)
 
 
 def merge(others, keep, got, gain):
     tok, width = others.shape
     return pl.pallas_call(
         merge_kernel,
-        out_shape=[pltpu.VMEM((n, width), jnp.bfloat16) for n in (tok // 2, tok // 2 + GAIN)],
+        out_shape=[pltpu.VMEM((n, width), jnp.bfloat16) for n in (tok * 5 // 8, tok * 3 // 8 + GAIN)],
         in_specs=[VMEM] * 4,
         out_specs=[VMEM] * 2,
         compiler_params=pltpu.CompilerParams(vmem_limit_bytes=8 * MIB),

time: 43.4 us -> 43.7 us (level)
  starting transfers between devices: 19.9 us -> 21.4 us
  waiting for transfers between devices: 7.31 us -> 5.98 us
    ppermute x6, starting transfers between devices: 3.19 us -> 9.6 us  [per_device(): lax.ppermute(back[i], 'col', shift(-1))]
    ppermute x6, starting transfers between devices: 8.82 us -> 2.79 us  [per_device(): lax.ppermute(up[i], 'col', shift(1))]
    ppermute x1, waiting for transfers between devices: 1.79 us -> 0.01 us  [per_device(): lax.ppermute(opposite[1], 'col', shift(-2))]
    ppermute x1, starting transfers between devices: 1.27 us -> 2.82 us  [per_device(): lax.ppermute(opposite[1], 'col', shift(-2))]
    ppermute x6, waiting for transfers between devices: 2.57 us -> 1.02 us  [per_device(): lax.ppermute(up[i], 'col', shift(1))]
    ppermute x1, waiting for transfers between devices: 0.31 us -> 1.57 us  [per_device(): lax.ppermute(opposite[0], 'col', shift(2))]
    ppermute x6, waiting for transfers between devices: 0.2 us -> 0.96 us  [per_device(): lax.ppermute(back[i], 'col', shift(-1))]
  transfers between devices with their start and end apart: 17 -> 17, of which waited for: 8 -> 6; matrix products, arithmetic and copies ran while one was open for 0% -> 0% of each run, Pallas kernels for 18% -> 18%
where the time goes in v19:
time: 43.7 us; the launch traced here: 43.5 us
  starting transfers between devices  21.4 us (49%)
  Pallas kernels  15.2 us (35%)
  waiting for transfers between devices  5.98 us (14%)
  between operations  0.75 us (2%)
    pallas_call x2, Pallas kernels, down(): pl.pallas_call(functools.partial(down_kernel, chips_y, tok, parts, own),...  10 us
    ppermute x6, starting transfers between devices, per_device(): lax.ppermute(back[i], 'col', shift(-1))  9.6 us
    pallas_call x3, Pallas kernels, project(): pl.pallas_call(functools.partial(project_kernel, cycle, hops, [len(parts)...  5.14 us
    ppermute x1, starting transfers between devices, per_device(): lax.ppermute(both[step - 1], 'row', move).astype(jnp.float32)  2.95 us
    ppermute x1, starting transfers between devices, per_device(): lax.ppermute(opposite[1], 'col', shift(-2))  2.82 us
    ppermute x6, starting transfers between devices, per_device(): lax.ppermute(up[i], 'col', shift(1))  2.79 us
    ppermute x1, starting transfers between devices, per_device(): lax.ppermute(opposite[0], 'col', shift(2))  2.7 us
    ppermute x1, waiting for transfers between devices, per_device(): lax.ppermute(opposite[0], 'col', shift(2))  1.57 us
  transfers between devices with their start and end apart: 17, of which 6 were waited for; matrix products, arithmetic and copies ran while one was open for 0% of the time, Pallas kernels for 18%

profile of v19, /device:TPU:0, one launch (start us, length us, event | category | flops | bytes accessed | tf_op | source)
XLA Modules:
  0.0 43.5 jit_solution(2885964577084112070)
XLA Ops:
  0.7 5.6 %down.2 = (bf16[1,128,768]{2,1,0:T(8,128)(2,1)S(1)}, bf16[1,128,768]{2,1,0:T(8,128)(2,1)S(1)}, bf16[6144,768]{1,0:T(8,128)(2,1)S(1)}) custom-call(bf16[512,6144]{1,0:T(8,128)(2,1)} %hidden.2, bf16[6144,768]{1,0:T(8,128)(2,1)} %weight.1), custom_call_target="tpu_custom_call" | custom-call | flops 2415919104 | bytes 12582912 | tf_op jit(solution)/shard_map/down/pallas_call | solution.py:99
  6.3 0.5 %collective-permute-start = (bf16[1,128,768]{2,1,0:T(8,128)(2,1)S(1)}, bf16[1,128,768]{2,1,0:T(8,128)(2,1)S(1)}, u32[]{:S(2)}, u32[]{:S(2)}) collective-permute-start(bf16[1,128,768]{2,1,0:T(8,128)(2,1)S(1)} %get-tuple-element.18), channel_id=1, source_target_pairs={{0,8},{8,0},{16,24},{24,16},{1,9},{9,1},{17,25},{25,17},{2,10},{10... | collective-permute-start | bytes 589832 | tf_op jit(solution)/shard_map/ppermute | solution.py:270
  6.8 1.1 %collective-permute-done = bf16[1,128,768]{2,1,0:T(8,128)(2,1)S(1)} collective-permute-done((bf16[1,128,768]{2,1,0:T(8,128)(2,1)S(1)}, bf16[1,128,768]{2,1,0:T(8,128)(2,1)S(1)}, u32[]{:S(2)}, u32[]{:S(2)}) %collective-permute-start) | collective-permute-done | bytes 196640 | tf_op jit(solution)/shard_map/ppermute | solution.py:270
  7.9 3.0 %collective-permute-start.1 = (bf16[128,768]{1,0:T(8,128)(2,1)S(1)}, bf16[128,768]{1,0:T(8,128)(2,1)S(1)}, u32[]{:S(2)}, u32[]{:S(2)}) collective-permute-start(bf16[128,768]{1,0:T(8,128)(2,1)S(1)} %bitcast.5), channel_id=1, source_target_pairs={{0,16},{8,24},{16,0},{24,8},{1,17},{9,25},{17,1},{25,9},{2,18},{10... | collective-permute-start | bytes 589832 | tf_op jit(solution)/shard_map/ppermute | solution.py:276
  10.9 4.4 %down.3 = (bf16[1,128,768]{2,1,0:T(8,128)(2,1)S(1)}, bf16[1,128,768]{2,1,0:T(8,128)(2,1)S(1)}) custom-call(bf16[512,6144]{1,0:T(8,128)(2,1)} %hidden.2, bf16[6144,768]{1,0:T(8,128)(2,1)S(1)} %get-tuple-element.21.weight), custom_call_target="tpu_custom_call" | custom-call | flops 2415919104 | bytes 3145728 | tf_op jit(solution)/shard_map/down/pallas_call | solution.py:99
  15.4 0.7 %collective-permute-done.1 = bf16[128,768]{1,0:T(8,128)(2,1)S(1)} collective-permute-done((bf16[128,768]{1,0:T(8,128)(2,1)S(1)}, bf16[128,768]{1,0:T(8,128)(2,1)S(1)}, u32[]{:S(2)}, u32[]{:S(2)}) %collective-permute-start.1) | collective-permute-done | bytes 196640 | tf_op jit(solution)/shard_map/ppermute | solution.py:276
  16.1 0.7 %collective-permute-done.2.got = bf16[128,768]{1,0:T(8,128)(2,1)S(1)} collective-permute-done((bf16[128,768]{1,0:T(8,128)(2,1)S(1)}, bf16[128,768]{1,0:T(8,128)(2,1)S(1)}, u32[]{:S(2)}, u32[]{:S(2)}) %collective-permute-start.2) | collective-permute-done | bytes 196640 | tf_op jit(solution)/shard_map/ppermute | solution.py:278
  16.9 2.0 %collective-permute-start.6 = (bf16[56,768]{1,0:T(8,128)(2,1)S(1)}, bf16[56,768]{1,0:T(8,128)(2,1)S(1)}, u32[]{:S(2)}, u32[]{:S(2)}) collective-permute-start(bf16[56,768]{1,0:T(8,128)(2,1)S(1)} %get-tuple-element.25.refs_1_), channel_id=1, source_target_pairs={{0,2},{1,0},{3,1},{5,3},{7,5},{6,7},{4,6},{2,4},{8,10},{9,8},{11,9... | collective-permute-start | bytes 258056 | tf_op jit(solution)/shard_map/ppermute | solution.py:287
  19.0 1.9 %collective-permute-start.5 = (bf16[80,768]{1,0:T(8,128)(2,1)S(1)}, bf16[80,768]{1,0:T(8,128)(2,1)S(1)}, u32[]{:S(2)}, u32[]{:S(2)}) collective-permute-start(bf16[80,768]{1,0:T(8,128)(2,1)S(1)} %get-tuple-element.24.refs_0_), channel_id=1, source_target_pairs={{0,2},{1,0},{3,1},{5,3},{7,5},{6,7},{4,6},{2,4},{8,10},{9,8},{11,9... | collective-permute-start | bytes 368648 | tf_op jit(solution)/shard_map/ppermute | solution.py:287
  21.0 0.9 %collective-permute-done.6.refs_5_ = bf16[56,768]{1,0:T(8,128)(2,1)S(1)} collective-permute-done((bf16[56,768]{1,0:T(8,128)(2,1)S(1)}, bf16[56,768]{1,0:T(8,128)(2,1)S(1)}, u32[]{:S(2)}, u32[]{:S(2)}) %collective-permute-start.6) | collective-permute-done | bytes 86048 | tf_op jit(solution)/shard_map/ppermute | solution.py:287
  21.9 1.9 %collective-permute-start.10 = (bf16[56,768]{1,0:T(8,128)(2,1)S(1)}, bf16[56,768]{1,0:T(8,128)(2,1)S(1)}, u32[]{:S(2)}, u32[]{:S(2)}) collective-permute-start(bf16[56,768]{1,0:T(8,128)(2,1)S(1)} %collective-permute-done.6.refs_5_), channel_id=1, source_target_pairs={{0,2},{1,0},{3,1},{5,3},{7,5},{6,7},{4,6},{2,4},{8,10},{9,8},{11,9... | collective-permute-start | bytes 258056 | tf_op jit(solution)/shard_map/ppermute | solution.py:287
  23.9 1.0 %collective-permute-done.3.refs_2_ = bf16[80,768]{1,0:T(8,128)(2,1)S(1)} collective-permute-done((bf16[80,768]{1,0:T(8,128)(2,1)S(1)}, bf16[80,768]{1,0:T(8,128)(2,1)S(1)}, u32[]{:S(2)}, u32[]{:S(2)}) %collective-permute-start.3) | collective-permute-done | bytes 122912 | tf_op jit(solution)/shard_map/ppermute | solution.py:287
  25.1 1.7 %collective-permute-start.9 = (bf16[80,768]{1,0:T(8,128)(2,1)S(1)}, bf16[80,768]{1,0:T(8,128)(2,1)S(1)}, u32[]{:S(2)}, u32[]{:S(2)}) collective-permute-start(bf16[80,768]{1,0:T(8,128)(2,1)S(1)} %collective-permute-done.5.refs_4_), channel_id=1, source_target_pairs={{0,2},{1,0},{3,1},{5,3},{7,5},{6,7},{4,6},{2,4},{8,10},{9,8},{11,9... | collective-permute-start | bytes 368648 | tf_op jit(solution)/shard_map/ppermute | solution.py:287
  26.9 0.3 collective-permute-start.8
  27.2 2.8 %collective-permute-start.16 = (bf16[56,768]{1,0:T(8,128)(2,1)S(1)}, bf16[56,768]{1,0:T(8,128)(2,1)S(1)}, u32[]{:S(2)}, u32[]{:S(2)}) collective-permute-start(bf16[56,768]{1,0:T(8,128)(2,1)S(1)} %collective-permute-done.10.refs_9_), channel_id=1, source_target_pairs={{0,4},{1,2},{3,0},{5,1},{7,3},{6,5},{4,7},{2,6},{8,12},{9,10},{11,... | collective-permute-start | bytes 258056 | tf_op jit(solution)/shard_map/ppermute | solution.py:289
  30.0 1.6 %collective-permute-start.14 = (bf16[56,768]{1,0:T(8,128)(2,1)S(1)}, bf16[56,768]{1,0:T(8,128)(2,1)S(1)}, u32[]{:S(2)}, u32[]{:S(2)}) collective-permute-start(bf16[56,768]{1,0:T(8,128)(2,1)S(1)} %collective-permute-done.10.refs_9_), channel_id=1, source_target_pairs={{0,2},{1,0},{3,1},{5,3},{7,5},{6,7},{4,6},{2,4},{8,10},{9,8},{11,9... | collective-permute-start | bytes 258056 | tf_op jit(solution)/shard_map/ppermute | solution.py:287
  31.6 0.4 %collective-permute-start.12 = (bf16[56,768]{1,0:T(8,128)(2,1)S(1)}, bf16[56,768]{1,0:T(8,128)(2,1)S(1)}, u32[]{:S(2)}, u32[]{:S(2)}) collective-permute-start(bf16[56,768]{1,0:T(8,128)(2,1)S(1)} %collective-permute-done.8.refs_7_), channel_id=1, source_target_pairs={{0,1},{1,3},{3,5},{5,7},{7,6},{6,4},{4,2},{2,0},{8,9},{9,11},{11,1... | collective-permute-start | bytes 258056 | tf_op jit(solution)/shard_map/ppermute | solution.py:287
  32.0 2.7 %collective-permute-start.15 = (bf16[80,768]{1,0:T(8,128)(2,1)S(1)}, bf16[80,768]{1,0:T(8,128)(2,1)S(1)}, u32[]{:S(2)}, u32[]{:S(2)}) collective-permute-start(bf16[80,768]{1,0:T(8,128)(2,1)S(1)} %collective-permute-done.7.refs_6_), channel_id=1, source_target_pairs={{0,3},{1,5},{3,7},{5,6},{7,4},{6,2},{4,0},{2,1},{8,11},{9,13},{11,... | collective-permute-start | bytes 368648 | tf_op jit(solution)/shard_map/ppermute | solution.py:289
  34.7 1.6 %collective-permute-start.11 = (bf16[80,768]{1,0:T(8,128)(2,1)S(1)}, bf16[80,768]{1,0:T(8,128)(2,1)S(1)}, u32[]{:S(2)}, u32[]{:S(2)}) collective-permute-start(bf16[80,768]{1,0:T(8,128)(2,1)S(1)} %collective-permute-done.7.refs_6_), channel_id=1, source_target_pairs={{0,1},{1,3},{3,5},{5,7},{7,6},{6,4},{4,2},{2,0},{8,9},{9,11},{11,1... | collective-permute-start | bytes 368648 | tf_op jit(solution)/shard_map/ppermute | solution.py:287
  36.3 0.4 %collective-permute-start.13 = (bf16[80,768]{1,0:T(8,128)(2,1)S(1)}, bf16[80,768]{1,0:T(8,128)(2,1)S(1)}, u32[]{:S(2)}, u32[]{:S(2)}) collective-permute-start(bf16[80,768]{1,0:T(8,128)(2,1)S(1)} %collective-permute-done.9.refs_8_), channel_id=1, source_target_pairs={{0,2},{1,0},{3,1},{5,3},{7,5},{6,7},{4,6},{2,4},{8,10},{9,8},{11,9... | collective-permute-start | bytes 368648 | tf_op jit(solution)/shard_map/ppermute | solution.py:287
  36.8 2.7 %project.3 = (bf16[128,768]{1,0:T(8,128)(2,1)}, f32[128,1]{1,0:T(8,128)S(1)}, f32[2,128,1]{2,1,0:T(8,128)S(1)}, f32[144,1536]{1,0:T(8,128)S(1)}) custom-call(bf16[80,768]{1,0:T(8,128)(2,1)S(1)} %get-tuple-element.24.refs_0_, bf16[56,768]{1,0:T(8,128)(2,1)S(1)} %get-tuple-element.25.refs_1_, bf16[80,768]{1,0:T(8,128)(2,1)S(1)} %collective-permute-done.3.refs_2_, ...), custom_call_target="tpu_custom_call" | custom-call | flops 1698693120 | tf_op jit(solution)/shard_map/project/pallas_call | solution.py:235
  39.5 1.6 %collective-permute-done.15.refs_0_ = bf16[80,768]{1,0:T(8,128)(2,1)S(1)} collective-permute-done((bf16[80,768]{1,0:T(8,128)(2,1)S(1)}, bf16[80,768]{1,0:T(8,128)(2,1)S(1)}, u32[]{:S(2)}, u32[]{:S(2)}) %collective-permute-start.15) | collective-permute-done | bytes 122912 | tf_op jit(solution)/shard_map/ppermute | solution.py:289
  41.1 0.7 %project.4 = (f32[2,128,1]{2,1,0:T(8,128)S(1)}, f32[144,1536]{1,0:T(8,128)S(1)}) custom-call(bf16[80,768]{1,0:T(8,128)(2,1)S(1)} %collective-permute-done.15.refs_0_, bf16[56,768]{1,0:T(8,128)(2,1)S(1)} %collective-permute-done.16.refs_1_, bf16[6144,1536]{1,0:T(8,128)(2,1)S(1)} %copy-done, ...), custom_call_target="tpu_custom_call", output_to_operand_aliasing={{0}: (4, {}), {1}: (5, {})} | custom-call | flops 339738624 | tf_op jit(solution)/shard_map/project/pallas_call | solution.py:235
  41.8 1.7 %project.5 = bf16[128,1536]{1,0:T(8,128)(2,1)} custom-call(bf16[80,768]{1,0:T(8,128)(2,1)S(1)} %collective-permute-done.11.refs_0_, bf16[56,768]{1,0:T(8,128)(2,1)S(1)} %collective-permute-done.12.refs_1_, bf16[80,768]{1,0:T(8,128)(2,1)S(1)} %collective-permute-done.13.refs_2_, bf16[56,768]{1,0:T(8,128)(2,1)S(1)} %collective-permute-done.14.refs_3_, ...), custom_call_target="tpu_custom_call" | custom-call | flops 679477248 | tf_op jit(solution)/shard_map/project/pallas_call | solution.py:235
  (25 shorter events, 0.8 us)
Async XLA Ops:
  0.6 6.2 %copy-start.2 = (bf16[768]{0:T(1024)(128)(2,1)S(1)}, bf16[768]{0:T(1024)(128)(2,1)}, u32[]{:S(2)}) copy-start(bf16[768]{0:T(1024)(128)(2,1)} %param.8) | copy-start | bytes 4612
  0.6 36.1 %copy-start = (bf16[6144,1536]{1,0:T(8,128)(2,1)S(1)}, bf16[6144,1536]{1,0:T(8,128)(2,1)}, u32[]{:S(2)}) copy-start(bf16[6144,1536]{1,0:T(8,128)(2,1)} %refs_4_.1) | copy-start | bytes 56623108
  6.3 9.8 %copy-start.1 = (bf16[128,768]{1,0:T(8,128)(2,1)S(1)}, bf16[128,768]{1,0:T(8,128)(2,1)}, u32[]{:S(2)}) copy-start(bf16[128,768]{1,0:T(8,128)(2,1)} %param.7) | copy-start | bytes 589828
  6.3 1.6 %collective-permute-start = (bf16[1,128,768]{2,1,0:T(8,128)(2,1)S(1)}, bf16[1,128,768]{2,1,0:T(8,128)(2,1)S(1)}, u32[]{:S(2)}, u32[]{:S(2)}) collective-permute-start(bf16[1,128,768]{2,1,0:T(8,128)(2,1)S(1)} %get-tuple-element.18), channel_id=1, source_target_pairs={{0,8},{8,0},{16,24},{24,16},{1,9},{9,1},{17,25},{25,17},{2,10},{10... | collective-permute-start | bytes 589832 | tf_op jit(solution)/shard_map/ppermute | solution.py:270
  7.9 8.2 %collective-permute-start.1 = (bf16[128,768]{1,0:T(8,128)(2,1)S(1)}, bf16[128,768]{1,0:T(8,128)(2,1)S(1)}, u32[]{:S(2)}, u32[]{:S(2)}) collective-permute-start(bf16[128,768]{1,0:T(8,128)(2,1)S(1)} %bitcast.5), channel_id=1, source_target_pairs={{0,16},{8,24},{16,0},{24,8},{1,17},{9,25},{17,1},{25,9},{2,18},{10... | collective-permute-start | bytes 589832 | tf_op jit(solution)/shard_map/ppermute | solution.py:276
  15.3 1.5 %collective-permute-start.2 = (bf16[128,768]{1,0:T(8,128)(2,1)S(1)}, bf16[128,768]{1,0:T(8,128)(2,1)S(1)}, u32[]{:S(2)}, u32[]{:S(2)}) collective-permute-start(bf16[128,768]{1,0:T(8,128)(2,1)S(1)} %bitcast.4), channel_id=1, source_target_pairs={{0,8},{8,0},{16,24},{24,16},{1,9},{9,1},{17,25},{25,17},{2,10},{10... | collective-permute-start | bytes 589832 | tf_op jit(solution)/shard_map/ppermute | solution.py:278
  16.9 5.1 %collective-permute-start.6 = (bf16[56,768]{1,0:T(8,128)(2,1)S(1)}, bf16[56,768]{1,0:T(8,128)(2,1)S(1)}, u32[]{:S(2)}, u32[]{:S(2)}) collective-permute-start(bf16[56,768]{1,0:T(8,128)(2,1)S(1)} %get-tuple-element.25.refs_1_), channel_id=1, source_target_pairs={{0,2},{1,0},{3,1},{5,3},{7,5},{6,7},{4,6},{2,4},{8,10},{9,8},{11,9... | collective-permute-start | bytes 258056 | tf_op jit(solution)/shard_map/ppermute | solution.py:287
  18.9 6.0 %collective-permute-start.3 = (bf16[80,768]{1,0:T(8,128)(2,1)S(1)}, bf16[80,768]{1,0:T(8,128)(2,1)S(1)}, u32[]{:S(2)}, u32[]{:S(2)}) collective-permute-start(bf16[80,768]{1,0:T(8,128)(2,1)S(1)} %get-tuple-element.24.refs_0_), channel_id=1, source_target_pairs={{0,1},{1,3},{3,5},{5,7},{7,6},{6,4},{4,2},{2,0},{8,9},{9,11},{11,1... | collective-permute-start | bytes 368648 | tf_op jit(solution)/shard_map/ppermute | solution.py:287
  19.0 6.2 %collective-permute-start.5 = (bf16[80,768]{1,0:T(8,128)(2,1)S(1)}, bf16[80,768]{1,0:T(8,128)(2,1)S(1)}, u32[]{:S(2)}, u32[]{:S(2)}) collective-permute-start(bf16[80,768]{1,0:T(8,128)(2,1)S(1)} %get-tuple-element.24.refs_0_), channel_id=1, source_target_pairs={{0,2},{1,0},{3,1},{5,3},{7,5},{6,7},{4,6},{2,4},{8,10},{9,8},{11,9... | collective-permute-start | bytes 368648 | tf_op jit(solution)/shard_map/ppermute | solution.py:287
  20.9 6.0 %collective-permute-start.4 = (bf16[56,768]{1,0:T(8,128)(2,1)S(1)}, bf16[56,768]{1,0:T(8,128)(2,1)S(1)}, u32[]{:S(2)}, u32[]{:S(2)}) collective-permute-start(bf16[56,768]{1,0:T(8,128)(2,1)S(1)} %get-tuple-element.25.refs_1_), channel_id=1, source_target_pairs={{0,1},{1,3},{3,5},{5,7},{7,6},{6,4},{4,2},{2,0},{8,9},{9,11},{11,1... | collective-permute-start | bytes 258056 | tf_op jit(solution)/shard_map/ppermute | solution.py:287
  21.9 5.2 %collective-permute-start.10 = (bf16[56,768]{1,0:T(8,128)(2,1)S(1)}, bf16[56,768]{1,0:T(8,128)(2,1)S(1)}, u32[]{:S(2)}, u32[]{:S(2)}) collective-permute-start(bf16[56,768]{1,0:T(8,128)(2,1)S(1)} %collective-permute-done.6.refs_5_), channel_id=1, source_target_pairs={{0,2},{1,0},{3,1},{5,3},{7,5},{6,7},{4,6},{2,4},{8,10},{9,8},{11,9... | collective-permute-start | bytes 258056 | tf_op jit(solution)/shard_map/ppermute | solution.py:287
  24.9 7.2 %collective-permute-start.7 = (bf16[80,768]{1,0:T(8,128)(2,1)S(1)}, bf16[80,768]{1,0:T(8,128)(2,1)S(1)}, u32[]{:S(2)}, u32[]{:S(2)}) collective-permute-start(bf16[80,768]{1,0:T(8,128)(2,1)S(1)} %collective-permute-done.3.refs_2_), channel_id=1, source_target_pairs={{0,1},{1,3},{3,5},{5,7},{7,6},{6,4},{4,2},{2,0},{8,9},{9,11},{11,1... | collective-permute-start | bytes 368648 | tf_op jit(solution)/shard_map/ppermute | solution.py:287
  25.1 9.6 %collective-permute-start.9 = (bf16[80,768]{1,0:T(8,128)(2,1)S(1)}, bf16[80,768]{1,0:T(8,128)(2,1)S(1)}, u32[]{:S(2)}, u32[]{:S(2)}) collective-permute-start(bf16[80,768]{1,0:T(8,128)(2,1)S(1)} %collective-permute-done.5.refs_4_), channel_id=1, source_target_pairs={{0,2},{1,0},{3,1},{5,3},{7,5},{6,7},{4,6},{2,4},{8,10},{9,8},{11,9... | collective-permute-start | bytes 368648 | tf_op jit(solution)/shard_map/ppermute | solution.py:287
  26.9 4.7 %collective-permute-start.8 = (bf16[56,768]{1,0:T(8,128)(2,1)S(1)}, bf16[56,768]{1,0:T(8,128)(2,1)S(1)}, u32[]{:S(2)}, u32[]{:S(2)}) collective-permute-start(bf16[56,768]{1,0:T(8,128)(2,1)S(1)} %collective-permute-done.4.refs_3_), channel_id=1, source_target_pairs={{0,1},{1,3},{3,5},{5,7},{7,6},{6,4},{4,2},{2,0},{8,9},{9,11},{11,1... | collective-permute-start | bytes 258056 | tf_op jit(solution)/shard_map/ppermute | solution.py:287
  27.2 9.1 %collective-permute-start.16 = (bf16[56,768]{1,0:T(8,128)(2,1)S(1)}, bf16[56,768]{1,0:T(8,128)(2,1)S(1)}, u32[]{:S(2)}, u32[]{:S(2)}) collective-permute-start(bf16[56,768]{1,0:T(8,128)(2,1)S(1)} %collective-permute-done.10.refs_9_), channel_id=1, source_target_pairs={{0,4},{1,2},{3,0},{5,1},{7,3},{6,5},{4,7},{2,6},{8,12},{9,10},{11,... | collective-permute-start | bytes 258056 | tf_op jit(solution)/shard_map/ppermute | solution.py:289
  30.0 11.7 %collective-permute-start.14 = (bf16[56,768]{1,0:T(8,128)(2,1)S(1)}, bf16[56,768]{1,0:T(8,128)(2,1)S(1)}, u32[]{:S(2)}, u32[]{:S(2)}) collective-permute-start(bf16[56,768]{1,0:T(8,128)(2,1)S(1)} %collective-permute-done.10.refs_9_), channel_id=1, source_target_pairs={{0,2},{1,0},{3,1},{5,3},{7,5},{6,7},{4,6},{2,4},{8,10},{9,8},{11,9... | collective-permute-start | bytes 258056 | tf_op jit(solution)/shard_map/ppermute | solution.py:287
  31.6 10.2 %collective-permute-start.12 = (bf16[56,768]{1,0:T(8,128)(2,1)S(1)}, bf16[56,768]{1,0:T(8,128)(2,1)S(1)}, u32[]{:S(2)}, u32[]{:S(2)}) collective-permute-start(bf16[56,768]{1,0:T(8,128)(2,1)S(1)} %collective-permute-done.8.refs_7_), channel_id=1, source_target_pairs={{0,1},{1,3},{3,5},{5,7},{7,6},{6,4},{4,2},{2,0},{8,9},{9,11},{11,1... | collective-permute-start | bytes 258056 | tf_op jit(solution)/shard_map/ppermute | solution.py:287
  32.0 9.0 %collective-permute-start.15 = (bf16[80,768]{1,0:T(8,128)(2,1)S(1)}, bf16[80,768]{1,0:T(8,128)(2,1)S(1)}, u32[]{:S(2)}, u32[]{:S(2)}) collective-permute-start(bf16[80,768]{1,0:T(8,128)(2,1)S(1)} %collective-permute-done.7.refs_6_), channel_id=1, source_target_pairs={{0,3},{1,5},{3,7},{5,6},{7,4},{6,2},{4,0},{2,1},{8,11},{9,13},{11,... | collective-permute-start | bytes 368648 | tf_op jit(solution)/shard_map/ppermute | solution.py:289
  34.7 7.0 %collective-permute-start.11 = (bf16[80,768]{1,0:T(8,128)(2,1)S(1)}, bf16[80,768]{1,0:T(8,128)(2,1)S(1)}, u32[]{:S(2)}, u32[]{:S(2)}) collective-permute-start(bf16[80,768]{1,0:T(8,128)(2,1)S(1)} %collective-permute-done.7.refs_6_), channel_id=1, source_target_pairs={{0,1},{1,3},{3,5},{5,7},{7,6},{6,4},{4,2},{2,0},{8,9},{9,11},{11,1... | collective-permute-start | bytes 368648 | tf_op jit(solution)/shard_map/ppermute | solution.py:287
  36.3 5.5 %collective-permute-start.13 = (bf16[80,768]{1,0:T(8,128)(2,1)S(1)}, bf16[80,768]{1,0:T(8,128)(2,1)S(1)}, u32[]{:S(2)}, u32[]{:S(2)}) collective-permute-start(bf16[80,768]{1,0:T(8,128)(2,1)S(1)} %collective-permute-done.9.refs_8_), channel_id=1, source_target_pairs={{0,2},{1,0},{3,1},{5,3},{7,5},{6,7},{4,6},{2,4},{8,10},{9,8},{11,9... | collective-permute-start | bytes 368648 | tf_op jit(solution)/shard_map/ppermute | solution.py:287

commit v20 on v19

--- a/solution.py
+++ b/solution.py
@@ -134,7 +134,7 @@
     tok, width = others.shape
     return pl.pallas_call(
         merge_kernel,
-        out_shape=[pltpu.VMEM((n, width), jnp.bfloat16) for n in (tok * 5 // 8, tok * 3 // 8 + GAIN)],
+        out_shape=[pltpu.VMEM((n, width), jnp.bfloat16) for n in (tok * 3 // 8, tok * 5 // 8 + GAIN)],
         in_specs=[VMEM] * 4,
         out_specs=[VMEM] * 2,
         compiler_params=pltpu.CompilerParams(vmem_limit_bytes=8 * MIB),

time: 43.7 us -> 45.4 us (1.039)
  waiting for transfers between devices: 5.98 us -> 9.39 us
  starting transfers between devices: 21.4 us -> 19.8 us
    ppermute x6, waiting for transfers between devices: 1.02 us -> 6.55 us  [per_device(): lax.ppermute(up[i], 'col', shift(1))]
    ppermute x6, starting transfers between devices: 2.79 us -> 4.69 us  [per_device(): lax.ppermute(up[i], 'col', shift(1))]
    ppermute x6, starting transfers between devices: 9.6 us -> 7.92 us  [per_device(): lax.ppermute(back[i], 'col', shift(-1))]
    ppermute x1, waiting for transfers between devices: 1.57 us -> 0.12 us  [per_device(): lax.ppermute(opposite[0], 'col', shift(2))]
    ppermute x1, starting transfers between devices: 2.7 us -> 1.38 us  [per_device(): lax.ppermute(opposite[0], 'col', shift(2))]
    ppermute x6, waiting for transfers between devices: 0.96 us -> 0.28 us  [per_device(): lax.ppermute(back[i], 'col', shift(-1))]
    ppermute x1, starting transfers between devices: 2.82 us -> 2.29 us  [per_device(): lax.ppermute(opposite[1], 'col', shift(-2))]
  transfers between devices with their start and end apart: 17 -> 17, of which waited for: 6 -> 8; matrix products, arithmetic and copies ran while one was open for 0% -> 0% of each run, Pallas kernels for 18% -> 17%
where the time goes in v20:
time: 45.4 us; the launch traced here: 45.3 us
  starting transfers between devices  19.8 us (44%)
  Pallas kernels  15.2 us (33%)
  waiting for transfers between devices  9.39 us (21%)
  between operations  0.73 us (2%)
    pallas_call x2, Pallas kernels, down(): pl.pallas_call(functools.partial(down_kernel, chips_y, tok, parts, own),...  10 us
    ppermute x6, starting transfers between devices, per_device(): lax.ppermute(back[i], 'col', shift(-1))  7.92 us
    ppermute x6, waiting for transfers between devices, per_device(): lax.ppermute(up[i], 'col', shift(1))  6.55 us
    pallas_call x3, Pallas kernels, project(): pl.pallas_call(functools.partial(project_kernel, cycle, hops, [len(parts)...  5.14 us
    ppermute x6, starting transfers between devices, per_device(): lax.ppermute(up[i], 'col', shift(1))  4.69 us
    ppermute x1, starting transfers between devices, per_device(): lax.ppermute(both[step - 1], 'row', move).astype(jnp.float32)  2.95 us
    ppermute x1, starting transfers between devices, per_device(): lax.ppermute(opposite[1], 'col', shift(-2))  2.29 us
    ppermute x1, starting transfers between devices, per_device(): lax.ppermute(opposite[0], 'col', shift(2))  1.38 us
  transfers between devices with their start and end apart: 17, of which 8 were waited for; matrix products, arithmetic and copies ran while one was open for 0% of the time, Pallas kernels for 17%

profile of v20, /device:TPU:0, one launch (start us, length us, event | category | flops | bytes accessed | tf_op | source)
XLA Modules:
  0.0 45.3 jit_solution(17012385290970857330)
XLA Ops:
  0.7 5.6 %down.2 = (bf16[1,128,768]{2,1,0:T(8,128)(2,1)S(1)}, bf16[1,128,768]{2,1,0:T(8,128)(2,1)S(1)}, bf16[6144,768]{1,0:T(8,128)(2,1)S(1)}) custom-call(bf16[512,6144]{1,0:T(8,128)(2,1)} %hidden.2, bf16[6144,768]{1,0:T(8,128)(2,1)} %weight.1), custom_call_target="tpu_custom_call" | custom-call | flops 2415919104 | bytes 12582912 | tf_op jit(solution)/shard_map/down/pallas_call | solution.py:99
  6.3 0.5 %collective-permute-start = (bf16[1,128,768]{2,1,0:T(8,128)(2,1)S(1)}, bf16[1,128,768]{2,1,0:T(8,128)(2,1)S(1)}, u32[]{:S(2)}, u32[]{:S(2)}) collective-permute-start(bf16[1,128,768]{2,1,0:T(8,128)(2,1)S(1)} %get-tuple-element.18), channel_id=1, source_target_pairs={{0,8},{8,0},{16,24},{24,16},{1,9},{9,1},{17,25},{25,17},{2,10},{10... | collective-permute-start | bytes 589832 | tf_op jit(solution)/shard_map/ppermute | solution.py:270
  6.8 1.1 %collective-permute-done = bf16[1,128,768]{2,1,0:T(8,128)(2,1)S(1)} collective-permute-done((bf16[1,128,768]{2,1,0:T(8,128)(2,1)S(1)}, bf16[1,128,768]{2,1,0:T(8,128)(2,1)S(1)}, u32[]{:S(2)}, u32[]{:S(2)}) %collective-permute-start) | collective-permute-done | bytes 196640 | tf_op jit(solution)/shard_map/ppermute | solution.py:270
  7.9 3.0 %collective-permute-start.1 = (bf16[128,768]{1,0:T(8,128)(2,1)S(1)}, bf16[128,768]{1,0:T(8,128)(2,1)S(1)}, u32[]{:S(2)}, u32[]{:S(2)}) collective-permute-start(bf16[128,768]{1,0:T(8,128)(2,1)S(1)} %bitcast.5), channel_id=1, source_target_pairs={{0,16},{8,24},{16,0},{24,8},{1,17},{9,25},{17,1},{25,9},{2,18},{10... | collective-permute-start | bytes 589832 | tf_op jit(solution)/shard_map/ppermute | solution.py:276
  10.9 4.4 %down.3 = (bf16[1,128,768]{2,1,0:T(8,128)(2,1)S(1)}, bf16[1,128,768]{2,1,0:T(8,128)(2,1)S(1)}) custom-call(bf16[512,6144]{1,0:T(8,128)(2,1)} %hidden.2, bf16[6144,768]{1,0:T(8,128)(2,1)S(1)} %get-tuple-element.21.weight), custom_call_target="tpu_custom_call" | custom-call | flops 2415919104 | bytes 3145728 | tf_op jit(solution)/shard_map/down/pallas_call | solution.py:99
  15.4 0.7 %collective-permute-done.1 = bf16[128,768]{1,0:T(8,128)(2,1)S(1)} collective-permute-done((bf16[128,768]{1,0:T(8,128)(2,1)S(1)}, bf16[128,768]{1,0:T(8,128)(2,1)S(1)}, u32[]{:S(2)}, u32[]{:S(2)}) %collective-permute-start.1) | collective-permute-done | bytes 196640 | tf_op jit(solution)/shard_map/ppermute | solution.py:276
  16.1 0.7 %collective-permute-done.2.got = bf16[128,768]{1,0:T(8,128)(2,1)S(1)} collective-permute-done((bf16[128,768]{1,0:T(8,128)(2,1)S(1)}, bf16[128,768]{1,0:T(8,128)(2,1)S(1)}, u32[]{:S(2)}, u32[]{:S(2)}) %collective-permute-start.2) | collective-permute-done | bytes 196640 | tf_op jit(solution)/shard_map/ppermute | solution.py:278
  16.9 2.0 %collective-permute-start.6 = (bf16[88,768]{1,0:T(8,128)(2,1)S(1)}, bf16[88,768]{1,0:T(8,128)(2,1)S(1)}, u32[]{:S(2)}, u32[]{:S(2)}) collective-permute-start(bf16[88,768]{1,0:T(8,128)(2,1)S(1)} %get-tuple-element.25.refs_1_), channel_id=1, source_target_pairs={{0,2},{1,0},{3,1},{5,3},{7,5},{6,7},{4,6},{2,4},{8,10},{9,8},{11,9... | collective-permute-start | bytes 405512 | tf_op jit(solution)/shard_map/ppermute | solution.py:287
  19.0 1.8 %collective-permute-start.3 = (bf16[48,768]{1,0:T(8,128)(2,1)S(1)}, bf16[48,768]{1,0:T(8,128)(2,1)S(1)}, u32[]{:S(2)}, u32[]{:S(2)}) collective-permute-start(bf16[48,768]{1,0:T(8,128)(2,1)S(1)} %get-tuple-element.24.refs_0_), channel_id=1, source_target_pairs={{0,1},{1,3},{3,5},{5,7},{7,6},{6,4},{4,2},{2,0},{8,9},{9,11},{11,1... | collective-permute-start | bytes 221192 | tf_op jit(solution)/shard_map/ppermute | solution.py:287
  21.0 4.8 %collective-permute-done.3.refs_2_ = bf16[48,768]{1,0:T(8,128)(2,1)S(1)} collective-permute-done((bf16[48,768]{1,0:T(8,128)(2,1)S(1)}, bf16[48,768]{1,0:T(8,128)(2,1)S(1)}, u32[]{:S(2)}, u32[]{:S(2)}) %collective-permute-start.3) | collective-permute-done | bytes 73760 | tf_op jit(solution)/shard_map/ppermute | solution.py:287
  26.1 1.7 %collective-permute-start.10 = (bf16[88,768]{1,0:T(8,128)(2,1)S(1)}, bf16[88,768]{1,0:T(8,128)(2,1)S(1)}, u32[]{:S(2)}, u32[]{:S(2)}) collective-permute-start(bf16[88,768]{1,0:T(8,128)(2,1)S(1)} %collective-permute-done.6.refs_5_), channel_id=1, source_target_pairs={{0,2},{1,0},{3,1},{5,3},{7,5},{6,7},{4,6},{2,4},{8,10},{9,8},{11,9... | collective-permute-start | bytes 405512 | tf_op jit(solution)/shard_map/ppermute | solution.py:287
  27.8 0.3 collective-permute-start.8
  28.1 1.7 %collective-permute-start.9 = (bf16[48,768]{1,0:T(8,128)(2,1)S(1)}, bf16[48,768]{1,0:T(8,128)(2,1)S(1)}, u32[]{:S(2)}, u32[]{:S(2)}) collective-permute-start(bf16[48,768]{1,0:T(8,128)(2,1)S(1)} %collective-permute-done.5.refs_4_), channel_id=1, source_target_pairs={{0,2},{1,0},{3,1},{5,3},{7,5},{6,7},{4,6},{2,4},{8,10},{9,8},{11,9... | collective-permute-start | bytes 221192 | tf_op jit(solution)/shard_map/ppermute | solution.py:287
  29.8 1.0 %collective-permute-done.7.refs_6_ = bf16[48,768]{1,0:T(8,128)(2,1)S(1)} collective-permute-done((bf16[48,768]{1,0:T(8,128)(2,1)S(1)}, bf16[48,768]{1,0:T(8,128)(2,1)S(1)}, u32[]{:S(2)}, u32[]{:S(2)}) %collective-permute-start.7) | collective-permute-done | bytes 73760 | tf_op jit(solution)/shard_map/ppermute | solution.py:287
  30.9 1.4 %collective-permute-start.15 = (bf16[48,768]{1,0:T(8,128)(2,1)S(1)}, bf16[48,768]{1,0:T(8,128)(2,1)S(1)}, u32[]{:S(2)}, u32[]{:S(2)}) collective-permute-start(bf16[48,768]{1,0:T(8,128)(2,1)S(1)} %collective-permute-done.7.refs_6_), channel_id=1, source_target_pairs={{0,3},{1,5},{3,7},{5,6},{7,4},{6,2},{4,0},{2,1},{8,11},{9,13},{11,... | collective-permute-start | bytes 221192 | tf_op jit(solution)/shard_map/ppermute | solution.py:289
  32.2 1.6 %collective-permute-start.11 = (bf16[48,768]{1,0:T(8,128)(2,1)S(1)}, bf16[48,768]{1,0:T(8,128)(2,1)S(1)}, u32[]{:S(2)}, u32[]{:S(2)}) collective-permute-start(bf16[48,768]{1,0:T(8,128)(2,1)S(1)} %collective-permute-done.7.refs_6_), channel_id=1, source_target_pairs={{0,1},{1,3},{3,5},{5,7},{7,6},{6,4},{4,2},{2,0},{8,9},{9,11},{11,1... | collective-permute-start | bytes 221192 | tf_op jit(solution)/shard_map/ppermute | solution.py:287
  33.8 0.8 %collective-permute-start.13 = (bf16[48,768]{1,0:T(8,128)(2,1)S(1)}, bf16[48,768]{1,0:T(8,128)(2,1)S(1)}, u32[]{:S(2)}, u32[]{:S(2)}) collective-permute-start(bf16[48,768]{1,0:T(8,128)(2,1)S(1)} %collective-permute-done.9.refs_8_), channel_id=1, source_target_pairs={{0,2},{1,0},{3,1},{5,3},{7,5},{6,7},{4,6},{2,4},{8,10},{9,8},{11,9... | collective-permute-start | bytes 221192 | tf_op jit(solution)/shard_map/ppermute | solution.py:287
  34.7 2.3 %collective-permute-start.16 = (bf16[88,768]{1,0:T(8,128)(2,1)S(1)}, bf16[88,768]{1,0:T(8,128)(2,1)S(1)}, u32[]{:S(2)}, u32[]{:S(2)}) collective-permute-start(bf16[88,768]{1,0:T(8,128)(2,1)S(1)} %collective-permute-done.10.refs_9_), channel_id=1, source_target_pairs={{0,4},{1,2},{3,0},{5,1},{7,3},{6,5},{4,7},{2,6},{8,12},{9,10},{11,... | collective-permute-start | bytes 405512 | tf_op jit(solution)/shard_map/ppermute | solution.py:289
  37.1 1.4 %collective-permute-start.14 = (bf16[88,768]{1,0:T(8,128)(2,1)S(1)}, bf16[88,768]{1,0:T(8,128)(2,1)S(1)}, u32[]{:S(2)}, u32[]{:S(2)}) collective-permute-start(bf16[88,768]{1,0:T(8,128)(2,1)S(1)} %collective-permute-done.10.refs_9_), channel_id=1, source_target_pairs={{0,2},{1,0},{3,1},{5,3},{7,5},{6,7},{4,6},{2,4},{8,10},{9,8},{11,9... | collective-permute-start | bytes 405512 | tf_op jit(solution)/shard_map/ppermute | solution.py:287
  38.5 0.6 %collective-permute-start.12 = (bf16[88,768]{1,0:T(8,128)(2,1)S(1)}, bf16[88,768]{1,0:T(8,128)(2,1)S(1)}, u32[]{:S(2)}, u32[]{:S(2)}) collective-permute-start(bf16[88,768]{1,0:T(8,128)(2,1)S(1)} %collective-permute-done.8.refs_7_), channel_id=1, source_target_pairs={{0,1},{1,3},{3,5},{5,7},{7,6},{6,4},{4,2},{2,0},{8,9},{9,11},{11,1... | collective-permute-start | bytes 405512 | tf_op jit(solution)/shard_map/ppermute | solution.py:287
  39.1 2.7 %project.3 = (bf16[128,768]{1,0:T(8,128)(2,1)}, f32[128,1]{1,0:T(8,128)S(1)}, f32[2,128,1]{2,1,0:T(8,128)S(1)}, f32[144,1536]{1,0:T(8,128)S(1)}) custom-call(bf16[48,768]{1,0:T(8,128)(2,1)S(1)} %get-tuple-element.24.refs_0_, bf16[88,768]{1,0:T(8,128)(2,1)S(1)} %get-tuple-element.25.refs_1_, bf16[48,768]{1,0:T(8,128)(2,1)S(1)} %collective-permute-done.3.refs_2_, ...), custom_call_target="tpu_custom_call" | custom-call | flops 1698693120 | tf_op jit(solution)/shard_map/project/pallas_call | solution.py:235
  41.8 0.7 %project.4 = (f32[2,128,1]{2,1,0:T(8,128)S(1)}, f32[144,1536]{1,0:T(8,128)S(1)}) custom-call(bf16[48,768]{1,0:T(8,128)(2,1)S(1)} %collective-permute-done.15.refs_0_, bf16[88,768]{1,0:T(8,128)(2,1)S(1)} %collective-permute-done.16.refs_1_, bf16[6144,1536]{1,0:T(8,128)(2,1)S(1)} %copy-done, ...), custom_call_target="tpu_custom_call", output_to_operand_aliasing={{0}: (4, {}), {1}: (5, {})} | custom-call | flops 339738624 | tf_op jit(solution)/shard_map/project/pallas_call | solution.py:235
  42.8 0.7 %collective-permute-done.12.refs_1_ = bf16[88,768]{1,0:T(8,128)(2,1)S(1)} collective-permute-done((bf16[88,768]{1,0:T(8,128)(2,1)S(1)}, bf16[88,768]{1,0:T(8,128)(2,1)S(1)}, u32[]{:S(2)}, u32[]{:S(2)}) %collective-permute-start.12) | collective-permute-done | bytes 135200 | tf_op jit(solution)/shard_map/ppermute | solution.py:287
  43.5 1.7 %project.5 = bf16[128,1536]{1,0:T(8,128)(2,1)} custom-call(bf16[48,768]{1,0:T(8,128)(2,1)S(1)} %collective-permute-done.11.refs_0_, bf16[88,768]{1,0:T(8,128)(2,1)S(1)} %collective-permute-done.12.refs_1_, bf16[48,768]{1,0:T(8,128)(2,1)S(1)} %collective-permute-done.13.refs_2_, bf16[88,768]{1,0:T(8,128)(2,1)S(1)} %collective-permute-done.14.refs_3_, ...), custom_call_target="tpu_custom_call" | custom-call | flops 679477248 | tf_op jit(solution)/shard_map/project/pallas_call | solution.py:235
  (25 shorter events, 1.2 us)
Async XLA Ops:
  0.6 6.2 %copy-start.2 = (bf16[768]{0:T(1024)(128)(2,1)S(1)}, bf16[768]{0:T(1024)(128)(2,1)}, u32[]{:S(2)}) copy-start(bf16[768]{0:T(1024)(128)(2,1)} %param.8) | copy-start | bytes 4612
  0.6 38.5 %copy-start = (bf16[6144,1536]{1,0:T(8,128)(2,1)S(1)}, bf16[6144,1536]{1,0:T(8,128)(2,1)}, u32[]{:S(2)}) copy-start(bf16[6144,1536]{1,0:T(8,128)(2,1)} %refs_4_.1) | copy-start | bytes 56623108
  6.3 9.8 %copy-start.1 = (bf16[128,768]{1,0:T(8,128)(2,1)S(1)}, bf16[128,768]{1,0:T(8,128)(2,1)}, u32[]{:S(2)}) copy-start(bf16[128,768]{1,0:T(8,128)(2,1)} %param.7) | copy-start | bytes 589828
  6.3 1.6 %collective-permute-start = (bf16[1,128,768]{2,1,0:T(8,128)(2,1)S(1)}, bf16[1,128,768]{2,1,0:T(8,128)(2,1)S(1)}, u32[]{:S(2)}, u32[]{:S(2)}) collective-permute-start(bf16[1,128,768]{2,1,0:T(8,128)(2,1)S(1)} %get-tuple-element.18), channel_id=1, source_target_pairs={{0,8},{8,0},{16,24},{24,16},{1,9},{9,1},{17,25},{25,17},{2,10},{10... | collective-permute-start | bytes 589832 | tf_op jit(solution)/shard_map/ppermute | solution.py:270
  7.9 8.2 %collective-permute-start.1 = (bf16[128,768]{1,0:T(8,128)(2,1)S(1)}, bf16[128,768]{1,0:T(8,128)(2,1)S(1)}, u32[]{:S(2)}, u32[]{:S(2)}) collective-permute-start(bf16[128,768]{1,0:T(8,128)(2,1)S(1)} %bitcast.5), channel_id=1, source_target_pairs={{0,16},{8,24},{16,0},{24,8},{1,17},{9,25},{17,1},{25,9},{2,18},{10... | collective-permute-start | bytes 589832 | tf_op jit(solution)/shard_map/ppermute | solution.py:276
  15.3 1.5 %collective-permute-start.2 = (bf16[128,768]{1,0:T(8,128)(2,1)S(1)}, bf16[128,768]{1,0:T(8,128)(2,1)S(1)}, u32[]{:S(2)}, u32[]{:S(2)}) collective-permute-start(bf16[128,768]{1,0:T(8,128)(2,1)S(1)} %bitcast.4), channel_id=1, source_target_pairs={{0,8},{8,0},{16,24},{24,16},{1,9},{9,1},{17,25},{25,17},{2,10},{10... | collective-permute-start | bytes 589832 | tf_op jit(solution)/shard_map/ppermute | solution.py:278
  16.9 9.2 %collective-permute-start.6 = (bf16[88,768]{1,0:T(8,128)(2,1)S(1)}, bf16[88,768]{1,0:T(8,128)(2,1)S(1)}, u32[]{:S(2)}, u32[]{:S(2)}) collective-permute-start(bf16[88,768]{1,0:T(8,128)(2,1)S(1)} %get-tuple-element.25.refs_1_), channel_id=1, source_target_pairs={{0,2},{1,0},{3,1},{5,3},{7,5},{6,7},{4,6},{2,4},{8,10},{9,8},{11,9... | collective-permute-start | bytes 405512 | tf_op jit(solution)/shard_map/ppermute | solution.py:287
  18.9 9.0 %collective-permute-start.4 = (bf16[88,768]{1,0:T(8,128)(2,1)S(1)}, bf16[88,768]{1,0:T(8,128)(2,1)S(1)}, u32[]{:S(2)}, u32[]{:S(2)}) collective-permute-start(bf16[88,768]{1,0:T(8,128)(2,1)S(1)} %get-tuple-element.25.refs_1_), channel_id=1, source_target_pairs={{0,1},{1,3},{3,5},{5,7},{7,6},{6,4},{4,2},{2,0},{8,9},{9,11},{11,1... | collective-permute-start | bytes 405512 | tf_op jit(solution)/shard_map/ppermute | solution.py:287
  19.0 6.8 %collective-permute-start.3 = (bf16[48,768]{1,0:T(8,128)(2,1)S(1)}, bf16[48,768]{1,0:T(8,128)(2,1)S(1)}, u32[]{:S(2)}, u32[]{:S(2)}) collective-permute-start(bf16[48,768]{1,0:T(8,128)(2,1)S(1)} %get-tuple-element.24.refs_0_), channel_id=1, source_target_pairs={{0,1},{1,3},{3,5},{5,7},{7,6},{6,4},{4,2},{2,0},{8,9},{9,11},{11,1... | collective-permute-start | bytes 221192 | tf_op jit(solution)/shard_map/ppermute | solution.py:287
  20.8 7.3 %collective-permute-start.5 = (bf16[48,768]{1,0:T(8,128)(2,1)S(1)}, bf16[48,768]{1,0:T(8,128)(2,1)S(1)}, u32[]{:S(2)}, u32[]{:S(2)}) collective-permute-start(bf16[48,768]{1,0:T(8,128)(2,1)S(1)} %get-tuple-element.24.refs_0_), channel_id=1, source_target_pairs={{0,2},{1,0},{3,1},{5,3},{7,5},{6,7},{4,6},{2,4},{8,10},{9,8},{11,9... | collective-permute-start | bytes 221192 | tf_op jit(solution)/shard_map/ppermute | solution.py:287
  25.8 5.1 %collective-permute-start.7 = (bf16[48,768]{1,0:T(8,128)(2,1)S(1)}, bf16[48,768]{1,0:T(8,128)(2,1)S(1)}, u32[]{:S(2)}, u32[]{:S(2)}) collective-permute-start(bf16[48,768]{1,0:T(8,128)(2,1)S(1)} %collective-permute-done.3.refs_2_), channel_id=1, source_target_pairs={{0,1},{1,3},{3,5},{5,7},{7,6},{6,4},{4,2},{2,0},{8,9},{9,11},{11,1... | collective-permute-start | bytes 221192 | tf_op jit(solution)/shard_map/ppermute | solution.py:287
  26.1 8.6 %collective-permute-start.10 = (bf16[88,768]{1,0:T(8,128)(2,1)S(1)}, bf16[88,768]{1,0:T(8,128)(2,1)S(1)}, u32[]{:S(2)}, u32[]{:S(2)}) collective-permute-start(bf16[88,768]{1,0:T(8,128)(2,1)S(1)} %collective-permute-done.6.refs_5_), channel_id=1, source_target_pairs={{0,2},{1,0},{3,1},{5,3},{7,5},{6,7},{4,6},{2,4},{8,10},{9,8},{11,9... | collective-permute-start | bytes 405512 | tf_op jit(solution)/shard_map/ppermute | solution.py:287
  27.8 10.7 %collective-permute-start.8 = (bf16[88,768]{1,0:T(8,128)(2,1)S(1)}, bf16[88,768]{1,0:T(8,128)(2,1)S(1)}, u32[]{:S(2)}, u32[]{:S(2)}) collective-permute-start(bf16[88,768]{1,0:T(8,128)(2,1)S(1)} %collective-permute-done.4.refs_3_), channel_id=1, source_target_pairs={{0,1},{1,3},{3,5},{5,7},{7,6},{6,4},{4,2},{2,0},{8,9},{9,11},{11,1... | collective-permute-start | bytes 405512 | tf_op jit(solution)/shard_map/ppermute | solution.py:287
  28.1 5.7 %collective-permute-start.9 = (bf16[48,768]{1,0:T(8,128)(2,1)S(1)}, bf16[48,768]{1,0:T(8,128)(2,1)S(1)}, u32[]{:S(2)}, u32[]{:S(2)}) collective-permute-start(bf16[48,768]{1,0:T(8,128)(2,1)S(1)} %collective-permute-done.5.refs_4_), channel_id=1, source_target_pairs={{0,2},{1,0},{3,1},{5,3},{7,5},{6,7},{4,6},{2,4},{8,10},{9,8},{11,9... | collective-permute-start | bytes 221192 | tf_op jit(solution)/shard_map/ppermute | solution.py:287
  30.9 6.2 %collective-permute-start.15 = (bf16[48,768]{1,0:T(8,128)(2,1)S(1)}, bf16[48,768]{1,0:T(8,128)(2,1)S(1)}, u32[]{:S(2)}, u32[]{:S(2)}) collective-permute-start(bf16[48,768]{1,0:T(8,128)(2,1)S(1)} %collective-permute-done.7.refs_6_), channel_id=1, source_target_pairs={{0,3},{1,5},{3,7},{5,6},{7,4},{6,2},{4,0},{2,1},{8,11},{9,13},{11,... | collective-permute-start | bytes 221192 | tf_op jit(solution)/shard_map/ppermute | solution.py:289
  32.2 10.3 %collective-permute-start.11 = (bf16[48,768]{1,0:T(8,128)(2,1)S(1)}, bf16[48,768]{1,0:T(8,128)(2,1)S(1)}, u32[]{:S(2)}, u32[]{:S(2)}) collective-permute-start(bf16[48,768]{1,0:T(8,128)(2,1)S(1)} %collective-permute-done.7.refs_6_), channel_id=1, source_target_pairs={{0,1},{1,3},{3,5},{5,7},{7,6},{6,4},{4,2},{2,0},{8,9},{9,11},{11,1... | collective-permute-start | bytes 221192 | tf_op jit(solution)/shard_map/ppermute | solution.py:287
  33.8 8.7 %collective-permute-start.13 = (bf16[48,768]{1,0:T(8,128)(2,1)S(1)}, bf16[48,768]{1,0:T(8,128)(2,1)S(1)}, u32[]{:S(2)}, u32[]{:S(2)}) collective-permute-start(bf16[48,768]{1,0:T(8,128)(2,1)S(1)} %collective-permute-done.9.refs_8_), channel_id=1, source_target_pairs={{0,2},{1,0},{3,1},{5,3},{7,5},{6,7},{4,6},{2,4},{8,10},{9,8},{11,9... | collective-permute-start | bytes 221192 | tf_op jit(solution)/shard_map/ppermute | solution.py:287
  34.7 7.2 %collective-permute-start.16 = (bf16[88,768]{1,0:T(8,128)(2,1)S(1)}, bf16[88,768]{1,0:T(8,128)(2,1)S(1)}, u32[]{:S(2)}, u32[]{:S(2)}) collective-permute-start(bf16[88,768]{1,0:T(8,128)(2,1)S(1)} %collective-permute-done.10.refs_9_), channel_id=1, source_target_pairs={{0,4},{1,2},{3,0},{5,1},{7,3},{6,5},{4,7},{2,6},{8,12},{9,10},{11,... | collective-permute-start | bytes 405512 | tf_op jit(solution)/shard_map/ppermute | solution.py:289
  37.1 5.7 %collective-permute-start.14 = (bf16[88,768]{1,0:T(8,128)(2,1)S(1)}, bf16[88,768]{1,0:T(8,128)(2,1)S(1)}, u32[]{:S(2)}, u32[]{:S(2)}) collective-permute-start(bf16[88,768]{1,0:T(8,128)(2,1)S(1)} %collective-permute-done.10.refs_9_), channel_id=1, source_target_pairs={{0,2},{1,0},{3,1},{5,3},{7,5},{6,7},{4,6},{2,4},{8,10},{9,8},{11,9... | collective-permute-start | bytes 405512 | tf_op jit(solution)/shard_map/ppermute | solution.py:287
  38.5 5.0 %collective-permute-start.12 = (bf16[88,768]{1,0:T(8,128)(2,1)S(1)}, bf16[88,768]{1,0:T(8,128)(2,1)S(1)}, u32[]{:S(2)}, u32[]{:S(2)}) collective-permute-start(bf16[88,768]{1,0:T(8,128)(2,1)S(1)} %collective-permute-done.8.refs_7_), channel_id=1, source_target_pairs={{0,1},{1,3},{3,5},{5,7},{7,6},{6,4},{4,2},{2,0},{8,9},{9,11},{11,1... | collective-permute-start | bytes 405512 | tf_op jit(solution)/shard_map/ppermute | solution.py:287
